TPU v7x, 32 devices: a whole 2x2x4 slice. The times are simulated.
32 devices in a mesh: dp: 2 (over core), ctx: 4 (over y, x), tensor: 4 (over z).
Axes of the slice: x: 2, y: 2, z: 4, core: 2. Of those that a mesh axis runs over, the one named last changes fastest.
Arguments:
- residual: bfloat16 [2, 4096, 1536], P('dp', 'ctx'), may hold values from -6 to 6
- pre_gain: float32 [1536], replicated, may hold values from 0.1 to 1.9
- gate_weight: bfloat16 [1536, 3072], P(None, 'tensor'), may hold values from -0.15625 to 0.15625
- input_weight: bfloat16 [1536, 3072], P(None, 'tensor'), may hold values from -0.15625 to 0.15625
- state_weight: bfloat16 [1536, 256], replicated, may hold values from -0.15625 to 0.15625
- step_weight: bfloat16 [1536, 48], P(None, 'tensor'), may hold values from -0.15625 to 0.15625
- input_kernel: bfloat16 [4, 3072], P(None, 'tensor'), may hold values from -3 to 3
- state_kernel: bfloat16 [4, 256], replicated, may hold values from -3 to 3
- step_bias: float32 [48], P('tensor'), may hold values from -4.5 to -2.5
- decay_log: float32 [48], P('tensor'), may hold values from -9.5 to 0.5
- skip_gain: float32 [48], P('tensor'), may hold values from 0.5 to 2
- norm_gain: float32 [3072], P('tensor'), may hold values from 0.1 to 1.9
- out_weight: bfloat16 [3072, 1536], P('tensor'), may hold values from -0.109375 to 0.109375
- cotangent: bfloat16 [2, 4096, 1536], P('dp', 'ctx'), may hold values from -6 to 6
Outputs:
- output: bfloat16 [2, 4096, 1536], P('dp', 'ctx', 'tensor')
- input_grad: float32 [2, 4096, 1536], P('dp', 'ctx', 'tensor')
- pre_gain_grad: float32 [1536], P('tensor')
- gate_weight_grad: float32 [1536, 3072], P(None, 'tensor')
- input_weight_grad: float32 [1536, 3072], P(None, 'tensor')
- state_weight_grad: float32 [1536, 256], P(None, 'tensor')
- step_weight_grad: float32 [1536, 48], P(None, 'tensor')
- input_kernel_grad: float32 [4, 3072], P(None, 'tensor')
- state_kernel_grad: float32 [4, 256], replicated
- step_bias_grad: float32 [48], P('tensor')
- decay_log_grad: float32 [48], P('tensor')
- skip_gain_grad: float32 [48], P('tensor')
- norm_gain_grad: float32 [3072], P('tensor')
- out_weight_grad: float32 [3072, 1536], P('tensor')
All inputs are finite; a program needn't handle non-finite values.
Results may differ from a plain program's by a relative error of at most 0.0024.
The roundings to bfloat16 on the way count: a program that leaves them out, or rounds other values in their place, can miss the bound.
Values may be sent and summed in bfloat16 or wider, within the bound.
No kernel may reach another device: no remote copies, remote signals or barrier semaphores. Data moves between devices by JAX's collectives and lax.ppermute only.
A program may use at most 192 MiB of HBM per device.

v0:
```python
import jax
import jax.numpy as jnp
from jax import lax
from jax.sharding import PartitionSpec as P

HEAD_DIM = 64
CONV = 4
GROUP = 256


epsilon = 1e-05
highest = lax.Precision.HIGHEST


def passed_along(value, axis, by):
    count = lax.axis_size(axis)
    pairs = [(i, i + by) for i in range(count) if 0 <= i + by < count]
    return lax.ppermute(value, axis, pairs)


def entering(part, axis, combine, identity, reverse):
    count = lax.axis_size(axis)
    place = lax.axis_index(axis)
    ahead = count - 1 - place if reverse else place
    gathered = jax.tree.map(lambda a: lax.all_gather(a, axis), part)
    state = jax.tree.map(lambda a, e: jnp.zeros_like(a) + jnp.asarray(e, a.dtype), part, identity)

    def one(lap, state):
        source = count - 1 - lap if reverse else lap
        return combine(
            state, jax.tree.map(lambda a: lax.dynamic_index_in_dim(a, source, 0, False), gathered)
        )

    return lax.fori_loop(0, ahead, one, state)


def silu_gate(value):
    return value * jax.nn.sigmoid(value)


def causal_conv(extended, kernel):
    span_rows = extended.shape[-2] - kernel.shape[0] + 1
    summed = kernel[0] * extended[..., 0:span_rows, :]
    for offset in range(1, kernel.shape[0]):
        summed = summed + kernel[offset] * extended[..., offset : offset + span_rows, :]
    return silu_gate(summed)


def ssd_block(carry_state, pieces):
    driven, b_block, c_block, decay_block = pieces
    cumulative = jnp.cumsum(decay_block, axis=0)
    block_size = decay_block.shape[0]
    row_index = lax.broadcasted_iota(jnp.int32, (block_size, block_size), 0)
    column_index = lax.broadcasted_iota(jnp.int32, (block_size, block_size), 1)
    causal = (row_index >= column_index)[:, :, None]
    log_gap = jnp.where(causal, cumulative[:, None, :] - cumulative[None, :, :], 0.0)
    scores = jnp.dot(c_block, b_block.T, precision=highest)
    mixing = jnp.where(causal, jnp.exp(log_gap), 0.0) * scores[:, :, None]
    inner_out = jnp.einsum("tsh,shp->thp", mixing, driven, precision=highest)
    carried = (
        jnp.einsum("tn,hpn->thp", c_block, carry_state, precision=highest)
        * jnp.exp(cumulative)[:, :, None]
    )
    tail_decay = jnp.exp(cumulative[-1][None, :] - cumulative)
    new_state = carry_state * jnp.exp(cumulative[-1])[:, None, None] + jnp.einsum(
        "sh,shp,sn->hpn", tail_decay, driven, b_block, precision=highest
    )
    return (new_state, inner_out + carried)


def ssd_scan(driven, b_rows, c_rows, decay_rates, start_state):
    blocks = driven.shape[0] // GROUP
    pieces = (
        driven.reshape(blocks, GROUP, driven.shape[1], driven.shape[2]),
        b_rows.reshape(blocks, GROUP, b_rows.shape[1]),
        c_rows.reshape(blocks, GROUP, c_rows.shape[1]),
        decay_rates.reshape(blocks, GROUP, decay_rates.shape[1]),
    )
    final_state, outputs = lax.scan(jax.checkpoint(ssd_block), start_state, pieces)
    return (final_state, outputs.reshape(driven.shape))


def local_part(value_ext, state_rows, step_raw, value_kernel, step_bias, decay_log, skip_gain):
    heads = step_raw.shape[1]
    state_size = state_rows.shape[1] // 2
    conv_values = causal_conv(value_ext, value_kernel)
    conv_values = conv_values.reshape(conv_values.shape[0], heads, -1)
    step_size = jax.nn.softplus(step_raw + step_bias)
    decay_rates = -step_size * jnp.exp(decay_log)
    zero_state = jnp.zeros((heads, conv_values.shape[2], state_size), jnp.float32)
    local_state, mixed = ssd_scan(
        conv_values * step_size[:, :, None],
        state_rows[:, :state_size],
        state_rows[:, state_size:],
        decay_rates,
        zero_state,
    )
    mixed = mixed + skip_gain[:, None] * conv_values
    return (mixed.reshape(mixed.shape[0], -1), local_state, jnp.cumsum(decay_rates, axis=0))


def mixer_local(
    value_ext, state_rows, step_raw, value_kernel, step_bias, decay_log, skip_gain, start_state
):
    base_out, local_state, cumulative = local_part(
        value_ext, state_rows, step_raw, value_kernel, step_bias, decay_log, skip_gain
    )
    state_size = state_rows.shape[1] // 2
    carried = (
        jnp.einsum("tn,hpn->thp", state_rows[:, state_size:], start_state, precision=highest)
        * jnp.exp(cumulative)[:, :, None]
    )
    mixed = base_out + carried.reshape(base_out.shape)
    end_state = local_state + jnp.exp(cumulative[-1])[:, None, None] * start_state
    return (mixed, end_state)


def mixer_back(
    value_ext,
    state_rows,
    step_raw,
    start_state,
    grad_mixed,
    later_grad,
    value_kernel,
    step_bias,
    decay_log,
    skip_gain,
):
    unused_out, pullback = jax.vjp(
        mixer_local,
        value_ext,
        state_rows,
        step_raw,
        value_kernel,
        step_bias,
        decay_log,
        skip_gain,
        start_state,
    )
    return pullback((grad_mixed, later_grad))


def chain_step(earlier, later):
    return (earlier[0] * later[0], later[0][..., None, None] * earlier[1] + later[1])


def per_device(
    residual,
    pre_gain,
    gate_weight,
    input_weight,
    state_weight,
    step_weight,
    input_kernel,
    state_kernel,
    step_bias,
    decay_log,
    skip_gain,
    norm_gain,
    out_weight,
    cotangent,
):
    seq_count, tok_count, width = residual.shape
    row_count = seq_count * tok_count
    tensor_index = lax.axis_index("tensor")
    tensor_size = lax.axis_size("tensor")
    width_part = width // tensor_size
    inner_part = gate_weight.shape[1]
    inner_total = inner_part * tensor_size
    state_size = state_weight.shape[1] // 2
    state_part = 2 * state_size // tensor_size
    margin = CONV - 1
    contract_first = (((0,), (0,)), ((), ()))
    contract_last = (((1,), (1,)), ((), ()))
    flat_input = residual.reshape(row_count, width).astype(jnp.float32)
    scaling = lax.rsqrt(jnp.mean(flat_input * flat_input, axis=-1, keepdims=True) + epsilon)
    normed = (flat_input * scaling * pre_gain).astype(jnp.bfloat16)
    gate_in = jnp.dot(normed, gate_weight, preferred_element_type=jnp.float32)
    value_in = (
        jnp.dot(normed, input_weight, preferred_element_type=jnp.float32)
        .astype(jnp.bfloat16)
        .reshape(seq_count, tok_count, inner_part)
    )
    state_in = (
        jnp.dot(normed, state_weight, preferred_element_type=jnp.float32)
        .astype(jnp.bfloat16)
        .reshape(seq_count, tok_count, 2 * state_size)
    )
    step_raw = jnp.dot(normed, step_weight, preferred_element_type=jnp.float32).reshape(
        seq_count, tok_count, -1
    )
    rim_send = jnp.concatenate(
        [value_in[:, tok_count - margin :], state_in[:, tok_count - margin :]], axis=2
    )
    rim_recv = passed_along(rim_send, "ctx", 1)
    value_ext = jnp.concatenate([rim_recv[:, :, :inner_part], value_in], axis=1).astype(jnp.float32)
    state_ext = jnp.concatenate([rim_recv[:, :, inner_part:], state_in], axis=1).astype(jnp.float32)
    value_kernel = input_kernel.astype(jnp.float32)
    state_taps = state_kernel.astype(jnp.float32)
    state_rows, state_pullback = jax.vjp(causal_conv, state_ext, state_taps)
    base_out, local_state, cumulative = jax.vmap(
        local_part, in_axes=(0, 0, 0, None, None, None, None)
    )(value_ext, state_rows, step_raw, value_kernel, step_bias, decay_log, skip_gain)
    decay_total = jnp.exp(cumulative[:, -1])
    identity = (jnp.ones_like(decay_total), jnp.zeros_like(local_state))
    start_state = entering((decay_total, local_state), "ctx", chain_step, identity, False)[1]
    entry_decay = jnp.exp(cumulative)
    carried = (
        jnp.einsum("stn,shpn->sthp", state_rows[:, :, state_size:], start_state, precision=highest)
        * entry_decay[..., None]
    )
    mixed = (base_out + carried.reshape(seq_count, tok_count, inner_part)).reshape(
        row_count, inner_part
    )
    gate_sig = jax.nn.sigmoid(gate_in)
    gated = mixed * gate_in * gate_sig
    square_sum = lax.psum(jnp.sum(gated * gated, axis=-1), "tensor")
    rms_inv = lax.rsqrt(square_sum[:, None] / inner_total + epsilon)
    normed_out = (gated * rms_inv * norm_gain).astype(jnp.bfloat16)
    partial_out = jnp.dot(normed_out, out_weight, preferred_element_type=jnp.float32)
    branch = lax.psum_scatter(partial_out, "tensor", scatter_dimension=1, tiled=True)
    resid_part = lax.dynamic_slice_in_dim(flat_input, tensor_index * width_part, width_part, 1)
    output = (resid_part + branch).astype(jnp.bfloat16).reshape(seq_count, tok_count, width_part)
    grad_out = cotangent.reshape(row_count, width)
    out_weight_grad = lax.dot_general(
        normed_out, grad_out, contract_first, preferred_element_type=jnp.float32
    )
    grad_normed = lax.dot_general(
        grad_out, out_weight, contract_last, preferred_element_type=jnp.float32
    )
    norm_gain_grad = jnp.sum(grad_normed * gated * rms_inv, axis=0)
    norm_total = lax.psum(jnp.sum(grad_normed * norm_gain * gated, axis=-1), "tensor")
    rms_cube = rms_inv * rms_inv * rms_inv
    grad_gated = (
        rms_inv * norm_gain * grad_normed - gated * rms_cube * norm_total[:, None] / inner_total
    )
    grad_mixed = grad_gated * gate_in * gate_sig
    grad_gate = (grad_gated * mixed * gate_sig * (1.0 + gate_in * (1.0 - gate_sig))).astype(
        jnp.bfloat16
    )
    grad_mixed_seq = grad_mixed.reshape(seq_count, tok_count, inner_part)
    grad_heads = grad_mixed_seq.reshape(seq_count, tok_count, -1, HEAD_DIM)
    direct = jnp.einsum(
        "sthp,stn,sth->shpn",
        grad_heads,
        state_rows[:, :, state_size:],
        entry_decay,
        precision=highest,
    )
    later_grad = entering((decay_total, direct), "ctx", chain_step, identity, True)[1]
    mixer_grads = jax.vmap(mixer_back, in_axes=(0, 0, 0, 0, 0, 0, None, None, None, None))(
        value_ext,
        state_rows,
        step_raw,
        start_state,
        grad_mixed_seq,
        later_grad,
        value_kernel,
        step_bias,
        decay_log,
        skip_gain,
    )
    value_ext_grad = mixer_grads[0]
    state_rows_grad = lax.psum(mixer_grads[1], "tensor")
    step_grad = mixer_grads[2].astype(jnp.bfloat16).reshape(row_count, -1)
    kernel_value_grad = jnp.sum(mixer_grads[3], axis=0)
    step_bias_grad = jnp.sum(mixer_grads[4], axis=0)
    decay_log_grad = jnp.sum(mixer_grads[5], axis=0)
    skip_gain_grad = jnp.sum(mixer_grads[6], axis=0)
    state_ext_grad, kernel_state_grad = state_pullback(state_rows_grad)
    rim_back_send = jnp.concatenate(
        [value_ext_grad[:, :margin], state_ext_grad[:, :margin]], axis=2
    )
    rim_back = passed_along(rim_back_send, "ctx", -1)
    value_grad = jnp.concatenate(
        [
            value_ext_grad[:, margin:tok_count],
            value_ext_grad[:, tok_count:] + rim_back[:, :, :inner_part],
        ],
        axis=1,
    )
    value_grad = value_grad.astype(jnp.bfloat16).reshape(row_count, inner_part)
    state_grad = jnp.concatenate(
        [
            state_ext_grad[:, margin:tok_count],
            state_ext_grad[:, tok_count:] + rim_back[:, :, inner_part:],
        ],
        axis=1,
    )
    state_grad = state_grad.astype(jnp.bfloat16).reshape(row_count, 2 * state_size)
    state_quarter = lax.dynamic_slice_in_dim(state_grad, tensor_index * state_part, state_part, 1)
    weight_quarter = lax.dynamic_slice_in_dim(
        state_weight, tensor_index * state_part, state_part, 1
    )
    input_partial = lax.dot_general(
        grad_gate, gate_weight, contract_last, preferred_element_type=jnp.float32
    )
    input_partial = input_partial + lax.dot_general(
        value_grad, input_weight, contract_last, preferred_element_type=jnp.float32
    )
    input_partial = input_partial + lax.dot_general(
        step_grad, step_weight, contract_last, preferred_element_type=jnp.float32
    )
    input_partial = input_partial + lax.dot_general(
        state_quarter, weight_quarter, contract_last, preferred_element_type=jnp.float32
    )
    normed_grad = lax.psum_scatter(input_partial, "tensor", scatter_dimension=1, tiled=True)
    gain_part = lax.dynamic_slice_in_dim(pre_gain, tensor_index * width_part, width_part, 0)
    row_total = lax.psum(jnp.sum(normed_grad * gain_part * resid_part, axis=-1), "tensor")
    grad_out_part = lax.dynamic_slice_in_dim(
        grad_out, tensor_index * width_part, width_part, 1
    ).astype(jnp.float32)
    scale_cube = scaling * scaling * scaling
    input_grad = (
        grad_out_part
        + scaling * gain_part * normed_grad
        - resid_part * scale_cube * row_total[:, None] / width
    )
    input_grad = input_grad.reshape(seq_count, tok_count, width_part)
    pre_gain_grad = jnp.sum(normed_grad * resid_part * scaling, axis=0)
    gate_weight_grad = lax.dot_general(
        normed, grad_gate, contract_first, preferred_element_type=jnp.float32
    )
    input_weight_grad = lax.dot_general(
        normed, value_grad, contract_first, preferred_element_type=jnp.float32
    )
    state_weight_grad = lax.dot_general(
        normed, state_quarter, contract_first, preferred_element_type=jnp.float32
    )
    step_weight_grad = lax.dot_general(
        normed, step_grad, contract_first, preferred_element_type=jnp.float32
    )
    summed = lax.psum(
        (
            pre_gain_grad,
            gate_weight_grad,
            input_weight_grad,
            state_weight_grad,
            step_weight_grad,
            kernel_value_grad,
            kernel_state_grad,
            step_bias_grad,
            decay_log_grad,
            skip_gain_grad,
            out_weight_grad,
            norm_gain_grad,
        ),
        ("dp", "ctx"),
    )
    final_out_grad = summed[10]
    final_gain_grad = summed[11]
    return (
        output,
        input_grad,
        summed[0],
        summed[1],
        summed[2],
        summed[3],
        summed[4],
        summed[5],
        summed[6],
        summed[7],
        summed[8],
        summed[9],
        final_gain_grad,
        final_out_grad,
    )


def solution(mesh):
    in_specs = (
        P("dp", "ctx", None),
        P(),
        P(None, "tensor"),
        P(None, "tensor"),
        P(),
        P(None, "tensor"),
        P(None, "tensor"),
        P(),
        P("tensor"),
        P("tensor"),
        P("tensor"),
        P("tensor"),
        P("tensor", None),
        P("dp", "ctx", None),
    )
    out_specs = (
        P("dp", "ctx", "tensor"),
        P("dp", "ctx", "tensor"),
        P("tensor"),
        P(None, "tensor"),
        P(None, "tensor"),
        P(None, "tensor"),
        P(None, "tensor"),
        P(None, "tensor"),
        P(),
        P("tensor"),
        P("tensor"),
        P("tensor"),
        P("tensor"),
        P("tensor", None),
    )
    return jax.shard_map(
        per_device, mesh=mesh, in_specs=in_specs, out_specs=out_specs, check_vma=False
    )
```

profile of v0, /device:TPU:0, one launch (start us, length us, event | category | flops | bytes accessed | tf_op | source)
XLA Modules:
  0.0 1093.7 jit_solution(12257228600141918255)
XLA Ops:
  10.6 4.4 fusion.141
  16.2 5.3 collective-permute-start
  25.9 3.6 fusion.130
  29.6 3.6 copy.350
  33.2 5.1 reshape.1219
  49.1 126.6 %while.77 = (s32[]{:T(128)}, f32[1,12,64,128]{3,2,1,0:T(8,128)S(1)}, f32[4,1,256,12,64]{2,0,4,3,1:T(4,128)}, f32[4,1,256,12]{2,0,3,1:T(4,128)}, f32[4,1,256,12,6...) while((s32[]{:T(128)}, ...), condition=%wide.region_4.5_spmd.clone, body=%wide.region_1.4_spmd.clone.sunk | while | flops 1313213440 | bytes 9809755 | solution.py:79
  57.2 4.9 fusion.289
  62.9 17.9 %dynamic_update_slice.61 = f32[4,1,256,12,64]{2,0,4,3,1:T(4,128)} dynamic-update-slice(f32[4,1,256,12,64]{2,0,4,3,1:T(4,128)} %get-tuple-element.1202, f32[1,1,256,12,64]{2,0,4,3,1:T(1,128)S(1)} %copy.512, s32[]{:T(128)S(6)} %copy.526, s32[]{:T(128)} %constant.188.clone.1..sunk.3, s32[]{:T(128)} %constant.188.clone.1..sunk.3, s32[]{:T(128)} %constant.188.clone.1..sunk.3, s32[]{:T(128)} %constant.188.clone.1..sunk.3) | dynamic-update-slice | bytes 1572868 | tf_op jit(solution)/shard_map/vmap()/while/body/jit(dynamic_update_index_in_dim)/dynamic_update_slice | solution.py:79
  88.8 4.9 fusion.289
  94.6 17.9 %dynamic_update_slice.61 = f32[4,1,256,12,64]{2,0,4,3,1:T(4,128)} dynamic-update-slice(f32[4,1,256,12,64]{2,0,4,3,1:T(4,128)} %get-tuple-element.1202, f32[1,1,256,12,64]{2,0,4,3,1:T(1,128)S(1)} %copy.512, s32[]{:T(128)S(6)} %copy.526, s32[]{:T(128)} %constant.188.clone.1..sunk.3, s32[]{:T(128)} %constant.188.clone.1..sunk.3, s32[]{:T(128)} %constant.188.clone.1..sunk.3, s32[]{:T(128)} %constant.188.clone.1..sunk.3) | dynamic-update-slice | bytes 1572868 | tf_op jit(solution)/shard_map/vmap()/while/body/jit(dynamic_update_index_in_dim)/dynamic_update_slice | solution.py:79
  120.5 4.9 fusion.289
  126.2 17.9 %dynamic_update_slice.61 = f32[4,1,256,12,64]{2,0,4,3,1:T(4,128)} dynamic-update-slice(f32[4,1,256,12,64]{2,0,4,3,1:T(4,128)} %get-tuple-element.1202, f32[1,1,256,12,64]{2,0,4,3,1:T(1,128)S(1)} %copy.512, s32[]{:T(128)S(6)} %copy.526, s32[]{:T(128)} %constant.188.clone.1..sunk.3, s32[]{:T(128)} %constant.188.clone.1..sunk.3, s32[]{:T(128)} %constant.188.clone.1..sunk.3, s32[]{:T(128)} %constant.188.clone.1..sunk.3) | dynamic-update-slice | bytes 1572868 | tf_op jit(solution)/shard_map/vmap()/while/body/jit(dynamic_update_index_in_dim)/dynamic_update_slice | solution.py:79
  152.2 4.9 fusion.289
  157.9 17.9 %dynamic_update_slice.61 = f32[4,1,256,12,64]{2,0,4,3,1:T(4,128)} dynamic-update-slice(f32[4,1,256,12,64]{2,0,4,3,1:T(4,128)} %get-tuple-element.1202, f32[1,1,256,12,64]{2,0,4,3,1:T(1,128)S(1)} %copy.512, s32[]{:T(128)S(6)} %copy.526, s32[]{:T(128)} %constant.188.clone.1..sunk.3, s32[]{:T(128)} %constant.188.clone.1..sunk.3, s32[]{:T(128)} %constant.188.clone.1..sunk.3, s32[]{:T(128)} %constant.188.clone.1..sunk.3) | dynamic-update-slice | bytes 1572868 | tf_op jit(solution)/shard_map/vmap()/while/body/jit(dynamic_update_index_in_dim)/dynamic_update_slice | solution.py:79
  184.1 8.1 all_gather.18
  203.8 5.3 transpose.166
  212.7 5.6 broadcast_multiply_fusion
  218.2 3.6 copy.361
  221.9 11.1 %multiply_reduce_fusion.9 = (f32[1024]{0:T(1024)S(1)}, f32[1024,768]{1,0:T(8,128)}, f32[1,1024,768]{2,1,0:T(8,128)}, f32[1024,768]{1,0:T(8,128)}) fusion(f32[1,1024,768]{2,1,0:T(8,128)} %copy.361, f32[1,1024,768]{2,1,0:T(8,128)} %copy.355, f32[1,1024,768]{2,1,0:T(8,128)} %get-tuple-element.876, f32[768]{0:T(1024)S(1)} %mul.821, ...), kind=kOutput, calls=%fused_computation.204 | convolution fusion | flops 2433219584 | bytes 24396800 | tf_op jit(solution)/shard_map/dot_general | solution.py:179
  233.0 12.0 %psum.112 = f32[1024]{0:T(1024)S(1)} all-reduce(f32[1024]{0:T(1024)S(1)} %get-tuple-element.868), channel_id=1, replica_groups=mesh['dp'=2,'ctx'=4,'tensor'=4] {'tensor'}, use_global_device_ids=true, to_apply=%region_10.11 | all-reduce | flops 1024 | bytes 8192 | tf_op jit(solution)/shard_map/psum | solution.py:218
  245.0 8.6 multiply_reduce_fusion.1
  253.5 8.3 psum.113
  261.8 8.9 fusion.119
  274.3 5.3 fusion.128
  280.1 20.5 %while.78 = (s32[]{:T(128)}, f32[1,12,64,128]{3,2,1,0:T(8,128)S(1)}, f32[4,1,12,64,128]{4,3,2,1,0:T(8,128)}, f32[4,1,256,12]{2,0,3,1:T(4,128)}, f32[4,1,256,12,6...) while((s32[]{:T(128)}, ...), condition=%wide.region_19.20_spmd.clone, body=%wide.region_16.19_spmd.clone.sunk | while | flops 302976032 | bytes 2702127 | solution.py:79
  300.6 5.1 reshape_reshape.2
  305.7 3.6 multiply_reduce_fusion.6
  310.4 4.9 mul.868
  318.9 7.8 convolution_bitcast_fusion.8
  326.8 4.6 fusion.199
  340.1 213.7 %while.76 = (s32[]{:T(128)}, f32[1,12,64,128]{3,2,1,0:T(8,128)S(1)}, f32[4,1,256,12,64]{2,0,4,3,1:T(4,128)}, f32[4,1,256,128]{3,2,0,1:T(8,128)}, f32[4,1,256,128...) while((s32[]{:T(128)}, ...), condition=%wide.region_31.32_spmd, body=%wide.region_20.31_spmd.sunk | while | flops 3034737664 | bytes 27044352 | solution.py:79
  348.8 4.4 fusion.272
  363.1 4.2 fusion.275
  368.1 17.9 %dynamic_update_slice.59 = f32[4,1,256,12,64]{2,0,4,3,1:T(4,128)} dynamic-update-slice(f32[4,1,256,12,64]{2,0,4,3,1:T(4,128)} %get-tuple-element.1316, f32[1,1,256,12,64]{2,0,4,3,1:T(1,128)S(1)} %copy.502, s32[]{:T(128)S(6)} %sub.310, s32[]{:T(128)} %constant.188.clone.1..sunk.2, s32[]{:T(128)} %constant.188.clone.1..sunk.2, s32[]{:T(128)} %constant.188.clone.1..sunk.2, s32[]{:T(128)} %constant.188.clone.1..sunk.2) | dynamic-update-slice | bytes 1572868 | tf_op jit(solution)/shard_map/vmap(transpose(jvp()))/while/body/jit(dynamic_update_index_in_dim)/dynamic_update_slice | solution.py:79
  402.1 4.4 fusion.272
  416.4 4.1 fusion.275
  421.4 17.9 %dynamic_update_slice.59 = f32[4,1,256,12,64]{2,0,4,3,1:T(4,128)} dynamic-update-slice(f32[4,1,256,12,64]{2,0,4,3,1:T(4,128)} %get-tuple-element.1316, f32[1,1,256,12,64]{2,0,4,3,1:T(1,128)S(1)} %copy.502, s32[]{:T(128)S(6)} %sub.310, s32[]{:T(128)} %constant.188.clone.1..sunk.2, s32[]{:T(128)} %constant.188.clone.1..sunk.2, s32[]{:T(128)} %constant.188.clone.1..sunk.2, s32[]{:T(128)} %constant.188.clone.1..sunk.2) | dynamic-update-slice | bytes 1572868 | tf_op jit(solution)/shard_map/vmap(transpose(jvp()))/while/body/jit(dynamic_update_index_in_dim)/dynamic_update_slice | solution.py:79
  455.4 4.4 fusion.272
  469.7 4.1 fusion.275
  474.7 17.9 %dynamic_update_slice.59 = f32[4,1,256,12,64]{2,0,4,3,1:T(4,128)} dynamic-update-slice(f32[4,1,256,12,64]{2,0,4,3,1:T(4,128)} %get-tuple-element.1316, f32[1,1,256,12,64]{2,0,4,3,1:T(1,128)S(1)} %copy.502, s32[]{:T(128)S(6)} %sub.310, s32[]{:T(128)} %constant.188.clone.1..sunk.2, s32[]{:T(128)} %constant.188.clone.1..sunk.2, s32[]{:T(128)} %constant.188.clone.1..sunk.2, s32[]{:T(128)} %constant.188.clone.1..sunk.2) | dynamic-update-slice | bytes 1572868 | tf_op jit(solution)/shard_map/vmap(transpose(jvp()))/while/body/jit(dynamic_update_index_in_dim)/dynamic_update_slice | solution.py:79
  508.7 4.4 fusion.272
  523.0 4.1 fusion.275
  528.0 17.9 %dynamic_update_slice.59 = f32[4,1,256,12,64]{2,0,4,3,1:T(4,128)} dynamic-update-slice(f32[4,1,256,12,64]{2,0,4,3,1:T(4,128)} %get-tuple-element.1316, f32[1,1,256,12,64]{2,0,4,3,1:T(1,128)S(1)} %copy.502, s32[]{:T(128)S(6)} %sub.310, s32[]{:T(128)} %constant.188.clone.1..sunk.2, s32[]{:T(128)} %constant.188.clone.1..sunk.2, s32[]{:T(128)} %constant.188.clone.1..sunk.2, s32[]{:T(128)} %constant.188.clone.1..sunk.2) | dynamic-update-slice | bytes 1572868 | tf_op jit(solution)/shard_map/vmap(transpose(jvp()))/while/body/jit(dynamic_update_index_in_dim)/dynamic_update_slice | solution.py:79
  556.0 14.9 %reduce-window.86 = f32[1,12,8,128]{3,2,1,0:T(8,128)S(1)} reduce-window(f32[1,12,8,128]{3,2,1,0:T(8,128)S(1)} %copy.381, f32[]{:T(128)} %constant.192.clone.1), window={size=1x1x1x128 pad=0_0x0_0x0_0x0_127}, to_apply=%region_36.37 | reduce-window | flops 1560576 | bytes 98308 | tf_op jit(solution)/shard_map/reduce-window.10
  571.0 5.2 transpose.172
  581.4 3.7 copy.373
  585.2 6.1 multiply_reduce_fusion.5
  591.3 3.9 broadcast_multiply_fusion.2
  595.3 4.8 multiply_reduce_fusion.7
  606.5 3.7 fusion.168
  610.1 19.7 %all-reduce.27.cloned.1.call-done = f32[1,1024,256]{2,1,0:T(8,128)} async-done(((f32[1,1024,256]{2,1,0:T(8,128)}), f32[1,1024,256]{2,1,0:T(8,128)}) %all-reduce.27.cloned.1.call-update) | async-done | bytes 1048592 | tf_op jit(solution)/shard_map/psum | solution.py:265
  635.0 3.8 collective-permute-done.1
  643.8 3.8 add_add_fusion
  649.5 6.3 fusion.182
  656.6 7.6 fusion.184
  664.1 4.4 fusion.120
  672.0 4.7 fusion.146
  682.4 75.5 %reduce-scatter.5.cloned.1.call-done = f32[1024,384]{1,0:T(8,128)} async-done(((f32[1024,1536]{1,0:T(8,128)}), f32[1024,384]{1,0:T(8,128)}) %reduce-scatter.5.cloned.1.call-update) | async-done | bytes 1572880 | tf_op jit(solution)/shard_map/reduce_scatter | solution.py:308
  760.4 27.3 %all-reduce.22 = (f32[384]{0:T(512)}, f32[4,768]{1,0:T(4,128)}, f32[4,256]{1,0:T(4,128)}, f32[12]{0:T(128)}, f32[12]{0:T(128)}, /*index=5*/f32[12]{0:T(128)}, f32[768]{0:T(1024)}) all-reduce(f32[384]{0:T(512)S(1)} %get-tuple-element.760, ...), channel_id=1, replica_groups=mesh['dp'=2,'ctx'=4,'tensor'=4] {'dp','ctx'}, use_global_device_ids=true, to_apply=%region_42.43 | all-reduce | flops 5284 | bytes 42272 | tf_op jit(solution)/shard_map/psum | solution.py:334
  787.7 11.7 %psum.115 = f32[1024]{0:T(1024)S(1)} all-reduce(f32[1024]{0:T(1024)S(1)} %get-tuple-element.761), channel_id=1, replica_groups=mesh['dp'=2,'ctx'=4,'tensor'=4] {'tensor'}, use_global_device_ids=true, to_apply=%region_40.41 | all-reduce | flops 1024 | bytes 8192 | tf_op jit(solution)/shard_map/psum | solution.py:310
  799.4 72.4 %reduce-scatter.3.cloned.1.call-done = f32[1024,384]{1,0:T(8,128)} async-done(((f32[1024,1536]{1,0:T(8,128)}), f32[1024,384]{1,0:T(8,128)}) %reduce-scatter.3.cloned.1.call-update) | async-done | bytes 1572880 | tf_op jit(solution)/shard_map/reduce_scatter | solution.py:222
  871.8 4.1 fusion.133
  875.9 198.9 %all-reduce.29.cloned.1.call-done = (f32[1536,768]{1,0:T(8,128)}, f32[1536,768]{1,0:T(8,128)}, f32[1536,64]{0,1:T(8,128)}, f32[1536,12]{0,1:T(8,128)}, f32[768,1536]{1,0:T(8,128)}) async-done(((f32[1536,768]{1,0:T(8,128)}, f32[1536,768]{1,0:T(8,128)}, f32[1536,64]{0,1:T(8,128)}, f32[1536,12]{0,1:T(8,128)}, f32[768,1536]{1,0:T(8,128)}), (f32[1536,768]{1,0:T(8,128)}, f32[1536,768]{1,0:T(8,128)}, ...) | async-done | bytes 14622736 | tf_op jit(solution)/shard_map/psum | solution.py:334
  1074.8 5.2 copy.585
  (666 shorter events, 270.3 us)
Async XLA Ops:
  7.2 214.7 %copy-start = (bf16[1536,768]{1,0:T(8,128)(2,1)S(1)}, bf16[1536,768]{1,0:T(8,128)(2,1)}, u32[]{:S(2)}) copy-start(bf16[1536,768]{1,0:T(8,128)(2,1)} %param.26) | copy-start | bytes 7077892
  7.2 205.4 %all-gather.5.cloned.1.call-start = ((), (), s32[]{:S(2)}) async-start(), calls=%async_computation.5 | async-start | bytes 1966080 | tf_op jit(solution)/shard_map/all_gather | solution.py:25
  10.6 211.3 %copy-start.52 = (f32[1024]{0:T(1024)}, f32[1024]{0:T(1024)S(1)}, u32[]{:S(2)}) copy-start(f32[1024]{0:T(1024)S(1)} %get-tuple-element.906) | copy-start | bytes 12292
  15.1 6.5 copy-start.85
  15.1 6.5 copy-start.75
  15.1 6.5 copy-start.74
  15.1 6.5 copy-start.50
  15.1 6.5 copy-start.84
  16.2 7.9 collective-permute-start
  21.6 21.5 %copy-start.66 = (f32[1,256]{1,0:T(1,128)}, f32[1,256]{1,0:T(1,128)S(1)}, u32[]{:S(2)}) copy-start(f32[1,256]{1,0:T(1,128)S(1)} %get-tuple-element.909) | copy-start | bytes 3076
  21.7 21.5 %copy-start.68 = (f32[1,256]{1,0:T(1,128)}, f32[1,256]{1,0:T(1,128)S(1)}, u32[]{:S(2)}) copy-start(f32[1,256]{1,0:T(1,128)S(1)} %get-tuple-element.910) | copy-start | bytes 3076
  21.7 21.5 %copy-start.70 = (f32[1,256]{1,0:T(1,128)}, f32[1,256]{1,0:T(1,128)S(1)}, u32[]{:S(2)}) copy-start(f32[1,256]{1,0:T(1,128)S(1)} %get-tuple-element.911) | copy-start | bytes 3076
  21.7 21.5 %copy-start.72 = (f32[1,256]{1,0:T(1,128)}, f32[1,256]{1,0:T(1,128)S(1)}, u32[]{:S(2)}) copy-start(f32[1,256]{1,0:T(1,128)S(1)} %get-tuple-element.912) | copy-start | bytes 3076
  23.4 6.2 copy-start.38
  23.4 6.2 copy-start.40
  23.4 6.1 copy-start.54
  23.4 6.1 copy-start.56
  23.4 6.1 copy-start.58
  23.4 6.1 copy-start.60
  51.6 5.6 copy-start.36
  83.3 5.6 copy-start.36
  114.9 5.6 copy-start.36
  146.6 5.6 copy-start.36
  175.8 16.6 %copy-start.79 = (f32[12]{0:T(128)S(1)}, f32[12]{0:T(128)}, u32[]{:S(2)}) copy-start(f32[12]{0:T(128)} %param.34) | copy-start | bytes 148
  176.5 154.8 %all-gather.7.cloned.1.call-start = ((), (), s32[]{:S(2)}) async-start(), calls=%async_computation.6 | async-start | bytes 1966080 | tf_op jit(solution)/shard_map/all_gather | solution.py:25
  192.5 29.4 %copy-start.64 = (f32[768]{0:T(1024)}, f32[768]{0:T(1024)S(1)}, u32[]{:S(2)}) copy-start(f32[768]{0:T(1024)S(1)} %mul.821) | copy-start | bytes 9220
  221.9 23.0 %copy-start.43 = (f32[768]{0:T(1024)S(1)}, f32[768]{0:T(1024)}, u32[]{:S(2)}) copy-start(f32[768]{0:T(1024)} %param.35) | copy-start | bytes 9220
  244.9 16.9 %copy-start.41 = (f32[1024]{0:T(1024)}, f32[1024]{0:T(1024)S(1)}, u32[]{:S(2)}) copy-start(f32[1024]{0:T(1024)S(1)} %get-tuple-element.908) | copy-start | bytes 12292
  279.7 350.2 %all-reduce.27.cloned.1.call-start = ((), (), s32[]{:S(2)}) async-start(), calls=%async_computation.3 | async-start | bytes 2097152 | tf_op jit(solution)/shard_map/psum | solution.py:265
  318.9 7.9 copy-start.32
  347.7 5.5 copy-start.21
  348.8 4.4 copy-start.35
  401.0 5.5 copy-start.21
  402.1 4.4 copy-start.35
  454.3 5.5 copy-start.21
  455.4 4.4 copy-start.35
  507.6 5.5 copy-start.21
  508.7 4.4 copy-start.35
  579.0 179.0 %reduce-scatter.5.cloned.1.call-start = ((), (), s32[]{:S(2)}) async-start(), calls=%async_computation.4 | async-start | bytes 7864320 | tf_op jit(solution)/shard_map/reduce_scatter | solution.py:308
  585.1 6.1 copy-start.55
  585.1 6.1 copy-start.57
  585.1 6.1 copy-start.59
  585.2 6.1 copy-start.61
  595.3 6.3 copy-start.6
  595.3 4.8 copy-start.45
  606.4 23.4 %copy-start.5 = (f32[1,1027,256]{2,1,0:T(8,128)S(1)}, f32[1,1027,256]{2,1,0:T(8,128)}, u32[]{:S(2)}) copy-start(f32[1,1027,256]{2,1,0:T(8,128)} %copy-done.4) | copy-start | bytes 3154948
  606.5 23.4 %copy-start.26 = (f32[1,1024,256]{2,1,0:T(8,128)S(1)}, f32[1,1024,256]{2,1,0:T(8,128)}, u32[]{:S(2)}) copy-start(f32[1,1024,256]{2,1,0:T(8,128)} %get-tuple-element.874) | copy-start | bytes 3145732
  632.0 6.8 copy-start.13
  632.4 6.4 copy-start.9
  632.4 6.4 copy-start.11
  632.7 6.1 copy-start.7
  632.7 6.0 collective-permute-start.1
  635.0 6.6 copy-start.28
  638.9 4.6 slice-start.3
  647.7 224.1 %reduce-scatter.3.cloned.1.call-start = ((), (), s32[]{:S(2)}) async-start(), calls=%async_computation.2 | async-start | bytes 7864320 | tf_op jit(solution)/shard_map/reduce_scatter | solution.py:222
  655.9 418.9 %all-reduce.29.cloned.1.call-start = ((), (), s32[]{:S(2)}) async-start(), calls=%async_computation.7 | async-start | bytes 29294592 | tf_op jit(solution)/shard_map/psum | solution.py:334
  656.6 7.6 copy-start.24
  664.1 4.4 copy-start.18
  682.1 78.4 %copy-start.76 = (f32[768]{0:T(1024)S(1)}, f32[768]{0:T(1024)}, u32[]{:S(2)}) copy-start(f32[768]{0:T(1024)} %get-tuple-element.766) | copy-start | bytes 9220
  682.1 189.7 %copy-start.62 = (f32[1024]{0:T(1024)S(1)}, f32[1024]{0:T(1024)}, u32[]{:S(2)}) copy-start(f32[1024]{0:T(1024)} %get-tuple-element.905) | copy-start | bytes 12292
  758.0 113.8 %copy-start.23 = (f32[1024,384]{1,0:T(8,128)S(1)}, f32[1024,384]{1,0:T(8,128)}, u32[]{:S(2)}) copy-start(f32[1024,384]{1,0:T(8,128)} %reduce-scatter.5.cloned.1.call-done) | copy-start | bytes 4718596
  1074.8 5.2 copy-start.25
  1074.8 9.7 slice-start.4
  1080.0 4.5 slice-start.5
  (49 other events, 131.7 us)
Sparse Core Ops, SparseCore 0:
  176.7 31.3 all-gather.4
  279.8 33.2 all-gather.6
  579.1 50.7 all-reduce.26
  647.8 110.1 reduce-scatter.4
  760.2 111.5 reduce-scatter.2
  877.7 197.0 all-reduce.28
where the time goes:
time: 1100 us; the launch traced here: 1090 us
  waiting for transfers between devices  370 us (34%)
  local copies, waits for them, and re-layouts  312 us (28%)
  matrix products  199 us (18%)
  other arithmetic  120 us (11%)
  blocking collectives  67.3 us (6%)
  between operations  15.4 us (1%)
    psum x1, waiting for transfers between devices, per_device(): lax.psum((pre_gain_grad, gate_weight_grad, input_weight_grad, state_weigh...  199 us
    dynamic_update_slice x28, local copies, waits for them, and re-layouts, ssd_scan(): lax.scan(jax.checkpoint(ssd_block), start_state, pieces)  158 us
    reduce_scatter x1, waiting for transfers between devices, per_device(): lax.psum_scatter(input_partial, 'tensor', scatter_dimension=1, tiled=True)  75.5 us
    reduce_scatter x1, waiting for transfers between devices, per_device(): lax.psum_scatter(partial_out, 'tensor', scatter_dimension=1, tiled=True)  72.4 us
    dot_general x12, matrix products, ssd_block(): inner_out = jnp.einsum('tsh,shp->thp', mixing, driven, precision=highest)  53.7 us
    another operation x41, other arithmetic  36.1 us
    unnamed x186, local copies, waits for them, and re-layouts  29.5 us
    psum x1, blocking collectives, per_device(): lax.psum((pre_gain_grad, gate_weight_grad, input_weight_grad, state_weigh...  27.3 us
  transfers between devices with their start and end apart: 8, of which 5 were waited for; matrix products, arithmetic and copies ran while one was open for 13% of the time, Pallas kernels for 0%

commit v1 on v0

v1 whole, which is shorter than its diff:
```python
import functools

import jax
import jax.numpy as jnp
from jax import lax
from jax.experimental import pallas as pl
from jax.experimental.pallas import tpu as pltpu
from jax.sharding import PartitionSpec as P

HEAD_DIM = 64
CONV = 4
EDGE = 8
BLOCK = 128
LANES = 128
epsilon = 1e-05
f32 = jnp.float32
bf16 = jnp.bfloat16

NN = (((1,), (0,)), ((), ()))
NT = (((1,), (1,)), ((), ()))
TN = (((0,), (0,)), ((), ()))


def dot(a, b, dims=NN):
    return lax.dot_general(a, b, dims, preferred_element_type=f32)


def split2(x):
    high = x.astype(bf16)
    return high, (x - high.astype(f32)).astype(bf16)


def split3(x):
    high = x.astype(bf16)
    rest = x - high.astype(f32)
    middle = rest.astype(bf16)
    return high, middle, (rest - middle.astype(f32)).astype(bf16)


def dot3(a, b, dims=NN):
    ah, al = split2(a)
    bh, bl = split2(b)
    return dot(ah, bh, dims) + (dot(ah, bl, dims) + dot(al, bh, dims))


def dot_exact(x, ones, dims):
    high, middle, low = split3(x)
    return dot(high, ones, dims) + (dot(middle, ones, dims) + dot(low, ones, dims))


def exact_dot(ones, x, dims):
    high, middle, low = split3(x)
    return dot(ones, high, dims) + (dot(ones, middle, dims) + dot(ones, low, dims))


def iota(shape, axis):
    return lax.broadcasted_iota(jnp.int32, shape, axis)


def head_map(width):
    return (iota((LANES, width), 0) == iota((LANES, width), 1) // HEAD_DIM).astype(f32).astype(bf16)


def spread(per_head, heads):
    return dot_exact(per_head, heads, NN)


def gather_heads(per_channel, heads):
    return dot_exact(per_channel, heads, NT)


def padded(row):
    return jnp.concatenate([row, jnp.zeros((1, LANES - row.shape[1]), f32)], axis=1)


def sig(v):
    return jax.nn.sigmoid(v)


def params(limit=56):
    return pltpu.CompilerParams(
        dimension_semantics=("arbitrary",), vmem_limit_bytes=limit * 1024 * 1024
    )


def whole(shape):
    return pl.BlockSpec(shape, lambda b: (0,) * len(shape))


def rows(size, width, count=0):
    if count:
        return pl.BlockSpec((size, width), lambda b: (count - 1 - b, 0))
    return pl.BlockSpec((size, width), lambda b: (b, 0))


def norm_rows(x, gain):
    scaling = lax.rsqrt(jnp.mean(x * x, axis=-1, keepdims=True) + epsilon)
    return (x * scaling * gain).astype(bf16)


def project_kernel(x_ref, gain_ref, gate_ref, value_ref, state_ref, step_ref, normed_out, gate_out, value_out, state_out, step_out):
    normed = norm_rows(x_ref[...].astype(f32), gain_ref[...])
    normed_out[...] = normed
    value_out[...] = dot(normed, value_ref[...]).astype(bf16)
    state_out[...] = dot(normed, state_ref[...]).astype(bf16)
    step_out[...] = jnp.zeros(step_out.shape, f32)
    step_out[:, : step_ref.shape[1]] = dot(normed, step_ref[...])
    gate_out[...] = dot(normed, gate_ref[...])


def project(residual, pre_gain, gate_weight, input_weight, state_weight, step_weight):
    tokens, width = residual.shape
    inner, state2 = gate_weight.shape[1], state_weight.shape[1]
    tile = min(tokens, 256)
    return pl.pallas_call(
        project_kernel,
        grid=(tokens // tile,),
        in_specs=[
            rows(tile, width),
            whole((1, width)),
            whole(gate_weight.shape),
            whole(input_weight.shape),
            whole(state_weight.shape),
            whole(step_weight.shape),
        ],
        out_specs=[rows(tile, width), rows(tile, inner), rows(tile, inner), rows(tile, state2), rows(tile, LANES)],
        out_shape=[
            jax.ShapeDtypeStruct((tokens, width), bf16),
            jax.ShapeDtypeStruct((tokens, inner), f32),
            jax.ShapeDtypeStruct((tokens, inner), bf16),
            jax.ShapeDtypeStruct((tokens, state2), bf16),
            jax.ShapeDtypeStruct((tokens, LANES), f32),
        ],
        compiler_params=params(),
        cost_estimate=pl.CostEstimate(
            flops=2 * tokens * width * (2 * inner + state2 + LANES),
            bytes_accessed=4 * tokens * width + 4 * width * inner + 6 * tokens * inner,
            transcendentals=0,
        ),
    )(residual, pre_gain, gate_weight, input_weight, state_weight, step_weight)


def convolve(before, here, kernel):
    extended = jnp.concatenate([before, here], axis=0)
    count = here.shape[0]
    first = EDGE - CONV + 1
    summed = kernel[0:1] * extended[first : first + count]
    for k in range(1, CONV):
        summed = summed + kernel[k : k + 1] * extended[first + k : first + k + count]
    return summed


def local_kernel(
    value_ref, state_ref, step_ref, halo_ref, gain_ref, value_w, state_w, value_k, state_k, bias_ref, log_ref,
    conv_out, pre_out, rows_out, spre_out, dt_out, cum_out, cumt_out, held_out, message_out, vhalo_out,
    value_before, state_before, held, total,
):
    b = pl.program_id(0)
    width = value_ref.shape[1]

    @pl.when(b == 0)
    def _():
        normed = norm_rows(halo_ref[...].astype(f32), gain_ref[...])
        value_halo = dot(normed, value_w[...]).astype(bf16)
        state_halo = dot(normed, state_w[...]).astype(bf16)
        vhalo_out[...] = value_halo
        value_before[...] = value_halo.astype(f32)[-EDGE:]
        state_before[...] = state_halo.astype(f32)[-EDGE:]
        held[...] = jnp.zeros(held.shape, f32)
        total[...] = jnp.zeros(total.shape, f32)

    value = value_ref[...].astype(f32)
    state = state_ref[...].astype(f32)
    pre = convolve(value_before[...], value, value_k[...].astype(f32))
    spre = convolve(state_before[...], state, state_k[...].astype(f32))
    value_before[...] = value[-EDGE:]
    state_before[...] = state[-EDGE:]
    conv = pre * sig(pre)
    mixed_rows = spre * sig(spre)
    pre_out[...] = pre
    spre_out[...] = spre
    conv_out[...] = conv
    rows_out[...] = mixed_rows

    dt = jax.nn.softplus(step_ref[...] + padded(bias_ref[...]))
    decay = -dt * jnp.exp(padded(log_ref[...]))
    size = value.shape[0]
    lower = (iota((size, size), 0) >= iota((size, size), 1)).astype(f32).astype(bf16)
    cum = exact_dot(lower, decay, NN)
    dt_out[...] = dt
    cum_out[...] = cum
    cumt_out[...] = cum.T[: cumt_out.shape[0]]

    heads = head_map(width)
    cum_wide = spread(cum, heads)
    last = cum_wide[size - 1 : size]
    weighted = conv * spread(dt, heads) * jnp.exp(last - cum_wide)
    held_out[0] = held[...]
    new = jnp.exp(last) * held[...] + dot3(mixed_rows[:, :LANES], weighted, TN)
    held[...] = new
    total[...] = total[...] + last

    @pl.when(b == pl.num_programs(0) - 1)
    def _():
        message_out[:LANES] = new
        message_out[LANES:] = total[...]


def local_states(value_in, state_in, step_raw, halo, pre_gain, input_weight, state_weight, input_kernel, state_kernel, step_bias, decay_log):
    tokens, inner = value_in.shape
    state2 = state_in.shape[1]
    state = state2 // 2
    blocks = tokens // BLOCK
    headrows = 16
    return pl.pallas_call(
        local_kernel,
        grid=(blocks,),
        in_specs=[
            rows(BLOCK, inner),
            rows(BLOCK, state2),
            rows(BLOCK, LANES),
            whole(halo.shape),
            whole(pre_gain.shape),
            whole(input_weight.shape),
            whole(state_weight.shape),
            whole(input_kernel.shape),
            whole(state_kernel.shape),
            whole(step_bias.shape),
            whole(decay_log.shape),
        ],
        out_specs=[
            rows(BLOCK, inner),
            rows(BLOCK, inner),
            rows(BLOCK, state2),
            rows(BLOCK, state2),
            rows(BLOCK, LANES),
            rows(BLOCK, LANES),
            pl.BlockSpec((headrows, BLOCK), lambda b: (0, b)),
            pl.BlockSpec((1, state, inner), lambda b: (b, 0, 0)),
            whole((state + EDGE, inner)),
            whole((halo.shape[0], inner)),
        ],
        out_shape=[
            jax.ShapeDtypeStruct((tokens, inner), f32),
            jax.ShapeDtypeStruct((tokens, inner), f32),
            jax.ShapeDtypeStruct((tokens, state2), f32),
            jax.ShapeDtypeStruct((tokens, state2), f32),
            jax.ShapeDtypeStruct((tokens, LANES), f32),
            jax.ShapeDtypeStruct((tokens, LANES), f32),
            jax.ShapeDtypeStruct((headrows, tokens), f32),
            jax.ShapeDtypeStruct((blocks, state, inner), f32),
            jax.ShapeDtypeStruct((state + EDGE, inner), f32),
            jax.ShapeDtypeStruct((halo.shape[0], inner), bf16),
        ],
        scratch_shapes=[
            pltpu.VMEM((EDGE, inner), f32),
            pltpu.VMEM((EDGE, state2), f32),
            pltpu.VMEM((state, inner), f32),
            pltpu.VMEM((EDGE, inner), f32),
        ],
        compiler_params=params(),
        cost_estimate=pl.CostEstimate(flops=2 * tokens * inner * 1500, bytes_accessed=tokens * inner * 14, transcendentals=tokens * inner * 2),
    )(value_in, state_in, step_raw, halo, pre_gain, input_weight, state_weight, input_kernel, state_kernel, step_bias, decay_log)


def pairs_of(heads_count):
    return heads_count * HEAD_DIM // LANES


def inner_kernel(heads_count, conv_ref, dt_ref, rows_ref, cum_ref, cumt_ref, out_ref):
    size, width = conv_ref.shape
    heads = head_map(width)
    driven = conv_ref[...] * spread(dt_ref[...], heads)
    high, low = split2(driven)
    scores = dot3(rows_ref[:, LANES:], rows_ref[:, :LANES], NT)
    causal = iota((size, size), 0) >= iota((size, size), 1)
    left = iota((size, LANES), 1) < HEAD_DIM
    cum = cum_ref[...]
    cumt = cumt_ref[...]
    for pair in range(pairs_of(heads_count)):
        span = slice(pair * LANES, (pair + 1) * LANES)
        across = jnp.concatenate([high[:, span], low[:, span]], axis=1)
        right_side = jnp.concatenate([across, across], axis=0)
        mixes = []
        for h in (2 * pair, 2 * pair + 1):
            gap = cum[:, h : h + 1] - cumt[h : h + 1, :]
            mix = jnp.exp(jnp.where(causal, gap, -1e30)) * scores
            mixes.append(jnp.concatenate(split2(mix), axis=1))
        both = dot(jnp.concatenate(mixes, axis=0), right_side)
        both = both[:, :LANES] + both[:, LANES:]
        out_ref[:, span] = jnp.where(left, both[:size], both[size:])


def inner_forward(heads_count, conv, dt, state_rows, cum, cumt):
    tokens, inner = conv.shape
    return pl.pallas_call(
        functools.partial(inner_kernel, heads_count),
        grid=(tokens // BLOCK,),
        in_specs=[
            rows(BLOCK, inner),
            rows(BLOCK, LANES),
            rows(BLOCK, state_rows.shape[1]),
            rows(BLOCK, LANES),
            pl.BlockSpec((cumt.shape[0], BLOCK), lambda b: (0, b)),
        ],
        out_specs=rows(BLOCK, inner),
        out_shape=jax.ShapeDtypeStruct((tokens, inner), f32),
        compiler_params=params(),
        cost_estimate=pl.CostEstimate(flops=2 * tokens * inner * 2000, bytes_accessed=tokens * inner * 8, transcendentals=tokens * BLOCK * heads_count),
    )(conv, dt, state_rows, cum, cumt)


def combine_kernel(
    count, intra_ref, conv_ref, rows_ref, cum_ref, held_ref, own_ref, *refs
):
    message_refs, (gate_ref, grad_ref, gain_ref, skip_ref, mixed_out, sums_out, held_out, end_out, start, total) = refs[:count], refs[count:]
    b = pl.program_id(0)
    size, width = conv_ref.shape
    state = held_ref.shape[1]

    @pl.when(b == 0)
    def _():
        entering = jnp.zeros((state, width), f32)
        passed = jnp.zeros((EDGE, width), f32)
        for ref in message_refs:
            entering = entering + jnp.exp(passed[0:1]) * ref[:state]
            passed = passed + ref[state:]
        start[...] = entering
        total[...] = jnp.zeros(total.shape, f32)
        end_out[...] = own_ref[:state] + jnp.exp(own_ref[state : state + 1]) * entering

    heads = head_map(width)
    cum_wide = spread(cum_ref[...], heads)
    held = held_ref[0] + jnp.exp(total[0:1]) * start[...]
    held_out[0] = held
    total[...] = total[...] + cum_wide[size - 1 : size]
    skip = spread(jnp.broadcast_to(padded(skip_ref[...]), (EDGE, LANES)), heads)[0:1]
    carried = jnp.exp(cum_wide) * dot3(rows_ref[:, LANES:], held)
    mixed = (intra_ref[...] + carried) + skip * conv_ref[...]
    mixed_out[...] = mixed
    gate = gate_ref[...]
    gated = mixed * (gate * sig(gate))
    ones = jnp.ones((EDGE, width), bf16)
    square = exact_dot(ones, gated * gated, NT)
    inner = exact_dot(ones, grad_ref[...] * gain_ref[...] * gated, NT)
    sums_out[...] = jnp.where(iota(square.shape, 0) == 0, square, inner)


def combine(intra, conv, state_rows, cum, held, own, messages, gate_in, grad_normed, norm_gain, skip_gain):
    tokens, inner = conv.shape
    blocks, state, _ = held.shape
    state_block = pl.BlockSpec((1, state, inner), lambda b: (b, 0, 0))
    return pl.pallas_call(
        functools.partial(combine_kernel, len(messages)),
        grid=(blocks,),
        in_specs=[
            rows(BLOCK, inner),
            rows(BLOCK, inner),
            rows(BLOCK, state_rows.shape[1]),
            rows(BLOCK, LANES),
            state_block,
            whole(own.shape),
            *[whole(own.shape) for _ in messages],
            rows(BLOCK, inner),
            rows(BLOCK, inner),
            whole(norm_gain.shape),
            whole(skip_gain.shape),
        ],
        out_specs=[
            rows(BLOCK, inner),
            pl.BlockSpec((EDGE, BLOCK), lambda b: (0, b)),
            state_block,
            whole((state, inner)),
        ],
        out_shape=[
            jax.ShapeDtypeStruct((tokens, inner), f32),
            jax.ShapeDtypeStruct((EDGE, tokens), f32),
            jax.ShapeDtypeStruct(held.shape, f32),
            jax.ShapeDtypeStruct((state, inner), f32),
        ],
        scratch_shapes=[pltpu.VMEM((state, inner), f32), pltpu.VMEM((EDGE, inner), f32)],
        compiler_params=params(),
        cost_estimate=pl.CostEstimate(flops=2 * tokens * inner * 1000, bytes_accessed=tokens * inner * 28, transcendentals=tokens * inner * 2),
    )(intra, conv, state_rows, cum, held, own, *messages, gate_in, grad_normed, norm_gain, skip_gain)


def column(row, width):
    return jnp.concatenate([jnp.broadcast_to(row, (LANES, row.shape[1])).T] * (width // LANES), axis=1)


def gate_back_kernel(count, inner_total, mixed_ref, gate_ref, grad_ref, rows_ref, cum_ref, gain_ref, *refs):
    sums_refs, (normed_out, gate_out, dmix_out, later_out, message_out, gain_out, later, total) = refs[:count], refs[count:]
    b = pl.program_id(0)
    size, width = mixed_ref.shape

    @pl.when(b == 0)
    def _():
        later[...] = jnp.zeros(later.shape, f32)
        total[...] = jnp.zeros(total.shape, f32)
        gain_out[...] = jnp.zeros(gain_out.shape, f32)

    sums = sums_refs[0][...]
    for ref in sums_refs[1:]:
        sums = sums + ref[...]
    rms_row = lax.rsqrt(sums[0:1] / inner_total + epsilon)
    pull_row = rms_row * rms_row * rms_row * sums[1:2] / inner_total
    rms = column(rms_row, width)
    pull = column(pull_row, width)
    gain = gain_ref[...]
    gate = gate_ref[...]
    mixed = mixed_ref[...]
    grad = grad_ref[...]
    gate_sig = sig(gate)
    gate_silu = gate * gate_sig
    gated = mixed * gate_silu
    normed_out[...] = (gated * rms * gain).astype(bf16)
    gain_part = (grad * gated * rms).reshape(size // EDGE, EDGE, width)
    gain_out[...] = gain_out[...] + jnp.sum(gain_part, axis=0)
    grad_gated = rms * gain * grad - gated * pull
    gate_out[...] = (grad_gated * mixed * gate_sig * (1.0 + gate * (1.0 - gate_sig))).astype(bf16)
    grad_mixed = grad_gated * gate_silu
    dmix_out[...] = grad_mixed

    cum_wide = spread(cum_ref[...], head_map(width))
    last = cum_wide[size - 1 : size]
    later_out[0] = later[...]
    new = jnp.exp(last) * later[...] + dot3(rows_ref[:, LANES:], jnp.exp(cum_wide) * grad_mixed, TN)
    later[...] = new
    total[...] = total[...] + last

    @pl.when(b == pl.num_programs(0) - 1)
    def _():
        message_out[:LANES] = new
        message_out[LANES:] = total[...]


def gate_back(mixed, gate_in, grad_normed, state_rows, cum, norm_gain, sums, inner_total):
    tokens, inner = mixed.shape
    blocks = tokens // BLOCK
    state = state_rows.shape[1] // 2
    return pl.pallas_call(
        functools.partial(gate_back_kernel, len(sums), inner_total),
        grid=(blocks,),
        in_specs=[
            rows(BLOCK, inner, blocks),
            rows(BLOCK, inner, blocks),
            rows(BLOCK, inner, blocks),
            rows(BLOCK, 2 * state, blocks),
            rows(BLOCK, LANES, blocks),
            whole(norm_gain.shape),
            *[pl.BlockSpec((EDGE, BLOCK), lambda b: (0, blocks - 1 - b)) for _ in sums],
        ],
        out_specs=[
            rows(BLOCK, inner, blocks),
            rows(BLOCK, inner, blocks),
            rows(BLOCK, inner, blocks),
            pl.BlockSpec((1, state, inner), lambda b: (blocks - 1 - b, 0, 0)),
            whole((state + EDGE, inner)),
            whole((EDGE, inner)),
        ],
        out_shape=[
            jax.ShapeDtypeStruct((tokens, inner), bf16),
            jax.ShapeDtypeStruct((tokens, inner), bf16),
            jax.ShapeDtypeStruct((tokens, inner), f32),
            jax.ShapeDtypeStruct((blocks, state, inner), f32),
            jax.ShapeDtypeStruct((state + EDGE, inner), f32),
            jax.ShapeDtypeStruct((EDGE, inner), f32),
        ],
        scratch_shapes=[pltpu.VMEM((state, inner), f32), pltpu.VMEM((EDGE, inner), f32)],
        compiler_params=params(),
        cost_estimate=pl.CostEstimate(flops=2 * tokens * inner * 1000, bytes_accessed=tokens * inner * 26, transcendentals=tokens * inner * 2),
    )(mixed, gate_in, grad_normed, state_rows, cum, norm_gain, *sums)


def inner_back_kernel(heads_count, conv_ref, dt_ref, rows_ref, cum_ref, cumt_ref, dmix_ref, driven_out, rows_out):
    size, width = conv_ref.shape
    heads = head_map(width)
    driven = conv_ref[...] * spread(dt_ref[...], heads)
    dmix_high, dmix_low = split2(dmix_ref[...])
    b_rows = rows_ref[:, :LANES]
    c_rows = rows_ref[:, LANES:]
    scores = dot3(b_rows, c_rows, NT)
    causal = iota((size, size), 1) >= iota((size, size), 0)
    left = iota((size, LANES), 1) < HEAD_DIM
    cum = cum_ref[...]
    cumt = cumt_ref[...]
    score_grad = jnp.zeros((size, size), f32)
    for pair in range(pairs_of(heads_count)):
        span = slice(pair * LANES, (pair + 1) * LANES)
        across = jnp.concatenate([dmix_high[:, span], dmix_low[:, span]], axis=1)
        right_side = jnp.concatenate([across, across], axis=0)
        taking = jnp.concatenate([dmix_high[:, span], dmix_high[:, span], dmix_low[:, span]], axis=1)
        mixes = []
        for h in (2 * pair, 2 * pair + 1):
            mine = left if h % 2 == 0 else jnp.logical_not(left)
            own_high, own_low = split2(jnp.where(mine, driven[:, span], 0.0))
            mix_grad = dot(jnp.concatenate([own_high, own_low, own_high], axis=1), taking, NT)
            gap = cumt[h : h + 1, :] - cum[:, h : h + 1]
            kept = jnp.exp(jnp.where(causal, gap, -1e30))
            score_grad = score_grad + mix_grad * kept
            mixes.append(jnp.concatenate(split2(kept * scores), axis=1))
        both = dot(jnp.concatenate(mixes, axis=0), right_side)
        both = both[:, :LANES] + both[:, LANES:]
        driven_out[:, span] = jnp.where(left, both[:size], both[size:])
    rows_out[:, :LANES] = dot3(score_grad, c_rows, NN)
    rows_out[:, LANES:] = dot3(score_grad, b_rows, TN)


def inner_back(heads_count, conv, dt, state_rows, cum, cumt, grad_mixed):
    tokens, inner = conv.shape
    return pl.pallas_call(
        functools.partial(inner_back_kernel, heads_count),
        grid=(tokens // BLOCK,),
        in_specs=[
            rows(BLOCK, inner),
            rows(BLOCK, LANES),
            rows(BLOCK, state_rows.shape[1]),
            rows(BLOCK, LANES),
            pl.BlockSpec((cumt.shape[0], BLOCK), lambda b: (0, b)),
            rows(BLOCK, inner),
        ],
        out_specs=[rows(BLOCK, inner), rows(BLOCK, state_rows.shape[1])],
        out_shape=[
            jax.ShapeDtypeStruct((tokens, inner), f32),
            jax.ShapeDtypeStruct(state_rows.shape, f32),
        ],
        compiler_params=params(),
        cost_estimate=pl.CostEstimate(flops=2 * tokens * inner * 3000, bytes_accessed=tokens * inner * 12, transcendentals=tokens * BLOCK * heads_count),
    )(conv, dt, state_rows, cum, cumt, grad_mixed)


def finish_kernel(
    count, driven_ref, drows_ref, dmix_ref, mixed_ref, conv_ref, pre_ref, value_ref, dt_ref, cum_ref, step_ref, rows_ref,
    held_ref, end_ref, later_ref, *refs
):
    message_refs = refs[:count]
    (
        vhalo_ref, kernel_ref, skip_ref, bias_ref, log_ref,
        grad_value_out, grad_rows_out, grad_step_out, last_out, first_out, kernel_out, small_out,
        entering, total, held_next, pre_next, skip_sum,
    ) = refs[count:]
    b = pl.program_id(0)
    size, width = conv_ref.shape
    state = held_ref.shape[1]
    heads = head_map(width)

    @pl.when(b == 0)
    def _():
        coming = jnp.zeros((state, width), f32)
        passed = jnp.zeros((EDGE, width), f32)
        for ref in message_refs:
            coming = coming + jnp.exp(passed[0:1]) * ref[:state]
            passed = passed + ref[state:]
        entering[...] = coming
        total[...] = jnp.zeros(total.shape, f32)
        held_next[...] = end_ref[...]
        pre_next[...] = jnp.zeros(pre_next.shape, f32)
        kernel_out[...] = jnp.zeros(kernel_out.shape, f32)
        small_out[...] = jnp.zeros(small_out.shape, f32)
        skip_sum[...] = jnp.zeros(skip_sum.shape, f32)

    b_rows = rows_ref[:, :LANES]
    cum_wide = spread(cum_ref[...], heads)
    last = cum_wide[size - 1 : size]
    dt = dt_ref[...]
    dt_wide = spread(dt, heads)
    conv = conv_ref[...]
    dmix = dmix_ref[...]
    driven = conv * dt_wide
    later = later_ref[0] + jnp.exp(total[0:1]) * entering[...]
    total[...] = total[...] + last
    tail = jnp.exp(last - cum_wide)
    ddriven = driven_ref[...] + tail * dot3(b_rows, later)
    held = held_ref[0]
    grad_rows_out[:, :LANES] = drows_ref[:, :LANES] + dot3(tail * driven, later, NT)
    grad_rows_out[:, LANES:] = drows_ref[:, LANES:] + dot3(jnp.exp(cum_wide) * dmix, held, NT)

    skip = spread(jnp.broadcast_to(padded(skip_ref[...]), (EDGE, LANES)), heads)[0:1]
    from_skip = dmix * conv
    skip_sum[...] = skip_sum[...] + jnp.sum(from_skip.reshape(size // EDGE, EDGE, width), axis=0)
    level = gather_heads(dmix * (mixed_ref[...] - skip * conv) - driven * ddriven, heads)
    through = gather_heads(ddriven * conv, heads)
    boundary = jnp.sum((later * held_next[...]).reshape(state // EDGE, EDGE, width), axis=0)
    boundary = jnp.sum(gather_heads(boundary, heads), axis=0, keepdims=True)
    held_next[...] = held
    upper = (iota((size, size), 1) >= iota((size, size), 0)).astype(f32).astype(bf16)
    ddecay = exact_dot(upper, level, NN) + boundary
    rate = jnp.exp(padded(log_ref[...]))
    dstep = (through - ddecay * rate) * sig(step_ref[...] + padded(bias_ref[...]))
    grad_step_out[...] = dstep[:, : grad_step_out.shape[1]].astype(bf16)
    dlog = jnp.sum(-ddecay * dt * rate, axis=0, keepdims=True)
    small_out[1:2] = small_out[1:2] + jnp.sum(dstep, axis=0, keepdims=True)
    small_out[2:3] = small_out[2:3] + dlog

    pre = pre_ref[...]
    pre_sig = sig(pre)
    dpre = (ddriven * dt_wide + skip * dmix) * (pre_sig * (1.0 + pre * (1.0 - pre_sig)))
    extended = jnp.concatenate([dpre, pre_next[...]], axis=0)
    value = value_ref[...].astype(f32)
    taps = kernel_ref[...].astype(f32)
    dvalue = jnp.zeros((size, width), f32)
    for k in range(CONV):
        shifted = extended[CONV - 1 - k : CONV - 1 - k + size]
        dvalue = dvalue + taps[k : k + 1] * shifted
        kernel_out[k : k + 1] = kernel_out[k : k + 1] + jnp.sum(value * shifted, axis=0, keepdims=True)
    grad_value_out[...] = dvalue.astype(bf16)
    pre_next[...] = dpre[:EDGE]

    @pl.when(b == 0)
    def _():
        last_out[...] = dvalue[-2 * EDGE :]

    @pl.when(b == pl.num_programs(0) - 1)
    def _():
        first_out[...] = dpre[:EDGE]
        ahead = jnp.concatenate([jnp.zeros((EDGE, width), f32), dpre[:EDGE]], axis=0)
        halo = vhalo_ref[...].astype(f32)[-EDGE:]
        for k in range(CONV):
            shifted = ahead[CONV - 1 - k : CONV - 1 - k + EDGE]
            kernel_out[k : k + 1] = kernel_out[k : k + 1] + jnp.sum(halo * shifted, axis=0, keepdims=True)
        small_out[0:1] = jnp.sum(gather_heads(skip_sum[...], heads), axis=0, keepdims=True)


def finish(grad_driven, grad_rows, grad_mixed, mixed, conv, pre, value_in, dt, cum, step_raw, state_rows, held, end_state, later,
           messages, vhalo, input_kernel, skip_gain, step_bias, decay_log):
    tokens, inner = conv.shape
    blocks, state, _ = held.shape
    head_count = skip_gain.shape[1]
    state_block = pl.BlockSpec((1, state, inner), lambda b: (blocks - 1 - b, 0, 0))
    wide = rows(BLOCK, inner, blocks)
    narrow = rows(BLOCK, LANES, blocks)
    return pl.pallas_call(
        functools.partial(finish_kernel, len(messages)),
        grid=(blocks,),
        in_specs=[
            wide, rows(BLOCK, 2 * state, blocks), wide, wide, wide, wide, wide, narrow, narrow, narrow,
            rows(BLOCK, 2 * state, blocks),
            state_block, whole(end_state.shape), state_block,
            *[whole(m.shape) for m in messages],
            whole(vhalo.shape), whole(input_kernel.shape), whole(skip_gain.shape), whole(step_bias.shape), whole(decay_log.shape),
        ],
        out_specs=[
            wide,
            rows(BLOCK, 2 * state, blocks),
            rows(BLOCK, head_count, blocks),
            whole((2 * EDGE, inner)),
            whole((EDGE, inner)),
            whole((EDGE, inner)),
            whole((EDGE, LANES)),
        ],
        out_shape=[
            jax.ShapeDtypeStruct((tokens, inner), bf16),
            jax.ShapeDtypeStruct((tokens, 2 * state), f32),
            jax.ShapeDtypeStruct((tokens, head_count), bf16),
            jax.ShapeDtypeStruct((2 * EDGE, inner), f32),
            jax.ShapeDtypeStruct((EDGE, inner), f32),
            jax.ShapeDtypeStruct((EDGE, inner), f32),
            jax.ShapeDtypeStruct((EDGE, LANES), f32),
        ],
        scratch_shapes=[
            pltpu.VMEM((state, inner), f32),
            pltpu.VMEM((EDGE, inner), f32),
            pltpu.VMEM((state, inner), f32),
            pltpu.VMEM((EDGE, inner), f32),
            pltpu.VMEM((EDGE, inner), f32),
        ],
        compiler_params=params(),
        cost_estimate=pl.CostEstimate(flops=2 * tokens * inner * 3000, bytes_accessed=tokens * inner * 36, transcendentals=tokens * inner * 3),
    )(grad_driven, grad_rows, grad_mixed, mixed, conv, pre, value_in, dt, cum, step_raw, state_rows, held, end_state, later,
      *messages, vhalo, input_kernel, skip_gain, step_bias, decay_log)


def from_before(value, axis, by=1):
    count = lax.axis_size(axis)
    return lax.ppermute(value, axis, [(i, i + by) for i in range(count - by)])


def from_after(value, axis, by=1):
    count = lax.axis_size(axis)
    return lax.ppermute(value, axis, [(i + by, i) for i in range(count - by)])


def from_all(value, axis):
    count = lax.axis_size(axis)
    return [lax.ppermute(value, axis, [(i, (i + by) % count) for i in range(count)]) for by in range(1, count)]


def own_part(array, axis_name, dim):
    size = array.shape[dim] // lax.axis_size(axis_name)
    return lax.dynamic_slice_in_dim(array, lax.axis_index(axis_name) * size, size, dim)


def state_conv_back(grad_rows, spre, taps, state_in, shalo, spre_after, grad_after):
    def through(grad, pre):
        s = sig(pre)
        return grad * (s * (1.0 + pre * (1.0 - s)))

    tokens = grad_rows.shape[0]
    dpre = through(grad_rows, spre)
    after = through(grad_after, spre_after)
    extended = jnp.concatenate([dpre, after], axis=0)
    dstate = sum(taps[k : k + 1] * extended[CONV - 1 - k : CONV - 1 - k + tokens] for k in range(CONV))
    inputs = jnp.concatenate([shalo, state_in], axis=0).astype(f32)
    first = shalo.shape[0] - CONV + 1
    dtaps = jnp.stack([jnp.sum(dpre * inputs[first + k : first + k + tokens], axis=0) for k in range(CONV)])
    return dstate.astype(bf16), dtaps


def per_device(residual, pre_gain, gate_weight, input_weight, state_weight, step_weight, input_kernel, state_kernel,
               step_bias, decay_log, skip_gain, norm_gain, out_weight, cotangent):
    seqs, tokens, width = residual.shape
    outs = [
        one_sequence(residual[i], pre_gain, gate_weight, input_weight, state_weight, step_weight, input_kernel, state_kernel,
                     step_bias, decay_log, skip_gain, norm_gain, out_weight, cotangent[i])
        for i in range(seqs)
    ]
    output = jnp.stack([o[0] for o in outs])
    input_grad = jnp.stack([o[1] for o in outs])
    sums = [functools.reduce(jnp.add, parts) for parts in zip(*[o[2:] for o in outs])]
    sums = lax.psum(tuple(sums), ("dp", "ctx"))
    state_taps = sums[6]
    spread_taps = lax.dynamic_update_slice_in_dim(
        jnp.zeros((CONV, state_weight.shape[1]), f32), state_taps, lax.axis_index("tensor") * state_taps.shape[1], 1
    )
    return (output, input_grad, *sums[:6], lax.psum(spread_taps, "tensor"), *sums[7:])


def one_sequence(residual, pre_gain, gate_weight, input_weight, state_weight, step_weight, input_kernel, state_kernel,
                 step_bias, decay_log, skip_gain, norm_gain, out_weight, cotangent):
    tokens, width = residual.shape
    tensor_size = lax.axis_size("tensor")
    ctx_size = lax.axis_size("ctx")
    inner = gate_weight.shape[1]
    inner_total = inner * tensor_size
    head_count = step_weight.shape[1]
    row = lambda v: v.reshape(1, -1)

    halo = from_before(residual[-2 * EDGE :], "ctx")
    normed, gate_in, value_in, state_in, step_raw = project(
        residual, row(pre_gain), gate_weight, input_weight, state_weight, step_weight
    )
    conv, pre, state_rows, spre, dt, cum, cumt, held, message, vhalo = local_states(
        value_in, state_in, step_raw, halo, row(pre_gain), input_weight, state_weight, input_kernel, state_kernel,
        row(step_bias), row(decay_log)
    )
    messages = [from_before(message, "ctx", by) for by in range(1, ctx_size)]
    intra = inner_forward(head_count, conv, dt, state_rows, cum, cumt)
    grad_normed = dot(cotangent, out_weight, NT)
    mixed, sums, held, end_state = combine(
        intra, conv, state_rows, cum, held, message, messages, gate_in, grad_normed, row(norm_gain), row(skip_gain)
    )
    all_sums = [sums, *from_all(sums, "tensor")]
    normed_out, grad_gate, grad_mixed, later, message, gain_grad = gate_back(
        mixed, gate_in, grad_normed, state_rows, cum, row(norm_gain), all_sums, inner_total
    )
    messages = [from_after(message, "ctx", by) for by in range(1, ctx_size)]

    resid_part = own_part(residual, "tensor", 1).astype(f32)
    partial_out = dot(normed_out, out_weight)
    branch = lax.psum_scatter(partial_out, "tensor", scatter_dimension=1, tiled=True)
    output = (resid_part + branch).astype(bf16)
    out_weight_grad = dot(normed_out, cotangent, TN)
    gate_weight_grad = dot(normed, grad_gate, TN)

    grad_driven, grad_rows = inner_back(head_count, conv, dt, state_rows, cum, cumt, grad_mixed)
    grad_value, grad_rows, grad_step, last_rows, first_rows, kernel_grad, small = finish(
        grad_driven, grad_rows, grad_mixed, mixed, conv, pre, value_in, dt, cum, step_raw, state_rows, held, end_state, later,
        messages, vhalo, input_kernel, row(skip_gain), row(step_bias), row(decay_log)
    )
    ahead = from_after(first_rows, "ctx")
    taps = input_kernel.astype(f32)
    ahead = jnp.concatenate([jnp.zeros((2 * EDGE, inner), f32), ahead], axis=0)
    fixed = last_rows + sum(taps[k : k + 1] * ahead[CONV - 1 - k : CONV - 1 - k + 2 * EDGE] for k in range(CONV))
    grad_value = lax.dynamic_update_slice_in_dim(grad_value, fixed.astype(bf16), tokens - 2 * EDGE, 0)

    part = state_weight.shape[1] // tensor_size
    shalo = from_before(own_part(state_in[-2 * EDGE :], "tensor", 1), "ctx")
    spre_after = from_after(own_part(spre[:EDGE], "tensor", 1), "ctx")
    grad_after = from_after(grad_rows[:EDGE], "ctx")
    quarter = lax.psum_scatter(jnp.concatenate([grad_rows, grad_after], axis=0), "tensor", scatter_dimension=1, tiled=True)
    grad_state, state_taps_grad = state_conv_back(
        quarter[:tokens], own_part(spre, "tensor", 1), own_part(state_kernel, "tensor", 1).astype(f32),
        own_part(state_in, "tensor", 1), shalo, spre_after, quarter[tokens:]
    )
    input_partial = dot(grad_gate, gate_weight, NT) + dot(grad_value, input_weight, NT) + dot(grad_step, step_weight, NT)
    input_partial = input_partial + dot(grad_state, own_part(state_weight, "tensor", 1), NT)
    normed_grad = lax.psum_scatter(input_partial, "tensor", scatter_dimension=1, tiled=True)
    flat = residual.astype(f32)
    scaling = lax.rsqrt(jnp.mean(flat * flat, axis=-1, keepdims=True) + epsilon)
    gain_part = own_part(pre_gain, "tensor", 0)
    row_total = lax.psum(jnp.sum(normed_grad * gain_part * resid_part, axis=-1), "tensor")
    grad_part = own_part(cotangent, "tensor", 1).astype(f32)
    input_grad = (
        grad_part + scaling * gain_part * normed_grad - resid_part * (scaling * scaling * scaling) * row_total[:, None] / width
    )
    pre_gain_grad = jnp.sum(normed_grad * resid_part * scaling, axis=0)
    return (
        output,
        input_grad,
        pre_gain_grad,
        gate_weight_grad,
        dot(normed, grad_value, TN),
        dot(normed, grad_state, TN),
        dot(normed, grad_step, TN),
        kernel_grad[:CONV],
        state_taps_grad,
        small[1, :head_count],
        small[2, :head_count],
        small[0, :head_count],
        jnp.sum(gain_grad, axis=0),
        out_weight_grad,
    )


def solution(mesh):
    in_specs = (
        P("dp", "ctx", None),
        P(),
        P(None, "tensor"),
        P(None, "tensor"),
        P(),
        P(None, "tensor"),
        P(None, "tensor"),
        P(),
        P("tensor"),
        P("tensor"),
        P("tensor"),
        P("tensor"),
        P("tensor", None),
        P("dp", "ctx", None),
    )
    out_specs = (
        P("dp", "ctx", "tensor"),
        P("dp", "ctx", "tensor"),
        P("tensor"),
        P(None, "tensor"),
        P(None, "tensor"),
        P(None, "tensor"),
        P(None, "tensor"),
        P(None, "tensor"),
        P(),
        P("tensor"),
        P("tensor"),
        P("tensor"),
        P("tensor"),
        P("tensor", None),
    )
    return jax.shard_map(per_device, mesh=mesh, in_specs=in_specs, out_specs=out_specs, check_vma=False)
```

time: 1100 us -> 660 us (0.60)
  local copies, waits for them, and re-layouts: 312 us -> 29.7 us
  matrix products: 199 us -> 57 us
  other arithmetic: 120 us -> 13.7 us
  Pallas kernels: 0 us -> 99.4 us
  blocking collectives: 67.3 us -> 40 us
  starting transfers between devices: 7.69 us -> 28.3 us
    dynamic_update_slice x28 -> x1, local copies, waits for them, and re-layouts: 158 us -> 0.08 us  [per_device(): lax.dynamic_update_slice_in_dim(jnp.zeros((CONV, state_weight.shape[1]),...]
    dot_general x78 -> x11, matrix products: 199 us -> 57 us  [dot(): return lax.dot_general(a, b, dims, preferred_element_type=f32)]
    pallas_call x0 -> x7, Pallas kernels: none -> 99.4 us  [the longest x1 23.1 us: finish(): pl.pallas_call(functools.partial(finish_kernel, len(messages)), grid=(blo...]
    another operation x41 -> x2, other arithmetic: 36.1 us -> 4.39 us  [the longest x1 4.38 us: per_device(): input_grad = jnp.stack([o[1] for o in outs])]
    reduce_sum x19 -> x4, other arithmetic: 32.7 us -> 6.62 us  [the longest x1 2.57 us: one_sequence(): scaling = lax.rsqrt(jnp.mean(flat * flat, axis=-1, keepdims=True) + epsilon)]
    mul x18 -> x1, local copies, waits for them, and re-layouts: 22.7 us -> 0.01 us  [state_conv_back(): taps[k:k + 1] * extended[CONV - 1 - k:CONV - 1 - k + tokens]]
    another operation x106 -> x0, local copies, waits for them, and re-layouts: 21.7 us -> none
    ppermute x2 -> x14, starting transfers between devices: 7.04 us -> 27.9 us  [the longest x5 14.4 us: from_before(): return lax.ppermute(value, axis, [(i, i + by) for i in range(count - by)])]
  transfers between devices with their start and end apart: 8 -> 18, of which waited for: 5 -> 11; matrix products, arithmetic and copies ran while one was open for 13% -> 11% of each run, Pallas kernels for 0% -> 15%
where the time goes in v1:
time: 660 us; the launch traced here: 658 us
  waiting for transfers between devices  375 us (57%)
  Pallas kernels  99.4 us (15%)
  matrix products  57 us (9%)
  blocking collectives  40 us (6%)
  local copies, waits for them, and re-layouts  29.7 us (4%)
  starting transfers between devices  28.3 us (4%)
  between operations  14.2 us (2%)
  other arithmetic  13.7 us (2%)
    psum x1, waiting for transfers between devices, per_device(): sums = lax.psum(tuple(sums), ('dp', 'ctx'))  198 us
    reduce_scatter x1, waiting for transfers between devices, one_sequence(): lax.psum_scatter(input_partial, 'tensor', scatter_dimension=1, tiled=True)  79.9 us
    reduce_scatter x1, waiting for transfers between devices, one_sequence(): lax.psum_scatter(partial_out, 'tensor', scatter_dimension=1, tiled=True)  71.7 us
    dot_general x11, matrix products, dot(): return lax.dot_general(a, b, dims, preferred_element_type=f32)  57 us
    psum x1, blocking collectives, per_device(): sums = lax.psum(tuple(sums), ('dp', 'ctx'))  27.5 us
    pallas_call x1, Pallas kernels, finish(): pl.pallas_call(functools.partial(finish_kernel, len(messages)), grid=(blo...  23.1 us
    unnamed x75, local copies, waits for them, and re-layouts  20.4 us
    pallas_call x1, Pallas kernels, local_states(): pl.pallas_call(local_kernel, grid=(blocks,), in_specs=[rows(BLOCK, inner)...  15.8 us
  transfers between devices with their start and end apart: 18, of which 11 were waited for; matrix products, arithmetic and copies ran while one was open for 11% of the time, Pallas kernels for 15%

profile of v1, /device:TPU:0, one launch (start us, length us, event | category | flops | bytes accessed | tf_op | source)
XLA Modules:
  0.0 657.7 jit_solution(7294237094177221788)
XLA Ops:
  7.2 1.0 slice_bitcast_fusion
  8.2 4.8 collective-permute-start
  13.0 1.3 reshape.73.gain_ref
  14.3 1.8 copy.29.step_ref
  16.1 12.1 %shard_map.245 = (bf16[1024,1536]{1,0:T(8,128)(2,1)}, f32[1024,768]{1,0:T(8,128)}, bf16[1024,768]{1,0:T(8,128)(2,1)}, bf16[1024,256]{1,0:T(8,128)(2,1)}, f32[1024,128]{1,0:T(8,128)}) custom-call(bf16[1024,1536]{1,0:T(8,128)(2,1)} %bitcast.64, f32[1,1536]{1,0:T(1,128)} %reshape.73.gain_ref, bf16[1536,768]{1,0:T(8,128)(2,1)} %gate_ref.1, ...), custom_call_target="tpu_custom_call" | custom-call | flops 6039797760 | bytes 15728640 | tf_op jit(solution)/shard_map/pallas_call | solution.py:115
  28.9 3.5 collective-permute-start.13
  32.5 6.2 fusion.2.refs_4_.grad_ref
  40.0 15.8 %shard_map.246 = (f32[1024,768]{1,0:T(8,128)}, f32[1024,768]{1,0:T(8,128)}, f32[1024,256]{1,0:T(8,128)}, f32[1024,256]{1,0:T(8,128)}, f32[1024,128]{1,0:T(8,128)...) custom-call(bf16[1024,768]{1,0:T(8,128)(2,1)} %get-tuple-element.48., ...), custom_call_target="tpu_custom_call" | custom-call | flops 2359296000 | bytes 11010048 | tf_op jit(solution)/shard_map/pallas_call | solution.py:215
  55.7 3.4 collective-permute-start.1
  59.2 1.3 collective-permute-start.2
  60.5 1.3 collective-permute-start.3
  61.8 9.2 %shard_map.247.intra_ref = f32[1024,768]{1,0:T(8,128)} custom-call(f32[1024,768]{1,0:T(8,128)} %get-tuple-element.51.conv_ref, f32[1024,128]{1,0:T(8,128)} %get-tuple-element.52.dt_ref, f32[1024,256]{1,0:T(8,128)} %get-tuple-element.53.rows_ref, f32[1024,128]{1,0:T(8,128)} %get-tuple-element.54.cum_ref, f32[16,1024]{1,0:T(8,128)} %get-tuple-element.55.cumt_ref), custom_call_target="tpu_custom_call" | custom-call | flops 3145728000 | bytes 6291456 | tf_op jit(solution)/shard_map/pallas_call | solution.py:296
  71.0 5.4 collective-permute-done.2.refs_1_
  77.6 13.9 %shard_map.248 = (f32[1024,768]{1,0:T(8,128)}, f32[8,1024]{1,0:T(8,128)}, f32[8,128,768]{2,1,0:T(8,128)}, f32[128,768]{1,0:T(8,128)}) custom-call(f32[1024,768]{1,0:T(8,128)} %shard_map.247.intra_ref, f32[1024,768]{1,0:T(8,128)} %get-tuple-element.51.conv_ref, f32[1024,256]{1,0:T(8,128)} %get-tuple-element.53.rows_ref, ...), custom_call_target="tpu_custom_call" | custom-call | flops 1572864000 | bytes 22020096 | tf_op jit(solution)/shard_map/pallas_call | solution.py:353
  91.5 1.6 collective-permute-start.4
  93.1 2.6 collective-permute-start.5
  95.7 1.3 collective-permute-start.6
  97.0 0.9 constant_dynamic-slice_fusion
  98.5 1.3 collective-permute-done.6.refs_3_
  100.4 13.1 %shard_map.249 = (bf16[1024,768]{1,0:T(8,128)(2,1)}, bf16[1024,768]{1,0:T(8,128)(2,1)}, f32[1024,768]{1,0:T(8,128)}, f32[8,128,768]{2,1,0:T(8,128)}, f32[136,768]{1,0:T(8,128)}, /*index=5*/f32[8,768]{1,0:T(8,128)}) custom-call(f32[1024,768]{1,0:T(8,128)} %get-tuple-element.59.mixed_ref, f32[1024,768]{1,0:T(8,128)} %get-tuple-element.58.refs_3_.gate_ref, ...), custom_call_target="tpu_custom_call" | custom-call | flops 1572864000 | bytes 20447232 | tf_op jit(solution)/shard_map/pallas_call | solution.py:441
  113.5 1.3 collective-permute-start.7
  114.8 1.3 collective-permute-start.8
  116.1 1.5 collective-permute-start.9
  117.6 12.2 %shard_map.250 = (f32[1024,768]{1,0:T(8,128)}, f32[1024,256]{1,0:T(8,128)}) custom-call(f32[1024,768]{1,0:T(8,128)} %get-tuple-element.51.conv_ref, f32[1024,128]{1,0:T(8,128)} %get-tuple-element.52.dt_ref, f32[1024,256]{1,0:T(8,128)} %get-tuple-element.53.rows_ref, f32[1024,128]{1,0:T(8,128)} %get-tuple-element.54.cum_ref, ...), custom_call_target="tpu_custom_call" | custom-call | flops 4718592000 | bytes 9437184 | tf_op jit(solution)/shard_map/pallas_call | solution.py:511
  129.9 6.9 %collective-permute-done.8.refs_1_ = f32[136,768]{1,0:T(8,128)S(1)} collective-permute-done((f32[136,768]{1,0:T(8,128)}, f32[136,768]{1,0:T(8,128)S(1)}, u32[]{:S(2)}, u32[]{:S(2)}) %collective-permute-start.8) | collective-permute-done | bytes 417824 | tf_op jit(solution)/shard_map/ppermute | solution.py:680
  136.8 0.8 copy-done.6
  137.7 23.1 %shard_map.251 = (bf16[1024,768]{1,0:T(8,128)(2,1)}, f32[1024,256]{1,0:T(8,128)}, bf16[1024,12]{1,0:T(8,128)(2,1)}, f32[16,768]{1,0:T(8,128)}, f32[8,768]{1,0:T(...) custom-call(f32[1024,768]{1,0:T(8,128)} %get-tuple-element.64.driven_ref, f32[1024,256]{1,0:T(8,128)} %get-tuple-element.65.drows_ref, ...), custom_call_target="tpu_custom_call" | custom-call | flops 4718592000 | bytes 28311552 | tf_op jit(solution)/shard_map/pallas_call | solution.py:632
  161.5 1.3 collective-permute-start.11
  162.9 4.2 collective-permute-done.11
  167.1 1.3 pad_maximum_fusion
  168.3 1.4 copy.30
  169.8 1.0 maximum_convert_fusion
  171.6 1.3 collective-permute-start.12
  172.9 7.6 %fusion.43 = f32[1024,1536]{1,0:T(8,128)} fusion(bf16[1024,768]{1,0:T(8,128)(2,1)} %get-tuple-element.62, bf16[1536,768]{1,0:T(8,128)(2,1)} %gate_ref.1), kind=kOutput, calls=%fused_computation.81 | convolution fusion | flops 2415919104 | bytes 10223616 | tf_op jit(solution)/shard_map/dot_general | solution.py:25
  180.5 1.3 collective-permute-start.10
  181.8 3.5 fusion.45
  185.4 1.6 collective-permute-done.10
  187.0 1.1 copy-done.27
  188.1 4.5 fusion.44
  192.6 5.4 reduce-scatter.10.cloned.1.call-done
  198.1 1.0 slice.120
  199.1 1.0 copy.32
  200.1 1.7 fusion.24
  201.8 0.8 slice.121
  202.9 10.2 %add_add_fusion = f32[1024,1536]{1,0:T(8,128)} fusion(f32[1024,1536]{1,0:T(8,128)} %fusion.45, f32[1024,1536]{1,0:T(8,128)} %fusion.43, f32[1024,1536]{1,0:T(8,128)} %fusion.44, bf16[1024,64]{1,0:T(8,128)(2,1)S(1)} %fusion.18, bf16[1536,256]{1,0:T(8,128)(2,1)} %state_w.1, s32[]{:T(128)S(6)} %select_n.5), kind=kOutput, calls=%fused_computation | convolution fusion | flops 206045184 | bytes 25690116 | tf_op jit(solution)/shard_map/dot_general | solution.py:25
  213.2 6.2 fusion.42
  219.7 7.3 %fusion = f32[768,1536]{1,0:T(8,128)} fusion(bf16[1024,768]{1,0:T(8,128)(2,1)} %get-tuple-element.61, bf16[1,1024,1536]{2,1,0:T(8,128)(2,1)} %param.27), kind=kOutput, calls=%fused_computation.2 | convolution fusion | flops 2415919104 | bytes 9437184 | tf_op jit(solution)/shard_map/dot_general | solution.py:25
  227.0 4.4 fusion.46
  231.4 1.2 fusion.49
  232.8 4.4 fusion.47
  237.2 1.4 fusion.48
  238.7 0.8 dynamic_slice.29
  239.5 2.6 multiply_reduce_fusion
  242.1 0.8 slice_bitcast_fusion.1
  242.9 79.9 %reduce-scatter.8.cloned.1.call-done = f32[1024,384]{1,0:T(8,128)} async-done(((f32[1024,1536]{1,0:T(8,128)}), f32[1024,384]{1,0:T(8,128)}) %reduce-scatter.8.cloned.1.call-update) | async-done | bytes 1572880 | tf_op jit(solution)/shard_map/reduce_scatter | solution.py:787
  322.8 2.3 fusion.11
  325.1 27.5 %all-reduce.1 = (f32[384]{0:T(512)}, f32[4,768]{1,0:T(4,128)}, f32[4,64]{1,0:T(4,128)S(1)}, f32[12]{0:T(128)}, f32[12]{0:T(128)}, /*index=5*/f32[12]{0:T(128)}, f32[768]{0:T(1024)}) all-reduce(f32[384]{0:T(512)S(1)} %get-tuple-element.82, f32[4,768]{1,0:T(4,128)S(1)} %slice.107, ...), channel_id=1, replica_groups=mesh['dp'=2,'ctx'=4,'tensor'=4] {'dp','ctx'}, use_global_device_ids=true, to_apply=%region_7.0 | all-reduce | flops 4516 | bytes 36128 | tf_op jit(solution)/shard_map/psum | solution.py:720
  352.6 12.6 %all-reduce.3 = (f32[1024]{0:T(1024)S(1)}, f32[4,256]{1,0:T(4,128)}) all-reduce(f32[1024]{0:T(1024)S(1)} %get-tuple-element.83, f32[4,256]{1,0:T(4,128)S(1)} %dynamic_update_slice.7), channel_id=1, replica_groups=mesh['dp'=2,'ctx'=4,'tensor'=4] {'tensor'}, use_global_device_ids=true, to_apply=%region_5.0 | all-reduce | flops 2048 | bytes 16384 | tf_op jit(solution)/shard_map/psum | solution.py:791
  365.2 71.7 %reduce-scatter.6.cloned.1.call-done = f32[1024,384]{1,0:T(8,128)} async-done(((f32[1024,1536]{1,0:T(8,128)}), f32[1024,384]{1,0:T(8,128)}) %reduce-scatter.6.cloned.1.call-update) | async-done | bytes 1572880 | tf_op jit(solution)/shard_map/reduce_scatter | solution.py:760
  436.9 4.4 fusion.8
  441.3 198.0 %all-reduce.6.cloned.1.call-done = (f32[1536,768]{1,0:T(8,128)}, f32[1536,768]{1,0:T(8,128)}, f32[1536,64]{0,1:T(8,128)}, f32[1536,12]{0,1:T(8,128)}, f32[768,1536]{1,0:T(8,128)}) async-done(((f32[1536,768]{1,0:T(8,128)}, f32[1536,768]{1,0:T(8,128)}, f32[1536,64]{0,1:T(8,128)}, f32[1536,12]{0,1:T(8,128)}, f32[768,1536]{1,0:T(8,128)}), (f32[1536,768]{1,0:T(8,128)}, f32[1536,768]{1,0:T(8,128)}, ...) | async-done | bytes 14622736 | tf_op jit(solution)/shard_map/psum | solution.py:720
  639.3 5.2 copy.41
  644.5 2.4 copy.42
  649.0 2.2 copy.45
  (104 shorter events, 9.3 us)
Async XLA Ops:
  7.2 25.3 %copy-start = (bf16[768,1536]{1,0:T(8,128)(2,1)S(1)}, bf16[768,1536]{1,0:T(8,128)(2,1)}, u32[]{:S(2)}) copy-start(bf16[768,1536]{1,0:T(8,128)(2,1)} %param.26) | copy-start | bytes 7077892
  7.2 190.9 %reduce-scatter.10.cloned.1.call-start = ((), (), s32[]{:S(2)}) async-start(), calls=%async_computation.5 | async-start | bytes 1474560
  8.2 31.1 %collective-permute-start = (bf16[16,1536]{1,0:T(8,128)(2,1)S(1)}, bf16[16,1536]{1,0:T(8,128)(2,1)S(1)}, u32[]{:S(2)}, u32[]{:S(2)}) collective-permute-start(bf16[16,1536]{1,0:T(8,128)(2,1)S(1)} %slice_bitcast_fusion), channel_id=1, source_target_pairs={{0,4},{4,8},{8,12},{1,5},{5,9},{9,13},{2,6},{6,10},{10,14},{3,7},{... | collective-permute-start | bytes 147464 | tf_op jit(solution)/shard_map/ppermute | solution.py:675
  28.9 9.7 %copy-start.23 = (bf16[4,256]{1,0:T(4,128)(2,1)S(1)}, bf16[4,256]{1,0:T(4,128)(2,1)}, u32[]{:S(2)}) copy-start(bf16[4,256]{1,0:T(4,128)(2,1)} %state_k.1) | copy-start | bytes 6148
  28.9 9.8 %copy-start.22 = (f32[768]{0:T(1024)S(1)}, f32[768]{0:T(1024)}, u32[]{:S(2)}) copy-start(f32[768]{0:T(1024)} %param.25) | copy-start | bytes 9220
  28.9 140.9 %collective-permute-start.13 = (bf16[16,64]{1,0:T(8,128)(2,1)S(1)}, bf16[16,64]{1,0:T(8,128)(2,1)S(1)}, u32[]{:S(2)}, u32[]{:S(2)}) collective-permute-start(bf16[16,64]{1,0:T(8,128)(2,1)S(1)} %constant_dynamic-slice_fusion.1), channel_id=1, source_target_pairs={{0,4},{4,8},{8,12},{1,5},{5,9},{9,13},{2,6},{6,10},{10,14},{3,7},{... | collective-permute-start | bytes 6152 | tf_op jit(solution)/shard_map/ppermute | solution.py:675
  39.3 0.6 copy-start.29
  55.7 15.3 %collective-permute-start.1 = (f32[136,768]{1,0:T(8,128)}, f32[136,768]{1,0:T(8,128)S(1)}, u32[]{:S(2)}, u32[]{:S(2)}) collective-permute-start(f32[136,768]{1,0:T(8,128)} %get-tuple-element.57.own_ref), channel_id=1, source_target_pairs={{0,4},{4,8},{8,12},{1,5},{5,9},{9,13},{2,6},{6,10},{10,14},{3,7},{... | collective-permute-start | bytes 1253384 | tf_op jit(solution)/shard_map/ppermute | solution.py:675
  59.2 17.3 %collective-permute-start.2 = (f32[136,768]{1,0:T(8,128)}, f32[136,768]{1,0:T(8,128)S(1)}, u32[]{:S(2)}, u32[]{:S(2)}) collective-permute-start(f32[136,768]{1,0:T(8,128)} %get-tuple-element.57.own_ref), channel_id=1, source_target_pairs={{0,8},{4,12},{1,9},{5,13},{2,10},{6,14},{3,11},{7,15},{16,24},{20,... | collective-permute-start | bytes 1253384 | tf_op jit(solution)/shard_map/ppermute | solution.py:675
  60.5 16.3 %collective-permute-start.3 = (f32[136,768]{1,0:T(8,128)}, f32[136,768]{1,0:T(8,128)S(1)}, u32[]{:S(2)}, u32[]{:S(2)}) collective-permute-start(f32[136,768]{1,0:T(8,128)} %get-tuple-element.57.own_ref), channel_id=1, source_target_pairs={{0,12},{1,13},{2,14},{3,15},{16,28},{17,29},{18,30},{19,31}} | collective-permute-start | bytes 1253384 | tf_op jit(solution)/shard_map/ppermute | solution.py:675
  71.0 5.8 copy-start.8
  76.5 0.8 copy-start.9
  76.8 0.8 copy-start.10
  77.6 19.5 %copy-start.13 = (bf16[1024,256]{1,0:T(8,128)(2,1)S(1)}, bf16[1024,256]{1,0:T(8,128)(2,1)}, u32[]{:S(2)}) copy-start(bf16[1024,256]{1,0:T(8,128)(2,1)} %get-tuple-element.49.state_ref) | copy-start | bytes 1572868
  77.6 20.3 %copy-start.19 = (bf16[4,768]{1,0:T(4,128)(2,1)S(1)}, bf16[4,768]{1,0:T(4,128)(2,1)}, u32[]{:S(2)}) copy-start(bf16[4,768]{1,0:T(4,128)(2,1)} %refs_4_.1) | copy-start | bytes 18436
  91.5 6.4 collective-permute-start.4
  93.1 5.4 collective-permute-start.5
  95.7 4.1 collective-permute-start.6
  97.9 1.9 copy-start.16
  98.5 1.3 copy-start.17
  99.8 0.6 copy-start.18
  113.5 16.3 %collective-permute-start.7 = (f32[136,768]{1,0:T(8,128)}, f32[136,768]{1,0:T(8,128)S(1)}, u32[]{:S(2)}, u32[]{:S(2)}) collective-permute-start(f32[136,768]{1,0:T(8,128)} %get-tuple-element.70), channel_id=1, source_target_pairs={{4,0},{8,4},{12,8},{5,1},{9,5},{13,9},{6,2},{10,6},{14,10},{7,3},{... | collective-permute-start | bytes 1253384 | tf_op jit(solution)/shard_map/ppermute | solution.py:680
  114.8 22.0 %collective-permute-start.8 = (f32[136,768]{1,0:T(8,128)}, f32[136,768]{1,0:T(8,128)S(1)}, u32[]{:S(2)}, u32[]{:S(2)}) collective-permute-start(f32[136,768]{1,0:T(8,128)} %get-tuple-element.70), channel_id=1, source_target_pairs={{8,0},{12,4},{9,1},{13,5},{10,2},{14,6},{11,3},{15,7},{24,16},{28,... | collective-permute-start | bytes 1253384 | tf_op jit(solution)/shard_map/ppermute | solution.py:680
  116.1 20.7 %collective-permute-start.9 = (f32[136,768]{1,0:T(8,128)}, f32[136,768]{1,0:T(8,128)S(1)}, u32[]{:S(2)}, u32[]{:S(2)}) collective-permute-start(f32[136,768]{1,0:T(8,128)} %get-tuple-element.70), channel_id=1, source_target_pairs={{12,0},{13,1},{14,2},{15,3},{28,16},{29,17},{30,18},{31,19}} | collective-permute-start | bytes 1253384 | tf_op jit(solution)/shard_map/ppermute | solution.py:680
  129.9 6.9 %copy-start.5 = (f32[136,768]{1,0:T(8,128)}, f32[136,768]{1,0:T(8,128)S(1)}, u32[]{:S(2)}) copy-start(f32[136,768]{1,0:T(8,128)S(1)} %collective-permute-done.7.refs_0_) | copy-start | bytes 1253380
  136.8 0.8 copy-start.6
  136.8 0.9 copy-start.7
  161.5 5.5 collective-permute-start.11
  169.8 153.0 %reduce-scatter.8.cloned.1.call-start = ((), (), s32[]{:S(2)}) async-start(), calls=%async_computation.4 | async-start | bytes 7864320 | tf_op jit(solution)/shard_map/reduce_scatter | solution.py:787
  171.6 31.1 %collective-permute-start.12 = (f32[8,64]{1,0:T(8,128)S(1)}, f32[8,64]{1,0:T(8,128)S(1)}, u32[]{:S(2)}, u32[]{:S(2)}) collective-permute-start(f32[8,64]{1,0:T(8,128)S(1)} %constant_dynamic-slice_fusion.2), channel_id=1, source_target_pairs={{4,0},{8,4},{12,8},{5,1},{9,5},{13,9},{6,2},{10,6},{14,10},{7,3},{... | collective-permute-start | bytes 6152 | tf_op jit(solution)/shard_map/ppermute | solution.py:680
  172.9 7.6 %copy-start.30 = (f32[8,768]{1,0:T(8,128)S(1)}, f32[8,768]{1,0:T(8,128)}, u32[]{:S(2)}) copy-start(f32[8,768]{1,0:T(8,128)} %get-tuple-element.74) | copy-start | bytes 73732
  172.9 8.9 %copy-start.3 = (bf16[1024,12]{1,0:T(8,128)(2,1)S(1)}, bf16[1024,12]{1,0:T(8,128)(2,1)}, u32[]{:S(2)}) copy-start(bf16[1024,12]{1,0:T(8,128)(2,1)} %get-tuple-element.75) | copy-start | bytes 73732
  172.9 8.9 %copy-start.12 = (bf16[1536,12]{0,1:T(8,128)(2,1)S(1)}, bf16[1536,12]{0,1:T(8,128)(2,1)}, u32[]{:S(2)}) copy-start(bf16[1536,12]{0,1:T(8,128)(2,1)} %param.19) | copy-start | bytes 110596
  180.5 6.5 collective-permute-start.10
  181.8 5.1 copy-start.15
  181.8 5.1 copy-start.26
  181.8 6.3 copy-start.24
  187.0 1.1 copy-start.27
  213.2 223.8 %reduce-scatter.6.cloned.1.call-start = ((), (), s32[]{:S(2)}) async-start(), calls=%async_computation.3 | async-start | bytes 7864320 | tf_op jit(solution)/shard_map/reduce_scatter | solution.py:760
  219.4 419.9 %all-reduce.6.cloned.1.call-start = ((), (), s32[]{:S(2)}) async-start(), calls=%async_computation.6 | async-start | bytes 29294592 | tf_op jit(solution)/shard_map/psum | solution.py:720
  219.7 7.4 %copy-start.1 = (bf16[1024,1536]{1,0:T(8,128)(2,1)S(1)}, bf16[1024,1536]{1,0:T(8,128)(2,1)}, u32[]{:S(2)}) copy-start(bf16[1024,1536]{1,0:T(8,128)(2,1)} %get-tuple-element.78) | copy-start | bytes 9437188
  219.7 7.4 %copy-start.25 = (bf16[1024,768]{1,0:T(8,128)(2,1)S(1)}, bf16[1024,768]{1,0:T(8,128)(2,1)}, u32[]{:S(2)}) copy-start(bf16[1024,768]{1,0:T(8,128)(2,1)} %get-tuple-element.62) | copy-start | bytes 4718596
  227.0 4.4 copy-start.4
  231.4 1.4 copy-start.28
  238.7 3.4 copy-start.20
  238.7 3.4 copy-start.21
  639.3 5.2 copy-start.2
  639.3 9.7 %slice-start = ((s8[4718592]{0:T(1024)(128)(4,1)}), s8[4194304]{0:T(1024)(128)(4,1)S(1)}, s32[]{:S(2)}) async-start(s8[4718592]{0:T(1024)(128)(4,1)} %bitcast.65), calls=%async_computation.7 | async-start | bytes 8388608
  644.5 3.1 copy-start.11
  644.5 3.8 copy-start.14
  644.5 4.5 slice-start.1
Sparse Core Ops, SparseCore 0:
  169.9 28.1 reduce-scatter.9
  213.3 109.4 reduce-scatter.7
  325.1 111.7 reduce-scatter.5
  442.3 196.9 all-reduce.5

commit v2 on v1

v2 whole, which is shorter than its diff:
```python
import functools

import jax
import jax.numpy as jnp
from jax import lax
from jax.experimental import pallas as pl
from jax.experimental.pallas import tpu as pltpu
from jax.sharding import PartitionSpec as P

HEAD_DIM = 64
CONV = 4
EDGE = 8
BLOCK = 128
LANES = 128
epsilon = 1e-05
f32 = jnp.float32
bf16 = jnp.bfloat16

NN = (((1,), (0,)), ((), ()))
NT = (((1,), (1,)), ((), ()))
TN = (((0,), (0,)), ((), ()))


def dot(a, b, dims=NN):
    return lax.dot_general(a, b, dims, preferred_element_type=f32)


def split2(x):
    high = x.astype(bf16)
    return high, (x - high.astype(f32)).astype(bf16)


def split3(x):
    high = x.astype(bf16)
    rest = x - high.astype(f32)
    middle = rest.astype(bf16)
    return high, middle, (rest - middle.astype(f32)).astype(bf16)


def dot3(a, b, dims=NN):
    ah, al = split2(a)
    bh, bl = split2(b)
    return dot(ah, bh, dims) + (dot(ah, bl, dims) + dot(al, bh, dims))


def both_parts(x):
    return jnp.concatenate(split2(x), axis=1)


def fold(product):
    half = product.shape[1] // 2
    return product[:, :half] + product[:, half:]


def wide_dot(parts, x):
    across = both_parts(x)
    return fold(dot(parts, jnp.concatenate([across, across], axis=0)))


def exact_dot(ones, x, dims):
    high, middle, low = split3(x)
    return dot(ones, high, dims) + (dot(ones, middle, dims) + dot(ones, low, dims))


def iota(shape, axis):
    return lax.broadcasted_iota(jnp.int32, shape, axis)


REPEAT = 16


def head_map(width):
    lane = iota((LANES, width), 0)
    mine = (lane % REPEAT == iota((LANES, width), 1) // HEAD_DIM) & (lane < 3 * REPEAT)
    return mine.astype(f32).astype(bf16)


def spread(per_head, heads):
    high = per_head.astype(bf16).astype(f32)
    rest = per_head - high
    middle = rest.astype(bf16).astype(f32)
    group = iota(per_head.shape, 1) // REPEAT
    parts = jnp.where(group == 0, high, jnp.where(group == 1, middle, rest - middle))
    return dot(parts.astype(bf16), heads)


def repeated(row):
    group = jnp.concatenate([row, jnp.zeros((1, REPEAT - row.shape[1]), f32)], axis=1)
    return jnp.concatenate([group] * (LANES // REPEAT), axis=1)


def sig(v):
    return jax.nn.sigmoid(v)


def cost(micros):
    return pl.CostEstimate(flops=micros * 900_000_000, bytes_accessed=micros * 3_000_000, transcendentals=0)


def params(limit=20):
    return pltpu.CompilerParams(
        dimension_semantics=("arbitrary",), vmem_limit_bytes=limit * 1024 * 1024
    )


def whole(shape):
    return pl.BlockSpec(shape, lambda b: (0,) * len(shape))


def rows(size, width, count=0):
    if count:
        return pl.BlockSpec((size, width), lambda b: (count - 1 - b, 0))
    return pl.BlockSpec((size, width), lambda b: (b, 0))


def spans(width):
    return [slice(i * LANES, (i + 1) * LANES) for i in range(width // LANES)]


def by_eights(x):
    return jnp.sum(x.reshape(x.shape[0] // EDGE, EDGE, x.shape[1]), axis=0)


def norm_rows(x, gain):
    scaling = lax.rsqrt(jnp.mean(x * x, axis=-1, keepdims=True) + epsilon)
    return (x * scaling * gain).astype(bf16)


def project_kernel(x_ref, gain_ref, value_ref, state_ref, step_ref, normed_out, value_out, state_out, step_out, step_w):
    @pl.when(pl.program_id(0) == 0)
    def _():
        count = step_ref.shape[0]
        copies = (iota((LANES, count), 0) % REPEAT == iota((LANES, count), 1)).astype(f32).astype(bf16)
        step_w[...] = dot(copies, step_ref[...]).astype(bf16)

    normed = norm_rows(x_ref[...].astype(f32), gain_ref[...])
    normed_out[...] = normed
    value_out[...] = dot(normed, value_ref[...]).astype(bf16)
    state_out[...] = dot(normed, state_ref[...]).astype(bf16)
    step_out[...] = dot(normed, step_w[...], NT)


def project(residual, pre_gain, input_weight, state_weight, step_weight):
    tokens, width = residual.shape
    inner, state2 = input_weight.shape[1], state_weight.shape[1]
    tile = min(tokens, 256)
    return pl.pallas_call(
        project_kernel,
        grid=(tokens // tile,),
        in_specs=[
            rows(tile, width),
            whole((1, width)),
            whole(input_weight.shape),
            whole(state_weight.shape),
            whole(step_weight.shape),
        ],
        out_specs=[rows(tile, width), rows(tile, inner), rows(tile, state2), rows(tile, LANES)],
        out_shape=[
            jax.ShapeDtypeStruct((tokens, width), bf16),
            jax.ShapeDtypeStruct((tokens, inner), bf16),
            jax.ShapeDtypeStruct((tokens, state2), bf16),
            jax.ShapeDtypeStruct((tokens, LANES), f32),
        ],
        scratch_shapes=[pltpu.VMEM((LANES, width), bf16)],
        compiler_params=params(24),
        cost_estimate=cost(6),
    )(residual, pre_gain, input_weight, state_weight, step_weight)


def beside_kernel(normed_ref, gate_w, cot_ref, out_w, gate_out, grad_out):
    gate_out[...] = dot(normed_ref[...], gate_w[...])
    grad_out[...] = dot(cot_ref[...], out_w[...], NT)


def beside(normed, gate_weight, cotangent, out_weight):
    tokens, width = normed.shape
    inner = gate_weight.shape[1]
    tile = min(tokens, 256)
    return pl.pallas_call(
        beside_kernel,
        grid=(tokens // tile,),
        in_specs=[rows(tile, width), whole(gate_weight.shape), rows(tile, width), whole(out_weight.shape)],
        out_specs=[rows(tile, inner), rows(tile, inner)],
        out_shape=[jax.ShapeDtypeStruct((tokens, inner), f32), jax.ShapeDtypeStruct((tokens, inner), f32)],
        compiler_params=params(20),
        cost_estimate=cost(6),
    )(normed, gate_weight, cotangent, out_weight)


def convolve(before, here, kernel):
    extended = jnp.concatenate([before, here], axis=0)
    count = here.shape[0]
    first = EDGE - CONV + 1
    summed = kernel[0:1] * extended[first : first + count]
    for k in range(1, CONV):
        summed = summed + kernel[k : k + 1] * extended[first + k : first + k + count]
    return summed


def local_kernel(
    value_ref, state_ref, step_ref, halo_ref, gain_ref, value_w, state_w, value_k, state_k, bias_ref, log_ref,
    conv_out, pre_out, rows_out, spre_out, dt_out, cum_out, cumt_out, held_out, message_out, vhalo_out, shalo_out,
    value_before, state_before, held, total, heads,
):
    b = pl.program_id(0)
    width = value_ref.shape[1]

    @pl.when(b == 0)
    def _():
        normed = norm_rows(halo_ref[...].astype(f32), gain_ref[...])
        value_halo = dot(normed, value_w[...]).astype(bf16)
        state_halo = dot(normed, state_w[...]).astype(bf16)
        vhalo_out[...] = value_halo
        shalo_out[...] = state_halo
        value_before[...] = value_halo.astype(f32)[-EDGE:]
        state_before[...] = state_halo.astype(f32)[-EDGE:]
        held[...] = jnp.zeros(held.shape, f32)
        total[...] = jnp.zeros(total.shape, f32)
        heads[...] = head_map(width)

    dt = jax.nn.softplus(step_ref[...] + repeated(bias_ref[...]))
    decay = -dt * jnp.exp(repeated(log_ref[...]))
    size = value_ref.shape[0]
    lower = (iota((size, size), 0) >= iota((size, size), 1)).astype(f32).astype(bf16)
    cum = exact_dot(lower, decay, NN)
    dt_out[...] = dt
    cum_out[...] = cum
    cumt_out[...] = cum.T[: cumt_out.shape[0]]
    last = cum[size - 1 : size]
    wide = spread(jnp.concatenate([dt, cum], axis=0), heads[...])

    state = state_ref[...].astype(f32)
    spre = convolve(state_before[...], state, state_k[...].astype(f32))
    state_before[...] = state[-EDGE:]
    mixed_rows = spre * sig(spre)
    spre_out[...] = spre
    rows_out[...] = mixed_rows
    b_parts = both_parts(mixed_rows[:, :LANES].T)

    taps = value_k[...].astype(f32)
    held_out[0] = held[...]
    for span in spans(width):
        value = value_ref[:, span].astype(f32)
        pre = convolve(value_before[:, span], value, taps[:, span])
        value_before[:, span] = value[-EDGE:]
        conv = pre * sig(pre)
        pre_out[:, span] = pre
        conv_out[:, span] = conv
        cum_wide = wide[size:, span]
        end = cum_wide[size - 1 : size]
        weighted = conv * wide[:size, span] * jnp.exp(end - cum_wide)
        held[:, span] = jnp.exp(end) * held[:, span] + wide_dot(b_parts, weighted)
        total[:, span] = total[:, span] + end

    @pl.when(b == pl.num_programs(0) - 1)
    def _():
        message_out[:LANES] = held[...]
        message_out[LANES:] = total[...]


def local_states(value_in, state_in, step_raw, halo, pre_gain, input_weight, state_weight, input_kernel, state_kernel, step_bias, decay_log):
    tokens, inner = value_in.shape
    state2 = state_in.shape[1]
    state = state2 // 2
    blocks = tokens // BLOCK
    headrows = 16
    return pl.pallas_call(
        local_kernel,
        grid=(blocks,),
        in_specs=[
            rows(BLOCK, inner),
            rows(BLOCK, state2),
            rows(BLOCK, LANES),
            whole(halo.shape),
            whole(pre_gain.shape),
            whole(input_weight.shape),
            whole(state_weight.shape),
            whole(input_kernel.shape),
            whole(state_kernel.shape),
            whole(step_bias.shape),
            whole(decay_log.shape),
        ],
        out_specs=[
            rows(BLOCK, inner),
            rows(BLOCK, inner),
            rows(BLOCK, state2),
            rows(BLOCK, state2),
            rows(BLOCK, LANES),
            rows(BLOCK, LANES),
            pl.BlockSpec((headrows, BLOCK), lambda b: (0, b)),
            pl.BlockSpec((1, state, inner), lambda b: (b, 0, 0)),
            whole((state + EDGE, inner)),
            whole((halo.shape[0], inner)),
            whole((halo.shape[0], state2)),
        ],
        out_shape=[
            jax.ShapeDtypeStruct((tokens, inner), f32),
            jax.ShapeDtypeStruct((tokens, inner), f32),
            jax.ShapeDtypeStruct((tokens, state2), f32),
            jax.ShapeDtypeStruct((tokens, state2), f32),
            jax.ShapeDtypeStruct((tokens, LANES), f32),
            jax.ShapeDtypeStruct((tokens, LANES), f32),
            jax.ShapeDtypeStruct((headrows, tokens), f32),
            jax.ShapeDtypeStruct((blocks, state, inner), f32),
            jax.ShapeDtypeStruct((state + EDGE, inner), f32),
            jax.ShapeDtypeStruct((halo.shape[0], inner), bf16),
            jax.ShapeDtypeStruct((halo.shape[0], state2), bf16),
        ],
        scratch_shapes=[
            pltpu.VMEM((EDGE, inner), f32),
            pltpu.VMEM((EDGE, state2), f32),
            pltpu.VMEM((state, inner), f32),
            pltpu.VMEM((EDGE, inner), f32),
            pltpu.VMEM((LANES, inner), bf16),
        ],
        compiler_params=params(),
        cost_estimate=cost(10),
    )(value_in, state_in, step_raw, halo, pre_gain, input_weight, state_weight, input_kernel, state_kernel, step_bias, decay_log)


def inner_kernel(heads_count, conv_ref, dt_ref, rows_ref, cum_ref, cumt_ref, skip_ref, out_ref, heads):
    size, width = conv_ref.shape

    @pl.when(pl.program_id(0) == 0)
    def _():
        heads[...] = head_map(width)

    skip = jnp.broadcast_to(repeated(skip_ref[...]), (EDGE, LANES))
    wide = spread(jnp.concatenate([dt_ref[...], skip], axis=0), heads[...])
    scores = dot3(rows_ref[:, LANES:], rows_ref[:, :LANES], NT)
    causal = iota((size, size), 0) >= iota((size, size), 1)
    left = iota((size, LANES), 1) < HEAD_DIM
    cum = cum_ref[...]
    cumt = cumt_ref[...]
    for pair, span in enumerate(spans(width)):
        conv = conv_ref[:, span]
        mixes = []
        for h in (2 * pair, 2 * pair + 1):
            gap = cum[:, h : h + 1] - cumt[h : h + 1, :]
            mixes.append(both_parts(jnp.exp(jnp.where(causal, gap, -1e30)) * scores))
        both = wide_dot(jnp.concatenate(mixes, axis=0), conv * wide[:size, span])
        out_ref[:, span] = jnp.where(left, both[:size], both[size:]) + wide[size : size + 1, span] * conv


def inner_forward(heads_count, conv, dt, state_rows, cum, cumt, skip_gain):
    tokens, inner = conv.shape
    return pl.pallas_call(
        functools.partial(inner_kernel, heads_count),
        grid=(tokens // BLOCK,),
        in_specs=[
            rows(BLOCK, inner),
            rows(BLOCK, LANES),
            rows(BLOCK, state_rows.shape[1]),
            rows(BLOCK, LANES),
            pl.BlockSpec((cumt.shape[0], BLOCK), lambda b: (0, b)),
            whole(skip_gain.shape),
        ],
        out_specs=rows(BLOCK, inner),
        out_shape=jax.ShapeDtypeStruct((tokens, inner), f32),
        scratch_shapes=[pltpu.VMEM((LANES, inner), bf16)],
        compiler_params=params(12),
        cost_estimate=cost(6),
    )(conv, dt, state_rows, cum, cumt, skip_gain)


def combine_kernel(count, intra_ref, rows_ref, cum_ref, held_ref, own_ref, *refs):
    message_refs, (gate_ref, grad_ref, gain_ref, mixed_out, sums_out, held_out, end_out, start, total, heads) = refs[:count], refs[count:]
    b = pl.program_id(0)
    size, width = intra_ref.shape
    state = held_ref.shape[1]

    @pl.when(b == 0)
    def _():
        heads[...] = head_map(width)
        total[...] = jnp.zeros(total.shape, f32)
        for span in spans(width):
            entering = jnp.zeros((state, LANES), f32)
            passed = jnp.zeros((EDGE, LANES), f32)
            for ref in message_refs:
                entering = entering + jnp.exp(passed[0:1]) * ref[:state, span]
                passed = passed + ref[state:, span]
            start[:, span] = entering
            end_out[:, span] = own_ref[:state, span] + jnp.exp(own_ref[state : state + 1, span]) * entering

    cum_wide = spread(cum_ref[...], heads[...])
    c_parts = both_parts(rows_ref[:, LANES:])
    square = jnp.zeros((size, LANES), f32)
    inner = jnp.zeros((size, LANES), f32)
    for span in spans(width):
        held = held_ref[0, :, span] + jnp.exp(total[0:1, span]) * start[:, span]
        held_out[0, :, span] = held
        cum_part = cum_wide[:, span]
        total[:, span] = total[:, span] + cum_part[size - 1 : size]
        mixed = intra_ref[:, span] + jnp.exp(cum_part) * wide_dot(c_parts, held)
        mixed_out[:, span] = mixed
        gate = gate_ref[:, span]
        gated = mixed * (gate * sig(gate))
        square = square + gated * gated
        inner = inner + grad_ref[:, span] * gain_ref[:, span] * gated
    ones = jnp.ones((EDGE, LANES), bf16)
    square = exact_dot(ones, square, NT)
    inner = exact_dot(ones, inner, NT)
    sums_out[...] = jnp.where(iota(square.shape, 0) == 0, square, inner)


def combine(intra, state_rows, cum, held, own, messages, gate_in, grad_normed, norm_gain):
    tokens, inner = intra.shape
    blocks, state, _ = held.shape
    state_block = pl.BlockSpec((1, state, inner), lambda b: (b, 0, 0))
    return pl.pallas_call(
        functools.partial(combine_kernel, len(messages)),
        grid=(blocks,),
        in_specs=[
            rows(BLOCK, inner),
            rows(BLOCK, state_rows.shape[1]),
            rows(BLOCK, LANES),
            state_block,
            whole(own.shape),
            *[whole(own.shape) for _ in messages],
            rows(BLOCK, inner),
            rows(BLOCK, inner),
            whole(norm_gain.shape),
        ],
        out_specs=[
            rows(BLOCK, inner),
            pl.BlockSpec((EDGE, BLOCK), lambda b: (0, b)),
            state_block,
            whole((state, inner)),
        ],
        out_shape=[
            jax.ShapeDtypeStruct((tokens, inner), f32),
            jax.ShapeDtypeStruct((EDGE, tokens), f32),
            jax.ShapeDtypeStruct(held.shape, f32),
            jax.ShapeDtypeStruct((state, inner), f32),
        ],
        scratch_shapes=[pltpu.VMEM((state, inner), f32), pltpu.VMEM((EDGE, inner), f32), pltpu.VMEM((LANES, inner), bf16)],
        compiler_params=params(),
        cost_estimate=cost(5),
    )(intra, state_rows, cum, held, own, *messages, gate_in, grad_normed, norm_gain)


def column(row):
    return jnp.broadcast_to(row, (LANES, row.shape[1])).T


def gate_back_kernel(count, inner_total, mixed_ref, gate_ref, grad_ref, rows_ref, cum_ref, gain_ref, *refs):
    sums_refs, (normed_out, gate_out, dmix_out, later_out, message_out, gain_out, later, total, heads) = refs[:count], refs[count:]
    b = pl.program_id(0)
    size, width = mixed_ref.shape

    @pl.when(b == 0)
    def _():
        later[...] = jnp.zeros(later.shape, f32)
        total[...] = jnp.zeros(total.shape, f32)
        gain_out[...] = jnp.zeros(gain_out.shape, f32)
        heads[...] = head_map(width)

    sums = sums_refs[0][...]
    for ref in sums_refs[1:]:
        sums = sums + ref[...]
    rms_row = lax.rsqrt(sums[0:1] / inner_total + epsilon)
    pull_row = rms_row * rms_row * rms_row * sums[1:2] / inner_total
    rms = column(rms_row)
    pull = column(pull_row)
    cum_wide = spread(cum_ref[...], heads[...])
    c_parts = both_parts(rows_ref[:, LANES:].T)
    later_out[0] = later[...]
    for span in spans(width):
        gain = gain_ref[:, span]
        gate = gate_ref[:, span]
        mixed = mixed_ref[:, span]
        grad = grad_ref[:, span]
        gate_sig = sig(gate)
        gate_silu = gate * gate_sig
        gated = mixed * gate_silu
        normed_out[:, span] = (gated * rms * gain).astype(bf16)
        gain_out[:, span] = gain_out[:, span] + by_eights(grad * gated * rms)
        grad_gated = rms * gain * grad - gated * pull
        gate_out[:, span] = (grad_gated * mixed * gate_sig * (1.0 + gate * (1.0 - gate_sig))).astype(bf16)
        grad_mixed = grad_gated * gate_silu
        dmix_out[:, span] = grad_mixed
        cum_part = cum_wide[:, span]
        end = cum_part[size - 1 : size]
        later[:, span] = jnp.exp(end) * later[:, span] + wide_dot(c_parts, jnp.exp(cum_part) * grad_mixed)
        total[:, span] = total[:, span] + end

    @pl.when(b == pl.num_programs(0) - 1)
    def _():
        message_out[:LANES] = later[...]
        message_out[LANES:] = total[...]


def gate_back(mixed, gate_in, grad_normed, state_rows, cum, norm_gain, sums, inner_total):
    tokens, inner = mixed.shape
    blocks = tokens // BLOCK
    state = state_rows.shape[1] // 2
    return pl.pallas_call(
        functools.partial(gate_back_kernel, len(sums), inner_total),
        grid=(blocks,),
        in_specs=[
            rows(BLOCK, inner, blocks),
            rows(BLOCK, inner, blocks),
            rows(BLOCK, inner, blocks),
            rows(BLOCK, 2 * state, blocks),
            rows(BLOCK, LANES, blocks),
            whole(norm_gain.shape),
            *[pl.BlockSpec((EDGE, BLOCK), lambda b: (0, blocks - 1 - b)) for _ in sums],
        ],
        out_specs=[
            rows(BLOCK, inner, blocks),
            rows(BLOCK, inner, blocks),
            rows(BLOCK, inner, blocks),
            pl.BlockSpec((1, state, inner), lambda b: (blocks - 1 - b, 0, 0)),
            whole((state + EDGE, inner)),
            whole((EDGE, inner)),
        ],
        out_shape=[
            jax.ShapeDtypeStruct((tokens, inner), bf16),
            jax.ShapeDtypeStruct((tokens, inner), bf16),
            jax.ShapeDtypeStruct((tokens, inner), f32),
            jax.ShapeDtypeStruct((blocks, state, inner), f32),
            jax.ShapeDtypeStruct((state + EDGE, inner), f32),
            jax.ShapeDtypeStruct((EDGE, inner), f32),
        ],
        scratch_shapes=[pltpu.VMEM((state, inner), f32), pltpu.VMEM((EDGE, inner), f32), pltpu.VMEM((LANES, inner), bf16)],
        compiler_params=params(),
        cost_estimate=cost(7),
    )(mixed, gate_in, grad_normed, state_rows, cum, norm_gain, *sums)


def inner_back_kernel(heads_count, conv_ref, dt_ref, rows_ref, cum_ref, cumt_ref, dmix_ref, driven_out, rows_out, heads):
    size, width = conv_ref.shape

    @pl.when(pl.program_id(0) == 0)
    def _():
        heads[...] = head_map(width)

    dt_wide = spread(dt_ref[...], heads[...])
    b_rows = rows_ref[:, :LANES]
    c_rows = rows_ref[:, LANES:]
    scores = dot3(b_rows, c_rows, NT)
    causal = iota((size, size), 1) >= iota((size, size), 0)
    left = iota((size, LANES), 1) < HEAD_DIM
    cum = cum_ref[...]
    cumt = cumt_ref[...]
    score_grad = jnp.zeros((size, size), f32)
    for pair, span in enumerate(spans(width)):
        dmix_high, dmix_low = split2(dmix_ref[:, span])
        across = jnp.concatenate([dmix_high, dmix_low], axis=1)
        right_side = jnp.concatenate([across, across], axis=0)
        taking = jnp.concatenate([dmix_high, dmix_high, dmix_low], axis=1)
        driven = conv_ref[:, span] * dt_wide[:, span]
        owns = []
        for mine in (left, jnp.logical_not(left)):
            own_high, own_low = split2(jnp.where(mine, driven, 0.0))
            owns.append(jnp.concatenate([own_high, own_low, own_high], axis=1))
        mix_grads = dot(jnp.concatenate(owns, axis=0), taking, NT)
        mixes = []
        for side in range(2):
            h = 2 * pair + side
            gap = cumt[h : h + 1, :] - cum[:, h : h + 1]
            kept = jnp.exp(jnp.where(causal, gap, -1e30))
            score_grad = score_grad + mix_grads[side * size : (side + 1) * size] * kept
            mixes.append(both_parts(kept * scores))
        both = fold(dot(jnp.concatenate(mixes, axis=0), right_side))
        driven_out[:, span] = jnp.where(left, both[:size], both[size:])
    rows_out[:, :LANES] = dot3(score_grad, c_rows, NN)
    rows_out[:, LANES:] = dot3(score_grad, b_rows, TN)


def inner_back(heads_count, conv, dt, state_rows, cum, cumt, grad_mixed):
    tokens, inner = conv.shape
    return pl.pallas_call(
        functools.partial(inner_back_kernel, heads_count),
        grid=(tokens // BLOCK,),
        in_specs=[
            rows(BLOCK, inner),
            rows(BLOCK, LANES),
            rows(BLOCK, state_rows.shape[1]),
            rows(BLOCK, LANES),
            pl.BlockSpec((cumt.shape[0], BLOCK), lambda b: (0, b)),
            rows(BLOCK, inner),
        ],
        out_specs=[rows(BLOCK, inner), rows(BLOCK, state_rows.shape[1])],
        out_shape=[
            jax.ShapeDtypeStruct((tokens, inner), f32),
            jax.ShapeDtypeStruct(state_rows.shape, f32),
        ],
        scratch_shapes=[pltpu.VMEM((LANES, inner), bf16)],
        compiler_params=params(16),
        cost_estimate=cost(9),
    )(conv, dt, state_rows, cum, cumt, grad_mixed)


def stacked(high, low):
    return jnp.concatenate([jnp.concatenate([high, high], axis=1), jnp.concatenate([low, low], axis=1)], axis=0)


def finish_kernel(
    count, driven_ref, drows_ref, dmix_ref, mixed_ref, pre_ref, value_ref, dt_ref, cum_ref, step_ref, rows_ref,
    held_ref, end_ref, later_ref, *refs
):
    message_refs = refs[:count]
    (
        spre_ref, vhalo_ref, kernel_ref, skip_ref, bias_ref, log_ref,
        grad_value_out, grad_rows_out, grad_step_out, last_out, first_out, kernel_out, small_out,
        entering, total, held_next, pre_next, skip_sum, heads, kernel_sum, heads_t, edge_rows,
    ) = refs[count:]
    b = pl.program_id(0)
    size, width = mixed_ref.shape
    state = held_ref.shape[1]
    final = b == pl.num_programs(0) - 1

    @pl.when(b == 0)
    def _():
        heads[...] = head_map(width)
        heads_t[...] = (iota((width, LANES), 1) == iota((width, LANES), 0) // HEAD_DIM).astype(f32).astype(bf16)
        for span in spans(width):
            coming = jnp.zeros((state, LANES), f32)
            passed = jnp.zeros((EDGE, LANES), f32)
            for ref in message_refs:
                coming = coming + jnp.exp(passed[0:1]) * ref[:state, span]
                passed = passed + ref[state:, span]
            entering[:, span] = coming
        total[...] = jnp.zeros(total.shape, f32)
        held_next[...] = end_ref[...]
        pre_next[...] = jnp.zeros(pre_next.shape, f32)
        kernel_sum[...] = jnp.zeros(kernel_sum.shape, f32)
        small_out[...] = jnp.zeros(small_out.shape, f32)
        skip_sum[...] = jnp.zeros(skip_sum.shape, f32)

    dt = dt_ref[...]
    cum = cum_ref[...]
    skip_row = jnp.broadcast_to(repeated(skip_ref[...]), (EDGE, LANES))
    wide = spread(jnp.concatenate([cum, dt, skip_row], axis=0), heads[...])
    b_parts = both_parts(rows_ref[:, :LANES])
    taps = kernel_ref[...].astype(f32)
    toward_b, toward_c, laters, helds, levels, throughs, boundaries = [], [], [], [], [], [], []
    for span in spans(width):
        cum_part = wide[:size, span]
        dt_wide = wide[size : 2 * size, span]
        skip = wide[2 * size : 2 * size + 1, span]
        end = cum_part[size - 1 : size]
        later = later_ref[0, :, span] + jnp.exp(total[0:1, span]) * entering[:, span]
        total[:, span] = total[:, span] + end
        held = held_ref[0, :, span]
        tail = jnp.exp(end - cum_part)
        dmix = dmix_ref[:, span]
        pre = pre_ref[:, span]
        pre_sig = sig(pre)
        conv = pre * pre_sig
        driven = conv * dt_wide
        later_high, later_low = split2(later)
        across = jnp.concatenate([later_high, later_low], axis=1)
        ddriven = driven_ref[:, span] + tail * fold(dot(b_parts, jnp.concatenate([across, across], axis=0)))
        toward_b.append(both_parts(tail * driven))
        laters.append(stacked(later_high, later_low))
        toward_c.append(both_parts(jnp.exp(cum_part) * dmix))
        helds.append(stacked(*split2(held)))
        skip_sum[:, span] = skip_sum[:, span] + by_eights(dmix * conv)
        levels.append(both_parts(dmix * (mixed_ref[:, span] - skip * conv) - driven * ddriven))
        throughs.append(both_parts(ddriven * conv))
        boundaries.append(both_parts(by_eights(later * held_next[:, span])))
        held_next[:, span] = held

        dpre = (ddriven * dt_wide + skip * dmix) * (pre_sig * (1.0 + pre * (1.0 - pre_sig)))
        extended = jnp.concatenate([dpre, pre_next[:, span]], axis=0)
        pre_next[:, span] = dpre[:EDGE]
        value = value_ref[:, span].astype(f32)
        dvalue = jnp.zeros((size, LANES), f32)
        for k in range(CONV):
            shifted = extended[CONV - 1 - k : CONV - 1 - k + size]
            dvalue = dvalue + taps[k : k + 1, span] * shifted
            kernel_sum[k, :, span] = kernel_sum[k, :, span] + by_eights(value * shifted)
        grad_value_out[:, span] = dvalue.astype(bf16)
        edge_rows[:, span] = dvalue[-2 * EDGE :]

    side = lambda parts: jnp.concatenate(parts, axis=1)
    grad_b = dot(side(toward_b), side(laters), NT)
    grad_c = dot(side(toward_c), side(helds), NT)
    picks = jnp.concatenate([heads_t[span] for span in spans(width) for _ in range(2)], axis=0)
    reduced = dot(jnp.concatenate([side(levels), side(throughs), side(boundaries)], axis=0), picks)
    level, through, boundary = reduced[:size], reduced[size : 2 * size], reduced[2 * size :]
    grad_rows_out[:, :LANES] = drows_ref[:, :LANES] + fold(grad_b)
    grad_rows_out[:, LANES:] = drows_ref[:, LANES:] + fold(grad_c)
    boundary = jnp.sum(boundary, axis=0, keepdims=True)
    upper = (iota((size, size), 1) >= iota((size, size), 0)).astype(f32).astype(bf16)
    ddecay = exact_dot(upper, level, NN) + boundary
    rate = jnp.exp(repeated(log_ref[...]))
    dstep = (through - ddecay * rate) * sig(step_ref[...] + repeated(bias_ref[...]))
    grad_step_out[...] = dstep[:, : grad_step_out.shape[1]].astype(bf16)
    small_out[1:2] = small_out[1:2] + jnp.sum(dstep, axis=0, keepdims=True)
    small_out[2:3] = small_out[2:3] + jnp.sum(-ddecay * dt * rate, axis=0, keepdims=True)

    @pl.when(b == 0)
    def _():
        last_out[...] = edge_rows[...]

    @pl.when(final)
    def _():
        first = pre_next[...]
        first_out[:, :width] = first
        first_out[:, width : width + 2 * LANES] = grad_rows_out[:EDGE]
        first_out[:, width + 2 * LANES :] = spre_ref[...]
        ahead = jnp.concatenate([jnp.zeros((EDGE, width), f32), first], axis=0)
        halo = vhalo_ref[...].astype(f32)[-EDGE:]
        kernel_out[...] = jnp.zeros(kernel_out.shape, f32)
        for k in range(CONV):
            shifted = ahead[CONV - 1 - k : CONV - 1 - k + EDGE]
            kernel_out[k : k + 1] = jnp.sum(kernel_sum[k] + halo * shifted, axis=0, keepdims=True)
        high, middle, low = split3(skip_sum[...])
        summed = dot(high, heads[...], NT) + (dot(middle, heads[...], NT) + dot(low, heads[...], NT))
        small_out[0:1] = jnp.sum(summed, axis=0, keepdims=True)


def finish(grad_driven, grad_rows, grad_mixed, mixed, pre, value_in, dt, cum, step_raw, state_rows, held, end_state, later,
           messages, spre, vhalo, input_kernel, skip_gain, step_bias, decay_log):
    tokens, inner = mixed.shape
    blocks, state, _ = held.shape
    head_count = skip_gain.shape[1]
    state_block = pl.BlockSpec((1, state, inner), lambda b: (blocks - 1 - b, 0, 0))
    wide = rows(BLOCK, inner, blocks)
    narrow = rows(BLOCK, LANES, blocks)
    return pl.pallas_call(
        functools.partial(finish_kernel, len(messages)),
        grid=(blocks,),
        in_specs=[
            wide, rows(BLOCK, 2 * state, blocks), wide, wide, wide, wide, narrow, narrow, narrow,
            rows(BLOCK, 2 * state, blocks),
            state_block, whole(end_state.shape), state_block,
            *[whole(m.shape) for m in messages],
            pl.BlockSpec((EDGE, 2 * state), lambda b: (0, 0)), whole(vhalo.shape), whole(input_kernel.shape), whole(skip_gain.shape), whole(step_bias.shape), whole(decay_log.shape),
        ],
        out_specs=[
            wide,
            rows(BLOCK, 2 * state, blocks),
            rows(BLOCK, head_count, blocks),
            whole((2 * EDGE, inner)),
            whole((EDGE, inner + 4 * state)),
            whole((EDGE, inner)),
            whole((EDGE, LANES)),
        ],
        out_shape=[
            jax.ShapeDtypeStruct((tokens, inner), bf16),
            jax.ShapeDtypeStruct((tokens, 2 * state), f32),
            jax.ShapeDtypeStruct((tokens, head_count), bf16),
            jax.ShapeDtypeStruct((2 * EDGE, inner), f32),
            jax.ShapeDtypeStruct((EDGE, inner + 4 * state), f32),
            jax.ShapeDtypeStruct((EDGE, inner), f32),
            jax.ShapeDtypeStruct((EDGE, LANES), f32),
        ],
        scratch_shapes=[
            pltpu.VMEM((state, inner), f32),
            pltpu.VMEM((EDGE, inner), f32),
            pltpu.VMEM((state, inner), f32),
            pltpu.VMEM((EDGE, inner), f32),
            pltpu.VMEM((EDGE, inner), f32),
            pltpu.VMEM((LANES, inner), bf16),
            pltpu.VMEM((CONV, EDGE, inner), f32),
            pltpu.VMEM((inner, LANES), bf16),
            pltpu.VMEM((2 * EDGE, inner), f32),
        ],
        compiler_params=params(56),
        cost_estimate=cost(16),
    )(grad_driven, grad_rows, grad_mixed, mixed, pre, value_in, dt, cum, step_raw, state_rows, held, end_state, later,
      *messages, spre, vhalo, input_kernel, skip_gain, step_bias, decay_log)


def from_before(value, axis, by=1):
    count = lax.axis_size(axis)
    return lax.ppermute(value, axis, [(i, i + by) for i in range(count - by)])


def from_after(value, axis, by=1):
    count = lax.axis_size(axis)
    return lax.ppermute(value, axis, [(i + by, i) for i in range(count - by)])


def from_all(value, axis):
    count = lax.axis_size(axis)
    return [lax.ppermute(value, axis, [(i, (i + by) % count) for i in range(count)]) for by in range(1, count)]


def after(first, then):
    return lax.optimization_barrier((first, then))[1]


def swapped(value, axis, flip):
    return lax.ppermute(value, axis, [(i, i ^ flip) for i in range(lax.axis_size(axis))])


def own_part(array, axis_name, dim):
    size = array.shape[dim] // lax.axis_size(axis_name)
    return lax.dynamic_slice_in_dim(array, lax.axis_index(axis_name) * size, size, dim)


def line_kernel(arrived, plan_ref, up_ref, down_ref, *refs):
    up, down = up_ref[0], down_ref[0]
    if arrived:
        up = up + refs[0][...].astype(f32)
        down = down + refs[1][...].astype(f32)
    refs[-2][...] = up.astype(bf16)
    refs[-1][...] = down.astype(bf16)


def line_step(parts, step, arrived, axis):
    count, tokens, width = parts.shape
    place = lax.axis_index(axis)
    plan = jnp.clip(jnp.stack([count - step + place, step - count + place]), 0, count - 1).astype(jnp.int32)
    tile = min(tokens, 512)
    block = pl.BlockSpec((tile, width), lambda b, plan: (b, 0))
    up, down = pl.pallas_call(
        functools.partial(line_kernel, len(arrived)),
        grid_spec=pltpu.PrefetchScalarGridSpec(
            num_scalar_prefetch=1,
            grid=(tokens // tile,),
            in_specs=[
                pl.BlockSpec((1, tile, width), lambda b, plan: (plan[0], b, 0)),
                pl.BlockSpec((1, tile, width), lambda b, plan: (plan[1], b, 0)),
                *[block for _ in arrived],
            ],
            out_specs=[block, block],
        ),
        out_shape=[jax.ShapeDtypeStruct((tokens, width), bf16)] * 2,
        compiler_params=params(12),
        cost_estimate=cost(2),
    )(plan, parts, parts, *arrived)
    return (up, down), [
        lax.ppermute(up, axis, [(k, k + 1) for k in range(step)]),
        lax.ppermute(down, axis, [(count - 1 - k, count - 2 - k) for k in range(step)]),
    ]


def input_kernel_body(pieces, gate_ref, value_ref, step_ref, last_ref, ahead_ref, taps_ref, x_ref, gain_ref, gate_w, value_w, step_w, *outs):
    part_out, value_out, row_out, col_out, fixed_out = outs
    b = pl.program_id(0)
    size, inner = value_ref.shape

    @pl.when(b == 0)
    def _():
        col_out[...] = jnp.zeros(col_out.shape, f32)
        fixed = last_ref[...]
        taps = taps_ref[...].astype(f32)
        extended = jnp.concatenate([jnp.zeros((2 * EDGE, inner), f32), ahead_ref[:, :inner]], axis=0)
        for k in range(CONV):
            fixed = fixed + taps[k : k + 1] * extended[CONV - 1 - k : CONV - 1 - k + 2 * EDGE]
        fixed_out[...] = fixed.astype(bf16)

    gate = gate_ref[...]
    value = value_ref[...]
    patched = jnp.concatenate([value[: size - 2 * EDGE], fixed_out[...]], axis=0)
    value = jnp.where(b == pl.num_programs(0) - 1, patched, value)
    value_out[...] = value
    step = step_ref[...]
    x = x_ref[...].astype(f32)
    scaling = lax.rsqrt(jnp.mean(x * x, axis=-1, keepdims=True) + epsilon)
    part = x.shape[1] // pieces
    row = jnp.zeros((size, LANES), f32)
    for j in range(pieces):
        span = slice(j * part, (j + 1) * part)
        partial = dot(gate, gate_w[span, :], NT) + dot(value, value_w[span, :], NT) + dot(step, step_w[:, span])
        part_out[j] = partial
        pulled = partial * x[:, span]
        gained = pulled * gain_ref[:, span]
        for inside in spans(part):
            row = row + gained[:, inside]
        col_out[:, span] = col_out[:, span] + by_eights(pulled * scaling)
    row_out[...] = exact_dot(jnp.ones((EDGE, LANES), bf16), row, NT)


def input_partials(pieces, grad_gate, grad_value, grad_step, last_rows, ahead, input_kernel, residual, pre_gain, gate_weight, input_weight, step_weight):
    tokens, width = residual.shape
    inner = grad_gate.shape[1]
    part = width // pieces
    tile = min(tokens, 256)
    return pl.pallas_call(
        functools.partial(input_kernel_body, pieces),
        grid=(tokens // tile,),
        in_specs=[
            rows(tile, inner),
            rows(tile, inner),
            rows(tile, grad_step.shape[1]),
            whole(last_rows.shape),
            whole(ahead.shape),
            whole(input_kernel.shape),
            rows(tile, width),
            whole(pre_gain.shape),
            whole(gate_weight.shape),
            whole(input_weight.shape),
            whole(step_weight.shape),
        ],
        out_specs=[
            pl.BlockSpec((pieces, tile, part), lambda b: (0, b, 0)),
            rows(tile, inner),
            pl.BlockSpec((EDGE, tile), lambda b: (0, b)),
            whole((EDGE, width)),
        ],
        out_shape=[
            jax.ShapeDtypeStruct((pieces, tokens, part), f32),
            jax.ShapeDtypeStruct((tokens, inner), bf16),
            jax.ShapeDtypeStruct((EDGE, tokens), f32),
            jax.ShapeDtypeStruct((EDGE, width), f32),
        ],
        scratch_shapes=[pltpu.VMEM((2 * EDGE, inner), bf16)],
        compiler_params=params(28),
        cost_estimate=cost(9),
    )(grad_gate, grad_value, grad_step, last_rows, ahead, input_kernel, residual, pre_gain, gate_weight, input_weight, step_weight)


def scalar_call(body, plan, operands, in_specs, out_specs, out_shape, grid=(1,), scratch=(), limit=16, micros=2):
    return pl.pallas_call(
        body,
        grid_spec=pltpu.PrefetchScalarGridSpec(
            num_scalar_prefetch=1, grid=grid, in_specs=in_specs, out_specs=out_specs, scratch_shapes=list(scratch)
        ),
        out_shape=out_shape,
        compiler_params=pltpu.CompilerParams(dimension_semantics=("arbitrary",) * len(grid), vmem_limit_bytes=limit * 1024 * 1024),
        cost_estimate=cost(micros),
    )(plan, *operands)


def all_of(a):
    return pl.BlockSpec(a.shape, lambda *_: (0,) * len(a.shape))


def pieces_kernel(count, plan_ref, rows_ref, ahead_ref, *outs):
    tokens, state2 = rows_ref.shape
    part = tokens // count
    first = ahead_ref.shape[1] - 2 * state2
    for k, out in enumerate(outs):
        at = lax.rem(plan_ref[0] + k, count)
        start = pl.multiple_of(at * part, EDGE)
        out[:part] = rows_ref[pl.ds(start, part)]
        beyond = pl.multiple_of(jnp.minimum(start + part, tokens - EDGE), EDGE)
        out[part:] = jnp.where(at == count - 1, ahead_ref[:, first : first + state2], rows_ref[pl.ds(beyond, EDGE)])


def pieces_of(place, count, grad_rows, ahead):
    tokens, state2 = grad_rows.shape
    shape = jax.ShapeDtypeStruct((tokens // count + EDGE, state2), f32)
    return scalar_call(
        functools.partial(pieces_kernel, count), place, (grad_rows, ahead), [all_of(grad_rows), all_of(ahead)],
        [all_of(shape)] * count, [shape] * count, limit=8, micros=1,
    )


def three_parts(x):
    return jnp.concatenate(split3(x), axis=0)


def three_sum(parts):
    size = parts.shape[0] // 3
    parts = parts.astype(f32)
    return parts[:size] + (parts[size : 2 * size] + parts[2 * size :])


PACK = 16


def state_kernel_body(count, plan_ref, *refs):
    grads = refs[:count]
    spre_ref, input_ref, halo_ref, ahead_ref, taps_ref, w_ref, x_ref, gain_ref, row_ref, col_ref, out_ref, inputs = refs[count:]
    tokens, state2 = spre_ref.shape
    part = tokens // count
    at = plan_ref[0]
    start = pl.multiple_of(at * part, 2 * EDGE)
    total = grads[0][...]
    for ref in grads[1:]:
        total = total + ref[...]
    beyond = pl.multiple_of(jnp.minimum(start + part, tokens - EDGE), EDGE)
    after_rows = jnp.where(at == count - 1, ahead_ref[:, ahead_ref.shape[1] - state2 :], spre_ref[pl.ds(beyond, EDGE)])
    pre = jnp.concatenate([spre_ref[pl.ds(start, part)], after_rows], axis=0)
    s = sig(pre)
    through = total * (s * (1.0 + pre * (1.0 - s)))
    taps = taps_ref[...].astype(f32)
    before = pl.multiple_of(jnp.maximum(start - 2 * EDGE, 0), 2 * EDGE)
    inputs[: 2 * EDGE] = jnp.where(at == 0, halo_ref[...].astype(f32), input_ref[pl.ds(before, 2 * EDGE)].astype(f32))
    inputs[2 * EDGE :] = input_ref[pl.ds(start, part)].astype(f32)
    grad = jnp.zeros((part, state2), f32)
    own = through[:part]
    first = 2 * EDGE - CONV + 1
    tap_rows = []
    for k in range(CONV):
        grad = grad + taps[k : k + 1] * through[CONV - 1 - k : CONV - 1 - k + part]
        tap_rows.append(jnp.sum(own * inputs[first + k : first + k + part], axis=0, keepdims=True))
    rounded = grad.astype(bf16)
    out_ref[:part] = rounded
    x = x_ref[...].astype(f32)
    width = x.shape[1]
    scaling = lax.rsqrt(jnp.mean(x * x, axis=-1, keepdims=True) + epsilon)
    row = jnp.zeros((part, LANES), f32)
    cols = []
    for span in spans(width):
        pulled = dot(rounded, w_ref[span, :], NT) * x[:, span]
        row = row + pulled * gain_ref[:, span]
        cols.append(jnp.sum(by_eights(pulled * scaling) + col_ref[:, span], axis=0, keepdims=True))
    row = exact_dot(jnp.ones((EDGE, LANES), bf16), row, NT)[:1]
    packed = [row_ref[:1, j * part : (j + 1) * part] + jnp.where(at == j, row, 0.0) for j in range(count)]
    wide = state2 // LANES
    packed += [jnp.concatenate(cols[i : i + wide], axis=1) for i in range(0, len(cols), wide)]
    packed += tap_rows
    packed.append(jnp.zeros((PACK - len(packed), state2), f32))
    out_ref[part:] = three_parts(jnp.concatenate(packed, axis=0))


def state_back(place, grads, spre, state_in, halo, ahead, taps, weight, residual, pre_gain, row_sums, col_sums):
    count = len(grads)
    tokens, state2 = spre.shape
    part = tokens // count
    shape = jax.ShapeDtypeStruct((part + 3 * PACK, state2), bf16)
    operands = (*grads, spre, state_in, halo, ahead, taps, weight, residual, pre_gain, row_sums, col_sums)
    in_specs = [all_of(a) for a in operands]
    in_specs[count + 6] = pl.BlockSpec((part, residual.shape[1]), lambda b, plan: (plan[0], 0))
    return scalar_call(
        functools.partial(state_kernel_body, count), place, operands, in_specs, all_of(shape), shape,
        scratch=[pltpu.VMEM((part + 2 * EDGE, state2), f32)], limit=16, micros=3,
    )


SMALL = 48


def narrow_kernel(count, plan_ref, *refs):
    messages = refs[:count]
    step_ref, kernel_ref, gain_ref, small_ref, out_ref, row_out = refs[count:]
    tokens, steps = step_ref.shape
    part = tokens // count
    state2 = messages[0].shape[1]
    mine = state2 // count
    me = plan_ref[0]
    pick = ((iota((state2, LANES), 0) == iota((state2, LANES), 1) + me * mine) & (iota((state2, LANES), 1) < mine)).astype(f32).astype(bf16)
    place = (iota((steps, LANES), 0) + mine == iota((steps, LANES), 1)).astype(f32).astype(bf16)
    sums = jnp.zeros((PACK, state2), f32)
    for k in range(count):
        start = pl.multiple_of(lax.rem(me - k + count, count) * part, 2 * EDGE)
        both = dot(messages[k][:part], pick) + dot(step_ref[pl.ds(start, part)], place)
        out_ref[pl.ds(start, part)] = both.astype(bf16)
        sums = sums + three_sum(messages[k][part:])
    row_out[...] = sums
    wide = state2 // LANES
    inner = kernel_ref.shape[1]
    rows_of = [kernel_ref[k : k + 1, span] for k in range(CONV) for span in spans(inner)]
    gain = jnp.sum(gain_ref[...], axis=0, keepdims=True)
    rows_of += [gain[:, span] for span in spans(inner)]
    rows_of += [small_ref[i : i + 1] for i in range(3)]
    cols = [sums[count + r : count + r + 1, i * LANES : (i + 1) * LANES] for r in range(PACK - count - CONV) for i in range(wide)]
    quarter = (PACK - count - CONV - 2) * wide // count
    for i in range(quarter):
        chosen = jnp.zeros((1, LANES), f32)
        for q in range(count):
            chosen = jnp.where(me == q, cols[q * quarter + i], chosen)
        rows_of.append(chosen)
    first = count + (PACK - count - CONV - 2)
    rows_of += [sums[first + k : first + k + 1, i * LANES : (i + 1) * LANES] for k in range(CONV) for i in range(wide)]
    rows_of.append(jnp.zeros((SMALL - len(rows_of), LANES), f32))
    out_ref[tokens:] = three_parts(jnp.concatenate(rows_of, axis=0))


def narrow_of(place, messages, grad_step, kernel_grad, gain_grad, small):
    count = len(messages)
    tokens = grad_step.shape[0]
    shapes = [jax.ShapeDtypeStruct((tokens + 3 * SMALL, LANES), bf16), jax.ShapeDtypeStruct((PACK, messages[0].shape[1]), f32)]
    operands = (*messages, grad_step, kernel_grad, gain_grad, small)
    return scalar_call(
        functools.partial(narrow_kernel, count), place, operands, [all_of(a) for a in operands],
        [all_of(a) for a in shapes], shapes, limit=8, micros=2,
    )


def wide_weights_kernel(plan_ref, normed_a, normed_b, gate_a, gate_b, out_a, out_b, cot_a, cot_b, *outs):
    k = pl.program_id(0)
    tile = normed_a.shape[1]
    gate = dot(normed_a[...], gate_a[...], TN) + dot(normed_b[...], gate_b[...], TN)
    out = dot(out_a[...], cot_a[...], TN) + dot(out_b[...], cot_b[...], TN)
    for i, ref in enumerate(outs):

        @pl.when(k == i)
        def _(ref=ref):
            ref[:tile] = gate
            ref[tile:] = out


def wide_weights(plan, count, normed, grad_gate, normed_out, cotangent):
    tokens, width = normed[0].shape
    tile = width // count
    moving = pl.BlockSpec((tokens, tile), lambda k, plan: (0, jnp.bitwise_xor(plan[1], k)))
    still = pl.BlockSpec((tokens, tile), lambda k, plan: (0, plan[0]))
    shape = jax.ShapeDtypeStruct((2 * tile, tile), f32)
    return scalar_call(
        wide_weights_kernel, plan, (*normed, *grad_gate, *normed_out, *cotangent),
        [moving, moving, still, still, still, still, moving, moving],
        [all_of(shape)] * count, [shape] * count, grid=(count,), limit=28, micros=8,
    )


def value_weights_kernel(plan_ref, normed_a, normed_b, value_a, value_b, *outs):
    k = pl.program_id(0)
    total = dot(normed_a[...], value_a[...], TN) + dot(normed_b[...], value_b[...], TN)
    for i, ref in enumerate(outs):

        @pl.when(k == i)
        def _(ref=ref):
            ref[...] = total


def value_weights(plan, count, normed, grad_value):
    tokens, width = normed[0].shape
    tile = width // count
    half = grad_value[0].shape[1] // 2
    moving = pl.BlockSpec((tokens, tile), lambda k, plan: (0, jnp.bitwise_xor(plan[1], k)))
    still = pl.BlockSpec((tokens, half), lambda k, plan: (0, plan[0]))
    shape = jax.ShapeDtypeStruct((tile, half), f32)
    return scalar_call(
        value_weights_kernel, plan, (*normed, *grad_value), [moving, moving, still, still],
        [all_of(shape)] * count, [shape] * count, grid=(count,), limit=20, micros=5,
    )


def narrow_weights_kernel(plan_ref, normed_a, normed_b, narrow_a, narrow_b, *outs):
    k = pl.program_id(0)
    tokens, tile = normed_a.shape
    total = dot(narrow_a[:tokens], normed_a[...], TN) + dot(narrow_b[:tokens], normed_b[...], TN)
    small = three_sum(narrow_a[tokens:]) + three_sum(narrow_b[tokens:])
    per_row = tile // LANES
    for i, ref in enumerate(outs):

        @pl.when(k == i)
        def _(ref=ref):
            ref[:LANES] = total
            for j in range(per_row):
                ref[LANES:, j * LANES : (j + 1) * LANES] = small[j * SMALL // per_row : (j + 1) * SMALL // per_row]


def narrow_weights(plan, count, normed, narrow):
    tokens, width = normed[0].shape
    tile = width // count
    moving = pl.BlockSpec((tokens, tile), lambda k, plan: (0, jnp.bitwise_xor(plan[1], k)))
    shape = jax.ShapeDtypeStruct((LANES + SMALL * LANES // tile, tile), f32)
    return scalar_call(
        narrow_weights_kernel, plan, (*normed, *narrow), [moving, moving, all_of(narrow[0]), all_of(narrow[1])],
        [all_of(shape)] * count, [shape] * count, grid=(count,), limit=16, micros=4,
    )


def sum_kernel(count, *refs):
    total = refs[0][...]
    for ref in refs[1:count]:
        total = total + ref[...]
    refs[count][...] = total.astype(refs[count].dtype)


def sum_of(arrays, dtype):
    shape = jax.ShapeDtypeStruct(arrays[0].shape, dtype)
    return pl.pallas_call(
        functools.partial(sum_kernel, len(arrays)),
        out_shape=shape,
        compiler_params=pltpu.CompilerParams(vmem_limit_bytes=16 * 1024 * 1024),
        cost_estimate=cost(2),
    )(*arrays)


def over_ctx(arrays, wait=()):
    arrived = [swapped(a, "ctx", k) for k, a in enumerate(arrays) if k]
    total = sum_of([arrays[0], *after(wait, arrived)], f32)
    step = 2
    while step < lax.axis_size("dp"):
        total = total + swapped(total, "dp", step)
        step *= 2
    return total


def gather_chunks(chunk):
    return jnp.concatenate([chunk, *[swapped(chunk, "ctx", k) for k in range(1, lax.axis_size("ctx"))]], axis=0)


def ordered(first, here, there):
    here, there = here.astype(f32), there.astype(f32)
    return jnp.where(first, here, there), jnp.where(first, there, here)


def wide_together_kernel(plan_ref, here, there, gate_out, out_out):
    tile = gate_out.shape[0]
    k = jnp.bitwise_xor(pl.program_id(0), plan_ref[1])
    first = plan_ref[0] == 0
    half = gate_out.shape[1] // 2
    span = pl.ds(pl.multiple_of(k * 2 * tile, 2 * EDGE), tile)
    gate_out[:, :half], gate_out[:, half:] = ordered(first, here[span], there[span])
    span = pl.ds(pl.multiple_of(k * 2 * tile + tile, 2 * EDGE), tile)
    out_out[:tile], out_out[tile:] = ordered(first, here[span], there[span])


def wide_together(plan, count, here, there):
    tile = here.shape[0] // (2 * count)
    width, inner = tile * count, 2 * here.shape[1]
    return scalar_call(
        wide_together_kernel, plan, (here, there), [all_of(here), all_of(there)],
        [pl.BlockSpec((tile, inner), lambda q, plan: (q, 0)), pl.BlockSpec((inner, tile), lambda q, plan: (0, q))],
        [jax.ShapeDtypeStruct((width, inner), f32), jax.ShapeDtypeStruct((inner, width), f32)],
        grid=(count,), limit=24, micros=6,
    )


def narrow_together_kernel(plan_ref, here, there, input_out, state_out, step_out):
    tile = input_out.shape[0]
    k = jnp.bitwise_xor(pl.program_id(0), plan_ref[1])
    half = input_out.shape[1] // 2
    start = pl.multiple_of(k * (tile + LANES), 2 * EDGE)
    span = pl.ds(start, tile)
    input_out[:, :half], input_out[:, half:] = ordered(plan_ref[0] == 0, here[span], there[span])
    rest = here[pl.ds(pl.multiple_of(start + tile, 2 * EDGE), LANES)].astype(f32)
    states = state_out.shape[0]
    state_out[...] = rest[:states]
    step_out[...] = rest[states : states + step_out.shape[0]]


def narrow_together(plan, count, here, there, state_part, steps):
    tile = here.shape[0] // count - LANES
    width, inner = tile * count, 2 * here.shape[1]
    by_lane = lambda size: pl.BlockSpec((size, tile), lambda q, plan: (0, q))
    return scalar_call(
        narrow_together_kernel, plan, (here, there), [all_of(here), all_of(there)],
        [pl.BlockSpec((tile, inner), lambda q, plan: (q, 0)), by_lane(state_part), by_lane(steps)],
        [
            jax.ShapeDtypeStruct((width, inner), f32),
            jax.ShapeDtypeStruct((state_part, width), f32),
            jax.ShapeDtypeStruct((steps, width), f32),
        ],
        grid=(count,), limit=20, micros=4,
    )


def final_kernel(count, plan_ref, part_ref, up_ref, down_ref, x_ref, mine_ref, cot_ref, gain_ref, w_ref, sums_ref, *refs):
    messages, out_ref = refs[:count], refs[count]
    b = pl.program_id(0)
    size, part = up_ref.shape
    k = lax.rem(plan_ref[0] - b + count, count)
    state = messages[0][:size]
    for i in range(1, count):
        state = jnp.where(k == i, messages[i][:size], state)
    normed_grad = part_ref[0] + up_ref[...].astype(f32) + down_ref[...].astype(f32) + dot(state, w_ref[...], NT)
    x = x_ref[...].astype(f32)
    width = x.shape[1]
    scaling = lax.rsqrt(jnp.mean(x * x, axis=-1, keepdims=True) + epsilon)
    row = jnp.zeros((1, size), f32)
    for q in range(count):
        row = jnp.where(b == q, sums_ref[q : q + 1], row)
    pull = column(row) * ((scaling * scaling * scaling) / width)
    for span in spans(part):
        out_ref[:, span] = (
            cot_ref[:, span].astype(f32) + scaling * gain_ref[:, span] * normed_grad[:, span] - mine_ref[:, span].astype(f32) * pull
        )


def final(place, parts, arrived, residual, cotangent, pre_gain, state_weight, sums, messages):
    count, tokens, part = parts.shape
    size = tokens // count
    state2 = state_weight.shape[1]
    mine = pl.BlockSpec((size, part), lambda b, plan: (b, plan[0]))
    return scalar_call(
        functools.partial(final_kernel, count), place,
        (parts, *arrived, residual, residual, cotangent, pre_gain, state_weight, sums, *messages),
        [
            pl.BlockSpec((1, size, part), lambda b, plan: (plan[0], b, 0)),
            pl.BlockSpec((size, part), lambda b, plan: (b, 0)),
            pl.BlockSpec((size, part), lambda b, plan: (b, 0)),
            pl.BlockSpec((size, residual.shape[1]), lambda b, plan: (b, 0)),
            mine,
            mine,
            pl.BlockSpec((1, part), lambda b, plan: (0, plan[0])),
            pl.BlockSpec((part, state2), lambda b, plan: (plan[0], 0)),
            all_of(sums),
            *[all_of(m) for m in messages],
        ],
        pl.BlockSpec((size, part), lambda b, plan: (b, 0)),
        jax.ShapeDtypeStruct((tokens, part), f32),
        grid=(count,), limit=16, micros=4,
    )


def per_device(residual, pre_gain, gate_weight, input_weight, state_weight, step_weight, input_kernel, state_kernel,
               step_bias, decay_log, skip_gain, norm_gain, out_weight, cotangent):
    residual, cotangent = residual[0], cotangent[0]
    tokens, width = residual.shape
    tensor_size = lax.axis_size("tensor")
    ctx_size = lax.axis_size("ctx")
    inner = gate_weight.shape[1]
    inner_total = inner * tensor_size
    head_count = step_weight.shape[1]
    state2 = state_weight.shape[1]
    state_part = state2 // tensor_size
    row = lambda v: v.reshape(1, -1)
    plan = jnp.stack([lax.axis_index("dp") % 2, lax.axis_index("ctx")]).astype(jnp.int32)
    place = lax.axis_index("tensor").astype(jnp.int32).reshape(1)

    halo = from_before(residual[-2 * EDGE :], "ctx")
    other_cotangent = swapped(cotangent, "dp", 1)
    step_weight = step_weight.T
    normed, value_in, state_in, step_raw = project(residual, row(pre_gain), input_weight, state_weight, step_weight)
    other_normed = swapped(normed, "dp", 1)
    conv, pre, state_rows, spre, dt, cum, cumt, held, message, vhalo, shalo = local_states(
        value_in, state_in, step_raw, halo, row(pre_gain), input_weight, state_weight, input_kernel, state_kernel,
        row(step_bias), row(decay_log)
    )
    messages = [from_before(message, "ctx", by) for by in range(1, ctx_size)]
    gate_in, grad_normed = beside(after(message, normed), gate_weight, cotangent, out_weight)
    intra = inner_forward(head_count, conv, dt, state_rows, cum, cumt, row(skip_gain))
    messages = after((gate_in, intra), messages)
    mixed, sums, held, end_state = combine(
        intra, state_rows, cum, held, message, messages, gate_in, grad_normed, row(norm_gain)
    )
    all_sums = [sums, *from_all(sums, "tensor")]
    normed_out, grad_gate, grad_mixed, later, message, gain_grad = gate_back(
        mixed, gate_in, grad_normed, state_rows, cum, row(norm_gain), all_sums, inner_total
    )
    messages = [from_after(message, "ctx", by) for by in range(1, ctx_size)]
    other_gate = swapped(grad_gate, "dp", 1)
    other_out = swapped(normed_out, "dp", 1)

    resid_part = own_part(residual, "tensor", 1).astype(f32)
    partial_out = dot(after(message, normed_out), out_weight)
    branch = lax.psum_scatter(partial_out, "tensor", scatter_dimension=1, tiled=True)
    output = (resid_part + branch).astype(bf16)

    wide = wide_weights(
        after(partial_out, plan), ctx_size, (normed, other_normed), (grad_gate, other_gate), (normed_out, other_out),
        (cotangent, other_cotangent)
    )
    grad_driven, grad_rows = inner_back(head_count, conv, dt, state_rows, cum, cumt, after(wide, grad_mixed))
    messages = after(grad_driven, messages)
    grad_value, grad_rows, grad_step, last_rows, first_rows, kernel_grad, small = finish(
        grad_driven, grad_rows, grad_mixed, mixed, pre, value_in, dt, cum, step_raw, state_rows, held, end_state, later,
        messages, spre, vhalo, input_kernel, row(skip_gain), row(step_bias), row(decay_log)
    )
    ahead = from_after(first_rows, "ctx")
    wide_chunk = over_ctx(wide, first_rows).astype(bf16)
    ahead = after(wide_chunk, ahead)

    pieces = pieces_of(place, tensor_size, grad_rows, ahead)
    arrived = [
        lax.ppermute(pieces[k], "tensor", [(i, (i + k) % tensor_size) for i in range(tensor_size)]) for k in range(1, tensor_size)
    ]
    parts, grad_value, row_sums, col_sums = input_partials(
        tensor_size, grad_gate, grad_value, grad_step, last_rows, ahead, input_kernel,
        residual, row(pre_gain), gate_weight, input_weight, step_weight
    )
    other_value = swapped(grad_value, "dp", 1)
    sent, moving = line_step(parts, 1, [], "tensor")
    wide_here = gather_chunks(wide_chunk)
    weights = value_weights(after(sent, plan), ctx_size, (normed, other_normed), (grad_value, other_value))
    arrived = after(weights, arrived)
    state_message = state_back(
        place, [pieces[0], *arrived], spre, state_in, shalo, ahead, state_kernel, state_weight, residual, row(pre_gain),
        row_sums, col_sums
    )
    arrived = from_all(state_message, "tensor")
    wide_there = swapped(wide_here, "dp", 1)
    sent, moving = line_step(parts, 2, moving, "tensor")
    state_messages = [state_message, *after(sent, arrived)]
    narrow, sums = narrow_of(place, state_messages, grad_step, kernel_grad, gain_grad, small)
    other_narrow = swapped(narrow, "dp", 1)
    value_chunk = over_ctx(weights, narrow)
    weights = narrow_weights(plan, ctx_size, (normed, other_normed), (narrow, other_narrow))
    gate_weight_grad, out_weight_grad = wide_together(plan, ctx_size, wide_here, wide_there)
    narrow_total = over_ctx(weights, (gate_weight_grad, output))
    sent, moving = line_step(parts, 3, moving, "tensor")
    chunk = after(sent, jnp.concatenate([value_chunk, narrow_total[:LANES]], axis=0).astype(bf16))
    arrived = [swapped(chunk, "ctx", k) for k in range(1, ctx_size)]
    input_grad = final(place, parts, moving, residual, cotangent, row(pre_gain), state_weight, sums, state_messages)
    narrow_here = jnp.concatenate([chunk, *after(input_grad, arrived)], axis=0)
    narrow_there = swapped(narrow_here, "dp", 1)
    input_weight_grad, state_weight_grad, step_weight_grad = narrow_together(
        plan, ctx_size, narrow_here, narrow_there, state_part, head_count
    )
    small_total = narrow_total[LANES:]
    small_total = jnp.concatenate([small_total[:, i : i + LANES] for i in range(0, small_total.shape[1], LANES)], axis=0)
    wide_rows = inner // LANES
    at = CONV * wide_rows
    kernel_grad = small_total[:at].reshape(CONV, inner)
    gain_grad = small_total[at : at + wide_rows].reshape(inner)
    at += wide_rows
    small = small_total[at : at + 3, :head_count]
    at += 3
    gain_rows = width // tensor_size // LANES
    pre_gain_grad = small_total[at : at + gain_rows].reshape(width // tensor_size)
    at += gain_rows
    taps_grad = small_total[at : at + CONV * state2 // LANES].reshape(CONV, state2)
    return (
        output[None],
        input_grad[None],
        pre_gain_grad,
        gate_weight_grad,
        input_weight_grad,
        state_weight_grad.T,
        step_weight_grad.T,
        kernel_grad,
        taps_grad,
        small[1],
        small[2],
        small[0],
        gain_grad,
        out_weight_grad,
    )


def solution(mesh):
    in_specs = (
        P("dp", "ctx", None),
        P(),
        P(None, "tensor"),
        P(None, "tensor"),
        P(),
        P(None, "tensor"),
        P(None, "tensor"),
        P(),
        P("tensor"),
        P("tensor"),
        P("tensor"),
        P("tensor"),
        P("tensor", None),
        P("dp", "ctx", None),
    )
    out_specs = (
        P("dp", "ctx", "tensor"),
        P("dp", "ctx", "tensor"),
        P("tensor"),
        P(None, "tensor"),
        P(None, "tensor"),
        P(None, "tensor"),
        P(None, "tensor"),
        P(None, "tensor"),
        P(),
        P("tensor"),
        P("tensor"),
        P("tensor"),
        P("tensor"),
        P("tensor", None),
    )
    return jax.shard_map(per_device, mesh=mesh, in_specs=in_specs, out_specs=out_specs, check_vma=False)
```

time: 660 us -> 372 us (0.56)
  waiting for transfers between devices: 375 us -> 97.4 us
  matrix products: 57 us -> 4.56 us
  blocking collectives: 40 us -> 0 us
  starting transfers between devices: 28.3 us -> 67.1 us
  Pallas kernels: 99.4 us -> 131 us
  local copies, waits for them, and re-layouts: 29.7 us -> 46.9 us
    psum x1 -> x0, waiting for transfers between devices: 198 us -> none  [per_device(): sums = lax.psum(tuple(sums), ('dp', 'ctx'))]
    reduce_scatter x2 -> x1, waiting for transfers between devices: 152 us -> 0.01 us  [per_device(): lax.psum_scatter(partial_out, 'tensor', scatter_dimension=1, tiled=True)]
    pallas_call x0 -> x17, Pallas kernels: none -> 70.1 us  [the longest x9 42.3 us: scalar_call(): pl.pallas_call(body, grid_spec=pltpu.PrefetchScalarGridSpec(num_scalar_pr...]
    ppermute x0 -> x32, waiting for transfers between devices: none -> 62.8 us  [the longest x23 62 us: swapped(): lax.ppermute(value, axis, [(i, i ^ flip) for i in range(lax.axis_size(axi...]
    dot_general x11 -> x1, matrix products: 57 us -> 4.56 us  [dot(): return lax.dot_general(a, b, dims, preferred_element_type=f32)]
    psum x2 -> x0, blocking collectives: 40 us -> none  [the longest x1 27.5 us: per_device(): sums = lax.psum(tuple(sums), ('dp', 'ctx'))]
    ppermute x0 -> x32, starting transfers between devices: none -> 38.8 us  [the longest x23 19.6 us: swapped(): lax.ppermute(value, axis, [(i, i ^ flip) for i in range(lax.axis_size(axi...]
    ppermute x3 -> x6, waiting for transfers between devices: 1.9 us -> 30.5 us  [from_all(): lax.ppermute(value, axis, [(i, (i + by) % count) for i in range(count)])]
  transfers between devices with their start and end apart: 18 -> 47, of which waited for: 11 -> 18; matrix products, arithmetic and copies ran while one was open for 11% -> 4% of each run, Pallas kernels for 15% -> 29%
where the time goes in v2:
time: 372 us; the launch traced here: 370 us
  Pallas kernels  131 us (35%)
  waiting for transfers between devices  97.4 us (26%)
  starting transfers between devices  67.1 us (18%)
  local copies, waits for them, and re-layouts  46.9 us (13%)
  between operations  15.2 us (4%)
  other arithmetic  7.71 us (2%)
  matrix products  4.56 us (1%)
    ppermute x23, waiting for transfers between devices, swapped(): lax.ppermute(value, axis, [(i, i ^ flip) for i in range(lax.axis_size(axi...  62 us
    pallas_call x9, Pallas kernels, scalar_call(): pl.pallas_call(body, grid_spec=pltpu.PrefetchScalarGridSpec(num_scalar_pr...  42.3 us
    unnamed x177, local copies, waits for them, and re-layouts  40.3 us
    ppermute x6, waiting for transfers between devices, from_all(): lax.ppermute(value, axis, [(i, (i + by) % count) for i in range(count)])  30.5 us
    pallas_call x1, Pallas kernels, finish(): pl.pallas_call(functools.partial(finish_kernel, len(messages)), grid=(blo...  20.4 us
    ppermute x23, starting transfers between devices, swapped(): lax.ppermute(value, axis, [(i, i ^ flip) for i in range(lax.axis_size(axi...  19.6 us
    ppermute x4, starting transfers between devices, from_before(): return lax.ppermute(value, axis, [(i, i + by) for i in range(count - by)])  11.5 us
    ppermute x6, starting transfers between devices, from_all(): lax.ppermute(value, axis, [(i, (i + by) % count) for i in range(count)])  11.2 us
  transfers between devices with their start and end apart: 47, of which 18 were waited for; matrix products, arithmetic and copies ran while one was open for 4% of the time, Pallas kernels for 29%

profile of v2, /device:TPU:0, one launch (start us, length us, event | category | flops | bytes accessed | tf_op | source)
XLA Modules:
  0.0 370.3 jit_solution(3356513361242153814)
XLA Ops:
  8.0 4.8 %collective-permute-start = (bf16[16,1536]{1,0:T(8,128)(2,1)S(1)}, bf16[16,1536]{1,0:T(8,128)(2,1)S(1)}, u32[]{:S(2)}, u32[]{:S(2)}) collective-permute-start(bf16[16,1536]{1,0:T(8,128)(2,1)S(1)} %slice_bitcast_fusion), channel_id=1, source_target_pairs={{0,4},{4,8},{8,12},{1,5},{5,9},{9,13},{2,6},{6,10},{10,14},{3,7},{... | collective-permute-start | bytes 147464 | tf_op jit(solution)/shard_map/ppermute | solution.py:771
  13.6 1.9 copy-done.5
  16.6 1.7 copy-done.23
  19.1 5.9 %shard_map.245 = (bf16[1024,1536]{1,0:T(8,128)(2,1)S(1)}, bf16[1024,768]{1,0:T(8,128)(2,1)S(1)}, bf16[1024,256]{1,0:T(8,128)(2,1)S(1)}, f32[1024,128]{1,0:T(8,128)S(1)}) custom-call(bf16[1024,1536]{1,0:T(8,128)(2,1)S(1)} %bitcast.36, f32[1,1536]{1,0:T(1,128)S(1)} %reshape.70.gain_ref.refs_11_, bf16[1536,768]{1,0:T(8,128)(2,1)S(1)} %copy-done.23, ...), custom_call_target="tpu_custom_call" | custom-call | flops 5400000000 | bytes 18000000 | tf_op jit(solution)/shard_map/pallas_call | solution.py:147
  25.2 9.9 %shard_map.246 = (f32[1024,768]{1,0:T(8,128)S(1)}, f32[1024,768]{1,0:T(8,128)S(1)}, f32[1024,256]{1,0:T(8,128)S(1)}, f32[1024,256]{1,0:T(8,128)S(1)}, f32[1024,1...) custom-call(bf16[1024,768]{1,0:T(8,128)(2,1)S(1)} %get-tuple-element, ...), custom_call_target="tpu_custom_call" | custom-call | flops 8999999488 | bytes 30000000 | tf_op jit(solution)/shard_map/pallas_call | solution.py:267
  35.2 3.4 collective-permute-start.1
  38.6 1.9 collective-permute-start.2
  42.0 5.6 %shard_map.248 = (f32[1024,768]{1,0:T(8,128)S(1)}, f32[1024,768]{1,0:T(8,128)S(1)}) custom-call(bf16[1024,1536]{1,0:T(8,128)(2,1)S(1)} %get-tuple-element.125.normed_ref.normed_a, bf16[1536,768]{1,0:T(8,128)(2,1)S(1)} %copy-done.26, bf16[1024,1536]{1,0:T(8,128)(2,1)S(1)} %bitcast.41, bf16[768,1536]{1,0:T(8,128)(2,1)S(1)} %copy-done.22), custom_call_target="tpu_custom_call" | custom-call | flops 5400000000 | bytes 18000000 | tf_op jit(solution)/shard_map/pallas_call | solution.py:179
  47.6 5.4 %shard_map.247.intra_ref = f32[1024,768]{1,0:T(8,128)S(1)} custom-call(f32[1024,768]{1,0:T(8,128)S(1)} %get-tuple-element.117.conv_ref, f32[1024,128]{1,0:T(8,128)S(1)} %get-tuple-element.118.dt_ref, f32[1024,256]{1,0:T(8,128)S(1)} %get-tuple-element.119.rows_ref, f32[1024,128]{1,0:T(8,128)S(1)} %get-tuple-element.120.cum_ref, ...), custom_call_target="tpu_custom_call" | custom-call | flops 5400000000 | bytes 18000000 | tf_op jit(solution)/shard_map/pallas_call | solution.py:347
  53.0 4.1 %collective-permute-done.2.refs_1_ = f32[136,768]{1,0:T(8,128)S(1)} collective-permute-done((f32[136,768]{1,0:T(8,128)S(1)}, f32[136,768]{1,0:T(8,128)S(1)}, u32[]{:S(2)}, u32[]{:S(2)}) %collective-permute-start.2) | collective-permute-done | bytes 417824 | tf_op jit(solution)/shard_map/ppermute | solution.py:771
  57.1 4.7 %shard_map.249 = (f32[1024,768]{1,0:T(8,128)S(1)}, f32[8,1024]{1,0:T(8,128)S(1)}, f32[8,128,768]{2,1,0:T(8,128)S(1)}, f32[128,768]{1,0:T(8,128)S(1)}) custom-call(f32[1024,768]{1,0:T(8,128)S(1)} %shard_map.247.intra_ref, f32[1024,256]{1,0:T(8,128)S(1)} %get-tuple-element.119.rows_ref, f32[1024,128]{1,0:T(8,128)S(1)} %get-tuple-element.120.cum_ref, ...), custom_call_target="tpu_custom_call" | custom-call | flops 4499999744 | bytes 15000000 | tf_op jit(solution)/shard_map/pallas_call | solution.py:410
  61.8 1.8 copy-done.46
  63.6 1.6 collective-permute-start.4
  65.2 2.6 collective-permute-start.5
  71.7 6.1 %shard_map.250 = (bf16[1024,768]{1,0:T(8,128)(2,1)S(1)}, bf16[1024,768]{1,0:T(8,128)(2,1)S(1)}, f32[1024,768]{1,0:T(8,128)S(1)}, f32[8,128,768]{2,1,0:T(8,128)S(...) custom-call(f32[1024,768]{1,0:T(8,128)S(1)} %get-tuple-element.131.mixed_ref, ...), custom_call_target="tpu_custom_call" | custom-call | flops 6300000256 | bytes 21000000 | tf_op jit(solution)/shard_map/pallas_call | solution.py:497
  79.6 1.7 copy-done.63
  81.3 1.7 copy-done.65
  84.2 4.6 %fusion.2 = f32[1024,1536]{1,0:T(8,128)} fusion(bf16[1024,768]{1,0:T(8,128)(2,1)S(1)} %get-tuple-element.135.out_a, bf16[768,1536]{1,0:T(8,128)(2,1)S(1)} %copy-done.22), kind=kOutput, calls=%fused_computation.21 | convolution fusion | flops 2415919104 | bytes 10223616 | tf_op jit(solution)/shard_map/dot_general | solution.py:25
  91.2 10.4 %collective-permute-done.8.gate_b = bf16[1024,768]{1,0:T(8,128)(2,1)} collective-permute-done((bf16[1024,768]{1,0:T(8,128)(2,1)}, bf16[1024,768]{1,0:T(8,128)(2,1)}, u32[]{:S(2)}, u32[]{:S(2)}) %collective-permute-start.8) | collective-permute-done | bytes 1572896 | tf_op jit(solution)/shard_map/ppermute | solution.py:789
  103.8 1.5 collective-permute-start.13
  105.3 1.9 copy-done.19
  108.6 1.5 copy-done.32
  110.1 12.9 %shard_map.251 = (f32[768,384]{1,0:T(8,128)S(1)}, f32[768,384]{1,0:T(8,128)}, f32[768,384]{1,0:T(8,128)}, f32[768,384]{1,0:T(8,128)}) custom-call(s32[2]{0:T(128)S(1)} %pad_add_fusion.plan_ref, bf16[1024,1536]{1,0:T(8,128)(2,1)S(1)} %copy-done.19, bf16[1024,1536]{1,0:T(8,128)(2,1)} %collective-permute-done.7.normed_b, bf16[1024,768]{1,0:T(8,128)(2,1)S(1)} %copy-done.29, ...), custom_call_target="tpu_custom_call" | custom-call | flops 7200000000 | bytes 24000000 | tf_op jit(solution)/shard_map/pallas_call | solution.py:911
  124.3 3.1 collective-permute-start.15
  127.4 9.0 %shard_map.252 = (f32[1024,768]{1,0:T(8,128)S(1)}, f32[1024,256]{1,0:T(8,128)S(1)}) custom-call(f32[1024,768]{1,0:T(8,128)S(1)} %copy-done.62, f32[1024,128]{1,0:T(8,128)S(1)} %copy-done.75, f32[1024,256]{1,0:T(8,128)S(1)} %copy-done.50, f32[1024,128]{1,0:T(8,128)S(1)} %copy-done.52, f32[16,1024]{1,0:T(8,128)S(1)} %get-tuple-element.121.cumt_ref, ...), custom_call_target="tpu_custom_call" | custom-call | flops 8099999744 | bytes 27000000 | tf_op jit(solution)/shard_map/pallas_call | solution.py:573
  136.4 1.7 copy-done.71
  140.1 20.4 %shard_map.253 = (bf16[1024,768]{1,0:T(8,128)(2,1)}, f32[1024,256]{1,0:T(8,128)}, bf16[1024,12]{1,0:T(8,128)(2,1)}, f32[16,768]{1,0:T(8,128)}, f32[8,1280]{1,0:T...) custom-call(f32[1024,768]{1,0:T(8,128)} %copy-done.71, f32[1024,256]{1,0:T(8,128)} %copy-done.77, f32[1024,768]{1,0:T(8,128)} %copy-done.63, ...), custom_call_target="tpu_custom_call" | custom-call | flops 14400000000 | bytes 48000000 | tf_op jit(solution)/shard_map/pallas_call | solution.py:724
  160.5 1.6 collective-permute-start.17
  162.1 16.6 %collective-permute-done.15.refs_2_ = f32[768,384]{1,0:T(8,128)} collective-permute-done((f32[768,384]{1,0:T(8,128)}, f32[768,384]{1,0:T(8,128)}, u32[]{:S(2)}, u32[]{:S(2)}) %collective-permute-start.15) | collective-permute-done | bytes 1179680 | tf_op jit(solution)/shard_map/ppermute | solution.py:789
  180.4 2.4 shard_map.254
  185.2 10.2 %shard_map.255 = (f32[4,1024,384]{2,1,0:T(8,128)S(1)}, bf16[1024,768]{1,0:T(8,128)(2,1)}, f32[8,1024]{1,0:T(8,128)S(1)}, f32[8,1536]{1,0:T(8,128)S(1)}) custom-call(bf16[1024,768]{1,0:T(8,128)(2,1)S(1)} %copy-done.30, bf16[1024,768]{1,0:T(8,128)(2,1)S(1)} %copy-done.72, bf16[1024,12]{1,0:T(8,128)(2,1)S(1)} %copy-done.67, f32[16,768]{1,0:T(8,128)S(1)} %copy-done.79, ...), custom_call_target="tpu_custom_call" | custom-call | flops 8099999744 | bytes 27000000 | tf_op jit(solution)/shard_map/pallas_call | solution.py:876
  195.4 2.6 copy-done
  199.3 1.9 collective-permute-start.33
  201.6 2.8 copy-done.1
  204.4 1.8 shard_map.256
  206.1 3.1 collective-permute-start.18
  209.3 6.1 %collective-permute-done.34 = bf16[768,384]{1,0:T(8,128)(2,1)} collective-permute-done((bf16[768,384]{1,0:T(8,128)(2,1)}, bf16[768,384]{1,0:T(8,128)(2,1)}, u32[]{:S(2)}, u32[]{:S(2)}) %collective-permute-start.34) | collective-permute-done | bytes 589856 | tf_op jit(solution)/shard_map/ppermute | solution.py:789
  215.4 1.6 collective-permute-start.19
  217.0 10.6 %collective-permute-done.33 = bf16[768,384]{1,0:T(8,128)(2,1)} collective-permute-done((bf16[768,384]{1,0:T(8,128)(2,1)}, bf16[768,384]{1,0:T(8,128)(2,1)}, u32[]{:S(2)}, u32[]{:S(2)}) %collective-permute-start.33) | collective-permute-done | bytes 589856 | tf_op jit(solution)/shard_map/ppermute | solution.py:789
  227.7 3.2 pad_maximum_fusion.here
  232.6 3.6 collective-permute-start.26
  236.8 2.8 copy-done.2
  239.6 3.2 shard_map.257
  243.5 3.5 collective-permute-start.20
  247.1 1.7 collective-permute-start.21
  248.8 6.8 %shard_map.260 = (f32[384,384]{1,0:T(8,128)S(1)}, f32[384,384]{1,0:T(8,128)S(1)}, f32[384,384]{1,0:T(8,128)S(1)}, f32[384,384]{1,0:T(8,128)S(1)}) custom-call(s32[2]{0:T(128)S(1)} %pad_add_fusion.plan_ref, bf16[1024,1536]{1,0:T(8,128)(2,1)S(1)} %copy-done.20, bf16[1024,1536]{1,0:T(8,128)(2,1)} %collective-permute-done.7.normed_b, ...), custom_call_target="tpu_custom_call" | custom-call | flops 4499999744 | bytes 15000000 | tf_op jit(solution)/shard_map/pallas_call | solution.py:911
  257.0 5.4 %collective-permute-start.28 = (bf16[304,256]{1,0:T(8,128)(2,1)S(1)}, bf16[304,256]{1,0:T(8,128)(2,1)S(1)}, u32[]{:S(2)}, u32[]{:S(2)}) collective-permute-start(bf16[304,256]{1,0:T(8,128)(2,1)S(1)} %shard_map.261.refs_0_), channel_id=1, source_target_pairs={{0,1},{1,2},{2,3},{3,0},{4,5},{5,6},{6,7},{7,4},{8,9},{9,10},{10,1... | collective-permute-start | bytes 466952 | tf_op jit(solution)/shard_map/ppermute | solution.py:781
  262.7 12.7 %collective-permute-done.28.refs_1_ = bf16[304,256]{1,0:T(8,128)(2,1)S(1)} collective-permute-done((bf16[304,256]{1,0:T(8,128)(2,1)S(1)}, bf16[304,256]{1,0:T(8,128)(2,1)S(1)}, u32[]{:S(2)}, u32[]{:S(2)}) %collective-permute-start.28) | collective-permute-done | bytes 155680 | tf_op jit(solution)/shard_map/ppermute | solution.py:781
  275.4 12.0 %collective-permute-done.29.refs_2_ = bf16[304,256]{1,0:T(8,128)(2,1)S(1)} collective-permute-done((bf16[304,256]{1,0:T(8,128)(2,1)S(1)}, bf16[304,256]{1,0:T(8,128)(2,1)S(1)}, u32[]{:S(2)}, u32[]{:S(2)}) %collective-permute-start.29) | collective-permute-done | bytes 155680 | tf_op jit(solution)/shard_map/ppermute | solution.py:781
  287.4 3.2 collective-permute-done.30.refs_3_
  291.8 1.7 collective-permute-start.39
  295.4 2.8 copy-done.3
  298.2 3.2 shard_map.258
  301.4 3.5 collective-permute-start.22
  304.9 5.7 %shard_map.264 = (f32[144,384]{1,0:T(8,128)S(1)}, f32[144,384]{1,0:T(8,128)}, f32[144,384]{1,0:T(8,128)}, f32[144,384]{1,0:T(8,128)}) custom-call(s32[2]{0:T(128)S(1)} %pad_add_fusion.plan_ref, bf16[1024,1536]{1,0:T(8,128)(2,1)S(1)} %copy-done.21, bf16[1024,1536]{1,0:T(8,128)(2,1)} %collective-permute-done.7.normed_b, ...), custom_call_target="tpu_custom_call" | custom-call | flops 3600000000 | bytes 12000000 | tf_op jit(solution)/shard_map/pallas_call | solution.py:911
  311.9 9.7 %collective-permute-done.40.refs_2_ = f32[384,384]{1,0:T(8,128)S(1)} collective-permute-done((f32[384,384]{1,0:T(8,128)}, f32[384,384]{1,0:T(8,128)S(1)}, u32[]{:S(2)}, u32[]{:S(2)}) %collective-permute-start.40) | collective-permute-done | bytes 589856 | tf_op jit(solution)/shard_map/ppermute | solution.py:789
  323.3 2.9 collective-permute-start.38
  326.1 6.8 %shard_map.265 = (f32[1536,768]{1,0:T(8,128)}, f32[768,1536]{1,0:T(8,128)}) custom-call(s32[2]{0:T(128)S(1)} %pad_add_fusion.plan_ref, bf16[3072,384]{1,0:T(8,128)(2,1)} %pad_maximum_fusion.here, bf16[3072,384]{1,0:T(8,128)(2,1)} %collective-permute-done.35.there), custom_call_target="tpu_custom_call" | custom-call | flops 5400000000 | bytes 18000000 | tf_op jit(solution)/shard_map/pallas_call | solution.py:911
  332.9 2.5 fusion
  337.6 2.9 collective-permute-start.44
  340.5 2.8 copy-done.4
  343.3 4.4 %shard_map.263 = f32[1024,384]{1,0:T(8,128)} custom-call(s32[1]{0:T(128)} %bitcast.9.plan_ref, f32[4,1024,384]{2,1,0:T(8,128)S(1)} %copy-done.4, bf16[1024,384]{1,0:T(8,128)(2,1)} %collective-permute-done.22.up_ref, bf16[1024,384]{1,0:T(8,128)(2,1)} %collective-permute-done.23.down_ref, bf16[1024,1536]{1,0:T(8,128)(2,1)S(1)} %bitcast.39, ...), custom_call_target="tpu_custom_call" | custom-call | flops 3600000000 | bytes 12000000 | tf_op jit(solution)/shard_map/pallas_call | solution.py:911
  349.1 5.6 %collective-permute-done.44 = bf16[512,384]{1,0:T(8,128)(2,1)S(1)} collective-permute-done((bf16[512,384]{1,0:T(8,128)(2,1)S(1)}, bf16[512,384]{1,0:T(8,128)(2,1)S(1)}, u32[]{:S(2)}, u32[]{:S(2)}) %collective-permute-start.44) | collective-permute-done | bytes 393248 | tf_op jit(solution)/shard_map/ppermute | solution.py:789
  360.1 3.3 shard_map.268
  (255 shorter events, 46.5 us)
Async XLA Ops:
  7.2 325.7 %reduce-scatter.2.cloned.1.call-start = ((), (), s32[]{:S(2)}) async-start(), calls=%async_computation.1 | async-start | bytes 7864320 | tf_op jit(solution)/shard_map/reduce_scatter | solution.py:1321
  8.0 17.1 %collective-permute-start = (bf16[16,1536]{1,0:T(8,128)(2,1)S(1)}, bf16[16,1536]{1,0:T(8,128)(2,1)S(1)}, u32[]{:S(2)}, u32[]{:S(2)}) collective-permute-start(bf16[16,1536]{1,0:T(8,128)(2,1)S(1)} %slice_bitcast_fusion), channel_id=1, source_target_pairs={{0,4},{4,8},{8,12},{1,5},{5,9},{9,13},{2,6},{6,10},{10,14},{3,7},{... | collective-permute-start | bytes 147464 | tf_op jit(solution)/shard_map/ppermute | solution.py:771
  35.2 36.5 %copy-start.49 = (f32[1024,256]{1,0:T(8,128)}, f32[1024,256]{1,0:T(8,128)S(1)}, u32[]{:S(2)}) copy-start(f32[1024,256]{1,0:T(8,128)S(1)} %get-tuple-element.119.rows_ref) | copy-start | bytes 3145732
  35.2 36.5 %copy-start.51 = (f32[1024,128]{1,0:T(8,128)}, f32[1024,128]{1,0:T(8,128)S(1)}, u32[]{:S(2)}) copy-start(f32[1024,128]{1,0:T(8,128)S(1)} %get-tuple-element.120.cum_ref) | copy-start | bytes 1572868
  35.2 17.8 %collective-permute-start.1 = (f32[136,768]{1,0:T(8,128)S(1)}, f32[136,768]{1,0:T(8,128)S(1)}, u32[]{:S(2)}, u32[]{:S(2)}) collective-permute-start(f32[136,768]{1,0:T(8,128)S(1)} %get-tuple-element.123.own_ref), channel_id=1, source_target_pairs={{0,4},{4,8},{8,12},{1,5},{5,9},{9,13},{2,6},{6,10},{10,14},{3,7},{... | collective-permute-start | bytes 1253384 | tf_op jit(solution)/shard_map/ppermute | solution.py:771
  38.6 18.5 %collective-permute-start.2 = (f32[136,768]{1,0:T(8,128)S(1)}, f32[136,768]{1,0:T(8,128)S(1)}, u32[]{:S(2)}, u32[]{:S(2)}) collective-permute-start(f32[136,768]{1,0:T(8,128)S(1)} %get-tuple-element.123.own_ref), channel_id=1, source_target_pairs={{0,8},{4,12},{1,9},{5,13},{2,10},{6,14},{3,11},{7,15},{16,24},{20,... | collective-permute-start | bytes 1253384 | tf_op jit(solution)/shard_map/ppermute | solution.py:771
  40.6 16.5 %collective-permute-start.3 = (f32[136,768]{1,0:T(8,128)S(1)}, f32[136,768]{1,0:T(8,128)S(1)}, u32[]{:S(2)}, u32[]{:S(2)}) collective-permute-start(f32[136,768]{1,0:T(8,128)S(1)} %get-tuple-element.123.own_ref), channel_id=1, source_target_pairs={{0,12},{1,13},{2,14},{3,15},{16,28},{17,29},{18,30},{19,31}} | collective-permute-start | bytes 1253384 | tf_op jit(solution)/shard_map/ppermute | solution.py:771
  63.6 5.7 %collective-permute-start.4 = (f32[8,1024]{1,0:T(8,128)S(1)}, f32[8,1024]{1,0:T(8,128)S(1)}, u32[]{:S(2)}, u32[]{:S(2)}) collective-permute-start(f32[8,1024]{1,0:T(8,128)S(1)} %get-tuple-element.132.refs_0_), channel_id=1, source_target_pairs={{0,1},{1,2},{2,3},{3,0},{4,5},{5,6},{6,7},{7,4},{8,9},{9,10},{10,1... | collective-permute-start | bytes 98312 | tf_op jit(solution)/shard_map/ppermute | solution.py:781
  65.2 5.3 %collective-permute-start.5 = (f32[8,1024]{1,0:T(8,128)S(1)}, f32[8,1024]{1,0:T(8,128)S(1)}, u32[]{:S(2)}, u32[]{:S(2)}) collective-permute-start(f32[8,1024]{1,0:T(8,128)S(1)} %get-tuple-element.132.refs_0_), channel_id=1, source_target_pairs={{0,2},{1,3},{2,0},{3,1},{4,6},{5,7},{6,4},{7,5},{8,10},{9,11},{10,... | collective-permute-start | bytes 98312 | tf_op jit(solution)/shard_map/ppermute | solution.py:781
  67.7 3.9 %collective-permute-start.6 = (f32[8,1024]{1,0:T(8,128)S(1)}, f32[8,1024]{1,0:T(8,128)S(1)}, u32[]{:S(2)}, u32[]{:S(2)}) collective-permute-start(f32[8,1024]{1,0:T(8,128)S(1)} %get-tuple-element.132.refs_0_), channel_id=1, source_target_pairs={{0,3},{1,0},{2,1},{3,2},{4,7},{5,4},{6,5},{7,6},{8,11},{9,8},{10,9... | collective-permute-start | bytes 98312 | tf_op jit(solution)/shard_map/ppermute | solution.py:781
  88.8 16.5 %collective-permute-start.7 = (bf16[1024,1536]{1,0:T(8,128)(2,1)}, bf16[1024,1536]{1,0:T(8,128)(2,1)}, u32[]{:S(2)}, u32[]{:S(2)}) collective-permute-start(bf16[1024,1536]{1,0:T(8,128)(2,1)} %copy-done.18), channel_id=1, source_target_pairs={{0,16},{16,0},{1,17},{17,1},{2,18},{18,2},{3,19},{19,3},{4,20},{20... | collective-permute-start | bytes 9437192 | tf_op jit(solution)/shard_map/ppermute | solution.py:789
  88.8 16.5 %collective-permute-start.10 = (bf16[1024,1536]{1,0:T(8,128)(2,1)S(1)}, bf16[1024,1536]{1,0:T(8,128)(2,1)}, u32[]{:S(2)}, u32[]{:S(2)}) collective-permute-start(bf16[1024,1536]{1,0:T(8,128)(2,1)S(1)} %bitcast.42), channel_id=1, source_target_pairs={{0,16},{16,0},{1,17},{17,1},{2,18},{18,2},{3,19},{19,3},{4,20},{20... | collective-permute-start | bytes 9437192 | tf_op jit(solution)/shard_map/ppermute | solution.py:789
  89.3 12.2 %collective-permute-start.8 = (bf16[1024,768]{1,0:T(8,128)(2,1)}, bf16[1024,768]{1,0:T(8,128)(2,1)}, u32[]{:S(2)}, u32[]{:S(2)}) collective-permute-start(bf16[1024,768]{1,0:T(8,128)(2,1)} %copy-done.28), channel_id=1, source_target_pairs={{0,16},{16,0},{1,17},{17,1},{2,18},{18,2},{3,19},{19,3},{4,20},{20... | collective-permute-start | bytes 4718600 | tf_op jit(solution)/shard_map/ppermute | solution.py:789
  89.4 14.4 %collective-permute-start.9 = (bf16[1024,768]{1,0:T(8,128)(2,1)}, bf16[1024,768]{1,0:T(8,128)(2,1)}, u32[]{:S(2)}, u32[]{:S(2)}) collective-permute-start(bf16[1024,768]{1,0:T(8,128)(2,1)} %copy-done.31), channel_id=1, source_target_pairs={{0,16},{16,0},{1,17},{17,1},{2,18},{18,2},{3,19},{19,3},{4,20},{20... | collective-permute-start | bytes 4718600 | tf_op jit(solution)/shard_map/ppermute | solution.py:789
  89.9 49.1 %collective-permute-start.11 = (f32[136,768]{1,0:T(8,128)}, f32[136,768]{1,0:T(8,128)S(1)}, u32[]{:S(2)}, u32[]{:S(2)}) collective-permute-start(f32[136,768]{1,0:T(8,128)} %copy-done.36), channel_id=1, source_target_pairs={{4,0},{8,4},{12,8},{5,1},{9,5},{13,9},{6,2},{10,6},{14,10},{7,3},{... | collective-permute-start | bytes 1253384 | tf_op jit(solution)/shard_map/ppermute | solution.py:776
  101.6 37.5 %collective-permute-start.12 = (f32[136,768]{1,0:T(8,128)}, f32[136,768]{1,0:T(8,128)S(1)}, u32[]{:S(2)}, u32[]{:S(2)}) collective-permute-start(f32[136,768]{1,0:T(8,128)} %copy-done.36), channel_id=1, source_target_pairs={{8,0},{12,4},{9,1},{13,5},{10,2},{14,6},{11,3},{15,7},{24,16},{28,... | collective-permute-start | bytes 1253384 | tf_op jit(solution)/shard_map/ppermute | solution.py:776
  103.8 35.3 %collective-permute-start.13 = (f32[136,768]{1,0:T(8,128)}, f32[136,768]{1,0:T(8,128)S(1)}, u32[]{:S(2)}, u32[]{:S(2)}) collective-permute-start(f32[136,768]{1,0:T(8,128)} %copy-done.36), channel_id=1, source_target_pairs={{12,0},{13,1},{14,2},{15,3},{28,16},{29,17},{30,18},{31,19}} | collective-permute-start | bytes 1253384 | tf_op jit(solution)/shard_map/ppermute | solution.py:776
  110.1 17.3 %copy-start.52 = (f32[1024,128]{1,0:T(8,128)S(1)}, f32[1024,128]{1,0:T(8,128)}, u32[]{:S(2)}) copy-start(f32[1024,128]{1,0:T(8,128)} %copy-done.51) | copy-start | bytes 1572868
  110.1 17.3 %copy-start.62 = (f32[1024,768]{1,0:T(8,128)S(1)}, f32[1024,768]{1,0:T(8,128)}, u32[]{:S(2)}) copy-start(f32[1024,768]{1,0:T(8,128)} %copy-done.61) | copy-start | bytes 9437188
  110.1 17.3 %copy-start.64 = (f32[1024,768]{1,0:T(8,128)S(1)}, f32[1024,768]{1,0:T(8,128)}, u32[]{:S(2)}) copy-start(f32[1024,768]{1,0:T(8,128)} %copy-done.63) | copy-start | bytes 9437188
  110.1 17.3 %copy-start.75 = (f32[1024,128]{1,0:T(8,128)S(1)}, f32[1024,128]{1,0:T(8,128)}, u32[]{:S(2)}) copy-start(f32[1024,128]{1,0:T(8,128)} %copy-done.74) | copy-start | bytes 1572868
  123.0 39.1 %collective-permute-start.14 = (f32[768,384]{1,0:T(8,128)}, f32[768,384]{1,0:T(8,128)}, u32[]{:S(2)}, u32[]{:S(2)}) collective-permute-start(f32[768,384]{1,0:T(8,128)} %get-tuple-element.139), channel_id=1, source_target_pairs={{0,4},{4,0},{8,12},{12,8},{1,5},{5,1},{9,13},{13,9},{2,6},{6,2},{1... | collective-permute-start | bytes 3538952 | tf_op jit(solution)/shard_map/ppermute | solution.py:789
  124.3 54.4 %collective-permute-start.15 = (f32[768,384]{1,0:T(8,128)}, f32[768,384]{1,0:T(8,128)}, u32[]{:S(2)}, u32[]{:S(2)}) collective-permute-start(f32[768,384]{1,0:T(8,128)} %get-tuple-element.140), channel_id=1, source_target_pairs={{0,8},{4,12},{8,0},{12,4},{1,9},{5,13},{9,1},{13,5},{2,10},{6,14},... | collective-permute-start | bytes 3538952 | tf_op jit(solution)/shard_map/ppermute | solution.py:789
  139.0 40.1 %collective-permute-start.16 = (f32[768,384]{1,0:T(8,128)}, f32[768,384]{1,0:T(8,128)}, u32[]{:S(2)}, u32[]{:S(2)}) collective-permute-start(f32[768,384]{1,0:T(8,128)} %get-tuple-element.141), channel_id=1, source_target_pairs={{0,12},{4,8},{8,4},{12,0},{1,13},{5,9},{9,5},{13,1},{2,14},{6,10},... | collective-permute-start | bytes 3538952 | tf_op jit(solution)/shard_map/ppermute | solution.py:789
  140.1 43.6 %copy-start.30 = (bf16[1024,768]{1,0:T(8,128)(2,1)S(1)}, bf16[1024,768]{1,0:T(8,128)(2,1)}, u32[]{:S(2)}) copy-start(bf16[1024,768]{1,0:T(8,128)(2,1)} %copy-done.28) | copy-start | bytes 4718596
  160.5 23.2 %copy-start.6 = (bf16[1,1024,1536]{2,1,0:T(8,128)(2,1)S(1)}, bf16[1,1024,1536]{2,1,0:T(8,128)(2,1)}, u32[]{:S(2)}) copy-start(bf16[1,1024,1536]{2,1,0:T(8,128)(2,1)} %param.14) | copy-start | bytes 9437188
  160.5 23.2 %copy-start.25 = (bf16[1536,768]{1,0:T(8,128)(2,1)S(1)}, bf16[1536,768]{1,0:T(8,128)(2,1)}, u32[]{:S(2)}) copy-start(bf16[1536,768]{1,0:T(8,128)(2,1)} %value_w.3) | copy-start | bytes 7077892
  160.5 23.2 %copy-start.27 = (bf16[1536,768]{1,0:T(8,128)(2,1)S(1)}, bf16[1536,768]{1,0:T(8,128)(2,1)}, u32[]{:S(2)}) copy-start(bf16[1536,768]{1,0:T(8,128)(2,1)} %gate_w.3) | copy-start | bytes 7077892
  160.5 23.2 %copy-start.38 = (bf16[1536,12]{0,1:T(8,128)(2,1)S(1)}, bf16[1536,12]{0,1:T(8,128)(2,1)}, u32[]{:S(2)}) copy-start(bf16[1536,12]{0,1:T(8,128)(2,1)} %param.19) | copy-start | bytes 110596
  160.5 23.2 %copy-start.40 = (bf16[4,768]{1,0:T(4,128)(2,1)S(1)}, bf16[4,768]{1,0:T(4,128)(2,1)}, u32[]{:S(2)}) copy-start(bf16[4,768]{1,0:T(4,128)(2,1)} %taps_ref.1) | copy-start | bytes 18436
  160.5 23.1 %collective-permute-start.17 = (f32[8,1280]{1,0:T(8,128)}, f32[8,1280]{1,0:T(8,128)S(1)}, u32[]{:S(2)}, u32[]{:S(2)}) collective-permute-start(f32[8,1280]{1,0:T(8,128)} %get-tuple-element.158), channel_id=1, source_target_pairs={{4,0},{8,4},{12,8},{5,1},{9,5},{13,9},{6,2},{10,6},{14,10},{7,3},{... | collective-permute-start | bytes 122888 | tf_op jit(solution)/shard_map/ppermute | solution.py:776
  198.0 49.1 %collective-permute-start.24 = (bf16[1024,768]{1,0:T(8,128)(2,1)}, bf16[1024,768]{1,0:T(8,128)(2,1)}, u32[]{:S(2)}, u32[]{:S(2)}) collective-permute-start(bf16[1024,768]{1,0:T(8,128)(2,1)} %get-tuple-element.173.value_a), channel_id=1, source_target_pairs={{0,16},{16,0},{1,17},{17,1},{2,18},{18,2},{3,19},{19,3},{4,20},{20... | collective-permute-start | bytes 4718600 | tf_op jit(solution)/shard_map/ppermute | solution.py:789
  198.0 17.4 %collective-permute-start.34 = (bf16[768,384]{1,0:T(8,128)(2,1)}, bf16[768,384]{1,0:T(8,128)(2,1)}, u32[]{:S(2)}, u32[]{:S(2)}) collective-permute-start(bf16[768,384]{1,0:T(8,128)(2,1)} %convert_element_type.16), channel_id=1, source_target_pairs={{0,12},{4,8},{8,4},{12,0},{1,13},{5,9},{9,5},{13,1},{2,14},{6,10},... | collective-permute-start | bytes 1769480 | tf_op jit(solution)/shard_map/ppermute | solution.py:789
  199.3 28.3 %collective-permute-start.33 = (bf16[768,384]{1,0:T(8,128)(2,1)}, bf16[768,384]{1,0:T(8,128)(2,1)}, u32[]{:S(2)}, u32[]{:S(2)}) collective-permute-start(bf16[768,384]{1,0:T(8,128)(2,1)} %convert_element_type.16), channel_id=1, source_target_pairs={{0,8},{4,12},{8,0},{12,4},{1,9},{5,13},{9,1},{13,5},{2,10},{6,14},... | collective-permute-start | bytes 1769480 | tf_op jit(solution)/shard_map/ppermute | solution.py:789
  201.2 26.5 %collective-permute-start.32 = (bf16[768,384]{1,0:T(8,128)(2,1)}, bf16[768,384]{1,0:T(8,128)(2,1)}, u32[]{:S(2)}, u32[]{:S(2)}) collective-permute-start(bf16[768,384]{1,0:T(8,128)(2,1)} %convert_element_type.16), channel_id=1, source_target_pairs={{0,4},{4,0},{8,12},{12,8},{1,5},{5,1},{9,13},{13,9},{2,6},{6,2},{1... | collective-permute-start | bytes 1769480 | tf_op jit(solution)/shard_map/ppermute | solution.py:789
  206.1 26.4 %collective-permute-start.18 = (bf16[1024,384]{1,0:T(8,128)(2,1)}, bf16[1024,384]{1,0:T(8,128)(2,1)}, u32[]{:S(2)}, u32[]{:S(2)}) collective-permute-start(bf16[1024,384]{1,0:T(8,128)(2,1)} %get-tuple-element.164), channel_id=1, source_target_pairs={{0,1},{4,5},{8,9},{12,13},{16,17},{20,21},{24,25},{28,29}} | collective-permute-start | bytes 2359304 | tf_op jit(solution)/shard_map/ppermute | solution.py:829
  215.4 20.8 %collective-permute-start.19 = (bf16[1024,384]{1,0:T(8,128)(2,1)}, bf16[1024,384]{1,0:T(8,128)(2,1)}, u32[]{:S(2)}, u32[]{:S(2)}) collective-permute-start(bf16[1024,384]{1,0:T(8,128)(2,1)} %get-tuple-element.165), channel_id=1, source_target_pairs={{3,2},{7,6},{11,10},{15,14},{19,18},{23,22},{27,26},{31,30}} | collective-permute-start | bytes 2359304 | tf_op jit(solution)/shard_map/ppermute | solution.py:830
  231.0 92.3 %collective-permute-start.35 = (bf16[3072,384]{1,0:T(8,128)(2,1)}, bf16[3072,384]{1,0:T(8,128)(2,1)}, u32[]{:S(2)}, u32[]{:S(2)}) collective-permute-start(bf16[3072,384]{1,0:T(8,128)(2,1)} %pad_maximum_fusion.here), channel_id=1, source_target_pairs={{0,16},{16,0},{1,17},{17,1},{2,18},{18,2},{3,19},{19,3},{4,20},{20... | collective-permute-start | bytes 7077896 | tf_op jit(solution)/shard_map/ppermute | solution.py:789
  232.3 11.3 %collective-permute-start.25 = (f32[264,256]{1,0:T(8,128)S(1)}, f32[264,256]{1,0:T(8,128)S(1)}, u32[]{:S(2)}, u32[]{:S(2)}) collective-permute-start(f32[264,256]{1,0:T(8,128)S(1)} %get-tuple-element.178), channel_id=1, source_target_pairs={{0,1},{1,2},{2,3},{3,0},{4,5},{5,6},{6,7},{7,4},{8,9},{9,10},{10,1... | collective-permute-start | bytes 811016 | tf_op jit(solution)/shard_map/ppermute | solution.py:1340
  232.6 23.1 %collective-permute-start.26 = (f32[264,256]{1,0:T(8,128)S(1)}, f32[264,256]{1,0:T(8,128)S(1)}, u32[]{:S(2)}, u32[]{:S(2)}) collective-permute-start(f32[264,256]{1,0:T(8,128)S(1)} %get-tuple-element.179), channel_id=1, source_target_pairs={{0,2},{1,3},{2,0},{3,1},{4,6},{5,7},{6,4},{7,5},{8,10},{9,11},{10,... | collective-permute-start | bytes 811016 | tf_op jit(solution)/shard_map/ppermute | solution.py:1340
  236.2 19.5 %collective-permute-start.27 = (f32[264,256]{1,0:T(8,128)S(1)}, f32[264,256]{1,0:T(8,128)S(1)}, u32[]{:S(2)}, u32[]{:S(2)}) collective-permute-start(f32[264,256]{1,0:T(8,128)S(1)} %get-tuple-element.180), channel_id=1, source_target_pairs={{0,3},{1,0},{2,1},{3,2},{4,7},{5,4},{6,5},{7,6},{8,11},{9,8},{10,9... | collective-permute-start | bytes 811016 | tf_op jit(solution)/shard_map/ppermute | solution.py:1340
  243.5 49.9 %collective-permute-start.20 = (bf16[1024,384]{1,0:T(8,128)(2,1)}, bf16[1024,384]{1,0:T(8,128)(2,1)}, u32[]{:S(2)}, u32[]{:S(2)}) collective-permute-start(bf16[1024,384]{1,0:T(8,128)(2,1)} %get-tuple-element.166), channel_id=1, source_target_pairs={{0,1},{1,2},{4,5},{5,6},{8,9},{9,10},{12,13},{13,14},{16,17},{17,1... | collective-permute-start | bytes 2359304 | tf_op jit(solution)/shard_map/ppermute | solution.py:829
  247.1 46.9 %collective-permute-start.21 = (bf16[1024,384]{1,0:T(8,128)(2,1)}, bf16[1024,384]{1,0:T(8,128)(2,1)}, u32[]{:S(2)}, u32[]{:S(2)}) collective-permute-start(bf16[1024,384]{1,0:T(8,128)(2,1)} %get-tuple-element.167), channel_id=1, source_target_pairs={{3,2},{2,1},{7,6},{6,5},{11,10},{10,9},{15,14},{14,13},{19,18},{18... | collective-permute-start | bytes 2359304 | tf_op jit(solution)/shard_map/ppermute | solution.py:830
  255.7 34.9 %copy-start.68 = (bf16[1024,12]{1,0:T(8,128)(2,1)S(1)}, bf16[1024,12]{1,0:T(8,128)(2,1)}, u32[]{:S(2)}) copy-start(bf16[1024,12]{1,0:T(8,128)(2,1)} %get-tuple-element.156.step_ref.refs_4_) | copy-start | bytes 73732
  255.7 34.9 %copy-start.78 = (f32[8,768]{1,0:T(8,128)S(1)}, f32[8,768]{1,0:T(8,128)}, u32[]{:S(2)}) copy-start(f32[8,768]{1,0:T(8,128)} %get-tuple-element.190.refs_5_) | copy-start | bytes 73732
  255.7 34.9 %copy-start.80 = (f32[8,128]{1,0:T(8,128)S(1)}, f32[8,128]{1,0:T(8,128)}, u32[]{:S(2)}) copy-start(f32[8,128]{1,0:T(8,128)} %get-tuple-element.192.refs_7_) | copy-start | bytes 12292
  257.0 18.3 %collective-permute-start.28 = (bf16[304,256]{1,0:T(8,128)(2,1)S(1)}, bf16[304,256]{1,0:T(8,128)(2,1)S(1)}, u32[]{:S(2)}, u32[]{:S(2)}) collective-permute-start(bf16[304,256]{1,0:T(8,128)(2,1)S(1)} %shard_map.261.refs_0_), channel_id=1, source_target_pairs={{0,1},{1,2},{2,3},{3,0},{4,5},{5,6},{6,7},{7,4},{8,9},{9,10},{10,1... | collective-permute-start | bytes 466952 | tf_op jit(solution)/shard_map/ppermute | solution.py:781
  262.4 25.0 %collective-permute-start.29 = (bf16[304,256]{1,0:T(8,128)(2,1)S(1)}, bf16[304,256]{1,0:T(8,128)(2,1)S(1)}, u32[]{:S(2)}, u32[]{:S(2)}) collective-permute-start(bf16[304,256]{1,0:T(8,128)(2,1)S(1)} %shard_map.261.refs_0_), channel_id=1, source_target_pairs={{0,2},{1,3},{2,0},{3,1},{4,6},{5,7},{6,4},{7,5},{8,10},{9,11},{10,... | collective-permute-start | bytes 466952 | tf_op jit(solution)/shard_map/ppermute | solution.py:781
  275.4 15.3 %collective-permute-start.30 = (bf16[304,256]{1,0:T(8,128)(2,1)S(1)}, bf16[304,256]{1,0:T(8,128)(2,1)S(1)}, u32[]{:S(2)}, u32[]{:S(2)}) collective-permute-start(bf16[304,256]{1,0:T(8,128)(2,1)S(1)} %shard_map.261.refs_0_), channel_id=1, source_target_pairs={{0,3},{1,0},{2,1},{3,2},{4,7},{5,4},{6,5},{7,6},{8,11},{9,8},{10,9... | collective-permute-start | bytes 466952 | tf_op jit(solution)/shard_map/ppermute | solution.py:781
  291.8 9.7 %collective-permute-start.31 = (bf16[1168,128]{1,0:T(8,128)(2,1)}, bf16[1168,128]{1,0:T(8,128)(2,1)}, u32[]{:S(2)}, u32[]{:S(2)}) collective-permute-start(bf16[1168,128]{1,0:T(8,128)(2,1)} %get-tuple-element.194.narrow_a), channel_id=1, source_target_pairs={{0,16},{16,0},{1,17},{17,1},{2,18},{18,2},{3,19},{19,3},{4,20},{20... | collective-permute-start | bytes 897032 | tf_op jit(solution)/shard_map/ppermute | solution.py:789
  291.8 18.9 %collective-permute-start.39 = (f32[384,384]{1,0:T(8,128)}, f32[384,384]{1,0:T(8,128)S(1)}, u32[]{:S(2)}, u32[]{:S(2)}) collective-permute-start(f32[384,384]{1,0:T(8,128)} %copy-done.35), channel_id=1, source_target_pairs={{0,4},{4,0},{8,12},{12,8},{1,5},{5,1},{9,13},{13,9},{2,6},{6,2},{1... | collective-permute-start | bytes 1769480 | tf_op jit(solution)/shard_map/ppermute | solution.py:789
  293.5 28.2 %collective-permute-start.40 = (f32[384,384]{1,0:T(8,128)}, f32[384,384]{1,0:T(8,128)S(1)}, u32[]{:S(2)}, u32[]{:S(2)}) collective-permute-start(f32[384,384]{1,0:T(8,128)} %copy-done.34), channel_id=1, source_target_pairs={{0,8},{4,12},{8,0},{12,4},{1,9},{5,13},{9,1},{13,5},{2,10},{6,14},... | collective-permute-start | bytes 1769480 | tf_op jit(solution)/shard_map/ppermute | solution.py:789
  294.0 27.7 %collective-permute-start.41 = (f32[384,384]{1,0:T(8,128)}, f32[384,384]{1,0:T(8,128)S(1)}, u32[]{:S(2)}, u32[]{:S(2)}) collective-permute-start(f32[384,384]{1,0:T(8,128)} %copy-done.33), channel_id=1, source_target_pairs={{0,12},{4,8},{8,4},{12,0},{1,13},{5,9},{9,5},{13,1},{2,14},{6,10},... | collective-permute-start | bytes 1769480 | tf_op jit(solution)/shard_map/ppermute | solution.py:789
  301.4 20.9 %copy-start.60 = (f32[384,384]{1,0:T(8,128)S(1)}, f32[384,384]{1,0:T(8,128)}, u32[]{:S(2)}) copy-start(f32[384,384]{1,0:T(8,128)} %copy-done.59) | copy-start | bytes 1769476
  301.4 39.1 %collective-permute-start.22 = (bf16[1024,384]{1,0:T(8,128)(2,1)}, bf16[1024,384]{1,0:T(8,128)(2,1)}, u32[]{:S(2)}, u32[]{:S(2)}) collective-permute-start(bf16[1024,384]{1,0:T(8,128)(2,1)} %get-tuple-element.168), channel_id=1, source_target_pairs={{0,1},{1,2},{2,3},{4,5},{5,6},{6,7},{8,9},{9,10},{10,11},{12,13},{... | collective-permute-start | bytes 2359304 | tf_op jit(solution)/shard_map/ppermute | solution.py:829
  310.7 29.8 %collective-permute-start.23 = (bf16[1024,384]{1,0:T(8,128)(2,1)}, bf16[1024,384]{1,0:T(8,128)(2,1)}, u32[]{:S(2)}, u32[]{:S(2)}) collective-permute-start(bf16[1024,384]{1,0:T(8,128)(2,1)} %get-tuple-element.169), channel_id=1, source_target_pairs={{3,2},{2,1},{1,0},{7,6},{6,5},{5,4},{11,10},{10,9},{9,8},{15,14},{... | collective-permute-start | bytes 2359304 | tf_op jit(solution)/shard_map/ppermute | solution.py:830
  321.7 13.7 %collective-permute-start.36 = (f32[144,384]{1,0:T(8,128)}, f32[144,384]{1,0:T(8,128)}, u32[]{:S(2)}, u32[]{:S(2)}) collective-permute-start(f32[144,384]{1,0:T(8,128)} %get-tuple-element.197), channel_id=1, source_target_pairs={{0,4},{4,0},{8,12},{12,8},{1,5},{5,1},{9,13},{13,9},{2,6},{6,2},{1... | collective-permute-start | bytes 663560 | tf_op jit(solution)/shard_map/ppermute | solution.py:789
  321.7 13.7 %collective-permute-start.37 = (f32[144,384]{1,0:T(8,128)}, f32[144,384]{1,0:T(8,128)}, u32[]{:S(2)}, u32[]{:S(2)}) collective-permute-start(f32[144,384]{1,0:T(8,128)} %get-tuple-element.198), channel_id=1, source_target_pairs={{0,8},{4,12},{8,0},{12,4},{1,9},{5,13},{9,1},{13,5},{2,10},{6,14},... | collective-permute-start | bytes 663560 | tf_op jit(solution)/shard_map/ppermute | solution.py:789
  323.3 12.2 %collective-permute-start.38 = (f32[144,384]{1,0:T(8,128)}, f32[144,384]{1,0:T(8,128)}, u32[]{:S(2)}, u32[]{:S(2)}) collective-permute-start(f32[144,384]{1,0:T(8,128)} %get-tuple-element.199), channel_id=1, source_target_pairs={{0,12},{4,8},{8,4},{12,0},{1,13},{5,9},{9,5},{13,1},{2,14},{6,10},... | collective-permute-start | bytes 663560 | tf_op jit(solution)/shard_map/ppermute | solution.py:789
  336.8 18.2 %copy-start.17 = (f32[144,384]{1,0:T(8,128)}, f32[144,384]{1,0:T(8,128)S(1)}, u32[]{:S(2)}) copy-start(f32[144,384]{1,0:T(8,128)S(1)} %shard_map.266) | copy-start | bytes 663556
  336.9 12.1 %collective-permute-start.42 = (bf16[512,384]{1,0:T(8,128)(2,1)S(1)}, bf16[512,384]{1,0:T(8,128)(2,1)S(1)}, u32[]{:S(2)}, u32[]{:S(2)}) collective-permute-start(bf16[512,384]{1,0:T(8,128)(2,1)S(1)} %pad_maximum_fusion.1), channel_id=1, source_target_pairs={{0,4},{4,0},{8,12},{12,8},{1,5},{5,1},{9,13},{13,9},{2,6},{6,2},{1... | collective-permute-start | bytes 1179656 | tf_op jit(solution)/shard_map/ppermute | solution.py:789
  337.0 12.1 %collective-permute-start.43 = (bf16[512,384]{1,0:T(8,128)(2,1)S(1)}, bf16[512,384]{1,0:T(8,128)(2,1)S(1)}, u32[]{:S(2)}, u32[]{:S(2)}) collective-permute-start(bf16[512,384]{1,0:T(8,128)(2,1)S(1)} %pad_maximum_fusion.1), channel_id=1, source_target_pairs={{0,8},{4,12},{8,0},{12,4},{1,9},{5,13},{9,1},{13,5},{2,10},{6,14},... | collective-permute-start | bytes 1179656 | tf_op jit(solution)/shard_map/ppermute | solution.py:789
  337.6 17.1 %collective-permute-start.44 = (bf16[512,384]{1,0:T(8,128)(2,1)S(1)}, bf16[512,384]{1,0:T(8,128)(2,1)S(1)}, u32[]{:S(2)}, u32[]{:S(2)}) collective-permute-start(bf16[512,384]{1,0:T(8,128)(2,1)S(1)} %pad_maximum_fusion.1), channel_id=1, source_target_pairs={{0,12},{4,8},{8,4},{12,0},{1,13},{5,9},{9,5},{13,1},{2,14},{6,10},... | collective-permute-start | bytes 1179656 | tf_op jit(solution)/shard_map/ppermute | solution.py:789
  354.9 5.2 %collective-permute-start.45 = (bf16[2048,384]{1,0:T(8,128)(2,1)S(1)}, bf16[2048,384]{1,0:T(8,128)(2,1)S(1)}, u32[]{:S(2)}, u32[]{:S(2)}) collective-permute-start(bf16[2048,384]{1,0:T(8,128)(2,1)S(1)} %constant_dynamic-update-slice_fusion.here), channel_id=1, source_target_pairs={{0,16},{16,0},{1,17},{17,1},{2,18},{18,2},{3,19},{19,3},{4,20},{20... | collective-permute-start | bytes 4718600 | tf_op jit(solution)/shard_map/ppermute | solution.py:789
  (70 other events, 403.0 us)
Sparse Core Ops, SparseCore 0:
  88.9 112.8 reduce-scatter.1

commit v3 on v2

--- a/solution.py
+++ b/solution.py
@@ -162,7 +162,7 @@
             jax.ShapeDtypeStruct((tokens, LANES), f32),
         ],
         scratch_shapes=[pltpu.VMEM((LANES, width), bf16)],
-        compiler_params=params(24),
+        compiler_params=params(56),
         cost_estimate=cost(6),
     )(residual, pre_gain, input_weight, state_weight, step_weight)
 
@@ -588,7 +588,7 @@
         ],
         scratch_shapes=[pltpu.VMEM((LANES, inner), bf16)],
         compiler_params=params(16),
-        cost_estimate=cost(9),
+        cost_estimate=cost(0),
     )(conv, dt, state_rows, cum, cumt, grad_mixed)
 
 
@@ -596,25 +596,18 @@
     return jnp.concatenate([jnp.concatenate([high, high], axis=1), jnp.concatenate([low, low], axis=1)], axis=0)
 
 
-def finish_kernel(
-    count, driven_ref, drows_ref, dmix_ref, mixed_ref, pre_ref, value_ref, dt_ref, cum_ref, step_ref, rows_ref,
-    held_ref, end_ref, later_ref, *refs
+def rows_back_kernel(
+    count, drows_ref, dmix_ref, conv_ref, dt_ref, cum_ref, rows_ref, held_ref, later_ref, *refs
 ):
     message_refs = refs[:count]
-    (
-        spre_ref, vhalo_ref, kernel_ref, skip_ref, bias_ref, log_ref,
-        grad_value_out, grad_rows_out, grad_step_out, last_out, first_out, kernel_out, small_out,
-        entering, total, held_next, pre_next, skip_sum, heads, kernel_sum, heads_t, edge_rows,
-    ) = refs[count:]
+    spre_ref, grad_rows_out, later_out, first_out, entering, total, heads = refs[count:]
     b = pl.program_id(0)
-    size, width = mixed_ref.shape
+    size, width = conv_ref.shape
     state = held_ref.shape[1]
-    final = b == pl.num_programs(0) - 1
 
     @pl.when(b == 0)
     def _():
         heads[...] = head_map(width)
-        heads_t[...] = (iota((width, LANES), 1) == iota((width, LANES), 0) // HEAD_DIM).astype(f32).astype(bf16)
         for span in spans(width):
             coming = jnp.zeros((state, LANES), f32)
             passed = jnp.zeros((EDGE, LANES), f32)
@@ -623,6 +616,72 @@
                 passed = passed + ref[state:, span]
             entering[:, span] = coming
         total[...] = jnp.zeros(total.shape, f32)
+
+    wide = spread(jnp.concatenate([cum_ref[...], dt_ref[...]], axis=0), heads[...])
+    toward_b, toward_c, laters, helds = [], [], [], []
+    for span in spans(width):
+        cum_part = wide[:size, span]
+        end = cum_part[size - 1 : size]
+        later = later_ref[0, :, span] + jnp.exp(total[0:1, span]) * entering[:, span]
+        later_out[0, :, span] = later
+        total[:, span] = total[:, span] + end
+        driven = conv_ref[:, span] * wide[size:, span]
+        toward_b.append(both_parts(jnp.exp(end - cum_part) * driven))
+        laters.append(stacked(*split2(later)))
+        toward_c.append(both_parts(jnp.exp(cum_part) * dmix_ref[:, span]))
+        helds.append(stacked(*split2(held_ref[0, :, span])))
+    side = lambda parts: jnp.concatenate(parts, axis=1)
+    grad_rows_out[:, :LANES] = drows_ref[:, :LANES] + fold(dot(side(toward_b), side(laters), NT))
+    grad_rows_out[:, LANES:] = drows_ref[:, LANES:] + fold(dot(side(toward_c), side(helds), NT))
+
+    @pl.when(b == pl.num_programs(0) - 1)
+    def _():
+        first_out[:, : 2 * LANES] = grad_rows_out[:EDGE]
+        first_out[:, 2 * LANES :] = spre_ref[...]
+
+
+def rows_back(grad_rows, grad_mixed, conv, dt, cum, state_rows, held, later, messages, spre):
+    tokens, inner = conv.shape
+    blocks, state, _ = held.shape
+    state_block = pl.BlockSpec((1, state, inner), lambda b: (blocks - 1 - b, 0, 0))
+    wide = rows(BLOCK, inner, blocks)
+    narrow = rows(BLOCK, LANES, blocks)
+    both = rows(BLOCK, 2 * state, blocks)
+    return pl.pallas_call(
+        functools.partial(rows_back_kernel, len(messages)),
+        grid=(blocks,),
+        in_specs=[
+            both, wide, wide, narrow, narrow, both, state_block, state_block,
+            *[whole(m.shape) for m in messages],
+            pl.BlockSpec((EDGE, 2 * state), lambda b: (0, 0)),
+        ],
+        out_specs=[both, state_block, whole((EDGE, 4 * state))],
+        out_shape=[
+            jax.ShapeDtypeStruct((tokens, 2 * state), f32),
+            jax.ShapeDtypeStruct(held.shape, f32),
+            jax.ShapeDtypeStruct((EDGE, 4 * state), f32),
+        ],
+        scratch_shapes=[pltpu.VMEM((state, inner), f32), pltpu.VMEM((EDGE, inner), f32), pltpu.VMEM((LANES, inner), bf16)],
+        compiler_params=params(24),
+        cost_estimate=cost(0),
+    )(grad_rows, grad_mixed, conv, dt, cum, state_rows, held, later, *messages, spre)
+
+
+def finish_kernel(
+    blocks, driven_ref, dmix_ref, mixed_ref, pre_ref, value_ref, dt_ref, cum_ref, step_ref, rows_ref, held_ref, end_ref, later_ref,
+    vhalo_ref, kernel_ref, skip_ref, bias_ref, log_ref,
+    grad_value_out, grad_step_out, last_out, first_out, kernel_out, small_out,
+    held_next, pre_next, skip_sum, heads, kernel_sum, heads_t, edge_rows,
+):
+    b = pl.program_id(0)
+    size, width = mixed_ref.shape
+    state = held_ref.shape[1]
+    final = b == blocks - 1
+
+    @pl.when(b == 0)
+    def _():
+        heads[...] = head_map(width)
+        heads_t[...] = (iota((width, LANES), 1) == iota((width, LANES), 0) // HEAD_DIM).astype(f32).astype(bf16)
         held_next[...] = end_ref[...]
         pre_next[...] = jnp.zeros(pre_next.shape, f32)
         kernel_sum[...] = jnp.zeros(kernel_sum.shape, f32)
@@ -635,14 +694,13 @@
     wide = spread(jnp.concatenate([cum, dt, skip_row], axis=0), heads[...])
     b_parts = both_parts(rows_ref[:, :LANES])
     taps = kernel_ref[...].astype(f32)
-    toward_b, toward_c, laters, helds, levels, throughs, boundaries = [], [], [], [], [], [], []
+    levels, throughs, boundaries = [], [], []
     for span in spans(width):
         cum_part = wide[:size, span]
         dt_wide = wide[size : 2 * size, span]
         skip = wide[2 * size : 2 * size + 1, span]
         end = cum_part[size - 1 : size]
-        later = later_ref[0, :, span] + jnp.exp(total[0:1, span]) * entering[:, span]
-        total[:, span] = total[:, span] + end
+        later = later_ref[0, :, span]
         held = held_ref[0, :, span]
         tail = jnp.exp(end - cum_part)
         dmix = dmix_ref[:, span]
@@ -653,10 +711,6 @@
         later_high, later_low = split2(later)
         across = jnp.concatenate([later_high, later_low], axis=1)
         ddriven = driven_ref[:, span] + tail * fold(dot(b_parts, jnp.concatenate([across, across], axis=0)))
-        toward_b.append(both_parts(tail * driven))
-        laters.append(stacked(later_high, later_low))
-        toward_c.append(both_parts(jnp.exp(cum_part) * dmix))
-        helds.append(stacked(*split2(held)))
         skip_sum[:, span] = skip_sum[:, span] + by_eights(dmix * conv)
         levels.append(both_parts(dmix * (mixed_ref[:, span] - skip * conv) - driven * ddriven))
         throughs.append(both_parts(ddriven * conv))
@@ -676,13 +730,9 @@
         edge_rows[:, span] = dvalue[-2 * EDGE :]
 
     side = lambda parts: jnp.concatenate(parts, axis=1)
-    grad_b = dot(side(toward_b), side(laters), NT)
-    grad_c = dot(side(toward_c), side(helds), NT)
     picks = jnp.concatenate([heads_t[span] for span in spans(width) for _ in range(2)], axis=0)
     reduced = dot(jnp.concatenate([side(levels), side(throughs), side(boundaries)], axis=0), picks)
     level, through, boundary = reduced[:size], reduced[size : 2 * size], reduced[2 * size :]
-    grad_rows_out[:, :LANES] = drows_ref[:, :LANES] + fold(grad_b)
-    grad_rows_out[:, LANES:] = drows_ref[:, LANES:] + fold(grad_c)
     boundary = jnp.sum(boundary, axis=0, keepdims=True)
     upper = (iota((size, size), 1) >= iota((size, size), 0)).astype(f32).astype(bf16)
     ddecay = exact_dot(upper, level, NN) + boundary
@@ -699,9 +749,7 @@
     @pl.when(final)
     def _():
         first = pre_next[...]
-        first_out[:, :width] = first
-        first_out[:, width : width + 2 * LANES] = grad_rows_out[:EDGE]
-        first_out[:, width + 2 * LANES :] = spre_ref[...]
+        first_out[...] = first
         ahead = jnp.concatenate([jnp.zeros((EDGE, width), f32), first], axis=0)
         halo = vhalo_ref[...].astype(f32)[-EDGE:]
         kernel_out[...] = jnp.zeros(kernel_out.shape, f32)
@@ -713,45 +761,46 @@
         small_out[0:1] = jnp.sum(summed, axis=0, keepdims=True)
 
 
-def finish(grad_driven, grad_rows, grad_mixed, mixed, pre, value_in, dt, cum, step_raw, state_rows, held, end_state, later,
-           messages, spre, vhalo, input_kernel, skip_gain, step_bias, decay_log):
+def finish(plan, count, wide_operands, grad_driven, grad_mixed, mixed, pre, value_in, dt, cum, step_raw, state_rows, held, end_state, later,
+           vhalo, input_kernel, skip_gain, step_bias, decay_log):
     tokens, inner = mixed.shape
     blocks, state, _ = held.shape
     head_count = skip_gain.shape[1]
-    state_block = pl.BlockSpec((1, state, inner), lambda b: (blocks - 1 - b, 0, 0))
-    wide = rows(BLOCK, inner, blocks)
-    narrow = rows(BLOCK, LANES, blocks)
-    return pl.pallas_call(
-        functools.partial(finish_kernel, len(messages)),
-        grid=(blocks,),
-        in_specs=[
-            wide, rows(BLOCK, 2 * state, blocks), wide, wide, wide, wide, narrow, narrow, narrow,
-            rows(BLOCK, 2 * state, blocks),
-            state_block, whole(end_state.shape), state_block,
-            *[whole(m.shape) for m in messages],
-            pl.BlockSpec((EDGE, 2 * state), lambda b: (0, 0)), whole(vhalo.shape), whole(input_kernel.shape), whole(skip_gain.shape), whole(step_bias.shape), whole(decay_log.shape),
-        ],
-        out_specs=[
-            wide,
-            rows(BLOCK, 2 * state, blocks),
-            rows(BLOCK, head_count, blocks),
-            whole((2 * EDGE, inner)),
-            whole((EDGE, inner + 4 * state)),
-            whole((EDGE, inner)),
-            whole((EDGE, LANES)),
-        ],
-        out_shape=[
-            jax.ShapeDtypeStruct((tokens, inner), bf16),
-            jax.ShapeDtypeStruct((tokens, 2 * state), f32),
-            jax.ShapeDtypeStruct((tokens, head_count), bf16),
-            jax.ShapeDtypeStruct((2 * EDGE, inner), f32),
-            jax.ShapeDtypeStruct((EDGE, inner + 4 * state), f32),
-            jax.ShapeDtypeStruct((EDGE, inner), f32),
-            jax.ShapeDtypeStruct((EDGE, LANES), f32),
-        ],
-        scratch_shapes=[
-            pltpu.VMEM((state, inner), f32),
-            pltpu.VMEM((EDGE, inner), f32),
+    width = wide_operands[0].shape[1]
+    tile = width // count
+    at = lambda b: jnp.maximum(blocks - 1 - b, 0)
+    by_rows = lambda cols: pl.BlockSpec((BLOCK, cols), lambda b, plan: (at(b), 0))
+    state_block = pl.BlockSpec((1, state, inner), lambda b, plan: (at(b), 0, 0))
+    moving = pl.BlockSpec((tokens, tile), lambda b, plan: (0, jnp.bitwise_xor(plan[1], jnp.maximum(b - blocks, 0))))
+    still = pl.BlockSpec((tokens, tile), lambda b, plan: (0, plan[0]))
+    wide, narrow = by_rows(inner), by_rows(LANES)
+    operands = (grad_driven, grad_mixed, mixed, pre, value_in, dt, cum, step_raw, state_rows, held, end_state, later,
+                vhalo, input_kernel, skip_gain, step_bias, decay_log)
+    outs = [
+        (wide, jax.ShapeDtypeStruct((tokens, inner), bf16)),
+        (by_rows(head_count), jax.ShapeDtypeStruct((tokens, head_count), bf16)),
+    ]
+    for shape in ((2 * EDGE, inner), (EDGE, inner), (EDGE, inner), (EDGE, LANES), *[(2 * tile, tile)] * 4):
+        outs.append((pl.BlockSpec(shape, lambda b, plan: (0, 0)), jax.ShapeDtypeStruct(shape, f32)))
+
+    def body(plan_ref, *refs):
+        b = pl.program_id(0)
+        ins, wide_ins, rest = refs[:17], refs[17:25], refs[25:]
+
+        @pl.when(b < blocks)
+        def _():
+            finish_kernel(blocks, *ins, *rest[:6], *rest[10:])
+
+        @pl.when(b >= blocks)
+        def _():
+            wide_weights_kernel(b - blocks, *wide_ins, *rest[6:10])
+
+    return scalar_call(
+        body, plan, (*operands, *wide_operands),
+        [wide, wide, wide, wide, wide, narrow, narrow, narrow, by_rows(2 * state), state_block, all_of(end_state), state_block,
+         *[all_of(a) for a in operands[12:]], moving, moving, still, still, still, still, moving, moving],
+        [o[0] for o in outs], [o[1] for o in outs], grid=(blocks + count,),
+        scratch=[
             pltpu.VMEM((state, inner), f32),
             pltpu.VMEM((EDGE, inner), f32),
             pltpu.VMEM((EDGE, inner), f32),
@@ -760,10 +809,8 @@
             pltpu.VMEM((inner, LANES), bf16),
             pltpu.VMEM((2 * EDGE, inner), f32),
         ],
-        compiler_params=params(56),
-        cost_estimate=cost(16),
-    )(grad_driven, grad_rows, grad_mixed, mixed, pre, value_in, dt, cum, step_raw, state_rows, held, end_state, later,
-      *messages, spre, vhalo, input_kernel, skip_gain, step_bias, decay_log)
+        limit=56, micros=0,
+    )
 
 
 def from_before(value, axis, by=1):
@@ -794,71 +841,93 @@
     return lax.dynamic_slice_in_dim(array, lax.axis_index(axis_name) * size, size, dim)
 
 
-def line_kernel(arrived, plan_ref, up_ref, down_ref, *refs):
-    up, down = up_ref[0], down_ref[0]
-    if arrived:
-        up = up + refs[0][...].astype(f32)
-        down = down + refs[1][...].astype(f32)
-    refs[-2][...] = up.astype(bf16)
-    refs[-1][...] = down.astype(bf16)
+def first_kernel(plan_ref, part_ref, out_ref):
+    out_ref[...] = part_ref[0].astype(bf16)
+
+
+def line_first(parts, axis):
+    count, tokens, width = parts.shape
+    plan = jnp.where(lax.axis_index(axis) == 0, count - 1, 0).astype(jnp.int32).reshape(1)
+    tile = min(tokens, 512)
+    sent = pl.pallas_call(
+        first_kernel,
+        grid_spec=pltpu.PrefetchScalarGridSpec(
+            num_scalar_prefetch=1,
+            grid=(tokens // tile,),
+            in_specs=[pl.BlockSpec((1, tile, width), lambda b, plan: (plan[0], b, 0))],
+            out_specs=pl.BlockSpec((tile, width), lambda b, plan: (b, 0)),
+        ),
+        out_shape=jax.ShapeDtypeStruct((tokens, width), bf16),
+        compiler_params=params(56),
+        cost_estimate=cost(0),
+    )(plan, parts)
+    return sent
 
 
 def line_step(parts, step, arrived, axis):
     count, tokens, width = parts.shape
     place = lax.axis_index(axis)
     plan = jnp.clip(jnp.stack([count - step + place, step - count + place]), 0, count - 1).astype(jnp.int32)
+    if step == 2:
+        arrived = [arrived, arrived]
+
+    def body(plan_ref, up_ref, down_ref, up_in, down_in, up_out, down_out):
+        up, down = up_in[...].astype(f32), down_in[...].astype(f32)
+        if step == 2:
+            up = jnp.where(plan_ref[2] == 1, up, 0.0)
+            down = jnp.where(plan_ref[2] == count - 2, down, 0.0)
+        up_out[...] = (up_ref[0] + up).astype(bf16)
+        down_out[...] = (down_ref[0] + down).astype(bf16)
+
     tile = min(tokens, 512)
     block = pl.BlockSpec((tile, width), lambda b, plan: (b, 0))
     up, down = pl.pallas_call(
-        functools.partial(line_kernel, len(arrived)),
+        body,
         grid_spec=pltpu.PrefetchScalarGridSpec(
             num_scalar_prefetch=1,
             grid=(tokens // tile,),
             in_specs=[
                 pl.BlockSpec((1, tile, width), lambda b, plan: (plan[0], b, 0)),
                 pl.BlockSpec((1, tile, width), lambda b, plan: (plan[1], b, 0)),
-                *[block for _ in arrived],
+                block,
+                block,
             ],
             out_specs=[block, block],
         ),
         out_shape=[jax.ShapeDtypeStruct((tokens, width), bf16)] * 2,
-        compiler_params=params(12),
-        cost_estimate=cost(2),
-    )(plan, parts, parts, *arrived)
+        compiler_params=params(56),
+        cost_estimate=cost(0),
+    )(jnp.concatenate([plan, place.astype(jnp.int32).reshape(1)]), parts, parts, *arrived)
     return (up, down), [
         lax.ppermute(up, axis, [(k, k + 1) for k in range(step)]),
         lax.ppermute(down, axis, [(count - 1 - k, count - 2 - k) for k in range(step)]),
     ]
 
 
-def input_kernel_body(pieces, gate_ref, value_ref, step_ref, last_ref, ahead_ref, taps_ref, x_ref, gain_ref, gate_w, value_w, step_w, *outs):
-    part_out, value_out, row_out, col_out, fixed_out = outs
+def input_kernel_body(
+    pieces, plan_ref, gate_ref, value_ref, narrow_ref, x_ref, gain_ref, gate_w, value_w, state_w, step_w, part_out, row_out, col_out, narrow_w
+):
     b = pl.program_id(0)
-    size, inner = value_ref.shape
+    size = value_ref.shape[0]
 
     @pl.when(b == 0)
     def _():
         col_out[...] = jnp.zeros(col_out.shape, f32)
-        fixed = last_ref[...]
-        taps = taps_ref[...].astype(f32)
-        extended = jnp.concatenate([jnp.zeros((2 * EDGE, inner), f32), ahead_ref[:, :inner]], axis=0)
-        for k in range(CONV):
-            fixed = fixed + taps[k : k + 1] * extended[CONV - 1 - k : CONV - 1 - k + 2 * EDGE]
-        fixed_out[...] = fixed.astype(bf16)
+        state2, steps = state_w.shape[1], step_w.shape[0]
+        mine = take_columns(plan_ref[0], pieces, state2)
+        beside = (iota((steps, LANES), 0) + state2 // pieces == iota((steps, LANES), 1)).astype(f32).astype(bf16)
+        narrow_w[...] = (dot(state_w[...], mine) + dot(step_w[...], beside, TN)).astype(bf16)
 
     gate = gate_ref[...]
     value = value_ref[...]
-    patched = jnp.concatenate([value[: size - 2 * EDGE], fixed_out[...]], axis=0)
-    value = jnp.where(b == pl.num_programs(0) - 1, patched, value)
-    value_out[...] = value
-    step = step_ref[...]
+    narrow = narrow_ref[...]
     x = x_ref[...].astype(f32)
     scaling = lax.rsqrt(jnp.mean(x * x, axis=-1, keepdims=True) + epsilon)
     part = x.shape[1] // pieces
     row = jnp.zeros((size, LANES), f32)
     for j in range(pieces):
         span = slice(j * part, (j + 1) * part)
-        partial = dot(gate, gate_w[span, :], NT) + dot(value, value_w[span, :], NT) + dot(step, step_w[:, span])
+        partial = dot(gate, gate_w[span, :], NT) + dot(value, value_w[span, :], NT) + dot(narrow, narrow_w[span, :], NT)
         part_out[j] = partial
         pulled = partial * x[:, span]
         gained = pulled * gain_ref[:, span]
@@ -866,45 +935,6 @@
             row = row + gained[:, inside]
         col_out[:, span] = col_out[:, span] + by_eights(pulled * scaling)
     row_out[...] = exact_dot(jnp.ones((EDGE, LANES), bf16), row, NT)
-
-
-def input_partials(pieces, grad_gate, grad_value, grad_step, last_rows, ahead, input_kernel, residual, pre_gain, gate_weight, input_weight, step_weight):
-    tokens, width = residual.shape
-    inner = grad_gate.shape[1]
-    part = width // pieces
-    tile = min(tokens, 256)
-    return pl.pallas_call(
-        functools.partial(input_kernel_body, pieces),
-        grid=(tokens // tile,),
-        in_specs=[
-            rows(tile, inner),
-            rows(tile, inner),
-            rows(tile, grad_step.shape[1]),
-            whole(last_rows.shape),
-            whole(ahead.shape),
-            whole(input_kernel.shape),
-            rows(tile, width),
-            whole(pre_gain.shape),
-            whole(gate_weight.shape),
-            whole(input_weight.shape),
-            whole(step_weight.shape),
-        ],
-        out_specs=[
-            pl.BlockSpec((pieces, tile, part), lambda b: (0, b, 0)),
-            rows(tile, inner),
-            pl.BlockSpec((EDGE, tile), lambda b: (0, b)),
-            whole((EDGE, width)),
-        ],
-        out_shape=[
-            jax.ShapeDtypeStruct((pieces, tokens, part), f32),
-            jax.ShapeDtypeStruct((tokens, inner), bf16),
-            jax.ShapeDtypeStruct((EDGE, tokens), f32),
-            jax.ShapeDtypeStruct((EDGE, width), f32),
-        ],
-        scratch_shapes=[pltpu.VMEM((2 * EDGE, inner), bf16)],
-        compiler_params=params(28),
-        cost_estimate=cost(9),
-    )(grad_gate, grad_value, grad_step, last_rows, ahead, input_kernel, residual, pre_gain, gate_weight, input_weight, step_weight)
 
 
 def scalar_call(body, plan, operands, in_specs, out_specs, out_shape, grid=(1,), scratch=(), limit=16, micros=2):
@@ -923,25 +953,67 @@
     return pl.BlockSpec(a.shape, lambda *_: (0,) * len(a.shape))
 
 
+def take_columns(at, count, width):
+    part = width // count
+    lane = iota((width, LANES), 1)
+    return ((iota((width, LANES), 0) == lane + at * part) & (lane < part)).astype(f32).astype(bf16)
+
+
+def extended_rows(x, beyond):
+    return jnp.concatenate([x, beyond, jnp.zeros((EDGE, x.shape[1]), f32)], axis=0)
+
+
 def pieces_kernel(count, plan_ref, rows_ref, ahead_ref, *outs):
     tokens, state2 = rows_ref.shape
-    part = tokens // count
-    first = ahead_ref.shape[1] - 2 * state2
+    extended = extended_rows(rows_ref[...], ahead_ref[:, :state2])
+    size = extended.shape[0] // 2
+    picks = [take_columns(lax.rem(plan_ref[0] + k, count), count, state2) for k in range(count)]
+    none = jnp.zeros((state2, LANES // 2), bf16)
+    half = LANES // 2
+    upper = jnp.concatenate([jnp.concatenate([p[:, :half], none], axis=1) for p in picks], axis=1)
+    lower = jnp.concatenate([jnp.concatenate([none, p[:, :half]], axis=1) for p in picks], axis=1)
+    both = dot_exact(extended[:size], upper) + dot_exact(extended[size:], lower)
     for k, out in enumerate(outs):
-        at = lax.rem(plan_ref[0] + k, count)
-        start = pl.multiple_of(at * part, EDGE)
-        out[:part] = rows_ref[pl.ds(start, part)]
-        beyond = pl.multiple_of(jnp.minimum(start + part, tokens - EDGE), EDGE)
-        out[part:] = jnp.where(at == count - 1, ahead_ref[:, first : first + state2], rows_ref[pl.ds(beyond, EDGE)])
+        out[...] = both[:, k * LANES : (k + 1) * LANES]
+
+
+def dot_exact(x, ones):
+    high, middle, low = split3(x)
+    return dot(high, ones) + (dot(middle, ones) + dot(low, ones))
 
 
 def pieces_of(place, count, grad_rows, ahead):
     tokens, state2 = grad_rows.shape
-    shape = jax.ShapeDtypeStruct((tokens // count + EDGE, state2), f32)
+    shape = jax.ShapeDtypeStruct((tokens // 2 + EDGE, LANES), f32)
     return scalar_call(
         functools.partial(pieces_kernel, count), place, (grad_rows, ahead), [all_of(grad_rows), all_of(ahead)],
-        [all_of(shape)] * count, [shape] * count, limit=8, micros=1,
-    )
+        [all_of(shape)] * count, [shape] * count, limit=12, micros=0,
+    )
+
+
+def complete_kernel(ahead_ref, last_ref, taps_ref, value_ref, out_ref):
+    fixed = last_ref[...]
+    taps = taps_ref[...].astype(f32)
+    extended = jnp.concatenate([jnp.zeros(last_ref.shape, f32), ahead_ref[...]], axis=0)
+    for k in range(CONV):
+        fixed = fixed + taps[k : k + 1] * extended[CONV - 1 - k : CONV - 1 - k + last_ref.shape[0]]
+    out_ref[...] = fixed.astype(bf16)
+
+
+def complete(ahead, last_rows, taps, grad_value):
+    tokens, inner = grad_value.shape
+    size = last_rows.shape[0]
+    final_rows = pl.BlockSpec((size, inner), lambda b: (tokens // size - 1, 0))
+    return pl.pallas_call(
+        complete_kernel,
+        grid=(1,),
+        in_specs=[whole(ahead.shape), whole(last_rows.shape), whole(taps.shape), final_rows],
+        out_specs=final_rows,
+        out_shape=jax.ShapeDtypeStruct(grad_value.shape, bf16),
+        input_output_aliases={3: 0},
+        compiler_params=params(4),
+        cost_estimate=cost(0),
+    )(ahead, last_rows, taps, grad_value)
 
 
 def three_parts(x):
@@ -955,152 +1027,156 @@
 
 
 PACK = 16
+SMALL = 48
 
 
 def state_kernel_body(count, plan_ref, *refs):
     grads = refs[:count]
-    spre_ref, input_ref, halo_ref, ahead_ref, taps_ref, w_ref, x_ref, gain_ref, row_ref, col_ref, out_ref, inputs = refs[count:]
+    spre_ref, input_ref, halo_ref, ahead_ref, taps_ref, step_ref, out_ref, taps_out = refs[count:]
     tokens, state2 = spre_ref.shape
-    part = tokens // count
-    at = plan_ref[0]
-    start = pl.multiple_of(at * part, 2 * EDGE)
+    part = state2 // count
+    pick = take_columns(plan_ref[0], count, state2)
     total = grads[0][...]
     for ref in grads[1:]:
         total = total + ref[...]
-    beyond = pl.multiple_of(jnp.minimum(start + part, tokens - EDGE), EDGE)
-    after_rows = jnp.where(at == count - 1, ahead_ref[:, ahead_ref.shape[1] - state2 :], spre_ref[pl.ds(beyond, EDGE)])
-    pre = jnp.concatenate([spre_ref[pl.ds(start, part)], after_rows], axis=0)
+    total = jnp.concatenate([total, pltpu.roll(total, LANES // 2, 1)], axis=0)
+    total = jnp.where(iota(total.shape, 1) < part, total, 0.0)
+    pre = dot_exact(extended_rows(spre_ref[...], ahead_ref[:, state2:]), pick)
     s = sig(pre)
     through = total * (s * (1.0 + pre * (1.0 - s)))
-    taps = taps_ref[...].astype(f32)
-    before = pl.multiple_of(jnp.maximum(start - 2 * EDGE, 0), 2 * EDGE)
-    inputs[: 2 * EDGE] = jnp.where(at == 0, halo_ref[...].astype(f32), input_ref[pl.ds(before, 2 * EDGE)].astype(f32))
-    inputs[2 * EDGE :] = input_ref[pl.ds(start, part)].astype(f32)
-    grad = jnp.zeros((part, state2), f32)
-    own = through[:part]
-    first = 2 * EDGE - CONV + 1
-    tap_rows = []
+    taps = dot(taps_ref[...], pick)
+    inputs = dot(jnp.concatenate([halo_ref[...], input_ref[...]], axis=0), pick)
+    steps = step_ref.shape[1]
+    place = (iota((steps, LANES), 0) + part == iota((steps, LANES), 1)).astype(f32).astype(bf16)
+    grad = dot(step_ref[...], place)
+    own = through[:tokens]
+    first = halo_ref.shape[0] - CONV + 1
+    taps_out[...] = jnp.zeros(taps_out.shape, f32)
     for k in range(CONV):
-        grad = grad + taps[k : k + 1] * through[CONV - 1 - k : CONV - 1 - k + part]
-        tap_rows.append(jnp.sum(own * inputs[first + k : first + k + part], axis=0, keepdims=True))
-    rounded = grad.astype(bf16)
-    out_ref[:part] = rounded
-    x = x_ref[...].astype(f32)
-    width = x.shape[1]
-    scaling = lax.rsqrt(jnp.mean(x * x, axis=-1, keepdims=True) + epsilon)
-    row = jnp.zeros((part, LANES), f32)
-    cols = []
-    for span in spans(width):
-        pulled = dot(rounded, w_ref[span, :], NT) * x[:, span]
-        row = row + pulled * gain_ref[:, span]
-        cols.append(jnp.sum(by_eights(pulled * scaling) + col_ref[:, span], axis=0, keepdims=True))
-    row = exact_dot(jnp.ones((EDGE, LANES), bf16), row, NT)[:1]
-    packed = [row_ref[:1, j * part : (j + 1) * part] + jnp.where(at == j, row, 0.0) for j in range(count)]
-    wide = state2 // LANES
-    packed += [jnp.concatenate(cols[i : i + wide], axis=1) for i in range(0, len(cols), wide)]
-    packed += tap_rows
-    packed.append(jnp.zeros((PACK - len(packed), state2), f32))
-    out_ref[part:] = three_parts(jnp.concatenate(packed, axis=0))
-
-
-def state_back(place, grads, spre, state_in, halo, ahead, taps, weight, residual, pre_gain, row_sums, col_sums):
+        grad = grad + taps[k : k + 1] * through[CONV - 1 - k : CONV - 1 - k + tokens]
+        taps_out[k : k + 1] = jnp.sum(own * inputs[first + k : first + k + tokens], axis=0, keepdims=True)
+    out_ref[...] = grad.astype(bf16)
+
+
+def state_back(place, grads, spre, state_in, halo, ahead, taps, grad_step):
     count = len(grads)
-    tokens, state2 = spre.shape
-    part = tokens // count
-    shape = jax.ShapeDtypeStruct((part + 3 * PACK, state2), bf16)
-    operands = (*grads, spre, state_in, halo, ahead, taps, weight, residual, pre_gain, row_sums, col_sums)
-    in_specs = [all_of(a) for a in operands]
-    in_specs[count + 6] = pl.BlockSpec((part, residual.shape[1]), lambda b, plan: (plan[0], 0))
+    tokens = spre.shape[0]
+    shapes = [jax.ShapeDtypeStruct((tokens, LANES), bf16), jax.ShapeDtypeStruct((EDGE, LANES), f32)]
+    operands = (*grads, spre, state_in, halo, ahead, taps, grad_step)
     return scalar_call(
-        functools.partial(state_kernel_body, count), place, operands, in_specs, all_of(shape), shape,
-        scratch=[pltpu.VMEM((part + 2 * EDGE, state2), f32)], limit=16, micros=3,
-    )
-
-
-SMALL = 48
-
-
-def narrow_kernel(count, plan_ref, *refs):
-    messages = refs[:count]
-    step_ref, kernel_ref, gain_ref, small_ref, out_ref, row_out = refs[count:]
-    tokens, steps = step_ref.shape
-    part = tokens // count
-    state2 = messages[0].shape[1]
-    mine = state2 // count
-    me = plan_ref[0]
-    pick = ((iota((state2, LANES), 0) == iota((state2, LANES), 1) + me * mine) & (iota((state2, LANES), 1) < mine)).astype(f32).astype(bf16)
-    place = (iota((steps, LANES), 0) + mine == iota((steps, LANES), 1)).astype(f32).astype(bf16)
-    sums = jnp.zeros((PACK, state2), f32)
-    for k in range(count):
-        start = pl.multiple_of(lax.rem(me - k + count, count) * part, 2 * EDGE)
-        both = dot(messages[k][:part], pick) + dot(step_ref[pl.ds(start, part)], place)
-        out_ref[pl.ds(start, part)] = both.astype(bf16)
-        sums = sums + three_sum(messages[k][part:])
-    row_out[...] = sums
+        functools.partial(state_kernel_body, count), place, operands, [all_of(a) for a in operands],
+        [all_of(a) for a in shapes], shapes, limit=16, micros=0,
+    )
+
+
+def sums_kernel(count, plan_ref, row_ref, col_ref, taps_ref, out_ref):
+    state2 = out_ref.shape[1]
+    tokens, width = row_ref.shape[1], col_ref.shape[1]
+    packed = [row_ref[:1, i : i + state2] for i in range(0, tokens, state2)]
+    col = jnp.sum(col_ref[...], axis=0, keepdims=True)
+    packed += [col[:, i : i + state2] for i in range(0, width, state2)]
+    high, middle, low = split3(taps_ref[:CONV])
+    pick = take_columns(plan_ref[0], count, state2)
+    packed.append(dot(high, pick, NT) + (dot(middle, pick, NT) + dot(low, pick, NT)))
+    packed = jnp.concatenate(packed, axis=0)
+    out_ref[...] = jnp.concatenate([packed, jnp.zeros((PACK - packed.shape[0], state2), f32)], axis=0)
+
+
+def sums_of(place, count, row_sums, col_sums, taps_grad, state2):
+    shape = jax.ShapeDtypeStruct((PACK, state2), f32)
+    operands = (row_sums, col_sums, taps_grad)
+    return scalar_call(
+        functools.partial(sums_kernel, count), place, operands, [all_of(a) for a in operands], all_of(shape), shape,
+        limit=8, micros=0,
+    )
+
+
+def small_kernel(count, tokens, plan_ref, *refs):
+    parts, (kernel_ref, gain_ref, small_ref, sums_out, out_ref) = refs[:count], refs[count:]
+    sums = parts[0][...]
+    for ref in parts[1:]:
+        sums = sums + ref[...]
+    sums_out[...] = sums
+    state2 = sums.shape[1]
     wide = state2 // LANES
     inner = kernel_ref.shape[1]
     rows_of = [kernel_ref[k : k + 1, span] for k in range(CONV) for span in spans(inner)]
     gain = jnp.sum(gain_ref[...], axis=0, keepdims=True)
     rows_of += [gain[:, span] for span in spans(inner)]
     rows_of += [small_ref[i : i + 1] for i in range(3)]
-    cols = [sums[count + r : count + r + 1, i * LANES : (i + 1) * LANES] for r in range(PACK - count - CONV) for i in range(wide)]
-    quarter = (PACK - count - CONV - 2) * wide // count
+    first = tokens // state2
+    last = PACK - 2 - CONV
+    cols = [sums[r : r + 1, i * LANES : (i + 1) * LANES] for r in range(first, last) for i in range(wide)]
+    quarter = len(cols) // count
     for i in range(quarter):
         chosen = jnp.zeros((1, LANES), f32)
         for q in range(count):
-            chosen = jnp.where(me == q, cols[q * quarter + i], chosen)
+            chosen = jnp.where(plan_ref[0] == q, cols[q * quarter + i], chosen)
         rows_of.append(chosen)
-    first = count + (PACK - count - CONV - 2)
-    rows_of += [sums[first + k : first + k + 1, i * LANES : (i + 1) * LANES] for k in range(CONV) for i in range(wide)]
+    rows_of += [sums[last + k : last + k + 1, i * LANES : (i + 1) * LANES] for k in range(CONV) for i in range(wide)]
     rows_of.append(jnp.zeros((SMALL - len(rows_of), LANES), f32))
-    out_ref[tokens:] = three_parts(jnp.concatenate(rows_of, axis=0))
-
-
-def narrow_of(place, messages, grad_step, kernel_grad, gain_grad, small):
-    count = len(messages)
-    tokens = grad_step.shape[0]
-    shapes = [jax.ShapeDtypeStruct((tokens + 3 * SMALL, LANES), bf16), jax.ShapeDtypeStruct((PACK, messages[0].shape[1]), f32)]
-    operands = (*messages, grad_step, kernel_grad, gain_grad, small)
+    out_ref[...] = jnp.concatenate(rows_of, axis=0)
+
+
+def small_sums(place, tokens, parts, kernel_grad, gain_grad, small):
+    shapes = [jax.ShapeDtypeStruct(parts[0].shape, f32), jax.ShapeDtypeStruct((SMALL, LANES), f32)]
+    operands = (*parts, kernel_grad, gain_grad, small)
     return scalar_call(
-        functools.partial(narrow_kernel, count), place, operands, [all_of(a) for a in operands],
-        [all_of(a) for a in shapes], shapes, limit=8, micros=2,
-    )
-
-
-def wide_weights_kernel(plan_ref, normed_a, normed_b, gate_a, gate_b, out_a, out_b, cot_a, cot_b, *outs):
-    k = pl.program_id(0)
+        functools.partial(small_kernel, len(parts), tokens), place, operands, [all_of(a) for a in operands],
+        [all_of(a) for a in shapes], shapes, limit=8, micros=0,
+    )
+
+
+def wide_weights_kernel(k, normed_a, normed_b, gate_a, gate_b, out_a, out_b, cot_a, cot_b, *outs):
     tile = normed_a.shape[1]
+    gate_keep, gate_send, out_keep, out_send = outs
     gate = dot(normed_a[...], gate_a[...], TN) + dot(normed_b[...], gate_b[...], TN)
     out = dot(out_a[...], cot_a[...], TN) + dot(out_b[...], cot_b[...], TN)
-    for i, ref in enumerate(outs):
+    targets = ((gate_keep, 0, out_keep, 0), (gate_send, 0, out_keep, 1), (gate_keep, 1, out_send, 0), (gate_send, 1, out_send, 1))
+    for i, (gate_ref, gate_at, out_ref, out_at) in enumerate(targets):
 
         @pl.when(k == i)
-        def _(ref=ref):
-            ref[:tile] = gate
-            ref[tile:] = out
-
-
-def wide_weights(plan, count, normed, grad_gate, normed_out, cotangent):
-    tokens, width = normed[0].shape
-    tile = width // count
-    moving = pl.BlockSpec((tokens, tile), lambda k, plan: (0, jnp.bitwise_xor(plan[1], k)))
-    still = pl.BlockSpec((tokens, tile), lambda k, plan: (0, plan[0]))
-    shape = jax.ShapeDtypeStruct((2 * tile, tile), f32)
+        def _(gate_ref=gate_ref, gate_at=gate_at, out_ref=out_ref, out_at=out_at):
+            gate_ref[gate_at * tile : (gate_at + 1) * tile] = gate
+            out_ref[out_at * tile : (out_at + 1) * tile] = out
+
+
+def value_weights_kernel(k, normed_a, normed_b, value_a, value_b, first_keep, first_send, second_keep, second_send):
+    total = dot(normed_a[...], value_a[...], TN) + dot(normed_b[...], value_b[...], TN)
+    half = total.shape[0] // 2
+    targets = ((first_keep, 0, second_keep, 0), (first_send, 0, second_keep, 1), (first_keep, 1, second_send, 0), (first_send, 1, second_send, 1))
+    for i, (first_ref, first_at, second_ref, second_at) in enumerate(targets):
+
+        @pl.when(k == i)
+        def _(first_ref=first_ref, first_at=first_at, second_ref=second_ref, second_at=second_at):
+            first_ref[first_at * half : (first_at + 1) * half] = total[:half]
+            second_ref[second_at * half : (second_at + 1) * half] = total[half:]
+
+
+def input_partials(place, pieces, grad_gate, grad_value, narrow, residual, pre_gain, gate_weight, input_weight, state_weight, step_weight):
+    tokens, width = residual.shape
+    inner = grad_gate.shape[1]
+    tile = min(tokens, 256)
+    by_rows = lambda cols: pl.BlockSpec((tile, cols), lambda b, plan: (b, 0))
     return scalar_call(
-        wide_weights_kernel, plan, (*normed, *grad_gate, *normed_out, *cotangent),
-        [moving, moving, still, still, still, still, moving, moving],
-        [all_of(shape)] * count, [shape] * count, grid=(count,), limit=28, micros=8,
-    )
-
-
-def value_weights_kernel(plan_ref, normed_a, normed_b, value_a, value_b, *outs):
-    k = pl.program_id(0)
-    total = dot(normed_a[...], value_a[...], TN) + dot(normed_b[...], value_b[...], TN)
-    for i, ref in enumerate(outs):
-
-        @pl.when(k == i)
-        def _(ref=ref):
-            ref[...] = total
+        functools.partial(input_kernel_body, pieces), place,
+        (grad_gate, grad_value, narrow, residual, pre_gain, gate_weight, input_weight, state_weight, step_weight),
+        [
+            by_rows(inner), by_rows(inner), by_rows(narrow.shape[1]), by_rows(width),
+            *[all_of(a) for a in (pre_gain, gate_weight, input_weight, state_weight, step_weight)],
+        ],
+        [
+            pl.BlockSpec((pieces, tile, width // pieces), lambda b, plan: (0, b, 0)),
+            pl.BlockSpec((EDGE, tile), lambda b, plan: (0, b)),
+            pl.BlockSpec((EDGE, width), lambda b, plan: (0, 0)),
+        ],
+        [
+            jax.ShapeDtypeStruct((pieces, tokens, width // pieces), f32),
+            jax.ShapeDtypeStruct((EDGE, tokens), f32),
+            jax.ShapeDtypeStruct((EDGE, width), f32),
+        ],
+        grid=(tokens // tile,), scratch=[pltpu.VMEM((width, LANES), bf16)], limit=56, micros=0,
+    )
 
 
 def value_weights(plan, count, normed, grad_value):
@@ -1110,17 +1186,21 @@
     moving = pl.BlockSpec((tokens, tile), lambda k, plan: (0, jnp.bitwise_xor(plan[1], k)))
     still = pl.BlockSpec((tokens, half), lambda k, plan: (0, plan[0]))
     shape = jax.ShapeDtypeStruct((tile, half), f32)
+
+    def body(plan_ref, *refs):
+        value_weights_kernel(pl.program_id(0), *refs)
+
     return scalar_call(
-        value_weights_kernel, plan, (*normed, *grad_value), [moving, moving, still, still],
-        [all_of(shape)] * count, [shape] * count, grid=(count,), limit=20, micros=5,
-    )
-
-
-def narrow_weights_kernel(plan_ref, normed_a, normed_b, narrow_a, narrow_b, *outs):
+        body, plan, (*normed, *grad_value), [moving, moving, still, still],
+        [all_of(shape)] * 4, [shape] * 4, grid=(count,), limit=56, micros=0,
+    )
+
+
+def narrow_weights_kernel(plan_ref, normed_a, normed_b, narrow_a, narrow_b, small_a, small_b, *outs):
     k = pl.program_id(0)
     tokens, tile = normed_a.shape
-    total = dot(narrow_a[:tokens], normed_a[...], TN) + dot(narrow_b[:tokens], normed_b[...], TN)
-    small = three_sum(narrow_a[tokens:]) + three_sum(narrow_b[tokens:])
+    total = dot(narrow_a[...], normed_a[...], TN) + dot(narrow_b[...], normed_b[...], TN)
+    small = small_a[...] + small_b[...]
     per_row = tile // LANES
     for i, ref in enumerate(outs):
 
@@ -1131,14 +1211,14 @@
                 ref[LANES:, j * LANES : (j + 1) * LANES] = small[j * SMALL // per_row : (j + 1) * SMALL // per_row]
 
 
-def narrow_weights(plan, count, normed, narrow):
+def narrow_weights(plan, count, normed, narrow, small):
     tokens, width = normed[0].shape
     tile = width // count
     moving = pl.BlockSpec((tokens, tile), lambda k, plan: (0, jnp.bitwise_xor(plan[1], k)))
     shape = jax.ShapeDtypeStruct((LANES + SMALL * LANES // tile, tile), f32)
     return scalar_call(
-        narrow_weights_kernel, plan, (*normed, *narrow), [moving, moving, all_of(narrow[0]), all_of(narrow[1])],
-        [all_of(shape)] * count, [shape] * count, grid=(count,), limit=16, micros=4,
+        narrow_weights_kernel, plan, (*normed, *narrow, *small), [moving, moving, *[all_of(a) for a in (*narrow, *small)]],
+        [all_of(shape)] * count, [shape] * count, grid=(count,), limit=16, micros=0,
     )
 
 
@@ -1155,13 +1235,16 @@
         functools.partial(sum_kernel, len(arrays)),
         out_shape=shape,
         compiler_params=pltpu.CompilerParams(vmem_limit_bytes=16 * 1024 * 1024),
-        cost_estimate=cost(2),
+        cost_estimate=cost(0),
     )(*arrays)
 
 
 def over_ctx(arrays, wait=()):
     arrived = [swapped(a, "ctx", k) for k, a in enumerate(arrays) if k]
-    total = sum_of([arrays[0], *after(wait, arrived)], f32)
+    return over_dp(sum_of([arrays[0], *after(wait, arrived)], f32))
+
+
+def over_dp(total):
     step = 2
     while step < lax.axis_size("dp"):
         total = total + swapped(total, "dp", step)
@@ -1169,8 +1252,44 @@
     return total
 
 
-def gather_chunks(chunk):
-    return jnp.concatenate([chunk, *[swapped(chunk, "ctx", k) for k in range(1, lax.axis_size("ctx"))]], axis=0)
+def halves_kernel(own_a, own_b, got_a, got_b, stay_out, away_a, away_b):
+    half = away_a.shape[0]
+    stay_out[:half] = own_a[:half] + got_a[:half]
+    stay_out[half:] = own_b[:half] + got_b[:half]
+    away_a[...] = own_a[half:] + got_a[half:]
+    away_b[...] = own_b[half:] + got_b[half:]
+
+
+def halves(own_a, own_b, got_a, got_b):
+    size, cols = own_a.shape
+    half = jax.ShapeDtypeStruct((size // 2, cols), f32)
+    return pl.pallas_call(
+        halves_kernel,
+        out_shape=[jax.ShapeDtypeStruct((size, cols), f32), half, half],
+        compiler_params=pltpu.CompilerParams(vmem_limit_bytes=16 * 1024 * 1024),
+        cost_estimate=cost(0),
+    )(own_a, own_b, got_a, got_b)
+
+
+def add_kernel(stay, got_a, got_b, out):
+    half = got_a.shape[0]
+    out[:half] = (stay[:half] + got_a[...]).astype(out.dtype)
+    out[half:] = (stay[half:] + got_b[...]).astype(out.dtype)
+
+
+def add_halves(stay, got_a, got_b, dtype):
+    return pl.pallas_call(
+        add_kernel,
+        out_shape=jax.ShapeDtypeStruct(stay.shape, dtype),
+        compiler_params=pltpu.CompilerParams(vmem_limit_bytes=16 * 1024 * 1024),
+        cost_estimate=cost(0),
+    )(stay, got_a, got_b)
+
+
+def summed(stay, got_a, got_b):
+    if lax.axis_size("dp") == 2:
+        return add_halves(stay, got_a, got_b, bf16)
+    return over_dp(add_halves(stay, got_a, got_b, f32)).astype(bf16)
 
 
 def ordered(first, here, there):
@@ -1180,7 +1299,7 @@
 
 def wide_together_kernel(plan_ref, here, there, gate_out, out_out):
     tile = gate_out.shape[0]
-    k = jnp.bitwise_xor(pl.program_id(0), plan_ref[1])
+    k = pl.program_id(0)
     first = plan_ref[0] == 0
     half = gate_out.shape[1] // 2
     span = pl.ds(pl.multiple_of(k * 2 * tile, 2 * EDGE), tile)
@@ -1196,7 +1315,7 @@
         wide_together_kernel, plan, (here, there), [all_of(here), all_of(there)],
         [pl.BlockSpec((tile, inner), lambda q, plan: (q, 0)), pl.BlockSpec((inner, tile), lambda q, plan: (0, q))],
         [jax.ShapeDtypeStruct((width, inner), f32), jax.ShapeDtypeStruct((inner, width), f32)],
-        grid=(count,), limit=24, micros=6,
+        grid=(count,), limit=24, micros=0,
     )
 
 
@@ -1225,19 +1344,13 @@
             jax.ShapeDtypeStruct((state_part, width), f32),
             jax.ShapeDtypeStruct((steps, width), f32),
         ],
-        grid=(count,), limit=20, micros=4,
-    )
-
-
-def final_kernel(count, plan_ref, part_ref, up_ref, down_ref, x_ref, mine_ref, cot_ref, gain_ref, w_ref, sums_ref, *refs):
-    messages, out_ref = refs[:count], refs[count]
+        grid=(count,), limit=20, micros=0,
+    )
+
+
+def final_kernel(count, plan_ref, part_ref, up_ref, down_ref, x_ref, mine_ref, cot_ref, gain_ref, sums_ref, out_ref):
     b = pl.program_id(0)
     size, part = up_ref.shape
-    k = lax.rem(plan_ref[0] - b + count, count)
-    state = messages[0][:size]
-    for i in range(1, count):
-        state = jnp.where(k == i, messages[i][:size], state)
-    normed_grad = part_ref[0] + up_ref[...].astype(f32) + down_ref[...].astype(f32) + dot(state, w_ref[...], NT)
     x = x_ref[...].astype(f32)
     width = x.shape[1]
     scaling = lax.rsqrt(jnp.mean(x * x, axis=-1, keepdims=True) + epsilon)
@@ -1246,34 +1359,33 @@
         row = jnp.where(b == q, sums_ref[q : q + 1], row)
     pull = column(row) * ((scaling * scaling * scaling) / width)
     for span in spans(part):
+        normed_grad = part_ref[0, :, span] + up_ref[:, span].astype(f32) + down_ref[:, span].astype(f32)
         out_ref[:, span] = (
-            cot_ref[:, span].astype(f32) + scaling * gain_ref[:, span] * normed_grad[:, span] - mine_ref[:, span].astype(f32) * pull
+            cot_ref[:, span].astype(f32) + scaling * gain_ref[:, span] * normed_grad - mine_ref[:, span].astype(f32) * pull
         )
 
 
-def final(place, parts, arrived, residual, cotangent, pre_gain, state_weight, sums, messages):
+def final(place, parts, arrived, residual, cotangent, pre_gain, sums):
     count, tokens, part = parts.shape
-    size = tokens // count
-    state2 = state_weight.shape[1]
+    size = sums.shape[1]
     mine = pl.BlockSpec((size, part), lambda b, plan: (b, plan[0]))
+    own = pl.BlockSpec((size, part), lambda b, plan: (b, 0))
     return scalar_call(
-        functools.partial(final_kernel, count), place,
-        (parts, *arrived, residual, residual, cotangent, pre_gain, state_weight, sums, *messages),
+        functools.partial(final_kernel, tokens // size), place,
+        (parts, *arrived, residual, residual, cotangent, pre_gain, sums),
         [
             pl.BlockSpec((1, size, part), lambda b, plan: (plan[0], b, 0)),
-            pl.BlockSpec((size, part), lambda b, plan: (b, 0)),
-            pl.BlockSpec((size, part), lambda b, plan: (b, 0)),
+            own,
+            own,
             pl.BlockSpec((size, residual.shape[1]), lambda b, plan: (b, 0)),
             mine,
             mine,
             pl.BlockSpec((1, part), lambda b, plan: (0, plan[0])),
-            pl.BlockSpec((part, state2), lambda b, plan: (plan[0], 0)),
             all_of(sums),
-            *[all_of(m) for m in messages],
-        ],
-        pl.BlockSpec((size, part), lambda b, plan: (b, 0)),
+        ],
+        own,
         jax.ShapeDtypeStruct((tokens, part), f32),
-        grid=(count,), limit=16, micros=4,
+        grid=(tokens // size,), limit=16, micros=0,
     )
 
 
@@ -1289,7 +1401,7 @@
     state2 = state_weight.shape[1]
     state_part = state2 // tensor_size
     row = lambda v: v.reshape(1, -1)
-    plan = jnp.stack([lax.axis_index("dp") % 2, lax.axis_index("ctx")]).astype(jnp.int32)
+    plan = jnp.stack([lax.axis_index("dp") % 2, lax.axis_index("ctx"), lax.axis_index("tensor")]).astype(jnp.int32)
     place = lax.axis_index("tensor").astype(jnp.int32).reshape(1)
 
     halo = from_before(residual[-2 * EDGE :], "ctx")
@@ -1304,11 +1416,11 @@
     messages = [from_before(message, "ctx", by) for by in range(1, ctx_size)]
     gate_in, grad_normed = beside(after(message, normed), gate_weight, cotangent, out_weight)
     intra = inner_forward(head_count, conv, dt, state_rows, cum, cumt, row(skip_gain))
-    messages = after((gate_in, intra), messages)
+    messages = after((gate_in, intra, other_cotangent), messages)
     mixed, sums, held, end_state = combine(
         intra, state_rows, cum, held, message, messages, gate_in, grad_normed, row(norm_gain)
     )
-    all_sums = [sums, *from_all(sums, "tensor")]
+    all_sums = [sums, *after(other_normed, from_all(sums, "tensor"))]
     normed_out, grad_gate, grad_mixed, later, message, gain_grad = gate_back(
         mixed, gate_in, grad_normed, state_rows, cum, row(norm_gain), all_sums, inner_total
     )
@@ -1321,56 +1433,64 @@
     branch = lax.psum_scatter(partial_out, "tensor", scatter_dimension=1, tiled=True)
     output = (resid_part + branch).astype(bf16)
 
-    wide = wide_weights(
-        after(partial_out, plan), ctx_size, (normed, other_normed), (grad_gate, other_gate), (normed_out, other_out),
-        (cotangent, other_cotangent)
-    )
-    grad_driven, grad_rows = inner_back(head_count, conv, dt, state_rows, cum, cumt, after(wide, grad_mixed))
+    grad_driven, grad_rows = inner_back(head_count, conv, dt, state_rows, cum, cumt, after(partial_out, grad_mixed))
     messages = after(grad_driven, messages)
-    grad_value, grad_rows, grad_step, last_rows, first_rows, kernel_grad, small = finish(
-        grad_driven, grad_rows, grad_mixed, mixed, pre, value_in, dt, cum, step_raw, state_rows, held, end_state, later,
-        messages, spre, vhalo, input_kernel, row(skip_gain), row(step_bias), row(decay_log)
-    )
+    grad_rows, later, first_rows = rows_back(grad_rows, grad_mixed, conv, dt, cum, state_rows, held, later, messages, spre)
     ahead = from_after(first_rows, "ctx")
-    wide_chunk = over_ctx(wide, first_rows).astype(bf16)
-    ahead = after(wide_chunk, ahead)
-
-    pieces = pieces_of(place, tensor_size, grad_rows, ahead)
+    pieces = list(pieces_of(place, tensor_size, grad_rows, ahead))
     arrived = [
         lax.ppermute(pieces[k], "tensor", [(i, (i + k) % tensor_size) for i in range(tensor_size)]) for k in range(1, tensor_size)
     ]
-    parts, grad_value, row_sums, col_sums = input_partials(
-        tensor_size, grad_gate, grad_value, grad_step, last_rows, ahead, input_kernel,
-        residual, row(pre_gain), gate_weight, input_weight, step_weight
-    )
+    (grad_value, grad_step, last_rows, first_rows, kernel_grad, small, gate_keep, gate_send, out_keep, out_send) = finish(
+        plan, ctx_size, (normed, other_normed, grad_gate, other_gate, normed_out, other_out, cotangent, other_cotangent),
+        grad_driven, after(pieces[0], grad_mixed), mixed, pre, value_in, dt, cum, step_raw, state_rows, held, end_state, later,
+        vhalo, input_kernel, row(skip_gain), row(step_bias), row(decay_log)
+    )
+    ahead_value = from_after(first_rows, "ctx")
+    arrived = after(first_rows, arrived)
+    narrow, taps_grad = state_back(place, [pieces[0], *arrived], spre, state_in, shalo, ahead, state_kernel, grad_step)
+    grad_value = complete(after(narrow, ahead_value), last_rows, input_kernel, grad_value)
     other_value = swapped(grad_value, "dp", 1)
-    sent, moving = line_step(parts, 1, [], "tensor")
-    wide_here = gather_chunks(wide_chunk)
-    weights = value_weights(after(sent, plan), ctx_size, (normed, other_normed), (grad_value, other_value))
-    arrived = after(weights, arrived)
-    state_message = state_back(
-        place, [pieces[0], *arrived], spre, state_in, shalo, ahead, state_kernel, state_weight, residual, row(pre_gain),
-        row_sums, col_sums
-    )
-    arrived = from_all(state_message, "tensor")
-    wide_there = swapped(wide_here, "dp", 1)
-    sent, moving = line_step(parts, 2, moving, "tensor")
-    state_messages = [state_message, *after(sent, arrived)]
-    narrow, sums = narrow_of(place, state_messages, grad_step, kernel_grad, gain_grad, small)
     other_narrow = swapped(narrow, "dp", 1)
-    value_chunk = over_ctx(weights, narrow)
-    weights = narrow_weights(plan, ctx_size, (normed, other_normed), (narrow, other_narrow))
-    gate_weight_grad, out_weight_grad = wide_together(plan, ctx_size, wide_here, wide_there)
-    narrow_total = over_ctx(weights, (gate_weight_grad, output))
-    sent, moving = line_step(parts, 3, moving, "tensor")
-    chunk = after(sent, jnp.concatenate([value_chunk, narrow_total[:LANES]], axis=0).astype(bf16))
-    arrived = [swapped(chunk, "ctx", k) for k in range(1, ctx_size)]
-    input_grad = final(place, parts, moving, residual, cotangent, row(pre_gain), state_weight, sums, state_messages)
-    narrow_here = jnp.concatenate([chunk, *after(input_grad, arrived)], axis=0)
+    gate_send, out_send = after(grad_value, (gate_send, out_send))
+    gate_got, out_got = swapped(gate_send, "ctx", 1), swapped(out_send, "ctx", 2)
+    parts, row_sums, col_sums = input_partials(
+        place, tensor_size, grad_gate, grad_value, narrow, residual, row(pre_gain), gate_weight, input_weight, state_weight,
+        step_weight
+    )
+    packed = sums_of(place, tensor_size, row_sums, col_sums, taps_grad, state2)
+    packed = [packed, *from_all(packed, "tensor")]
+    sent = line_first(parts, "tensor")
+    packed, sent = after(sent, packed), after(packed, sent)
+    moving = lax.ppermute(sent, "tensor", [(0, 1), (tensor_size - 1, tensor_size - 2)])
+    first_keep, first_send, second_keep, second_send = value_weights(
+        after(sent, plan), ctx_size, (normed, other_normed), (grad_value, other_value)
+    )
+    sums, small = small_sums(place, tokens, after(first_keep, packed), kernel_grad, gain_grad, small)
+    other_small = swapped(small, "dp", 1)
+    stay, gate_away, out_away = halves(gate_keep, out_keep, *after(small, (gate_got, out_got)))
+    gate_got, out_got = swapped(gate_away, "ctx", 2), swapped(out_away, "ctx", 1)
+    sent, moving = line_step(parts, 2, after(stay, moving), "tensor")
+    wide_chunk = summed(stay, *after(sent, (gate_got, out_got)))
+    first_send, second_send = after(wide_chunk, (first_send, second_send))
+    first_got, second_got = swapped(first_send, "ctx", 1), swapped(second_send, "ctx", 2)
+    wide_here = lax.all_gather(wide_chunk, "ctx", tiled=True)
+    weights = narrow_weights(after(small, plan), ctx_size, (normed, other_normed), (narrow, other_narrow), (small, other_small))
+    sent, moving = line_step(parts, 3, after(weights, moving), "tensor")
+    stay, first_away, second_away = halves(first_keep, second_keep, *after(sent, (first_got, second_got)))
+    first_got, second_got = swapped(first_away, "ctx", 2), swapped(second_away, "ctx", 1)
+    narrow_total = over_ctx(weights, stay)
+    value_chunk = summed(stay, *after((narrow_total, output), (first_got, second_got)))
+    chunk = jnp.concatenate([value_chunk, narrow_total[:LANES].astype(bf16)], axis=0)
+    chunks = [swapped(chunk, "ctx", k) for k in range(1, ctx_size)]
+    input_grad = final(place, parts, after(chunk, moving), residual, cotangent, row(pre_gain), sums)
+    narrow_here = jnp.concatenate([chunk, *after(input_grad, chunks)], axis=0)
     narrow_there = swapped(narrow_here, "dp", 1)
+    wide_there = swapped(after(narrow_here, wide_here), "dp", 1)
     input_weight_grad, state_weight_grad, step_weight_grad = narrow_together(
         plan, ctx_size, narrow_here, narrow_there, state_part, head_count
     )
+    gate_weight_grad, out_weight_grad = wide_together(after(input_weight_grad, plan), ctx_size, wide_here, wide_there)
     small_total = narrow_total[LANES:]
     small_total = jnp.concatenate([small_total[:, i : i + LANES] for i in range(0, small_total.shape[1], LANES)], axis=0)
     wide_rows = inner // LANES

time: 372 us -> 353 us (0.949)
  waiting for transfers between devices: 97.4 us -> 46 us
  starting transfers between devices: 67.1 us -> 83.4 us
  Pallas kernels: 131 us -> 145 us
  local copies, waits for them, and re-layouts: 46.9 us -> 52.4 us
  other arithmetic: 7.71 us -> 3.9 us
    ppermute x23, waiting for transfers between devices: 62 us -> 24.5 us  [swapped(): lax.ppermute(value, axis, [(i, i ^ flip) for i in range(lax.axis_size(axi...]
    pallas_call x9 -> x11, Pallas kernels: 42.3 us -> 73.4 us  [scalar_call(): pl.pallas_call(body, grid_spec=pltpu.PrefetchScalarGridSpec(num_scalar_pr...]
    ppermute x6, waiting for transfers between devices: 30.5 us -> 4.94 us  [from_all(): lax.ppermute(value, axis, [(i, (i + by) % count) for i in range(count)])]
    pallas_call x5 -> x9, Pallas kernels: 38.8 us -> 20.9 us  [the longest x2 8.21 us: line_step(): pl.pallas_call(body, grid_spec=pltpu.PrefetchScalarGridSpec(num_scalar_pr...]
    ppermute x6, starting transfers between devices: 11.2 us -> 25.1 us  [from_all(): lax.ppermute(value, axis, [(i, (i + by) % count) for i in range(count)])]
    ppermute x4 -> x5, waiting for transfers between devices: 0.01 us -> 12.1 us  [from_after(): return lax.ppermute(value, axis, [(i + by, i) for i in range(count - by)])]
    ppermute x0 -> x1, starting transfers between devices: none -> 7.94 us  [per_device(): lax.ppermute(sent, 'tensor', [(0, 1), (tensor_size - 1, tensor_size - 2)])]
    unnamed x177 -> x180, local copies, waits for them, and re-layouts: 40.3 us -> 46.6 us
  transfers between devices with their start and end apart: 47 -> 48, of which waited for: 18 -> 20; matrix products, arithmetic and copies ran while one was open for 4% -> 4% of each run, Pallas kernels for 29% -> 38%
where the time goes in v3:
time: 353 us; the launch traced here: 352 us
  Pallas kernels  145 us (41%)
  starting transfers between devices  83.4 us (24%)
  local copies, waits for them, and re-layouts  52.4 us (15%)
  waiting for transfers between devices  46 us (13%)
  between operations  16.4 us (5%)
  matrix products  4.61 us (1%)
  other arithmetic  3.9 us (1%)
    pallas_call x11, Pallas kernels, scalar_call(): pl.pallas_call(body, grid_spec=pltpu.PrefetchScalarGridSpec(num_scalar_pr...  73.4 us
    unnamed x180, local copies, waits for them, and re-layouts  46.6 us
    ppermute x6, starting transfers between devices, from_all(): lax.ppermute(value, axis, [(i, (i + by) % count) for i in range(count)])  25.1 us
    ppermute x23, waiting for transfers between devices, swapped(): lax.ppermute(value, axis, [(i, i ^ flip) for i in range(lax.axis_size(axi...  24.5 us
    ppermute x23, starting transfers between devices, swapped(): lax.ppermute(value, axis, [(i, i ^ flip) for i in range(lax.axis_size(axi...  18 us
    ppermute x4, starting transfers between devices, from_before(): return lax.ppermute(value, axis, [(i, i + by) for i in range(count - by)])  14 us
    ppermute x5, waiting for transfers between devices, from_after(): return lax.ppermute(value, axis, [(i + by, i) for i in range(count - by)])  12.1 us
    pallas_call x1, Pallas kernels, local_states(): pl.pallas_call(local_kernel, grid=(blocks,), in_specs=[rows(BLOCK, inner)...  9.84 us
  transfers between devices with their start and end apart: 48, of which 20 were waited for; matrix products, arithmetic and copies ran while one was open for 4% of the time, Pallas kernels for 38%

profile of v3, /device:TPU:0, one launch (start us, length us, event | category | flops | bytes accessed | tf_op | source)
XLA Modules:
  0.0 351.6 jit_solution(17542220212952132111)
XLA Ops:
  9.9 8.7 %shard_map.245 = (bf16[1024,1536]{1,0:T(8,128)(2,1)}, bf16[1024,768]{1,0:T(8,128)(2,1)}, bf16[1024,256]{1,0:T(8,128)(2,1)}, f32[1024,128]{1,0:T(8,128)}) custom-call(bf16[1024,1536]{1,0:T(8,128)(2,1)} %bitcast.35, f32[1,1536]{1,0:T(1,128)} %reshape.74.gain_ref, bf16[1536,768]{1,0:T(8,128)(2,1)} %value_w.3, bf16[1536,256]{1,0:T(8,128)(2,1)} %state_w.3, ...), custom_call_target="tpu_custom_call" | custom-call | flops 5400000000 | bytes 18000000 | tf_op jit(solution)/shard_map/pallas_call | solution.py:147
  19.5 4.8 %collective-permute-start = (bf16[16,1536]{1,0:T(8,128)(2,1)S(1)}, bf16[16,1536]{1,0:T(8,128)(2,1)S(1)}, u32[]{:S(2)}, u32[]{:S(2)}) collective-permute-start(bf16[16,1536]{1,0:T(8,128)(2,1)S(1)} %slice_bitcast_fusion), channel_id=1, source_target_pairs={{0,4},{4,8},{8,12},{1,5},{5,9},{9,13},{2,6},{6,10},{10,14},{3,7},{... | collective-permute-start | bytes 147464 | tf_op jit(solution)/shard_map/ppermute | solution.py:818
  24.4 1.7 collective-permute-done.halo_ref
  26.1 1.4 copy-done.39
  29.6 9.8 %shard_map.246 = (f32[1024,768]{1,0:T(8,128)S(1)}, f32[1024,768]{1,0:T(8,128)S(1)}, f32[1024,256]{1,0:T(8,128)S(1)}, f32[1024,256]{1,0:T(8,128)S(1)}, f32[1024,1...) custom-call(bf16[1024,768]{1,0:T(8,128)(2,1)S(1)} %copy-done.39, ...), custom_call_target="tpu_custom_call" | custom-call | flops 8999999488 | bytes 30000000 | tf_op jit(solution)/shard_map/pallas_call | solution.py:267
  40.5 1.6 copy-done.29
  42.1 4.4 %collective-permute-start.2 = (f32[136,768]{1,0:T(8,128)S(1)}, f32[136,768]{1,0:T(8,128)S(1)}, u32[]{:S(2)}, u32[]{:S(2)}) collective-permute-start(f32[136,768]{1,0:T(8,128)S(1)} %get-tuple-element.152.own_ref), channel_id=1, source_target_pairs={{0,4},{4,8},{8,12},{1,5},{5,9},{9,13},{2,6},{6,10},{10,14},{3,7},{... | collective-permute-start | bytes 1253384 | tf_op jit(solution)/shard_map/ppermute | solution.py:818
  46.5 3.4 collective-permute-start.3
  50.0 1.3 collective-permute-start.4
  51.3 5.7 %shard_map.248 = (f32[1024,768]{1,0:T(8,128)S(1)}, f32[1024,768]{1,0:T(8,128)S(1)}) custom-call(bf16[1024,1536]{1,0:T(8,128)(2,1)S(1)} %copy-done.2, bf16[1536,768]{1,0:T(8,128)(2,1)S(1)} %copy-done.38, bf16[1024,1536]{1,0:T(8,128)(2,1)S(1)} %bitcast.41, bf16[768,1536]{1,0:T(8,128)(2,1)S(1)} %copy-done.82), custom_call_target="tpu_custom_call" | custom-call | flops 5400000000 | bytes 18000000 | tf_op jit(solution)/shard_map/pallas_call | solution.py:179
  57.1 5.4 %shard_map.247.intra_ref = f32[1024,768]{1,0:T(8,128)S(1)} custom-call(f32[1024,768]{1,0:T(8,128)S(1)} %get-tuple-element.146.conv_ref, f32[1024,128]{1,0:T(8,128)S(1)} %get-tuple-element.147.dt_ref.refs_5_, f32[1024,256]{1,0:T(8,128)S(1)} %get-tuple-element.148.rows_ref.refs_8_, f32[1024,128]{1,0:T(8,128)S(1)} %get-tuple-element.149.cum_ref.refs_6_, ...), custom_call_target="tpu_custom_call" | custom-call | flops 5400000000 | bytes 18000000 | tf_op jit(solution)/shard_map/pallas_call | solution.py:347
  62.5 2.7 collective-permute-done.3.refs_1_
  65.2 4.8 %shard_map.249 = (f32[1024,768]{1,0:T(8,128)S(1)}, f32[8,1024]{1,0:T(8,128)S(1)}, f32[8,128,768]{2,1,0:T(8,128)S(1)}, f32[128,768]{1,0:T(8,128)S(1)}) custom-call(f32[1024,768]{1,0:T(8,128)S(1)} %shard_map.247.intra_ref, f32[1024,256]{1,0:T(8,128)S(1)} %get-tuple-element.148.rows_ref.refs_8_, f32[1024,128]{1,0:T(8,128)S(1)} %get-tuple-element.149.cum_ref.refs_6_, ...), custom_call_target="tpu_custom_call" | custom-call | flops 4499999744 | bytes 15000000 | tf_op jit(solution)/shard_map/pallas_call | solution.py:410
  70.0 1.7 copy-done.11
  71.7 1.6 collective-permute-start.6
  73.3 2.6 collective-permute-start.7
  75.8 1.3 collective-permute-start.8
  79.8 6.3 %shard_map.250 = (bf16[1024,768]{1,0:T(8,128)(2,1)S(1)}, bf16[1024,768]{1,0:T(8,128)(2,1)S(1)}, f32[1024,768]{1,0:T(8,128)S(1)}, f32[8,128,768]{2,1,0:T(8,128)S(...) custom-call(f32[1024,768]{1,0:T(8,128)S(1)} %get-tuple-element.160.mixed_ref.refs_2_, ...), custom_call_target="tpu_custom_call" | custom-call | flops 6300000256 | bytes 21000000 | tf_op jit(solution)/shard_map/pallas_call | solution.py:497
  87.3 1.7 copy-done.33
  90.8 4.6 %fusion.2 = f32[1024,1536]{1,0:T(8,128)} fusion(bf16[1024,768]{1,0:T(8,128)(2,1)S(1)} %get-tuple-element.167.refs_21_, bf16[768,1536]{1,0:T(8,128)(2,1)S(1)} %copy-done.82), kind=kOutput, calls=%fused_computation.22 | convolution fusion | flops 2415919104 | bytes 10223616 | tf_op jit(solution)/shard_map/dot_general | solution.py:25
  100.0 1.9 copy-done.14
  105.5 8.8 %shard_map.251 = (f32[1024,768]{1,0:T(8,128)S(1)}, f32[1024,256]{1,0:T(8,128)S(1)}) custom-call(f32[1024,768]{1,0:T(8,128)S(1)} %copy-done.14, f32[1024,128]{1,0:T(8,128)S(1)} %copy-done.21, f32[1024,256]{1,0:T(8,128)S(1)} %copy-done.17, f32[1024,128]{1,0:T(8,128)S(1)} %copy-done.24, f32[16,1024]{1,0:T(8,128)S(1)} %get-tuple-element.150.cumt_ref, ...), custom_call_target="tpu_custom_call" | custom-call | tf_op jit(solution)/shard_map/pallas_call | solution.py:573
  114.4 1.7 copy-done.31
  116.0 5.4 %collective-permute-done.10.refs_1_ = f32[136,768]{1,0:T(8,128)S(1)} collective-permute-done((f32[136,768]{1,0:T(8,128)}, f32[136,768]{1,0:T(8,128)S(1)}, u32[]{:S(2)}, u32[]{:S(2)}) %collective-permute-start.10) | collective-permute-done | bytes 417824 | tf_op jit(solution)/shard_map/ppermute | solution.py:823
  122.7 1.9 copy-done.34
  124.6 6.0 %shard_map.252 = (f32[1024,256]{1,0:T(8,128)S(1)}, f32[8,128,768]{2,1,0:T(8,128)S(1)}, f32[8,512]{1,0:T(8,128)S(1)}) custom-call(f32[1024,256]{1,0:T(8,128)S(1)} %get-tuple-element.171.drows_ref, f32[1024,768]{1,0:T(8,128)S(1)} %get-tuple-element.182.dmix_ref.refs_1_, f32[1024,768]{1,0:T(8,128)S(1)} %copy-done.15, f32[1024,128]{1,0:T(8,128)S(1)} %copy-done.22, ...), custom_call_target="tpu_custom_call" | custom-call | tf_op jit(solution)/shard_map/pallas_call | solution.py:650
  130.6 1.7 copy-done.32
  134.5 4.3 %collective-permute-done.12.ahead_ref.refs_7_ = f32[8,512]{1,0:T(8,128)S(1)} collective-permute-done((f32[8,512]{1,0:T(8,128)S(1)}, f32[8,512]{1,0:T(8,128)S(1)}, u32[]{:S(2)}, u32[]{:S(2)}) %collective-permute-start.12) | collective-permute-done | bytes 16416 | tf_op jit(solution)/shard_map/ppermute | solution.py:823
  141.4 3.6 %collective-permute-start.16 = (f32[520,128]{1,0:T(8,128)S(1)}, f32[520,128]{1,0:T(8,128)S(1)}, u32[]{:S(2)}, u32[]{:S(2)}) collective-permute-start(f32[520,128]{1,0:T(8,128)S(1)} %get-tuple-element.189), channel_id=1, source_target_pairs={{0,2},{1,3},{2,0},{3,1},{4,6},{5,7},{6,4},{7,5},{8,10},{9,11},{10,... | collective-permute-start | bytes 798728 | tf_op jit(solution)/shard_map/ppermute | solution.py:1442
  145.7 30.2 %shard_map.254 = (bf16[1024,768]{1,0:T(8,128)(2,1)}, bf16[1024,12]{1,0:T(8,128)(2,1)}, f32[16,768]{1,0:T(8,128)}, f32[8,768]{1,0:T(8,128)}, f32[8,768]{1,0:T(8,1...) custom-call(s32[3]{0:T(128)} %add_add_fusion.plan_ref, ...), custom_call_target="tpu_custom_call" | custom-call | tf_op jit(solution)/shard_map/pallas_call | solution.py:941
  176.0 1.4 collective-permute-start.18
  179.6 2.4 collective-permute-done.18.ahead_ref
  182.2 2.1 collective-permute-start.25
  184.3 14.1 %shard_map.257 = (f32[4,1024,384]{2,1,0:T(8,128)}, f32[8,1024]{1,0:T(8,128)}, f32[8,1536]{1,0:T(8,128)}) custom-call(s32[1]{0:T(128)} %bitcast.9.plan_ref, bf16[1024,768]{1,0:T(8,128)(2,1)} %copy-done.19, bf16[1024,768]{1,0:T(8,128)(2,1)} %copy-done.8, bf16[1024,128]{1,0:T(8,128)(2,1)} %copy-done.45, bf16[1024,1536]{1,0:T(8,128)(2,1)} %bitcast.36, ...), custom_call_target="tpu_custom_call" | custom-call | tf_op jit(solution)/shard_map/pallas_call | solution.py:941
  200.1 17.9 %collective-permute-start.19 = (f32[16,256]{1,0:T(8,128)S(1)}, f32[16,256]{1,0:T(8,128)S(1)}, u32[]{:S(2)}, u32[]{:S(2)}) collective-permute-start(f32[16,256]{1,0:T(8,128)S(1)} %shard_map.258.refs_0_), channel_id=1, source_target_pairs={{0,1},{1,2},{2,3},{3,0},{4,5},{5,6},{6,7},{7,4},{8,9},{9,10},{10,1... | collective-permute-start | bytes 49160 | tf_op jit(solution)/shard_map/ppermute | solution.py:828
  218.0 1.7 collective-permute-done.19.refs_1_
  219.7 1.7 collective-permute-start.21
  221.4 2.2 shard_map.259
  224.2 7.9 %collective-permute-start.27 = (bf16[1024,384]{1,0:T(8,128)(2,1)}, bf16[1024,384]{1,0:T(8,128)(2,1)}, u32[]{:S(2)}, u32[]{:S(2)}) collective-permute-start(bf16[1024,384]{1,0:T(8,128)(2,1)} %shard_map.259), channel_id=1, source_target_pairs={{0,1},{3,2},{4,5},{7,6},{8,9},{11,10},{12,13},{15,14},{16,17},{19,... | collective-permute-start | bytes 2359304 | tf_op jit(solution)/shard_map/ppermute | solution.py:1465
  232.2 8.6 %shard_map.260 = (f32[384,384]{1,0:T(8,128)}, f32[384,384]{1,0:T(8,128)}, f32[384,384]{1,0:T(8,128)}, f32[384,384]{1,0:T(8,128)}) custom-call(s32[3]{0:T(128)} %add_add_fusion.plan_ref, bf16[1024,1536]{1,0:T(8,128)(2,1)} %get-tuple-element.154.normed_ref.refs_17_.refs_0_.normed_a, bf16[1024,1536]{1,0:T(8,128)(2,1)} %copy-done.4, ...), custom_call_target="tpu_custom_call" | custom-call | tf_op jit(solution)/shard_map/pallas_call | solution.py:941
  240.9 2.3 shard_map.263
  244.2 1.9 collective-permute-start.30
  246.9 4.1 %shard_map.264 = (bf16[1024,384]{1,0:T(8,128)(2,1)}, bf16[1024,384]{1,0:T(8,128)(2,1)}) custom-call(s32[3]{0:T(128)} %get-tuple-element.280.plan_ref, f32[4,1024,384]{2,1,0:T(8,128)} %get-tuple-element.200.part_ref.up_ref.down_ref, f32[4,1024,384]{2,1,0:T(8,128)} %get-tuple-element.200.part_ref.up_ref.down_ref, ...), custom_call_target="tpu_custom_call" | custom-call | tf_op jit(solution)/shard_map/pallas_call | solution.py:884
  251.0 4.0 %collective-permute-done.30.got_a = f32[384,384]{1,0:T(8,128)S(1)} collective-permute-done((f32[384,384]{1,0:T(8,128)}, f32[384,384]{1,0:T(8,128)S(1)}, u32[]{:S(2)}, u32[]{:S(2)}) %collective-permute-start.30) | collective-permute-done | bytes 589856 | tf_op jit(solution)/shard_map/ppermute | solution.py:836
  260.2 1.5 collective-permute-start.28
  262.4 1.4 collective-permute-start.32
  264.8 1.5 collective-permute-done.23.narrow_b
  267.6 1.9 copy-done.5
  269.5 4.1 %shard_map.262 = (f32[144,384]{1,0:T(8,128)S(1)}, f32[144,384]{1,0:T(8,128)}, f32[144,384]{1,0:T(8,128)}, f32[144,384]{1,0:T(8,128)}) custom-call(s32[3]{0:T(128)S(1)} %copy-done.76, bf16[1024,1536]{1,0:T(8,128)(2,1)S(1)} %copy-done.3, bf16[1024,1536]{1,0:T(8,128)(2,1)S(1)} %copy-done.5, bf16[1024,128]{1,0:T(8,128)(2,1)S(1)} %copy-done.46, ...), custom_call_target="tpu_custom_call" | custom-call | tf_op jit(solution)/shard_map/pallas_call | solution.py:941
  276.2 1.6 collective-permute-start.36
  277.8 4.1 %shard_map.265 = (bf16[1024,384]{1,0:T(8,128)(2,1)}, bf16[1024,384]{1,0:T(8,128)(2,1)}) custom-call(s32[3]{0:T(128)} %get-tuple-element.279.plan_ref, f32[4,1024,384]{2,1,0:T(8,128)} %get-tuple-element.200.part_ref.up_ref.down_ref, f32[4,1024,384]{2,1,0:T(8,128)} %get-tuple-element.200.part_ref.up_ref.down_ref, bf16[1024,384]{1,0:T(8,128)(2,1)} %copy-done.85, ...), custom_call_target="tpu_custom_call" | custom-call | tf_op jit(solution)/shard_map/pallas_call | solution.py:884
  283.7 2.1 collective-permute-start.37
  286.5 4.4 %collective-permute-start.39 = (bf16[1024,384]{1,0:T(8,128)(2,1)}, bf16[1024,384]{1,0:T(8,128)(2,1)}, u32[]{:S(2)}, u32[]{:S(2)}) collective-permute-start(bf16[1024,384]{1,0:T(8,128)(2,1)} %get-tuple-element.239), channel_id=1, source_target_pairs={{0,1},{1,2},{2,3},{4,5},{5,6},{6,7},{8,9},{9,10},{10,11},{12,13},{... | collective-permute-start | bytes 2359304 | tf_op jit(solution)/shard_map/ppermute | solution.py:902
  290.9 1.5 collective-permute-done.35.refs_2_
  296.7 2.5 fusion
  299.3 4.6 %collective-permute-done.37.got_a = f32[192,384]{1,0:T(8,128)} collective-permute-done((f32[192,384]{1,0:T(8,128)}, f32[192,384]{1,0:T(8,128)}, u32[]{:S(2)}, u32[]{:S(2)}) %collective-permute-start.37) | collective-permute-done | bytes 294944 | tf_op jit(solution)/shard_map/ppermute | solution.py:836
  306.4 2.1 collective-permute-start.41
  308.5 1.7 collective-permute-start.42
  310.5 2.8 copy-done
  313.2 4.2 %shard_map.270 = f32[1024,384]{1,0:T(8,128)} custom-call(s32[1]{0:T(128)} %bitcast.9.plan_ref, f32[4,1024,384]{2,1,0:T(8,128)S(1)} %copy-done, bf16[1024,384]{1,0:T(8,128)(2,1)} %collective-permute-done.39.up_ref, bf16[1024,384]{1,0:T(8,128)(2,1)} %collective-permute-done.40.down_ref, bf16[1024,1536]{1,0:T(8,128)(2,1)S(1)} %bitcast.37, ...), custom_call_target="tpu_custom_call" | custom-call | tf_op jit(solution)/shard_map/pallas_call | solution.py:941
  318.5 6.9 %collective-permute-done.42 = bf16[512,384]{1,0:T(8,128)(2,1)S(1)} collective-permute-done((bf16[512,384]{1,0:T(8,128)(2,1)S(1)}, bf16[512,384]{1,0:T(8,128)(2,1)S(1)}, u32[]{:S(2)}, u32[]{:S(2)}) %collective-permute-start.42) | collective-permute-done | bytes 393248 | tf_op jit(solution)/shard_map/ppermute | solution.py:836
  331.3 3.3 collective-permute-done.44.there
  334.6 5.2 %shard_map.271 = (f32[1536,768]{1,0:T(8,128)}, f32[64,1536]{1,0:T(8,128)}, f32[12,1536]{1,0:T(8,128)}) custom-call(s32[3]{0:T(128)S(1)} %copy-done.76, bf16[2048,384]{1,0:T(8,128)(2,1)} %constant_dynamic-update-slice_fusion.here, bf16[2048,384]{1,0:T(8,128)(2,1)} %collective-permute-done.44.there), custom_call_target="tpu_custom_call" | custom-call | tf_op jit(solution)/shard_map/pallas_call | solution.py:941
  339.8 4.4 %shard_map.272 = (f32[1536,768]{1,0:T(8,128)}, f32[768,1536]{1,0:T(8,128)}) custom-call(s32[3]{0:T(128)S(1)} %copy-done.76, bf16[3072,384]{1,0:T(8,128)(2,1)S(1)} %copy-done.35, bf16[3072,384]{1,0:T(8,128)(2,1)S(1)} %collective-permute-done.45.there), custom_call_target="tpu_custom_call" | custom-call | tf_op jit(solution)/shard_map/pallas_call | solution.py:941
  (261 shorter events, 59.9 us)
Async XLA Ops:
  8.0 288.7 %reduce-scatter.2.cloned.1.call-start = ((), (), s32[]{:S(2)}) async-start(), calls=%async_computation.1 | async-start | bytes 7864320 | tf_op jit(solution)/shard_map/reduce_scatter | solution.py:1433
  8.1 57.2 %collective-permute-start.1 = (bf16[1024,1536]{1,0:T(8,128)(2,1)}, bf16[1024,1536]{1,0:T(8,128)(2,1)S(1)}, u32[]{:S(2)}, u32[]{:S(2)}) collective-permute-start(bf16[1024,1536]{1,0:T(8,128)(2,1)} %bitcast.39), channel_id=1, source_target_pairs={{0,16},{16,0},{1,17},{17,1},{2,18},{18,2},{3,19},{19,3},{4,20},{20... | collective-permute-start | bytes 9437192 | tf_op jit(solution)/shard_map/ppermute | solution.py:836
  9.9 16.2 %copy-start.49 = (bf16[1536,256]{1,0:T(8,128)(2,1)S(1)}, bf16[1536,256]{1,0:T(8,128)(2,1)}, u32[]{:S(2)}) copy-start(bf16[1536,256]{1,0:T(8,128)(2,1)} %state_w.3) | copy-start | bytes 2359300
  9.9 16.2 %copy-start.67 = (f32[1,1536]{1,0:T(1,128)S(1)}, f32[1,1536]{1,0:T(1,128)}, u32[]{:S(2)}) copy-start(f32[1,1536]{1,0:T(1,128)} %reshape.74.gain_ref) | copy-start | bytes 18436
  18.6 58.6 %collective-permute-start.5 = (bf16[1024,1536]{1,0:T(8,128)(2,1)}, bf16[1024,1536]{1,0:T(8,128)(2,1)S(1)}, u32[]{:S(2)}, u32[]{:S(2)}) collective-permute-start(bf16[1024,1536]{1,0:T(8,128)(2,1)} %get-tuple-element.154.normed_ref.refs_17_.refs_0_.normed_a), channel_id=1, source_target_pairs={{0,16},{16,0},{1,17},{17,1},{2,18},{18,2},{3,19},{19,3},{4,20},{20... | collective-permute-start | bytes 9437192 | tf_op jit(solution)/shard_map/ppermute | solution.py:836
  19.5 6.6 %collective-permute-start = (bf16[16,1536]{1,0:T(8,128)(2,1)S(1)}, bf16[16,1536]{1,0:T(8,128)(2,1)S(1)}, u32[]{:S(2)}, u32[]{:S(2)}) collective-permute-start(bf16[16,1536]{1,0:T(8,128)(2,1)S(1)} %slice_bitcast_fusion), channel_id=1, source_target_pairs={{0,4},{4,8},{8,12},{1,5},{5,9},{9,13},{2,6},{6,10},{10,14},{3,7},{... | collective-permute-start | bytes 147464 | tf_op jit(solution)/shard_map/ppermute | solution.py:818
  29.6 21.7 %copy-start.2 = (bf16[1024,1536]{1,0:T(8,128)(2,1)S(1)}, bf16[1024,1536]{1,0:T(8,128)(2,1)}, u32[]{:S(2)}) copy-start(bf16[1024,1536]{1,0:T(8,128)(2,1)} %get-tuple-element.154.normed_ref.refs_17_.refs_0_.normed_a) | copy-start | bytes 9437188
  29.6 21.7 %copy-start.9 = (bf16[1,1024,1536]{2,1,0:T(8,128)(2,1)S(1)}, bf16[1,1024,1536]{2,1,0:T(8,128)(2,1)}, u32[]{:S(2)}) copy-start(bf16[1,1024,1536]{2,1,0:T(8,128)(2,1)} %param.27) | copy-start | bytes 9437188
  29.6 21.7 %copy-start.38 = (bf16[1536,768]{1,0:T(8,128)(2,1)S(1)}, bf16[1536,768]{1,0:T(8,128)(2,1)}, u32[]{:S(2)}) copy-start(bf16[1536,768]{1,0:T(8,128)(2,1)} %gate_w.3) | copy-start | bytes 7077892
  29.6 21.7 %copy-start.82 = (bf16[768,1536]{1,0:T(8,128)(2,1)S(1)}, bf16[768,1536]{1,0:T(8,128)(2,1)}, u32[]{:S(2)}) copy-start(bf16[768,1536]{1,0:T(8,128)(2,1)} %out_w.1) | copy-start | bytes 7077892
  42.1 37.7 %copy-start.16 = (f32[1024,256]{1,0:T(8,128)}, f32[1024,256]{1,0:T(8,128)S(1)}, u32[]{:S(2)}) copy-start(f32[1024,256]{1,0:T(8,128)S(1)} %get-tuple-element.148.rows_ref.refs_8_) | copy-start | bytes 3145732
  42.1 37.7 %copy-start.23 = (f32[1024,128]{1,0:T(8,128)}, f32[1024,128]{1,0:T(8,128)S(1)}, u32[]{:S(2)}) copy-start(f32[1024,128]{1,0:T(8,128)S(1)} %get-tuple-element.149.cum_ref.refs_6_) | copy-start | bytes 1572868
  42.1 20.3 %collective-permute-start.2 = (f32[136,768]{1,0:T(8,128)S(1)}, f32[136,768]{1,0:T(8,128)S(1)}, u32[]{:S(2)}, u32[]{:S(2)}) collective-permute-start(f32[136,768]{1,0:T(8,128)S(1)} %get-tuple-element.152.own_ref), channel_id=1, source_target_pairs={{0,4},{4,8},{8,12},{1,5},{5,9},{9,13},{2,6},{6,10},{10,14},{3,7},{... | collective-permute-start | bytes 1253384 | tf_op jit(solution)/shard_map/ppermute | solution.py:818
  46.5 18.7 %collective-permute-start.3 = (f32[136,768]{1,0:T(8,128)S(1)}, f32[136,768]{1,0:T(8,128)S(1)}, u32[]{:S(2)}, u32[]{:S(2)}) collective-permute-start(f32[136,768]{1,0:T(8,128)S(1)} %get-tuple-element.152.own_ref), channel_id=1, source_target_pairs={{0,8},{4,12},{1,9},{5,13},{2,10},{6,14},{3,11},{7,15},{16,24},{20,... | collective-permute-start | bytes 1253384 | tf_op jit(solution)/shard_map/ppermute | solution.py:818
  50.0 15.2 %collective-permute-start.4 = (f32[136,768]{1,0:T(8,128)S(1)}, f32[136,768]{1,0:T(8,128)S(1)}, u32[]{:S(2)}, u32[]{:S(2)}) collective-permute-start(f32[136,768]{1,0:T(8,128)S(1)} %get-tuple-element.152.own_ref), channel_id=1, source_target_pairs={{0,12},{1,13},{2,14},{3,15},{16,28},{17,29},{18,30},{19,31}} | collective-permute-start | bytes 1253384 | tf_op jit(solution)/shard_map/ppermute | solution.py:818
  71.7 5.7 %collective-permute-start.6 = (f32[8,1024]{1,0:T(8,128)S(1)}, f32[8,1024]{1,0:T(8,128)S(1)}, u32[]{:S(2)}, u32[]{:S(2)}) collective-permute-start(f32[8,1024]{1,0:T(8,128)S(1)} %get-tuple-element.161.refs_0_), channel_id=1, source_target_pairs={{0,1},{1,2},{2,3},{3,0},{4,5},{5,6},{6,7},{7,4},{8,9},{9,10},{10,1... | collective-permute-start | bytes 98312 | tf_op jit(solution)/shard_map/ppermute | solution.py:828
  73.3 5.3 %collective-permute-start.7 = (f32[8,1024]{1,0:T(8,128)S(1)}, f32[8,1024]{1,0:T(8,128)S(1)}, u32[]{:S(2)}, u32[]{:S(2)}) collective-permute-start(f32[8,1024]{1,0:T(8,128)S(1)} %get-tuple-element.161.refs_0_), channel_id=1, source_target_pairs={{0,2},{1,3},{2,0},{3,1},{4,6},{5,7},{6,4},{7,5},{8,10},{9,11},{10,... | collective-permute-start | bytes 98312 | tf_op jit(solution)/shard_map/ppermute | solution.py:828
  75.8 3.9 %collective-permute-start.8 = (f32[8,1024]{1,0:T(8,128)S(1)}, f32[8,1024]{1,0:T(8,128)S(1)}, u32[]{:S(2)}, u32[]{:S(2)}) collective-permute-start(f32[8,1024]{1,0:T(8,128)S(1)} %get-tuple-element.161.refs_0_), channel_id=1, source_target_pairs={{0,3},{1,0},{2,1},{3,2},{4,7},{5,4},{6,5},{7,6},{8,11},{9,8},{10,9... | collective-permute-start | bytes 98312 | tf_op jit(solution)/shard_map/ppermute | solution.py:828
  89.7 31.7 %copy-start.6 = (f32[1024,768]{1,0:T(8,128)}, f32[1024,768]{1,0:T(8,128)S(1)}, u32[]{:S(2)}) copy-start(f32[1024,768]{1,0:T(8,128)S(1)} %get-tuple-element.182.dmix_ref.refs_1_) | copy-start | bytes 9437188
  95.5 232.3 %all-gather.2.cloned.1.call-start = ((), (), s32[]{:S(2)}) async-start(), calls=%async_computation.2 | async-start | bytes 2949120 | tf_op jit(solution)/shard_map/all_gather | solution.py:1477
  95.5 50.1 %collective-permute-start.13 = (bf16[1024,768]{1,0:T(8,128)(2,1)}, bf16[1024,768]{1,0:T(8,128)(2,1)}, u32[]{:S(2)}, u32[]{:S(2)}) collective-permute-start(bf16[1024,768]{1,0:T(8,128)(2,1)} %copy-done.19), channel_id=1, source_target_pairs={{0,16},{16,0},{1,17},{17,1},{2,18},{18,2},{3,19},{19,3},{4,20},{20... | collective-permute-start | bytes 4718600 | tf_op jit(solution)/shard_map/ppermute | solution.py:836
  95.6 50.1 %collective-permute-start.14 = (bf16[1024,768]{1,0:T(8,128)(2,1)}, bf16[1024,768]{1,0:T(8,128)(2,1)}, u32[]{:S(2)}, u32[]{:S(2)}) collective-permute-start(bf16[1024,768]{1,0:T(8,128)(2,1)} %copy-done.40), channel_id=1, source_target_pairs={{0,16},{16,0},{1,17},{17,1},{2,18},{18,2},{3,19},{19,3},{4,20},{20... | collective-permute-start | bytes 4718600 | tf_op jit(solution)/shard_map/ppermute | solution.py:836
  96.1 19.9 %collective-permute-start.9 = (f32[136,768]{1,0:T(8,128)}, f32[136,768]{1,0:T(8,128)S(1)}, u32[]{:S(2)}, u32[]{:S(2)}) collective-permute-start(f32[136,768]{1,0:T(8,128)} %copy-done.83), channel_id=1, source_target_pairs={{4,0},{8,4},{12,8},{5,1},{9,5},{13,9},{6,2},{10,6},{14,10},{7,3},{... | collective-permute-start | bytes 1253384 | tf_op jit(solution)/shard_map/ppermute | solution.py:823
  97.4 24.0 %collective-permute-start.10 = (f32[136,768]{1,0:T(8,128)}, f32[136,768]{1,0:T(8,128)S(1)}, u32[]{:S(2)}, u32[]{:S(2)}) collective-permute-start(f32[136,768]{1,0:T(8,128)} %copy-done.83), channel_id=1, source_target_pairs={{8,0},{12,4},{9,1},{13,5},{10,2},{14,6},{11,3},{15,7},{24,16},{28,... | collective-permute-start | bytes 1253384 | tf_op jit(solution)/shard_map/ppermute | solution.py:823
  98.7 22.7 %collective-permute-start.11 = (f32[136,768]{1,0:T(8,128)}, f32[136,768]{1,0:T(8,128)S(1)}, u32[]{:S(2)}, u32[]{:S(2)}) collective-permute-start(f32[136,768]{1,0:T(8,128)} %copy-done.83), channel_id=1, source_target_pairs={{12,0},{13,1},{14,2},{15,3},{28,16},{29,17},{30,18},{31,19}} | collective-permute-start | bytes 1253384 | tf_op jit(solution)/shard_map/ppermute | solution.py:823
  133.2 5.6 %collective-permute-start.12 = (f32[8,512]{1,0:T(8,128)S(1)}, f32[8,512]{1,0:T(8,128)S(1)}, u32[]{:S(2)}, u32[]{:S(2)}) collective-permute-start(f32[8,512]{1,0:T(8,128)S(1)} %get-tuple-element.180), channel_id=1, source_target_pairs={{4,0},{8,4},{12,8},{5,1},{9,5},{13,9},{6,2},{10,6},{14,10},{7,3},{... | collective-permute-start | bytes 49160 | tf_op jit(solution)/shard_map/ppermute | solution.py:823
  141.1 36.2 %collective-permute-start.15 = (f32[520,128]{1,0:T(8,128)S(1)}, f32[520,128]{1,0:T(8,128)S(1)}, u32[]{:S(2)}, u32[]{:S(2)}) collective-permute-start(f32[520,128]{1,0:T(8,128)S(1)} %get-tuple-element.188), channel_id=1, source_target_pairs={{0,1},{1,2},{2,3},{3,0},{4,5},{5,6},{6,7},{7,4},{8,9},{9,10},{10,1... | collective-permute-start | bytes 798728 | tf_op jit(solution)/shard_map/ppermute | solution.py:1442
  141.4 36.0 %collective-permute-start.16 = (f32[520,128]{1,0:T(8,128)S(1)}, f32[520,128]{1,0:T(8,128)S(1)}, u32[]{:S(2)}, u32[]{:S(2)}) collective-permute-start(f32[520,128]{1,0:T(8,128)S(1)} %get-tuple-element.189), channel_id=1, source_target_pairs={{0,2},{1,3},{2,0},{3,1},{4,6},{5,7},{6,4},{7,5},{8,10},{9,11},{10,... | collective-permute-start | bytes 798728 | tf_op jit(solution)/shard_map/ppermute | solution.py:1442
  145.0 32.4 %collective-permute-start.17 = (f32[520,128]{1,0:T(8,128)S(1)}, f32[520,128]{1,0:T(8,128)S(1)}, u32[]{:S(2)}, u32[]{:S(2)}) collective-permute-start(f32[520,128]{1,0:T(8,128)S(1)} %get-tuple-element.190), channel_id=1, source_target_pairs={{0,3},{1,0},{2,1},{3,2},{4,7},{5,4},{6,5},{7,6},{8,11},{9,8},{10,9... | collective-permute-start | bytes 798728 | tf_op jit(solution)/shard_map/ppermute | solution.py:1442
  145.7 31.8 %copy-start.28 = (f32[1024,256]{1,0:T(8,128)S(1)}, f32[1024,256]{1,0:T(8,128)}, u32[]{:S(2)}) copy-start(f32[1024,256]{1,0:T(8,128)} %copy-done.26) | copy-start | bytes 3145732
  145.7 31.8 %copy-start.60 = (bf16[1024,256]{1,0:T(8,128)(2,1)S(1)}, bf16[1024,256]{1,0:T(8,128)(2,1)}, u32[]{:S(2)}) copy-start(bf16[1024,256]{1,0:T(8,128)(2,1)} %get-tuple-element.144.state_ref.refs_5_) | copy-start | bytes 1572868
  145.7 36.3 %copy-start.75 = (bf16[4,768]{1,0:T(4,128)(2,1)S(1)}, bf16[4,768]{1,0:T(4,128)(2,1)}, u32[]{:S(2)}) copy-start(bf16[4,768]{1,0:T(4,128)(2,1)} %taps_ref.1) | copy-start | bytes 18436
  176.0 6.1 %collective-permute-start.18 = (f32[8,768]{1,0:T(8,128)}, f32[8,768]{1,0:T(8,128)S(1)}, u32[]{:S(2)}, u32[]{:S(2)}) collective-permute-start(f32[8,768]{1,0:T(8,128)} %get-tuple-element.187), channel_id=1, source_target_pairs={{4,0},{8,4},{12,8},{5,1},{9,5},{13,9},{6,2},{10,6},{14,10},{7,3},{... | collective-permute-start | bytes 73736 | tf_op jit(solution)/shard_map/ppermute | solution.py:823
  182.1 50.1 %collective-permute-start.22 = (bf16[1024,768]{1,0:T(8,128)(2,1)S(1)}, bf16[1024,768]{1,0:T(8,128)(2,1)}, u32[]{:S(2)}, u32[]{:S(2)}) collective-permute-start(bf16[1024,768]{1,0:T(8,128)(2,1)S(1)} %shard_map.256.value_ref.refs_2_), channel_id=1, source_target_pairs={{0,16},{16,0},{1,17},{17,1},{2,18},{18,2},{3,19},{19,3},{4,20},{20... | collective-permute-start | bytes 4718600 | tf_op jit(solution)/shard_map/ppermute | solution.py:836
  182.2 58.7 %collective-permute-start.25 = (f32[768,384]{1,0:T(8,128)}, f32[768,384]{1,0:T(8,128)S(1)}, u32[]{:S(2)}, u32[]{:S(2)}) collective-permute-start(f32[768,384]{1,0:T(8,128)} %get-tuple-element.229), channel_id=1, source_target_pairs={{0,4},{4,0},{8,12},{12,8},{1,5},{5,1},{9,13},{13,9},{2,6},{6,2},{1... | collective-permute-start | bytes 3538952 | tf_op jit(solution)/shard_map/ppermute | solution.py:836
  184.3 56.6 %collective-permute-start.26 = (f32[768,384]{1,0:T(8,128)}, f32[768,384]{1,0:T(8,128)}, u32[]{:S(2)}, u32[]{:S(2)}) collective-permute-start(f32[768,384]{1,0:T(8,128)} %get-tuple-element.230), channel_id=1, source_target_pairs={{0,8},{4,12},{8,0},{12,4},{1,9},{5,13},{9,1},{13,5},{2,10},{6,14},... | collective-permute-start | bytes 3538952 | tf_op jit(solution)/shard_map/ppermute | solution.py:836
  200.1 19.6 %collective-permute-start.19 = (f32[16,256]{1,0:T(8,128)S(1)}, f32[16,256]{1,0:T(8,128)S(1)}, u32[]{:S(2)}, u32[]{:S(2)}) collective-permute-start(f32[16,256]{1,0:T(8,128)S(1)} %shard_map.258.refs_0_), channel_id=1, source_target_pairs={{0,1},{1,2},{2,3},{3,0},{4,5},{5,6},{6,7},{7,4},{8,9},{9,10},{10,1... | collective-permute-start | bytes 49160 | tf_op jit(solution)/shard_map/ppermute | solution.py:828
  218.0 5.7 %collective-permute-start.20 = (f32[16,256]{1,0:T(8,128)S(1)}, f32[16,256]{1,0:T(8,128)S(1)}, u32[]{:S(2)}, u32[]{:S(2)}) collective-permute-start(f32[16,256]{1,0:T(8,128)S(1)} %shard_map.258.refs_0_), channel_id=1, source_target_pairs={{0,2},{1,3},{2,0},{3,1},{4,6},{5,7},{6,4},{7,5},{8,10},{9,11},{10,... | collective-permute-start | bytes 49160 | tf_op jit(solution)/shard_map/ppermute | solution.py:828
  219.7 4.6 %collective-permute-start.21 = (f32[16,256]{1,0:T(8,128)S(1)}, f32[16,256]{1,0:T(8,128)S(1)}, u32[]{:S(2)}, u32[]{:S(2)}) collective-permute-start(f32[16,256]{1,0:T(8,128)S(1)} %shard_map.258.refs_0_), channel_id=1, source_target_pairs={{0,3},{1,0},{2,1},{3,2},{4,7},{5,4},{6,5},{7,6},{8,11},{9,8},{10,9... | collective-permute-start | bytes 49160 | tf_op jit(solution)/shard_map/ppermute | solution.py:828
  223.5 17.3 %copy-start.73 = (f32[8,768]{1,0:T(8,128)S(1)}, f32[8,768]{1,0:T(8,128)}, u32[]{:S(2)}) copy-start(f32[8,768]{1,0:T(8,128)} %get-tuple-element.216.refs_4_) | copy-start | bytes 73732
  223.5 17.3 %copy-start.77 = (f32[8,128]{1,0:T(8,128)S(1)}, f32[8,128]{1,0:T(8,128)}, u32[]{:S(2)}) copy-start(f32[8,128]{1,0:T(8,128)} %get-tuple-element.218.refs_6_) | copy-start | bytes 12292
  223.5 17.3 %copy-start.41 = (f32[768,384]{1,0:T(8,128)S(1)}, f32[768,384]{1,0:T(8,128)}, u32[]{:S(2)}) copy-start(f32[768,384]{1,0:T(8,128)} %get-tuple-element.225.own_a) | copy-start | bytes 3538948
  223.5 17.3 %copy-start.42 = (f32[768,384]{1,0:T(8,128)S(1)}, f32[768,384]{1,0:T(8,128)}, u32[]{:S(2)}) copy-start(f32[768,384]{1,0:T(8,128)} %get-tuple-element.226.own_b) | copy-start | bytes 3538948
  224.2 22.6 %collective-permute-start.27 = (bf16[1024,384]{1,0:T(8,128)(2,1)}, bf16[1024,384]{1,0:T(8,128)(2,1)}, u32[]{:S(2)}, u32[]{:S(2)}) collective-permute-start(bf16[1024,384]{1,0:T(8,128)(2,1)} %shard_map.259), channel_id=1, source_target_pairs={{0,1},{3,2},{4,5},{7,6},{8,9},{11,10},{12,13},{15,14},{16,17},{19,... | collective-permute-start | bytes 2359304 | tf_op jit(solution)/shard_map/ppermute | solution.py:1465
  244.2 10.8 %collective-permute-start.30 = (f32[384,384]{1,0:T(8,128)}, f32[384,384]{1,0:T(8,128)S(1)}, u32[]{:S(2)}, u32[]{:S(2)}) collective-permute-start(f32[384,384]{1,0:T(8,128)} %get-tuple-element.241), channel_id=1, source_target_pairs={{0,8},{4,12},{8,0},{12,4},{1,9},{5,13},{9,1},{13,5},{2,10},{6,14},... | collective-permute-start | bytes 1769480 | tf_op jit(solution)/shard_map/ppermute | solution.py:836
  246.1 10.1 %collective-permute-start.31 = (f32[384,384]{1,0:T(8,128)S(1)}, f32[384,384]{1,0:T(8,128)S(1)}, u32[]{:S(2)}, u32[]{:S(2)}) collective-permute-start(f32[384,384]{1,0:T(8,128)S(1)} %get-tuple-element.242), channel_id=1, source_target_pairs={{0,4},{4,0},{8,12},{12,8},{1,5},{5,1},{9,13},{13,9},{2,6},{6,2},{1... | collective-permute-start | bytes 1769480 | tf_op jit(solution)/shard_map/ppermute | solution.py:836
  260.2 15.3 %collective-permute-start.28 = (bf16[1024,384]{1,0:T(8,128)(2,1)}, bf16[1024,384]{1,0:T(8,128)(2,1)S(1)}, u32[]{:S(2)}, u32[]{:S(2)}) collective-permute-start(bf16[1024,384]{1,0:T(8,128)(2,1)} %get-tuple-element.235), channel_id=1, source_target_pairs={{0,1},{1,2},{4,5},{5,6},{8,9},{9,10},{12,13},{13,14},{16,17},{17,1... | collective-permute-start | bytes 2359304 | tf_op jit(solution)/shard_map/ppermute | solution.py:902
  261.7 14.5 %collective-permute-start.29 = (bf16[1024,384]{1,0:T(8,128)(2,1)}, bf16[1024,384]{1,0:T(8,128)(2,1)S(1)}, u32[]{:S(2)}, u32[]{:S(2)}) collective-permute-start(bf16[1024,384]{1,0:T(8,128)(2,1)} %get-tuple-element.236), channel_id=1, source_target_pairs={{3,2},{2,1},{7,6},{6,5},{11,10},{10,9},{15,14},{14,13},{19,18},{18... | collective-permute-start | bytes 2359304 | tf_op jit(solution)/shard_map/ppermute | solution.py:903
  262.4 19.5 %collective-permute-start.32 = (f32[384,384]{1,0:T(8,128)}, f32[384,384]{1,0:T(8,128)S(1)}, u32[]{:S(2)}, u32[]{:S(2)}) collective-permute-start(f32[384,384]{1,0:T(8,128)} %get-tuple-element.247), channel_id=1, source_target_pairs={{0,4},{4,0},{8,12},{12,8},{1,5},{5,1},{9,13},{13,9},{2,6},{6,2},{1... | collective-permute-start | bytes 1769480 | tf_op jit(solution)/shard_map/ppermute | solution.py:836
  263.8 18.2 %collective-permute-start.33 = (f32[384,384]{1,0:T(8,128)}, f32[384,384]{1,0:T(8,128)S(1)}, u32[]{:S(2)}, u32[]{:S(2)}) collective-permute-start(f32[384,384]{1,0:T(8,128)} %get-tuple-element.248), channel_id=1, source_target_pairs={{0,8},{4,12},{8,0},{12,4},{1,9},{5,13},{9,1},{13,5},{2,10},{6,14},... | collective-permute-start | bytes 1769480 | tf_op jit(solution)/shard_map/ppermute | solution.py:836
  264.8 1.5 collective-permute-start.23
  266.4 1.2 collective-permute-start.24
  274.3 11.5 %collective-permute-start.34 = (f32[144,384]{1,0:T(8,128)}, f32[144,384]{1,0:T(8,128)S(1)}, u32[]{:S(2)}, u32[]{:S(2)}) collective-permute-start(f32[144,384]{1,0:T(8,128)} %get-tuple-element.222), channel_id=1, source_target_pairs={{0,4},{4,0},{8,12},{12,8},{1,5},{5,1},{9,13},{13,9},{2,6},{6,2},{1... | collective-permute-start | bytes 663560 | tf_op jit(solution)/shard_map/ppermute | solution.py:836
  275.5 17.0 %collective-permute-start.35 = (f32[144,384]{1,0:T(8,128)}, f32[144,384]{1,0:T(8,128)}, u32[]{:S(2)}, u32[]{:S(2)}) collective-permute-start(f32[144,384]{1,0:T(8,128)} %get-tuple-element.223), channel_id=1, source_target_pairs={{0,8},{4,12},{8,0},{12,4},{1,9},{5,13},{9,1},{13,5},{2,10},{6,14},... | collective-permute-start | bytes 663560 | tf_op jit(solution)/shard_map/ppermute | solution.py:836
  276.2 17.5 %collective-permute-start.36 = (f32[144,384]{1,0:T(8,128)}, f32[144,384]{1,0:T(8,128)}, u32[]{:S(2)}, u32[]{:S(2)}) collective-permute-start(f32[144,384]{1,0:T(8,128)} %get-tuple-element.224), channel_id=1, source_target_pairs={{0,12},{4,8},{8,4},{12,0},{1,13},{5,9},{9,5},{13,1},{2,14},{6,10},... | collective-permute-start | bytes 663560 | tf_op jit(solution)/shard_map/ppermute | solution.py:836
  283.7 20.1 %collective-permute-start.37 = (f32[192,384]{1,0:T(8,128)}, f32[192,384]{1,0:T(8,128)}, u32[]{:S(2)}, u32[]{:S(2)}) collective-permute-start(f32[192,384]{1,0:T(8,128)} %get-tuple-element.255), channel_id=1, source_target_pairs={{0,8},{4,12},{8,0},{12,4},{1,9},{5,13},{9,1},{13,5},{2,10},{6,14},... | collective-permute-start | bytes 884744 | tf_op jit(solution)/shard_map/ppermute | solution.py:836
  285.8 18.0 %collective-permute-start.38 = (f32[192,384]{1,0:T(8,128)}, f32[192,384]{1,0:T(8,128)}, u32[]{:S(2)}, u32[]{:S(2)}) collective-permute-start(f32[192,384]{1,0:T(8,128)} %get-tuple-element.256), channel_id=1, source_target_pairs={{0,4},{4,0},{8,12},{12,8},{1,5},{5,1},{9,13},{13,9},{2,6},{6,2},{1... | collective-permute-start | bytes 884744 | tf_op jit(solution)/shard_map/ppermute | solution.py:836
  286.5 23.9 %collective-permute-start.39 = (bf16[1024,384]{1,0:T(8,128)(2,1)}, bf16[1024,384]{1,0:T(8,128)(2,1)}, u32[]{:S(2)}, u32[]{:S(2)}) collective-permute-start(bf16[1024,384]{1,0:T(8,128)(2,1)} %get-tuple-element.239), channel_id=1, source_target_pairs={{0,1},{1,2},{2,3},{4,5},{5,6},{6,7},{8,9},{9,10},{10,11},{12,13},{... | collective-permute-start | bytes 2359304 | tf_op jit(solution)/shard_map/ppermute | solution.py:902
  292.4 18.0 %collective-permute-start.40 = (bf16[1024,384]{1,0:T(8,128)(2,1)}, bf16[1024,384]{1,0:T(8,128)(2,1)}, u32[]{:S(2)}, u32[]{:S(2)}) collective-permute-start(bf16[1024,384]{1,0:T(8,128)(2,1)} %get-tuple-element.240), channel_id=1, source_target_pairs={{3,2},{2,1},{1,0},{7,6},{6,5},{5,4},{11,10},{10,9},{9,8},{15,14},{... | collective-permute-start | bytes 2359304 | tf_op jit(solution)/shard_map/ppermute | solution.py:903
  306.4 12.1 %collective-permute-start.41 = (bf16[512,384]{1,0:T(8,128)(2,1)S(1)}, bf16[512,384]{1,0:T(8,128)(2,1)S(1)}, u32[]{:S(2)}, u32[]{:S(2)}) collective-permute-start(bf16[512,384]{1,0:T(8,128)(2,1)S(1)} %pad_maximum_fusion), channel_id=1, source_target_pairs={{0,4},{4,0},{8,12},{12,8},{1,5},{5,1},{9,13},{13,9},{2,6},{6,2},{1... | collective-permute-start | bytes 1179656 | tf_op jit(solution)/shard_map/ppermute | solution.py:836
  308.5 17.0 %collective-permute-start.42 = (bf16[512,384]{1,0:T(8,128)(2,1)S(1)}, bf16[512,384]{1,0:T(8,128)(2,1)S(1)}, u32[]{:S(2)}, u32[]{:S(2)}) collective-permute-start(bf16[512,384]{1,0:T(8,128)(2,1)S(1)} %pad_maximum_fusion), channel_id=1, source_target_pairs={{0,8},{4,12},{8,0},{12,4},{1,9},{5,13},{9,1},{13,5},{2,10},{6,14},... | collective-permute-start | bytes 1179656 | tf_op jit(solution)/shard_map/ppermute | solution.py:836
  310.2 15.3 %collective-permute-start.43 = (bf16[512,384]{1,0:T(8,128)(2,1)S(1)}, bf16[512,384]{1,0:T(8,128)(2,1)S(1)}, u32[]{:S(2)}, u32[]{:S(2)}) collective-permute-start(bf16[512,384]{1,0:T(8,128)(2,1)S(1)} %pad_maximum_fusion), channel_id=1, source_target_pairs={{0,12},{4,8},{8,4},{12,0},{1,13},{5,9},{9,5},{13,1},{2,14},{6,10},... | collective-permute-start | bytes 1179656 | tf_op jit(solution)/shard_map/ppermute | solution.py:836
  327.8 11.9 %collective-permute-start.45 = (bf16[3072,384]{1,0:T(8,128)(2,1)}, bf16[3072,384]{1,0:T(8,128)(2,1)S(1)}, u32[]{:S(2)}, u32[]{:S(2)}) collective-permute-start(bf16[3072,384]{1,0:T(8,128)(2,1)} %all-gather.2.cloned.1.call-done.here), channel_id=1, source_target_pairs={{0,16},{16,0},{1,17},{17,1},{2,18},{18,2},{3,19},{19,3},{4,20},{20... | collective-permute-start | bytes 7077896 | tf_op jit(solution)/shard_map/ppermute | solution.py:836
  327.8 6.8 %collective-permute-start.44 = (bf16[2048,384]{1,0:T(8,128)(2,1)}, bf16[2048,384]{1,0:T(8,128)(2,1)}, u32[]{:S(2)}, u32[]{:S(2)}) collective-permute-start(bf16[2048,384]{1,0:T(8,128)(2,1)} %constant_dynamic-update-slice_fusion.here), channel_id=1, source_target_pairs={{0,16},{16,0},{1,17},{17,1},{2,18},{18,2},{3,19},{19,3},{4,20},{20... | collective-permute-start | bytes 4718600 | tf_op jit(solution)/shard_map/ppermute | solution.py:836
  (72 other events, 435.6 us)
Sparse Core Ops, SparseCore 0:
  95.6 131.0 reduce-scatter.1
Sparse Core Ops, SparseCore 1:
  260.3 49.2 all-gather.1

commit v4 on v3

--- a/solution.py
+++ b/solution.py
@@ -101,6 +101,10 @@
     return pltpu.CompilerParams(
         dimension_semantics=("arbitrary",), vmem_limit_bytes=limit * 1024 * 1024
     )
+
+
+def in_hbm(x):
+    return pltpu.with_memory_space_constraint(x, pltpu.HBM)
 
 
 def whole(shape):
@@ -156,13 +160,13 @@
         ],
         out_specs=[rows(tile, width), rows(tile, inner), rows(tile, state2), rows(tile, LANES)],
         out_shape=[
-            jax.ShapeDtypeStruct((tokens, width), bf16),
+            pltpu.HBM((tokens, width), bf16),
             jax.ShapeDtypeStruct((tokens, inner), bf16),
             jax.ShapeDtypeStruct((tokens, state2), bf16),
             jax.ShapeDtypeStruct((tokens, LANES), f32),
         ],
         scratch_shapes=[pltpu.VMEM((LANES, width), bf16)],
-        compiler_params=params(56),
+        compiler_params=params(24),
         cost_estimate=cost(6),
     )(residual, pre_gain, input_weight, state_weight, step_weight)
 
@@ -295,7 +299,7 @@
         ],
         out_shape=[
             jax.ShapeDtypeStruct((tokens, inner), f32),
-            jax.ShapeDtypeStruct((tokens, inner), f32),
+            pltpu.HBM((tokens, inner), f32),
             jax.ShapeDtypeStruct((tokens, state2), f32),
             jax.ShapeDtypeStruct((tokens, state2), f32),
             jax.ShapeDtypeStruct((tokens, LANES), f32),
@@ -430,7 +434,7 @@
         out_shape=[
             jax.ShapeDtypeStruct((tokens, inner), f32),
             jax.ShapeDtypeStruct((EDGE, tokens), f32),
-            jax.ShapeDtypeStruct(held.shape, f32),
+            pltpu.HBM(held.shape, f32),
             jax.ShapeDtypeStruct((state, inner), f32),
         ],
         scratch_shapes=[pltpu.VMEM((state, inner), f32), pltpu.VMEM((EDGE, inner), f32), pltpu.VMEM((LANES, inner), bf16)],
@@ -515,10 +519,10 @@
             whole((EDGE, inner)),
         ],
         out_shape=[
-            jax.ShapeDtypeStruct((tokens, inner), bf16),
-            jax.ShapeDtypeStruct((tokens, inner), bf16),
-            jax.ShapeDtypeStruct((tokens, inner), f32),
-            jax.ShapeDtypeStruct((blocks, state, inner), f32),
+            pltpu.HBM((tokens, inner), bf16),
+            pltpu.HBM((tokens, inner), bf16),
+            pltpu.HBM((tokens, inner), f32),
+            pltpu.HBM((blocks, state, inner), f32),
             jax.ShapeDtypeStruct((state + EDGE, inner), f32),
             jax.ShapeDtypeStruct((EDGE, inner), f32),
         ],
@@ -528,10 +532,10 @@
     )(mixed, gate_in, grad_normed, state_rows, cum, norm_gain, *sums)
 
 
-def inner_back_kernel(heads_count, conv_ref, dt_ref, rows_ref, cum_ref, cumt_ref, dmix_ref, driven_out, rows_out, heads):
+def inner_back_kernel(b, conv_ref, dt_ref, rows_ref, cum_ref, cumt_ref, dmix_ref, driven_out, rows_out, heads):
     size, width = conv_ref.shape
 
-    @pl.when(pl.program_id(0) == 0)
+    @pl.when(b == 0)
     def _():
         heads[...] = head_map(width)
 
@@ -568,28 +572,50 @@
     rows_out[:, LANES:] = dot3(score_grad, b_rows, TN)
 
 
-def inner_back(heads_count, conv, dt, state_rows, cum, cumt, grad_mixed):
+def inner_back(normed_out, out_weight, conv, dt, state_rows, cum, cumt, grad_mixed):
     tokens, inner = conv.shape
+    width = out_weight.shape[1]
+    tile = min(tokens, 256)
+    first = tokens // tile
+    at = lambda b: jnp.maximum(b - first, 0)
+    by_rows = lambda cols: pl.BlockSpec((BLOCK, cols), lambda b: (at(b), 0))
+    early = lambda cols: pl.BlockSpec((tile, cols), lambda b: (jnp.minimum(b, first - 1), 0))
+
+    def body(normed_ref, weight_ref, *refs):
+        ins, partial_out, rest = refs[:6], refs[6], refs[7:]
+        b = pl.program_id(0)
+
+        @pl.when(b < first)
+        def _():
+            partial_out[...] = dot(normed_ref[...], weight_ref[...])
+
+        @pl.when(b >= first)
+        def _():
+            inner_back_kernel(b - first, *ins, *rest)
+
     return pl.pallas_call(
-        functools.partial(inner_back_kernel, heads_count),
-        grid=(tokens // BLOCK,),
+        body,
+        grid=(first + tokens // BLOCK,),
         in_specs=[
-            rows(BLOCK, inner),
-            rows(BLOCK, LANES),
-            rows(BLOCK, state_rows.shape[1]),
-            rows(BLOCK, LANES),
-            pl.BlockSpec((cumt.shape[0], BLOCK), lambda b: (0, b)),
-            rows(BLOCK, inner),
-        ],
-        out_specs=[rows(BLOCK, inner), rows(BLOCK, state_rows.shape[1])],
+            early(inner),
+            whole(out_weight.shape),
+            by_rows(inner),
+            by_rows(LANES),
+            by_rows(state_rows.shape[1]),
+            by_rows(LANES),
+            pl.BlockSpec((cumt.shape[0], BLOCK), lambda b: (0, at(b))),
+            by_rows(inner),
+        ],
+        out_specs=[early(width), by_rows(inner), by_rows(state_rows.shape[1])],
         out_shape=[
-            jax.ShapeDtypeStruct((tokens, inner), f32),
-            jax.ShapeDtypeStruct(state_rows.shape, f32),
+            pltpu.HBM((tokens, width), f32),
+            pltpu.HBM((tokens, inner), f32),
+            pltpu.HBM(state_rows.shape, f32),
         ],
         scratch_shapes=[pltpu.VMEM((LANES, inner), bf16)],
-        compiler_params=params(16),
-        cost_estimate=cost(0),
-    )(conv, dt, state_rows, cum, cumt, grad_mixed)
+        compiler_params=params(28),
+        cost_estimate=cost(1),
+    )(in_hbm(normed_out), in_hbm(out_weight), conv, *map(in_hbm, (dt, state_rows, cum, cumt, grad_mixed)))
 
 
 def stacked(high, low):
@@ -644,27 +670,28 @@
     tokens, inner = conv.shape
     blocks, state, _ = held.shape
     state_block = pl.BlockSpec((1, state, inner), lambda b: (blocks - 1 - b, 0, 0))
-    wide = rows(BLOCK, inner, blocks)
+    deep = rows(BLOCK, inner, blocks)
+    deep_state = pl.BlockSpec((1, state, inner), lambda b: (blocks - 1 - b, 0, 0))
     narrow = rows(BLOCK, LANES, blocks)
     both = rows(BLOCK, 2 * state, blocks)
     return pl.pallas_call(
         functools.partial(rows_back_kernel, len(messages)),
         grid=(blocks,),
         in_specs=[
-            both, wide, wide, narrow, narrow, both, state_block, state_block,
+            both, deep, deep, narrow, narrow, both, deep_state, deep_state,
             *[whole(m.shape) for m in messages],
             pl.BlockSpec((EDGE, 2 * state), lambda b: (0, 0)),
         ],
         out_specs=[both, state_block, whole((EDGE, 4 * state))],
         out_shape=[
             jax.ShapeDtypeStruct((tokens, 2 * state), f32),
-            jax.ShapeDtypeStruct(held.shape, f32),
+            pltpu.HBM(held.shape, f32),
             jax.ShapeDtypeStruct((EDGE, 4 * state), f32),
         ],
         scratch_shapes=[pltpu.VMEM((state, inner), f32), pltpu.VMEM((EDGE, inner), f32), pltpu.VMEM((LANES, inner), bf16)],
         compiler_params=params(24),
         cost_estimate=cost(0),
-    )(grad_rows, grad_mixed, conv, dt, cum, state_rows, held, later, *messages, spre)
+    )(*map(in_hbm, (grad_rows, grad_mixed, conv, dt, cum, state_rows, held, later, *messages, spre)))
 
 
 def finish_kernel(
@@ -796,7 +823,7 @@
             wide_weights_kernel(b - blocks, *wide_ins, *rest[6:10])
 
     return scalar_call(
-        body, plan, (*operands, *wide_operands),
+        body, plan, tuple(map(in_hbm, (*operands, *wide_operands))),
         [wide, wide, wide, wide, wide, narrow, narrow, narrow, by_rows(2 * state), state_block, all_of(end_state), state_block,
          *[all_of(a) for a in operands[12:]], moving, moving, still, still, still, still, moving, moving],
         [o[0] for o in outs], [o[1] for o in outs], grid=(blocks + count,),
@@ -809,7 +836,7 @@
             pltpu.VMEM((inner, LANES), bf16),
             pltpu.VMEM((2 * EDGE, inner), f32),
         ],
-        limit=56, micros=0,
+        limit=44, micros=0,
     )
 
 
@@ -858,9 +885,9 @@
             out_specs=pl.BlockSpec((tile, width), lambda b, plan: (b, 0)),
         ),
         out_shape=jax.ShapeDtypeStruct((tokens, width), bf16),
-        compiler_params=params(56),
+        compiler_params=params(8),
         cost_estimate=cost(0),
-    )(plan, parts)
+    )(plan, in_hbm(parts))
     return sent
 
 
@@ -895,9 +922,9 @@
             out_specs=[block, block],
         ),
         out_shape=[jax.ShapeDtypeStruct((tokens, width), bf16)] * 2,
-        compiler_params=params(56),
+        compiler_params=params(12),
         cost_estimate=cost(0),
-    )(jnp.concatenate([plan, place.astype(jnp.int32).reshape(1)]), parts, parts, *arrived)
+    )(jnp.concatenate([plan, place.astype(jnp.int32).reshape(1)]), in_hbm(parts), in_hbm(parts), *arrived)
     return (up, down), [
         lax.ppermute(up, axis, [(k, k + 1) for k in range(step)]),
         lax.ppermute(down, axis, [(count - 1 - k, count - 2 - k) for k in range(step)]),
@@ -1091,8 +1118,8 @@
     )
 
 
-def small_kernel(count, tokens, plan_ref, *refs):
-    parts, (kernel_ref, gain_ref, small_ref, sums_out, out_ref) = refs[:count], refs[count:]
+def small_kernel(count, given, tokens, plan_ref, *refs):
+    parts, (kernel_ref, gain_ref, small_ref, sums_out, out_ref) = refs[:given], refs[given:]
     sums = parts[0][...]
     for ref in parts[1:]:
         sums = sums + ref[...]
@@ -1118,11 +1145,11 @@
     out_ref[...] = jnp.concatenate(rows_of, axis=0)
 
 
-def small_sums(place, tokens, parts, kernel_grad, gain_grad, small):
+def small_sums(place, count, tokens, parts, kernel_grad, gain_grad, small):
     shapes = [jax.ShapeDtypeStruct(parts[0].shape, f32), jax.ShapeDtypeStruct((SMALL, LANES), f32)]
-    operands = (*parts, kernel_grad, gain_grad, small)
+    operands = tuple(map(in_hbm, (*parts, kernel_grad, gain_grad, small)))
     return scalar_call(
-        functools.partial(small_kernel, len(parts), tokens), place, operands, [all_of(a) for a in operands],
+        functools.partial(small_kernel, count, len(parts), tokens), place, operands, [all_of(a) for a in operands],
         [all_of(a) for a in shapes], shapes, limit=8, micros=0,
     )
 
@@ -1160,7 +1187,7 @@
     by_rows = lambda cols: pl.BlockSpec((tile, cols), lambda b, plan: (b, 0))
     return scalar_call(
         functools.partial(input_kernel_body, pieces), place,
-        (grad_gate, grad_value, narrow, residual, pre_gain, gate_weight, input_weight, state_weight, step_weight),
+        (in_hbm(grad_gate), grad_value, narrow, in_hbm(residual), pre_gain, gate_weight, input_weight, state_weight, step_weight),
         [
             by_rows(inner), by_rows(inner), by_rows(narrow.shape[1]), by_rows(width),
             *[all_of(a) for a in (pre_gain, gate_weight, input_weight, state_weight, step_weight)],
@@ -1171,11 +1198,11 @@
             pl.BlockSpec((EDGE, width), lambda b, plan: (0, 0)),
         ],
         [
-            jax.ShapeDtypeStruct((pieces, tokens, width // pieces), f32),
+            pltpu.HBM((pieces, tokens, width // pieces), f32),
             jax.ShapeDtypeStruct((EDGE, tokens), f32),
             jax.ShapeDtypeStruct((EDGE, width), f32),
         ],
-        grid=(tokens // tile,), scratch=[pltpu.VMEM((width, LANES), bf16)], limit=56, micros=0,
+        grid=(tokens // tile,), scratch=[pltpu.VMEM((width, LANES), bf16)], limit=36, micros=0,
     )
 
 
@@ -1191,57 +1218,52 @@
         value_weights_kernel(pl.program_id(0), *refs)
 
     return scalar_call(
-        body, plan, (*normed, *grad_value), [moving, moving, still, still],
-        [all_of(shape)] * 4, [shape] * 4, grid=(count,), limit=56, micros=0,
-    )
-
-
-def narrow_weights_kernel(plan_ref, normed_a, normed_b, narrow_a, narrow_b, small_a, small_b, *outs):
+        body, plan, (*map(in_hbm, normed), *grad_value), [moving, moving, still, still],
+        [all_of(shape)] * 4, [shape] * 4, grid=(count,), limit=20, micros=0,
+    )
+
+
+def narrow_weights_kernel(plan_ref, normed_a, normed_b, narrow_a, narrow_b, small_a, small_b, keep_out, send_out):
     k = pl.program_id(0)
-    tokens, tile = normed_a.shape
+    tile = normed_a.shape[1]
     total = dot(narrow_a[...], normed_a[...], TN) + dot(narrow_b[...], normed_b[...], TN)
     small = small_a[...] + small_b[...]
     per_row = tile // LANES
-    for i, ref in enumerate(outs):
+    size = keep_out.shape[0] // 2
+    for i, (ref, at) in enumerate(((keep_out, 0), (send_out, 0), (keep_out, size), (send_out, size))):
 
         @pl.when(k == i)
-        def _(ref=ref):
-            ref[:LANES] = total
+        def _(ref=ref, at=at):
+            ref[at : at + LANES] = total
             for j in range(per_row):
-                ref[LANES:, j * LANES : (j + 1) * LANES] = small[j * SMALL // per_row : (j + 1) * SMALL // per_row]
+                ref[at + LANES : at + size, j * LANES : (j + 1) * LANES] = small[j * SMALL // per_row : (j + 1) * SMALL // per_row]
 
 
 def narrow_weights(plan, count, normed, narrow, small):
     tokens, width = normed[0].shape
     tile = width // count
     moving = pl.BlockSpec((tokens, tile), lambda k, plan: (0, jnp.bitwise_xor(plan[1], k)))
-    shape = jax.ShapeDtypeStruct((LANES + SMALL * LANES // tile, tile), f32)
+    shape = jax.ShapeDtypeStruct((2 * (LANES + SMALL * LANES // tile), tile), f32)
     return scalar_call(
-        narrow_weights_kernel, plan, (*normed, *narrow, *small), [moving, moving, *[all_of(a) for a in (*narrow, *small)]],
-        [all_of(shape)] * count, [shape] * count, grid=(count,), limit=16, micros=0,
-    )
-
-
-def sum_kernel(count, *refs):
-    total = refs[0][...]
-    for ref in refs[1:count]:
-        total = total + ref[...]
-    refs[count][...] = total.astype(refs[count].dtype)
-
-
-def sum_of(arrays, dtype):
-    shape = jax.ShapeDtypeStruct(arrays[0].shape, dtype)
+        narrow_weights_kernel, plan, (*map(in_hbm, normed), *narrow, *small), [moving, moving, *[all_of(a) for a in (*narrow, *small)]],
+        [all_of(shape)] * 2, [shape] * 2, grid=(count,), limit=16, micros=0,
+    )
+
+
+def pair_kernel(keep_ref, got_ref, stay_out, away_out):
+    size = stay_out.shape[0]
+    stay_out[...] = keep_ref[:size] + got_ref[:size]
+    away_out[...] = keep_ref[size:] + got_ref[size:]
+
+
+def pair_sums(keep, got):
+    shape = jax.ShapeDtypeStruct((keep.shape[0] // 2, keep.shape[1]), f32)
     return pl.pallas_call(
-        functools.partial(sum_kernel, len(arrays)),
-        out_shape=shape,
-        compiler_params=pltpu.CompilerParams(vmem_limit_bytes=16 * 1024 * 1024),
+        pair_kernel,
+        out_shape=[shape, shape],
+        compiler_params=pltpu.CompilerParams(vmem_limit_bytes=6 * 1024 * 1024),
         cost_estimate=cost(0),
-    )(*arrays)
-
-
-def over_ctx(arrays, wait=()):
-    arrived = [swapped(a, "ctx", k) for k, a in enumerate(arrays) if k]
-    return over_dp(sum_of([arrays[0], *after(wait, arrived)], f32))
+    )(keep, got)
 
 
 def over_dp(total):
@@ -1265,10 +1287,10 @@
     half = jax.ShapeDtypeStruct((size // 2, cols), f32)
     return pl.pallas_call(
         halves_kernel,
-        out_shape=[jax.ShapeDtypeStruct((size, cols), f32), half, half],
+        out_shape=[pltpu.HBM((size, cols), f32), *[pltpu.HBM(half.shape, f32)] * 2],
         compiler_params=pltpu.CompilerParams(vmem_limit_bytes=16 * 1024 * 1024),
         cost_estimate=cost(0),
-    )(own_a, own_b, got_a, got_b)
+    )(*map(in_hbm, (own_a, own_b, got_a, got_b)))
 
 
 def add_kernel(stay, got_a, got_b, out):
@@ -1295,6 +1317,30 @@
 def ordered(first, here, there):
     here, there = here.astype(f32), there.astype(f32)
     return jnp.where(first, here, there), jnp.where(first, there, here)
+
+
+def joined_kernel(*refs):
+    *parts, out, done = refs
+    rows = parts[0].shape[0]
+    copies = [
+        pltpu.make_async_copy(part, out.at[pl.ds(i * rows, rows)], done.at[i]) for i, part in enumerate(parts)
+    ]
+    for copy in copies:
+        copy.start()
+    for copy in copies:
+        copy.wait()
+
+
+def joined(*parts):
+    rows, width = parts[0].shape
+    return pl.pallas_call(
+        joined_kernel,
+        out_shape=pltpu.HBM((len(parts) * rows, width), parts[0].dtype),
+        in_specs=[pl.BlockSpec(memory_space=pl.ANY)] * len(parts),
+        out_specs=pl.BlockSpec(memory_space=pl.ANY),
+        scratch_shapes=[pltpu.SemaphoreType.DMA((len(parts),))],
+        compiler_params=pltpu.CompilerParams(vmem_limit_bytes=2**20),
+    )(*parts)
 
 
 def wide_together_kernel(plan_ref, here, there, gate_out, out_out):
@@ -1372,7 +1418,7 @@
     own = pl.BlockSpec((size, part), lambda b, plan: (b, 0))
     return scalar_call(
         functools.partial(final_kernel, tokens // size), place,
-        (parts, *arrived, residual, residual, cotangent, pre_gain, sums),
+        (in_hbm(parts), *arrived, in_hbm(residual), in_hbm(residual), in_hbm(cotangent), pre_gain, sums),
         [
             pl.BlockSpec((1, size, part), lambda b, plan: (plan[0], b, 0)),
             own,
@@ -1425,16 +1471,16 @@
         mixed, gate_in, grad_normed, state_rows, cum, row(norm_gain), all_sums, inner_total
     )
     messages = [from_after(message, "ctx", by) for by in range(1, ctx_size)]
-    other_gate = swapped(grad_gate, "dp", 1)
-    other_out = swapped(normed_out, "dp", 1)
-
+
+    partial_out, grad_driven, grad_rows = inner_back(
+        normed_out, out_weight, conv, dt, state_rows, cum, cumt, after(message, grad_mixed)
+    )
+    messages = after(grad_driven, messages)
+    partial_out, gate_there, out_there = after(messages, (partial_out, grad_gate, normed_out))
     resid_part = own_part(residual, "tensor", 1).astype(f32)
-    partial_out = dot(after(message, normed_out), out_weight)
     branch = lax.psum_scatter(partial_out, "tensor", scatter_dimension=1, tiled=True)
-    output = (resid_part + branch).astype(bf16)
-
-    grad_driven, grad_rows = inner_back(head_count, conv, dt, state_rows, cum, cumt, after(partial_out, grad_mixed))
-    messages = after(grad_driven, messages)
+    other_gate = swapped(gate_there, "dp", 1)
+    other_out = swapped(out_there, "dp", 1)
     grad_rows, later, first_rows = rows_back(grad_rows, grad_mixed, conv, dt, cum, state_rows, held, later, messages, spre)
     ahead = from_after(first_rows, "ctx")
     pieces = list(pieces_of(place, tensor_size, grad_rows, ahead))
@@ -1450,47 +1496,50 @@
     arrived = after(first_rows, arrived)
     narrow, taps_grad = state_back(place, [pieces[0], *arrived], spre, state_in, shalo, ahead, state_kernel, grad_step)
     grad_value = complete(after(narrow, ahead_value), last_rows, input_kernel, grad_value)
+    gate_send, out_send = after(arrived, (gate_send, out_send))
+    gate_got, out_got = swapped(gate_send, "ctx", 1), swapped(out_send, "ctx", 2)
     other_value = swapped(grad_value, "dp", 1)
     other_narrow = swapped(narrow, "dp", 1)
     gate_send, out_send = after(grad_value, (gate_send, out_send))
     gate_got, out_got = swapped(gate_send, "ctx", 1), swapped(out_send, "ctx", 2)
+    first_keep, first_send, second_keep, second_send = value_weights(
+        plan, ctx_size, (normed, other_normed), (grad_value, other_value)
+    )
+    first_got, second_got = swapped(first_send, "ctx", 1), swapped(second_send, "ctx", 2)
     parts, row_sums, col_sums = input_partials(
-        place, tensor_size, grad_gate, grad_value, narrow, residual, row(pre_gain), gate_weight, input_weight, state_weight,
-        step_weight
+        place, tensor_size, grad_gate, after((first_keep, other_narrow), grad_value), narrow, residual, row(pre_gain), gate_weight,
+        input_weight, state_weight, step_weight
     )
     packed = sums_of(place, tensor_size, row_sums, col_sums, taps_grad, state2)
     packed = [packed, *from_all(packed, "tensor")]
-    sent = line_first(parts, "tensor")
+    sent = line_first(after(packed[0], parts), "tensor")
     packed, sent = after(sent, packed), after(packed, sent)
     moving = lax.ppermute(sent, "tensor", [(0, 1), (tensor_size - 1, tensor_size - 2)])
-    first_keep, first_send, second_keep, second_send = value_weights(
-        after(sent, plan), ctx_size, (normed, other_normed), (grad_value, other_value)
-    )
-    sums, small = small_sums(place, tokens, after(first_keep, packed), kernel_grad, gain_grad, small)
+    wide_stay, gate_away, out_away = halves(gate_keep, out_keep, *after(sent, (gate_got, out_got)))
+    gate_got, out_got = swapped(gate_away, "ctx", 2), swapped(out_away, "ctx", 1)
+    value_stay, first_away, second_away = halves(first_keep, second_keep, *after(wide_stay, (first_got, second_got)))
+    first_got, second_got = swapped(first_away, "ctx", 2), swapped(second_away, "ctx", 1)
+    sums, small = small_sums(place, tensor_size, tokens, after(value_stay, packed), kernel_grad, gain_grad, small)
     other_small = swapped(small, "dp", 1)
-    stay, gate_away, out_away = halves(gate_keep, out_keep, *after(small, (gate_got, out_got)))
-    gate_got, out_got = swapped(gate_away, "ctx", 2), swapped(out_away, "ctx", 1)
-    sent, moving = line_step(parts, 2, after(stay, moving), "tensor")
-    wide_chunk = summed(stay, *after(sent, (gate_got, out_got)))
-    first_send, second_send = after(wide_chunk, (first_send, second_send))
-    first_got, second_got = swapped(first_send, "ctx", 1), swapped(second_send, "ctx", 2)
+    narrow_keep, narrow_send = narrow_weights(
+        after(small, plan), ctx_size, (normed, other_normed), (narrow, other_narrow), (small, other_small)
+    )
+    narrow_got = swapped(narrow_send, "ctx", 1)
+    moving, gate_got, out_got, first_got, second_got = lax.optimization_barrier(
+        after(narrow_keep, (moving, gate_got, out_got, first_got, second_got))
+    )
+    sent, moving = line_step(parts, 2, moving, "tensor")
+    value_chunk = summed(value_stay, *after(sent, (first_got, second_got)))
+    wide_chunk = summed(wide_stay, *after(value_chunk, (gate_got, out_got)))
     wide_here = lax.all_gather(wide_chunk, "ctx", tiled=True)
-    weights = narrow_weights(after(small, plan), ctx_size, (normed, other_normed), (narrow, other_narrow), (small, other_small))
-    sent, moving = line_step(parts, 3, after(weights, moving), "tensor")
-    stay, first_away, second_away = halves(first_keep, second_keep, *after(sent, (first_got, second_got)))
-    first_got, second_got = swapped(first_away, "ctx", 2), swapped(second_away, "ctx", 1)
-    narrow_total = over_ctx(weights, stay)
-    value_chunk = summed(stay, *after((narrow_total, output), (first_got, second_got)))
+    moving, narrow_got = lax.optimization_barrier(after(wide_chunk, (moving, narrow_got)))
+    narrow_stay, narrow_away = pair_sums(narrow_keep, narrow_got)
+    narrow_got = swapped(narrow_away, "ctx", 2)
+    sent, moving = line_step(parts, 3, after(narrow_stay, moving), "tensor")
+    output = (resid_part + after(sent, branch)).astype(bf16)
+    narrow_total = over_dp(narrow_stay + after(output, narrow_got))
     chunk = jnp.concatenate([value_chunk, narrow_total[:LANES].astype(bf16)], axis=0)
     chunks = [swapped(chunk, "ctx", k) for k in range(1, ctx_size)]
-    input_grad = final(place, parts, after(chunk, moving), residual, cotangent, row(pre_gain), sums)
-    narrow_here = jnp.concatenate([chunk, *after(input_grad, chunks)], axis=0)
-    narrow_there = swapped(narrow_here, "dp", 1)
-    wide_there = swapped(after(narrow_here, wide_here), "dp", 1)
-    input_weight_grad, state_weight_grad, step_weight_grad = narrow_together(
-        plan, ctx_size, narrow_here, narrow_there, state_part, head_count
-    )
-    gate_weight_grad, out_weight_grad = wide_together(after(input_weight_grad, plan), ctx_size, wide_here, wide_there)
     small_total = narrow_total[LANES:]
     small_total = jnp.concatenate([small_total[:, i : i + LANES] for i in range(0, small_total.shape[1], LANES)], axis=0)
     wide_rows = inner // LANES
@@ -1504,20 +1553,26 @@
     pre_gain_grad = small_total[at : at + gain_rows].reshape(width // tensor_size)
     at += gain_rows
     taps_grad = small_total[at : at + CONV * state2 // LANES].reshape(CONV, state2)
+    smalls = (pre_gain_grad, kernel_grad, taps_grad, small[1], small[2], small[0], gain_grad)
+    moving, chunks, smalls = lax.optimization_barrier((moving, chunks, smalls))
+    narrow_here = joined(chunk, *chunks)
+    narrow_there = swapped(narrow_here, "dp", 1)
+    wide_here = after(chunks, wide_here)
+    wide_there = swapped(wide_here, "dp", 1)
+    input_grad = final(place, parts, after(narrow_here, moving), residual, cotangent, row(pre_gain), sums)
+    gate_weight_grad, out_weight_grad = wide_together(after(input_grad, plan), ctx_size, wide_here, wide_there)
+    input_weight_grad, state_weight_grad, step_weight_grad = narrow_together(
+        plan, ctx_size, narrow_here, after(gate_weight_grad, narrow_there), state_part, head_count
+    )
     return (
         output[None],
         input_grad[None],
-        pre_gain_grad,
+        smalls[0],
         gate_weight_grad,
         input_weight_grad,
         state_weight_grad.T,
         step_weight_grad.T,
-        kernel_grad,
-        taps_grad,
-        small[1],
-        small[2],
-        small[0],
-        gain_grad,
+        *smalls[1:],
         out_weight_grad,
     )
 

time: 353 us -> 343 us (0.972)
  local copies, waits for them, and re-layouts: 52.4 us -> 19.1 us
  waiting for transfers between devices: 46 us -> 64.5 us
  Pallas kernels: 145 us -> 157 us
  matrix products: 4.61 us -> 0 us
    unnamed x180 -> x124, local copies, waits for them, and re-layouts: 46.6 us -> 13.3 us
    ppermute x6, waiting for transfers between devices: 4.94 us -> 16.8 us  [from_all(): lax.ppermute(value, axis, [(i, (i + by) % count) for i in range(count)])]
    pallas_call x4 -> x5, Pallas kernels: 13.2 us -> 24.7 us  [the longest x1 17.1 us: inner_back(): pl.pallas_call(body, grid=(first + tokens // BLOCK,), in_specs=[early(inn...]
    pallas_call x1, Pallas kernels: 5.99 us -> 12.6 us  [rows_back(): pl.pallas_call(functools.partial(rows_back_kernel, len(messages)), grid=(...]
    ppermute x1, starting transfers between devices: 7.94 us -> 1.33 us  [per_device(): lax.ppermute(sent, 'tensor', [(0, 1), (tensor_size - 1, tensor_size - 2)])]
    ppermute x23 -> x22, waiting for transfers between devices: 24.5 us -> 29.4 us  [swapped(): lax.ppermute(value, axis, [(i, i ^ flip) for i in range(lax.axis_size(axi...]
    dot_general x1 -> x0, matrix products: 4.61 us -> none  [dot(): return lax.dot_general(a, b, dims, preferred_element_type=f32)]
    ppermute x5, waiting for transfers between devices: 12.1 us -> 7.52 us  [from_after(): return lax.ppermute(value, axis, [(i + by, i) for i in range(count - by)])]
  transfers between devices with their start and end apart: 48 -> 47, of which waited for: 20 -> 21; matrix products, arithmetic and copies ran while one was open for 4% -> 3% of each run, Pallas kernels for 38% -> 43%
where the time goes in v4:
time: 343 us; the launch traced here: 341 us
  Pallas kernels  157 us (46%)
  starting transfers between devices  80.9 us (24%)
  waiting for transfers between devices  64.5 us (19%)
  local copies, waits for them, and re-layouts  19.1 us (6%)
  between operations  16.3 us (5%)
    pallas_call x11, Pallas kernels, scalar_call(): pl.pallas_call(body, grid_spec=pltpu.PrefetchScalarGridSpec(num_scalar_pr...  70.1 us
    ppermute x22, waiting for transfers between devices, swapped(): lax.ppermute(value, axis, [(i, i ^ flip) for i in range(lax.axis_size(axi...  29.4 us
    ppermute x6, starting transfers between devices, from_all(): lax.ppermute(value, axis, [(i, (i + by) % count) for i in range(count)])  26.5 us
    ppermute x22, starting transfers between devices, swapped(): lax.ppermute(value, axis, [(i, i ^ flip) for i in range(lax.axis_size(axi...  19.6 us
    pallas_call x1, Pallas kernels, inner_back(): pl.pallas_call(body, grid=(first + tokens // BLOCK,), in_specs=[early(inn...  17.1 us
    ppermute x6, waiting for transfers between devices, from_all(): lax.ppermute(value, axis, [(i, (i + by) % count) for i in range(count)])  16.8 us
    ppermute x4, starting transfers between devices, from_before(): return lax.ppermute(value, axis, [(i, i + by) for i in range(count - by)])  14 us
    unnamed x124, local copies, waits for them, and re-layouts  13.3 us
  transfers between devices with their start and end apart: 47, of which 21 were waited for; matrix products, arithmetic and copies ran while one was open for 3% of the time, Pallas kernels for 43%

profile of v4, /device:TPU:0, one launch (start us, length us, event | category | flops | bytes accessed | tf_op | source)
XLA Modules:
  0.0 341.0 jit_solution(17533849248547176842)
XLA Ops:
  9.3 1.9 copy-done
  11.2 1.7 copy-done.13
  14.8 6.2 %shard_map.245 = (bf16[1024,1536]{1,0:T(8,128)(2,1)}, bf16[1024,768]{1,0:T(8,128)(2,1)S(1)}, bf16[1024,256]{1,0:T(8,128)(2,1)S(1)}, f32[1024,128]{1,0:T(8,128)S(1)}) custom-call(bf16[1024,1536]{1,0:T(8,128)(2,1)S(1)} %bitcast.36, f32[1,1536]{1,0:T(1,128)S(1)} %reshape.75.gain_ref, bf16[1536,768]{1,0:T(8,128)(2,1)S(1)} %copy-done.13, ...), custom_call_target="tpu_custom_call" | custom-call | flops 5400000000 | bytes 18000000 | tf_op jit(solution)/shard_map/pallas_call | solution.py:151
  21.1 4.8 %collective-permute-start = (bf16[16,1536]{1,0:T(8,128)(2,1)S(1)}, bf16[16,1536]{1,0:T(8,128)(2,1)S(1)}, u32[]{:S(2)}, u32[]{:S(2)}) collective-permute-start(bf16[16,1536]{1,0:T(8,128)(2,1)S(1)} %slice_bitcast_fusion), channel_id=1, source_target_pairs={{0,4},{4,8},{8,12},{1,5},{5,9},{9,13},{2,6},{6,10},{10,14},{3,7},{... | collective-permute-start | bytes 147464 | tf_op jit(solution)/shard_map/ppermute | solution.py:845
  26.0 1.7 collective-permute-done.halo_ref
  27.8 10.6 %shard_map.246 = (f32[1024,768]{1,0:T(8,128)S(1)}, f32[1024,768]{1,0:T(8,128)}, f32[1024,256]{1,0:T(8,128)S(1)}, f32[1024,256]{1,0:T(8,128)S(1)}, f32[1024,128]{...) custom-call(bf16[1024,768]{1,0:T(8,128)(2,1)S(1)} %get-tuple-element, ...), custom_call_target="tpu_custom_call" | custom-call | flops 8999999488 | bytes 30000000 | tf_op jit(solution)/shard_map/pallas_call | solution.py:271
  38.5 5.4 %collective-permute-start.4 = (f32[136,768]{1,0:T(8,128)S(1)}, f32[136,768]{1,0:T(8,128)S(1)}, u32[]{:S(2)}, u32[]{:S(2)}) collective-permute-start(f32[136,768]{1,0:T(8,128)S(1)} %get-tuple-element.180.own_ref), channel_id=1, source_target_pairs={{0,12},{1,13},{2,14},{3,15},{16,28},{17,29},{18,30},{19,31}} | collective-permute-start | bytes 1253384 | tf_op jit(solution)/shard_map/ppermute | solution.py:845
  43.9 1.3 collective-permute-start.3
  45.2 2.5 collective-permute-start.2
  47.7 5.6 %shard_map.248 = (f32[1024,768]{1,0:T(8,128)S(1)}, f32[1024,768]{1,0:T(8,128)S(1)}) custom-call(bf16[1024,1536]{1,0:T(8,128)(2,1)S(1)} %copy-done.1, bf16[1536,768]{1,0:T(8,128)(2,1)S(1)} %copy-done.15, bf16[1024,1536]{1,0:T(8,128)(2,1)S(1)} %bitcast.40, bf16[768,1536]{1,0:T(8,128)(2,1)S(1)} %copy-done.12), custom_call_target="tpu_custom_call" | custom-call | flops 5400000000 | bytes 18000000 | tf_op jit(solution)/shard_map/pallas_call | solution.py:183
  53.3 5.4 %shard_map.247.intra_ref = f32[1024,768]{1,0:T(8,128)S(1)} custom-call(f32[1024,768]{1,0:T(8,128)S(1)} %get-tuple-element.174.conv_ref.refs_0_, f32[1024,128]{1,0:T(8,128)S(1)} %get-tuple-element.175.dt_ref.refs_1_.refs_5_, f32[1024,256]{1,0:T(8,128)S(1)} %get-tuple-element.176.rows_ref.refs_2_.refs_8_, ...), custom_call_target="tpu_custom_call" | custom-call | flops 5400000000 | bytes 18000000 | tf_op jit(solution)/shard_map/pallas_call | solution.py:351
  58.7 3.3 collective-permute-done.3.refs_1_
  62.1 5.7 %shard_map.249 = (f32[1024,768]{1,0:T(8,128)S(1)}, f32[8,1024]{1,0:T(8,128)S(1)}, f32[8,128,768]{2,1,0:T(8,128)}, f32[128,768]{1,0:T(8,128)S(1)}) custom-call(f32[1024,768]{1,0:T(8,128)S(1)} %shard_map.247.intra_ref, f32[1024,256]{1,0:T(8,128)S(1)} %get-tuple-element.176.rows_ref.refs_2_.refs_8_, f32[1024,128]{1,0:T(8,128)S(1)} %get-tuple-element.177.cum_ref.refs_3_.refs_6_, ...), custom_call_target="tpu_custom_call" | custom-call | flops 4499999744 | bytes 15000000 | tf_op jit(solution)/shard_map/pallas_call | solution.py:414
  67.7 3.6 %collective-permute-start.8 = (f32[8,1024]{1,0:T(8,128)S(1)}, f32[8,1024]{1,0:T(8,128)S(1)}, u32[]{:S(2)}, u32[]{:S(2)}) collective-permute-start(f32[8,1024]{1,0:T(8,128)S(1)} %get-tuple-element.189.refs_0_), channel_id=1, source_target_pairs={{0,3},{1,0},{2,1},{3,2},{4,7},{5,4},{6,5},{7,6},{8,11},{9,8},{10,9... | collective-permute-start | bytes 98312 | tf_op jit(solution)/shard_map/ppermute | solution.py:855
  72.9 3.2 collective-permute-done.7.refs_2_
  77.0 7.8 %shard_map.250 = (bf16[1024,768]{1,0:T(8,128)(2,1)}, bf16[1024,768]{1,0:T(8,128)(2,1)}, f32[1024,768]{1,0:T(8,128)}, f32[8,128,768]{2,1,0:T(8,128)}, f32[136,768]{1,0:T(8,128)S(1)}, /*index=5*/f32[8,768]{1,0:T(8,128)S(1)}) custom-call(f32[1024,768]{1,0:T(8,128)S(1)} %get-tuple-element.188.mixed_ref.refs_2_, ...), custom_call_target="tpu_custom_call" | custom-call | flops 6300000256 | bytes 21000000 | tf_op jit(solution)/shard_map/pallas_call | solution.py:501
  84.8 1.3 collective-permute-start.11
  86.1 1.3 collective-permute-start.10
  87.4 1.3 collective-permute-start.9
  88.7 17.1 %shard_map.251 = (f32[1024,1536]{1,0:T(8,128)}, f32[1024,768]{1,0:T(8,128)}, f32[1024,256]{1,0:T(8,128)}) custom-call(bf16[1024,768]{1,0:T(8,128)(2,1)} %get-tuple-element.216.normed_ref.refs_21_, bf16[768,1536]{1,0:T(8,128)(2,1)} %weight_ref.1, f32[1024,768]{1,0:T(8,128)S(1)} %get-tuple-element.174.conv_ref.refs_0_, f32[1024,128]{1,0:T(8,128)} %copy-done.6, ...), custom_call_target="tpu_custom_call" | custom-call | flops 900000000 | bytes 3000000 | tf_op jit(solution)/shard_map/pallas_call | solution.py:596
  108.1 12.6 %shard_map.252 = (f32[1024,256]{1,0:T(8,128)S(1)}, f32[8,128,768]{2,1,0:T(8,128)}, f32[8,512]{1,0:T(8,128)S(1)}) custom-call(f32[1024,256]{1,0:T(8,128)} %get-tuple-element.198.drows_ref, f32[1024,768]{1,0:T(8,128)} %get-tuple-element.209.refs_5_.dmix_ref.refs_1_, f32[1024,768]{1,0:T(8,128)} %copy-done.3, f32[1024,128]{1,0:T(8,128)} %copy-done.6, ...), custom_call_target="tpu_custom_call" | custom-call | tf_op jit(solution)/shard_map/pallas_call | solution.py:677
  120.7 1.3 collective-permute-start.12
  122.0 4.7 %collective-permute-done.12.ahead_ref.refs_7_ = f32[8,512]{1,0:T(8,128)S(1)} collective-permute-done((f32[8,512]{1,0:T(8,128)S(1)}, f32[8,512]{1,0:T(8,128)S(1)}, u32[]{:S(2)}, u32[]{:S(2)}) %collective-permute-start.12) | collective-permute-done | bytes 16416 | tf_op jit(solution)/shard_map/ppermute | solution.py:850
  126.7 2.0 shard_map.253
  130.6 2.9 collective-permute-start.17
  133.6 28.4 %shard_map.254 = (bf16[1024,768]{1,0:T(8,128)(2,1)S(1)}, bf16[1024,12]{1,0:T(8,128)(2,1)S(1)}, f32[16,768]{1,0:T(8,128)S(1)}, f32[8,768]{1,0:T(8,128)S(1)}, f32[...) custom-call(s32[3]{0:T(128)S(1)} %add_add_fusion.plan_ref, ...), custom_call_target="tpu_custom_call" | custom-call | tf_op jit(solution)/shard_map/pallas_call | solution.py:968
  162.6 1.4 collective-permute-start.18
  165.1 1.3 shard_map.255
  166.4 2.8 collective-permute-done.18.ahead_ref
  169.4 3.0 collective-permute-start.24
  172.8 7.7 %shard_map.257 = (f32[384,384]{1,0:T(8,128)S(1)}, f32[384,384]{1,0:T(8,128)}, f32[384,384]{1,0:T(8,128)S(1)}, f32[384,384]{1,0:T(8,128)}) custom-call(s32[3]{0:T(128)S(1)} %add_add_fusion.plan_ref, bf16[1024,1536]{1,0:T(8,128)(2,1)} %get-tuple-element.182.normed_ref.refs_17_.refs_0_.normed_a, bf16[1024,1536]{1,0:T(8,128)(2,1)} %copy-done.52, ...), custom_call_target="tpu_custom_call" | custom-call | tf_op jit(solution)/shard_map/pallas_call | solution.py:968
  182.1 3.0 collective-permute-start.26
  185.1 12.0 %shard_map.258 = (f32[4,1024,384]{2,1,0:T(8,128)}, f32[8,1024]{1,0:T(8,128)S(1)}, f32[8,1536]{1,0:T(8,128)S(1)}) custom-call(s32[1]{0:T(128)} %bitcast.3.plan_ref, bf16[1024,768]{1,0:T(8,128)(2,1)} %get-tuple-element.215.refs_19_.gate_ref, bf16[1024,768]{1,0:T(8,128)(2,1)S(1)} %shard_map.256.refs_2_.value_ref, ...), custom_call_target="tpu_custom_call" | custom-call | tf_op jit(solution)/shard_map/pallas_call | solution.py:968
  197.3 19.6 %collective-permute-start.23 = (f32[16,256]{1,0:T(8,128)S(1)}, f32[16,256]{1,0:T(8,128)S(1)}, u32[]{:S(2)}, u32[]{:S(2)}) collective-permute-start(f32[16,256]{1,0:T(8,128)S(1)} %shard_map.259.refs_0_), channel_id=1, source_target_pairs={{0,3},{1,0},{2,1},{3,2},{4,7},{5,4},{6,5},{7,6},{8,11},{9,8},{10,9... | collective-permute-start | bytes 49160 | tf_op jit(solution)/shard_map/ppermute | solution.py:855
  216.9 1.8 collective-permute-done.23.refs_3_
  219.7 6.3 %collective-permute-done.22.refs_2_ = f32[16,256]{1,0:T(8,128)S(1)} collective-permute-done((f32[16,256]{1,0:T(8,128)S(1)}, f32[16,256]{1,0:T(8,128)S(1)}, u32[]{:S(2)}, u32[]{:S(2)}) %collective-permute-start.22) | collective-permute-done | bytes 16416 | tf_op jit(solution)/shard_map/ppermute | solution.py:855
  227.3 1.4 shard_map.260
  228.7 4.0 %collective-permute-done.21.refs_1_ = f32[16,256]{1,0:T(8,128)S(1)} collective-permute-done((f32[16,256]{1,0:T(8,128)S(1)}, f32[16,256]{1,0:T(8,128)S(1)}, u32[]{:S(2)}, u32[]{:S(2)}) %collective-permute-start.21) | collective-permute-done | bytes 16416 | tf_op jit(solution)/shard_map/ppermute | solution.py:855
  232.7 1.3 collective-permute-start.29
  234.1 3.8 %shard_map.261 = (f32[768,384]{1,0:T(8,128)}, f32[384,384]{1,0:T(8,128)}, f32[384,384]{1,0:T(8,128)}) custom-call(f32[768,384]{1,0:T(8,128)} %copy-done.18, f32[768,384]{1,0:T(8,128)} %copy-done.19, f32[768,384]{1,0:T(8,128)} %collective-permute-done.24.got_a, f32[768,384]{1,0:T(8,128)} %collective-permute-done.25.got_b), custom_call_target="tpu_custom_call" | custom-call | tf_op jit(solution)/shard_map/pallas_call | solution.py:1288
  237.9 1.9 collective-permute-start.30
  240.7 2.6 shard_map.262
  246.8 5.0 %shard_map.264 = (f32[288,384]{1,0:T(8,128)S(1)}, f32[288,384]{1,0:T(8,128)S(1)}) custom-call(s32[3]{0:T(128)S(1)} %add_add_fusion.plan_ref, bf16[1024,1536]{1,0:T(8,128)(2,1)} %get-tuple-element.182.normed_ref.refs_17_.refs_0_.normed_a, bf16[1024,1536]{1,0:T(8,128)(2,1)} %copy-done.52, bf16[1024,128]{1,0:T(8,128)(2,1)S(1)} %get-tuple-element.226.narrow_ref.narrow_a, ...), custom_call_target="tpu_custom_call" | custom-call | tf_op jit(solution)/shard_map/pallas_call | solution.py:968
  252.6 1.8 collective-permute-done.30.got_a
  254.4 1.9 collective-permute-done.31.got_b
  256.3 2.6 collective-permute-done.32.got_a
  259.5 2.6 shard_map.265
  264.0 1.3 collective-permute-start.34
  266.1 1.6 collective-permute-start.36
  267.6 14.8 %collective-permute-done.36.got_ref = f32[288,384]{1,0:T(8,128)S(1)} collective-permute-done((f32[288,384]{1,0:T(8,128)}, f32[288,384]{1,0:T(8,128)S(1)}, u32[]{:S(2)}, u32[]{:S(2)}) %collective-permute-start.36) | collective-permute-done | bytes 442400 | tf_op jit(solution)/shard_map/ppermute | solution.py:863
  283.5 1.5 collective-permute-start.37
  285.0 3.4 shard_map.269
  288.4 5.3 %collective-permute-start.38 = (bf16[1024,384]{1,0:T(8,128)(2,1)}, bf16[1024,384]{1,0:T(8,128)(2,1)S(1)}, u32[]{:S(2)}, u32[]{:S(2)}) collective-permute-start(bf16[1024,384]{1,0:T(8,128)(2,1)} %get-tuple-element.299), channel_id=1, source_target_pairs={{0,1},{1,2},{2,3},{4,5},{5,6},{6,7},{8,9},{9,10},{10,11},{12,13},{... | collective-permute-start | bytes 2359304 | tf_op jit(solution)/shard_map/ppermute | solution.py:929
  293.7 1.3 collective-permute-start.39
  295.0 2.6 fusion
  299.3 2.6 collective-permute-start.40
  303.1 1.3 slice_bitcast_fusion.2
  304.4 1.3 slice_bitcast_fusion.3
  305.7 1.3 slice_bitcast_fusion.1
  307.5 4.1 %collective-permute-done.39.down_ref = bf16[1024,384]{1,0:T(8,128)(2,1)S(1)} collective-permute-done((bf16[1024,384]{1,0:T(8,128)(2,1)}, bf16[1024,384]{1,0:T(8,128)(2,1)S(1)}, u32[]{:S(2)}, u32[]{:S(2)}) %collective-permute-start.39) | collective-permute-done | bytes 786464 | tf_op jit(solution)/shard_map/ppermute | solution.py:930
  312.8 6.1 %collective-permute-done.41.refs_2_ = bf16[512,384]{1,0:T(8,128)(2,1)S(1)} collective-permute-done((bf16[512,384]{1,0:T(8,128)(2,1)S(1)}, bf16[512,384]{1,0:T(8,128)(2,1)S(1)}, u32[]{:S(2)}, u32[]{:S(2)}) %collective-permute-start.41) | collective-permute-done | bytes 393248 | tf_op jit(solution)/shard_map/ppermute | solution.py:863
  320.7 5.1 %shard_map.271 = f32[1024,384]{1,0:T(8,128)} custom-call(s32[1]{0:T(128)} %bitcast.3.plan_ref, f32[4,1024,384]{2,1,0:T(8,128)} %get-tuple-element.239.part_ref.up_ref.down_ref, bf16[1024,384]{1,0:T(8,128)(2,1)S(1)} %collective-permute-done.38.up_ref, bf16[1024,384]{1,0:T(8,128)(2,1)S(1)} %collective-permute-done.39.down_ref, bf16[1024,1536]{1,0:T(8,128)(2,1)} %bitcast.34, ...), custom_call_target="tpu_custom_call" | custom-call | tf_op jit(solution)/shard_map/pallas_call | solution.py:968
  325.9 4.4 %shard_map.272 = (f32[1536,768]{1,0:T(8,128)}, f32[768,1536]{1,0:T(8,128)}) custom-call(s32[3]{0:T(128)S(1)} %add_add_fusion.plan_ref, bf16[3072,384]{1,0:T(8,128)(2,1)S(1)} %copy-done.11, bf16[3072,384]{1,0:T(8,128)(2,1)S(1)} %collective-permute-done.43.there), custom_call_target="tpu_custom_call" | custom-call | tf_op jit(solution)/shard_map/pallas_call | solution.py:968
  330.3 3.3 shard_map.273
  (204 shorter events, 32.1 us)
Async XLA Ops:
  8.0 287.0 %reduce-scatter.2.cloned.1.call-start = ((), (), s32[]{:S(2)}) async-start(), calls=%async_computation.1 | async-start | bytes 7864320 | tf_op jit(solution)/shard_map/reduce_scatter | solution.py:1481
  8.1 54.0 %collective-permute-start.1 = (bf16[1024,1536]{1,0:T(8,128)(2,1)}, bf16[1024,1536]{1,0:T(8,128)(2,1)S(1)}, u32[]{:S(2)}, u32[]{:S(2)}) collective-permute-start(bf16[1024,1536]{1,0:T(8,128)(2,1)} %bitcast.37), channel_id=1, source_target_pairs={{0,16},{16,0},{1,17},{17,1},{2,18},{18,2},{3,19},{19,3},{4,20},{20... | collective-permute-start | bytes 9437192 | tf_op jit(solution)/shard_map/ppermute | solution.py:863
  21.0 17.4 %copy-start.17 = (bf16[1024,768]{1,0:T(8,128)(2,1)}, bf16[1024,768]{1,0:T(8,128)(2,1)S(1)}, u32[]{:S(2)}) copy-start(bf16[1024,768]{1,0:T(8,128)(2,1)S(1)} %get-tuple-element.171.value_ref.refs_4_) | copy-start | bytes 4718596
  21.0 17.4 %copy-start.27 = (f32[1024,128]{1,0:T(8,128)}, f32[1024,128]{1,0:T(8,128)S(1)}, u32[]{:S(2)}) copy-start(f32[1024,128]{1,0:T(8,128)S(1)} %get-tuple-element.173.step_ref.refs_7_) | copy-start | bytes 1572868
  21.0 17.4 %copy-start.28 = (bf16[1024,256]{1,0:T(8,128)(2,1)}, bf16[1024,256]{1,0:T(8,128)(2,1)S(1)}, u32[]{:S(2)}) copy-start(bf16[1024,256]{1,0:T(8,128)(2,1)S(1)} %get-tuple-element.172.state_ref.refs_5_) | copy-start | bytes 1572868
  21.0 51.3 %collective-permute-start.5 = (bf16[1024,1536]{1,0:T(8,128)(2,1)}, bf16[1024,1536]{1,0:T(8,128)(2,1)S(1)}, u32[]{:S(2)}, u32[]{:S(2)}) collective-permute-start(bf16[1024,1536]{1,0:T(8,128)(2,1)} %get-tuple-element.182.normed_ref.refs_17_.refs_0_.normed_a), channel_id=1, source_target_pairs={{0,16},{16,0},{1,17},{17,1},{2,18},{18,2},{3,19},{19,3},{4,20},{20... | collective-permute-start | bytes 9437192 | tf_op jit(solution)/shard_map/ppermute | solution.py:863
  21.1 6.6 %collective-permute-start = (bf16[16,1536]{1,0:T(8,128)(2,1)S(1)}, bf16[16,1536]{1,0:T(8,128)(2,1)S(1)}, u32[]{:S(2)}, u32[]{:S(2)}) collective-permute-start(bf16[16,1536]{1,0:T(8,128)(2,1)S(1)} %slice_bitcast_fusion), channel_id=1, source_target_pairs={{0,4},{4,8},{8,12},{1,5},{5,9},{9,13},{2,6},{6,10},{10,14},{3,7},{... | collective-permute-start | bytes 147464 | tf_op jit(solution)/shard_map/ppermute | solution.py:845
  27.7 20.0 %copy-start.1 = (bf16[1024,1536]{1,0:T(8,128)(2,1)S(1)}, bf16[1024,1536]{1,0:T(8,128)(2,1)}, u32[]{:S(2)}) copy-start(bf16[1024,1536]{1,0:T(8,128)(2,1)} %get-tuple-element.182.normed_ref.refs_17_.refs_0_.normed_a) | copy-start | bytes 9437188
  27.7 20.0 %copy-start.2 = (bf16[1,1024,1536]{2,1,0:T(8,128)(2,1)S(1)}, bf16[1,1024,1536]{2,1,0:T(8,128)(2,1)}, u32[]{:S(2)}) copy-start(bf16[1,1024,1536]{2,1,0:T(8,128)(2,1)} %param.27) | copy-start | bytes 9437188
  27.7 20.0 %copy-start.12 = (bf16[768,1536]{1,0:T(8,128)(2,1)S(1)}, bf16[768,1536]{1,0:T(8,128)(2,1)}, u32[]{:S(2)}) copy-start(bf16[768,1536]{1,0:T(8,128)(2,1)} %weight_ref.1) | copy-start | bytes 7077892
  27.7 20.0 %copy-start.15 = (bf16[1536,768]{1,0:T(8,128)(2,1)S(1)}, bf16[1536,768]{1,0:T(8,128)(2,1)}, u32[]{:S(2)}) copy-start(bf16[1536,768]{1,0:T(8,128)(2,1)} %gate_w.3) | copy-start | bytes 7077892
  38.4 38.6 %copy-start.4 = (f32[1024,256]{1,0:T(8,128)}, f32[1024,256]{1,0:T(8,128)S(1)}, u32[]{:S(2)}) copy-start(f32[1024,256]{1,0:T(8,128)S(1)} %get-tuple-element.176.rows_ref.refs_2_.refs_8_) | copy-start | bytes 3145732
  38.5 38.6 %copy-start.7 = (f32[1024,128]{1,0:T(8,128)}, f32[1024,128]{1,0:T(8,128)S(1)}, u32[]{:S(2)}) copy-start(f32[1024,128]{1,0:T(8,128)S(1)} %get-tuple-element.177.cum_ref.refs_3_.refs_6_) | copy-start | bytes 1572868
  38.5 50.3 %copy-start.3 = (f32[1024,768]{1,0:T(8,128)}, f32[1024,768]{1,0:T(8,128)S(1)}, u32[]{:S(2)}) copy-start(f32[1024,768]{1,0:T(8,128)S(1)} %get-tuple-element.174.conv_ref.refs_0_) | copy-start | bytes 9437188
  38.5 20.2 %collective-permute-start.4 = (f32[136,768]{1,0:T(8,128)S(1)}, f32[136,768]{1,0:T(8,128)S(1)}, u32[]{:S(2)}, u32[]{:S(2)}) collective-permute-start(f32[136,768]{1,0:T(8,128)S(1)} %get-tuple-element.180.own_ref), channel_id=1, source_target_pairs={{0,12},{1,13},{2,14},{3,15},{16,28},{17,29},{18,30},{19,31}} | collective-permute-start | bytes 1253384 | tf_op jit(solution)/shard_map/ppermute | solution.py:845
  43.9 18.2 %collective-permute-start.3 = (f32[136,768]{1,0:T(8,128)S(1)}, f32[136,768]{1,0:T(8,128)S(1)}, u32[]{:S(2)}, u32[]{:S(2)}) collective-permute-start(f32[136,768]{1,0:T(8,128)S(1)} %get-tuple-element.180.own_ref), channel_id=1, source_target_pairs={{0,8},{4,12},{1,9},{5,13},{2,10},{6,14},{3,11},{7,15},{16,24},{20,... | collective-permute-start | bytes 1253384 | tf_op jit(solution)/shard_map/ppermute | solution.py:845
  45.2 16.9 %collective-permute-start.2 = (f32[136,768]{1,0:T(8,128)S(1)}, f32[136,768]{1,0:T(8,128)S(1)}, u32[]{:S(2)}, u32[]{:S(2)}) collective-permute-start(f32[136,768]{1,0:T(8,128)S(1)} %get-tuple-element.180.own_ref), channel_id=1, source_target_pairs={{0,4},{4,8},{8,12},{1,5},{5,9},{9,13},{2,6},{6,10},{10,14},{3,7},{... | collective-permute-start | bytes 1253384 | tf_op jit(solution)/shard_map/ppermute | solution.py:845
  67.7 17.1 %copy-start.10 = (f32[1024,768]{1,0:T(8,128)}, f32[1024,768]{1,0:T(8,128)S(1)}, u32[]{:S(2)}) copy-start(f32[1024,768]{1,0:T(8,128)S(1)} %get-tuple-element.188.mixed_ref.refs_2_) | copy-start | bytes 9437188
  67.7 17.1 %copy-start.32 = (f32[128,768]{1,0:T(8,128)}, f32[128,768]{1,0:T(8,128)S(1)}, u32[]{:S(2)}) copy-start(f32[128,768]{1,0:T(8,128)S(1)} %get-tuple-element.211.refs_10_) | copy-start | bytes 1179652
  67.7 5.2 %collective-permute-start.8 = (f32[8,1024]{1,0:T(8,128)S(1)}, f32[8,1024]{1,0:T(8,128)S(1)}, u32[]{:S(2)}, u32[]{:S(2)}) collective-permute-start(f32[8,1024]{1,0:T(8,128)S(1)} %get-tuple-element.189.refs_0_), channel_id=1, source_target_pairs={{0,3},{1,0},{2,1},{3,2},{4,7},{5,4},{6,5},{7,6},{8,11},{9,8},{10,9... | collective-permute-start | bytes 98312 | tf_op jit(solution)/shard_map/ppermute | solution.py:855
  71.3 4.8 %collective-permute-start.7 = (f32[8,1024]{1,0:T(8,128)S(1)}, f32[8,1024]{1,0:T(8,128)S(1)}, u32[]{:S(2)}, u32[]{:S(2)}) collective-permute-start(f32[8,1024]{1,0:T(8,128)S(1)} %get-tuple-element.189.refs_0_), channel_id=1, source_target_pairs={{0,2},{1,3},{2,0},{3,1},{4,6},{5,7},{6,4},{7,5},{8,10},{9,11},{10,... | collective-permute-start | bytes 98312 | tf_op jit(solution)/shard_map/ppermute | solution.py:855
  71.3 5.7 %collective-permute-start.6 = (f32[8,1024]{1,0:T(8,128)S(1)}, f32[8,1024]{1,0:T(8,128)S(1)}, u32[]{:S(2)}, u32[]{:S(2)}) collective-permute-start(f32[8,1024]{1,0:T(8,128)S(1)} %get-tuple-element.189.refs_0_), channel_id=1, source_target_pairs={{0,1},{1,2},{2,3},{3,0},{4,5},{5,6},{6,7},{7,4},{8,9},{9,10},{10,1... | collective-permute-start | bytes 98312 | tf_op jit(solution)/shard_map/ppermute | solution.py:855
  84.8 21.0 %copy-start.40 = (f32[8,768]{1,0:T(8,128)}, f32[8,768]{1,0:T(8,128)S(1)}, u32[]{:S(2)}) copy-start(f32[8,768]{1,0:T(8,128)S(1)} %get-tuple-element.264.refs_5_) | copy-start | bytes 73732
  84.8 21.0 %collective-permute-start.11 = (f32[136,768]{1,0:T(8,128)S(1)}, f32[136,768]{1,0:T(8,128)S(1)}, u32[]{:S(2)}, u32[]{:S(2)}) collective-permute-start(f32[136,768]{1,0:T(8,128)S(1)} %get-tuple-element.195), channel_id=1, source_target_pairs={{12,0},{13,1},{14,2},{15,3},{28,16},{29,17},{30,18},{31,19}} | collective-permute-start | bytes 1253384 | tf_op jit(solution)/shard_map/ppermute | solution.py:850
  86.1 19.7 %collective-permute-start.10 = (f32[136,768]{1,0:T(8,128)S(1)}, f32[136,768]{1,0:T(8,128)S(1)}, u32[]{:S(2)}, u32[]{:S(2)}) collective-permute-start(f32[136,768]{1,0:T(8,128)S(1)} %get-tuple-element.195), channel_id=1, source_target_pairs={{8,0},{12,4},{9,1},{13,5},{10,2},{14,6},{11,3},{15,7},{24,16},{28,... | collective-permute-start | bytes 1253384 | tf_op jit(solution)/shard_map/ppermute | solution.py:850
  87.4 18.4 %collective-permute-start.9 = (f32[136,768]{1,0:T(8,128)S(1)}, f32[136,768]{1,0:T(8,128)S(1)}, u32[]{:S(2)}, u32[]{:S(2)}) collective-permute-start(f32[136,768]{1,0:T(8,128)S(1)} %get-tuple-element.195), channel_id=1, source_target_pairs={{4,0},{8,4},{12,8},{5,1},{9,5},{13,9},{6,2},{10,6},{14,10},{7,3},{... | collective-permute-start | bytes 1253384 | tf_op jit(solution)/shard_map/ppermute | solution.py:850
  107.4 211.5 %all-gather.2.cloned.1.call-start = ((), (), s32[]{:S(2)}) async-start(), calls=%async_computation.2 | async-start | bytes 2949120 | tf_op jit(solution)/shard_map/all_gather | solution.py:1534
  107.5 26.1 %collective-permute-start.13 = (bf16[1024,768]{1,0:T(8,128)(2,1)}, bf16[1024,768]{1,0:T(8,128)(2,1)}, u32[]{:S(2)}, u32[]{:S(2)}) collective-permute-start(bf16[1024,768]{1,0:T(8,128)(2,1)} %get-tuple-element.215.refs_19_.gate_ref), channel_id=1, source_target_pairs={{0,16},{16,0},{1,17},{17,1},{2,18},{18,2},{3,19},{19,3},{4,20},{20... | collective-permute-start | bytes 4718600 | tf_op jit(solution)/shard_map/ppermute | solution.py:863
  107.6 26.0 %collective-permute-start.14 = (bf16[1024,768]{1,0:T(8,128)(2,1)}, bf16[1024,768]{1,0:T(8,128)(2,1)}, u32[]{:S(2)}, u32[]{:S(2)}) collective-permute-start(bf16[1024,768]{1,0:T(8,128)(2,1)} %get-tuple-element.216.normed_ref.refs_21_), channel_id=1, source_target_pairs={{0,16},{16,0},{1,17},{17,1},{2,18},{18,2},{3,19},{19,3},{4,20},{20... | collective-permute-start | bytes 4718600 | tf_op jit(solution)/shard_map/ppermute | solution.py:863
  120.7 6.0 %collective-permute-start.12 = (f32[8,512]{1,0:T(8,128)S(1)}, f32[8,512]{1,0:T(8,128)S(1)}, u32[]{:S(2)}, u32[]{:S(2)}) collective-permute-start(f32[8,512]{1,0:T(8,128)S(1)} %get-tuple-element.207), channel_id=1, source_target_pairs={{4,0},{8,4},{12,8},{5,1},{9,5},{13,9},{6,2},{10,6},{14,10},{7,3},{... | collective-permute-start | bytes 49160 | tf_op jit(solution)/shard_map/ppermute | solution.py:850
  129.4 34.6 %collective-permute-start.15 = (f32[520,128]{1,0:T(8,128)}, f32[520,128]{1,0:T(8,128)S(1)}, u32[]{:S(2)}, u32[]{:S(2)}) collective-permute-start(f32[520,128]{1,0:T(8,128)} %get-tuple-element.218), channel_id=1, source_target_pairs={{0,1},{1,2},{2,3},{3,0},{4,5},{5,6},{6,7},{7,4},{8,9},{9,10},{10,1... | collective-permute-start | bytes 798728 | tf_op jit(solution)/shard_map/ppermute | solution.py:1488
  129.4 35.7 %collective-permute-start.16 = (f32[520,128]{1,0:T(8,128)}, f32[520,128]{1,0:T(8,128)S(1)}, u32[]{:S(2)}, u32[]{:S(2)}) collective-permute-start(f32[520,128]{1,0:T(8,128)} %get-tuple-element.219), channel_id=1, source_target_pairs={{0,2},{1,3},{2,0},{3,1},{4,6},{5,7},{6,4},{7,5},{8,10},{9,11},{10,... | collective-permute-start | bytes 798728 | tf_op jit(solution)/shard_map/ppermute | solution.py:1488
  130.6 34.5 %collective-permute-start.17 = (f32[520,128]{1,0:T(8,128)}, f32[520,128]{1,0:T(8,128)S(1)}, u32[]{:S(2)}, u32[]{:S(2)}) collective-permute-start(f32[520,128]{1,0:T(8,128)} %get-tuple-element.220), channel_id=1, source_target_pairs={{0,3},{1,0},{2,1},{3,2},{4,7},{5,4},{6,5},{7,6},{8,11},{9,8},{10,9... | collective-permute-start | bytes 798728 | tf_op jit(solution)/shard_map/ppermute | solution.py:1488
  133.6 31.6 %copy-start.9 = (f32[1024,256]{1,0:T(8,128)S(1)}, f32[1024,256]{1,0:T(8,128)}, u32[]{:S(2)}) copy-start(f32[1024,256]{1,0:T(8,128)} %copy-done.8) | copy-start | bytes 3145732
  133.6 31.6 %copy-start.29 = (bf16[1024,256]{1,0:T(8,128)(2,1)S(1)}, bf16[1024,256]{1,0:T(8,128)(2,1)}, u32[]{:S(2)}) copy-start(bf16[1024,256]{1,0:T(8,128)(2,1)} %copy-done.28) | copy-start | bytes 1572868
  133.6 31.6 %copy-start.34 = (f32[520,128]{1,0:T(8,128)S(1)}, f32[520,128]{1,0:T(8,128)}, u32[]{:S(2)}) copy-start(f32[520,128]{1,0:T(8,128)} %copy-done.33) | copy-start | bytes 798724
  162.6 6.7 %collective-permute-start.18 = (f32[8,768]{1,0:T(8,128)S(1)}, f32[8,768]{1,0:T(8,128)S(1)}, u32[]{:S(2)}, u32[]{:S(2)}) collective-permute-start(f32[8,768]{1,0:T(8,128)S(1)} %get-tuple-element.217), channel_id=1, source_target_pairs={{4,0},{8,4},{12,8},{5,1},{9,5},{13,9},{6,2},{10,6},{14,10},{7,3},{... | collective-permute-start | bytes 73736 | tf_op jit(solution)/shard_map/ppermute | solution.py:850
  169.3 3.5 %collective-permute-start.19 = (bf16[1024,768]{1,0:T(8,128)(2,1)S(1)}, bf16[1024,768]{1,0:T(8,128)(2,1)S(1)}, u32[]{:S(2)}, u32[]{:S(2)}) collective-permute-start(bf16[1024,768]{1,0:T(8,128)(2,1)S(1)} %shard_map.256.refs_2_.value_ref), channel_id=1, source_target_pairs={{0,16},{16,0},{1,17},{17,1},{2,18},{18,2},{3,19},{19,3},{4,20},{20... | collective-permute-start | bytes 4718600 | tf_op jit(solution)/shard_map/ppermute | solution.py:863
  169.4 64.7 %collective-permute-start.24 = (f32[768,384]{1,0:T(8,128)}, f32[768,384]{1,0:T(8,128)}, u32[]{:S(2)}, u32[]{:S(2)}) collective-permute-start(f32[768,384]{1,0:T(8,128)} %get-tuple-element.245), channel_id=1, source_target_pairs={{0,4},{4,0},{8,12},{12,8},{1,5},{5,1},{9,13},{13,9},{2,6},{6,2},{1... | collective-permute-start | bytes 3538952 | tf_op jit(solution)/shard_map/ppermute | solution.py:863
  172.4 61.7 %collective-permute-start.25 = (f32[768,384]{1,0:T(8,128)}, f32[768,384]{1,0:T(8,128)}, u32[]{:S(2)}, u32[]{:S(2)}) collective-permute-start(f32[768,384]{1,0:T(8,128)} %get-tuple-element.246), channel_id=1, source_target_pairs={{0,8},{4,12},{8,0},{12,4},{1,9},{5,13},{9,1},{13,5},{2,10},{6,14},... | collective-permute-start | bytes 3538952 | tf_op jit(solution)/shard_map/ppermute | solution.py:863
  172.4 12.7 %collective-permute-start.20 = (bf16[1024,128]{1,0:T(8,128)(2,1)S(1)}, bf16[1024,128]{1,0:T(8,128)(2,1)S(1)}, u32[]{:S(2)}, u32[]{:S(2)}) collective-permute-start(bf16[1024,128]{1,0:T(8,128)(2,1)S(1)} %get-tuple-element.226.narrow_ref.narrow_a), channel_id=1, source_target_pairs={{0,16},{16,0},{1,17},{17,1},{2,18},{18,2},{3,19},{19,3},{4,20},{20... | collective-permute-start | bytes 786440 | tf_op jit(solution)/shard_map/ppermute | solution.py:863
  182.1 58.6 %collective-permute-start.26 = (f32[384,384]{1,0:T(8,128)}, f32[384,384]{1,0:T(8,128)}, u32[]{:S(2)}, u32[]{:S(2)}) collective-permute-start(f32[384,384]{1,0:T(8,128)} %get-tuple-element.250), channel_id=1, source_target_pairs={{0,4},{4,0},{8,12},{12,8},{1,5},{5,1},{9,13},{13,9},{2,6},{6,2},{1... | collective-permute-start | bytes 1769480 | tf_op jit(solution)/shard_map/ppermute | solution.py:863
  185.1 55.7 %collective-permute-start.27 = (f32[384,384]{1,0:T(8,128)}, f32[384,384]{1,0:T(8,128)}, u32[]{:S(2)}, u32[]{:S(2)}) collective-permute-start(f32[384,384]{1,0:T(8,128)} %get-tuple-element.251), channel_id=1, source_target_pairs={{0,8},{4,12},{8,0},{12,4},{1,9},{5,13},{9,1},{13,5},{2,10},{6,14},... | collective-permute-start | bytes 1769480 | tf_op jit(solution)/shard_map/ppermute | solution.py:863
  197.3 31.4 %copy-start.36 = (f32[16,256]{1,0:T(8,128)}, f32[16,256]{1,0:T(8,128)S(1)}, u32[]{:S(2)}) copy-start(f32[16,256]{1,0:T(8,128)S(1)} %shard_map.259.refs_0_) | copy-start | bytes 49156
  197.3 21.4 %collective-permute-start.23 = (f32[16,256]{1,0:T(8,128)S(1)}, f32[16,256]{1,0:T(8,128)S(1)}, u32[]{:S(2)}, u32[]{:S(2)}) collective-permute-start(f32[16,256]{1,0:T(8,128)S(1)} %shard_map.259.refs_0_), channel_id=1, source_target_pairs={{0,3},{1,0},{2,1},{3,2},{4,7},{5,4},{6,5},{7,6},{8,11},{9,8},{10,9... | collective-permute-start | bytes 49160 | tf_op jit(solution)/shard_map/ppermute | solution.py:855
  218.7 7.4 %collective-permute-start.22 = (f32[16,256]{1,0:T(8,128)S(1)}, f32[16,256]{1,0:T(8,128)S(1)}, u32[]{:S(2)}, u32[]{:S(2)}) collective-permute-start(f32[16,256]{1,0:T(8,128)S(1)} %shard_map.259.refs_0_), channel_id=1, source_target_pairs={{0,2},{1,3},{2,0},{3,1},{4,6},{5,7},{6,4},{7,5},{8,10},{9,11},{10,... | collective-permute-start | bytes 49160 | tf_op jit(solution)/shard_map/ppermute | solution.py:855
  226.1 6.7 %collective-permute-start.21 = (f32[16,256]{1,0:T(8,128)S(1)}, f32[16,256]{1,0:T(8,128)S(1)}, u32[]{:S(2)}, u32[]{:S(2)}) collective-permute-start(f32[16,256]{1,0:T(8,128)S(1)} %shard_map.259.refs_0_), channel_id=1, source_target_pairs={{0,1},{1,2},{2,3},{3,0},{4,5},{5,6},{6,7},{7,4},{8,9},{9,10},{10,1... | collective-permute-start | bytes 49160 | tf_op jit(solution)/shard_map/ppermute | solution.py:855
  232.7 23.6 %collective-permute-start.29 = (bf16[1024,384]{1,0:T(8,128)(2,1)S(1)}, bf16[1024,384]{1,0:T(8,128)(2,1)S(1)}, u32[]{:S(2)}, u32[]{:S(2)}) collective-permute-start(bf16[1024,384]{1,0:T(8,128)(2,1)S(1)} %shard_map.260), channel_id=1, source_target_pairs={{0,1},{3,2},{4,5},{7,6},{8,9},{11,10},{12,13},{15,14},{16,17},{19,... | collective-permute-start | bytes 2359304 | tf_op jit(solution)/shard_map/ppermute | solution.py:1517
  237.9 16.5 %collective-permute-start.30 = (f32[384,384]{1,0:T(8,128)}, f32[384,384]{1,0:T(8,128)S(1)}, u32[]{:S(2)}, u32[]{:S(2)}) collective-permute-start(f32[384,384]{1,0:T(8,128)} %get-tuple-element.269), channel_id=1, source_target_pairs={{0,8},{4,12},{8,0},{12,4},{1,9},{5,13},{9,1},{13,5},{2,10},{6,14},... | collective-permute-start | bytes 1769480 | tf_op jit(solution)/shard_map/ppermute | solution.py:863
  239.8 16.5 %collective-permute-start.31 = (f32[384,384]{1,0:T(8,128)}, f32[384,384]{1,0:T(8,128)S(1)}, u32[]{:S(2)}, u32[]{:S(2)}) collective-permute-start(f32[384,384]{1,0:T(8,128)} %get-tuple-element.270), channel_id=1, source_target_pairs={{0,4},{4,0},{8,12},{12,8},{1,5},{5,1},{9,13},{13,9},{2,6},{6,2},{1... | collective-permute-start | bytes 1769480 | tf_op jit(solution)/shard_map/ppermute | solution.py:863
  244.2 1.3 collective-permute-start.28
  244.3 14.6 %collective-permute-start.32 = (f32[192,384]{1,0:T(8,128)}, f32[192,384]{1,0:T(8,128)S(1)}, u32[]{:S(2)}, u32[]{:S(2)}) collective-permute-start(f32[192,384]{1,0:T(8,128)} %get-tuple-element.271), channel_id=1, source_target_pairs={{0,8},{4,12},{8,0},{12,4},{1,9},{5,13},{9,1},{13,5},{2,10},{6,14},... | collective-permute-start | bytes 884744 | tf_op jit(solution)/shard_map/ppermute | solution.py:863
  245.5 14.0 %collective-permute-start.33 = (f32[192,384]{1,0:T(8,128)}, f32[192,384]{1,0:T(8,128)S(1)}, u32[]{:S(2)}, u32[]{:S(2)}) collective-permute-start(f32[192,384]{1,0:T(8,128)} %get-tuple-element.272), channel_id=1, source_target_pairs={{0,4},{4,0},{8,12},{12,8},{1,5},{5,1},{9,13},{13,9},{2,6},{6,2},{1... | collective-permute-start | bytes 884744 | tf_op jit(solution)/shard_map/ppermute | solution.py:863
  264.0 18.4 %collective-permute-start.34 = (bf16[1024,384]{1,0:T(8,128)(2,1)}, bf16[1024,384]{1,0:T(8,128)(2,1)S(1)}, u32[]{:S(2)}, u32[]{:S(2)}) collective-permute-start(bf16[1024,384]{1,0:T(8,128)(2,1)} %copy-done.50), channel_id=1, source_target_pairs={{0,1},{1,2},{4,5},{5,6},{8,9},{9,10},{12,13},{13,14},{16,17},{17,1... | collective-permute-start | bytes 2359304 | tf_op jit(solution)/shard_map/ppermute | solution.py:929
  265.3 17.1 %collective-permute-start.35 = (bf16[1024,384]{1,0:T(8,128)(2,1)}, bf16[1024,384]{1,0:T(8,128)(2,1)S(1)}, u32[]{:S(2)}, u32[]{:S(2)}) collective-permute-start(bf16[1024,384]{1,0:T(8,128)(2,1)} %copy-done.49), channel_id=1, source_target_pairs={{3,2},{2,1},{7,6},{6,5},{11,10},{10,9},{15,14},{14,13},{19,18},{18... | collective-permute-start | bytes 2359304 | tf_op jit(solution)/shard_map/ppermute | solution.py:930
  266.1 16.3 %collective-permute-start.36 = (f32[288,384]{1,0:T(8,128)}, f32[288,384]{1,0:T(8,128)S(1)}, u32[]{:S(2)}, u32[]{:S(2)}) collective-permute-start(f32[288,384]{1,0:T(8,128)} %copy-done.51), channel_id=1, source_target_pairs={{0,4},{4,0},{8,12},{12,8},{1,5},{5,1},{9,13},{13,9},{2,6},{6,2},{1... | collective-permute-start | bytes 1327112 | tf_op jit(solution)/shard_map/ppermute | solution.py:863
  283.5 14.2 %collective-permute-start.37 = (f32[144,384]{1,0:T(8,128)S(1)}, f32[144,384]{1,0:T(8,128)S(1)}, u32[]{:S(2)}, u32[]{:S(2)}) collective-permute-start(f32[144,384]{1,0:T(8,128)S(1)} %get-tuple-element.303), channel_id=1, source_target_pairs={{0,8},{4,12},{8,0},{12,4},{1,9},{5,13},{9,1},{13,5},{2,10},{6,14},... | collective-permute-start | bytes 663560 | tf_op jit(solution)/shard_map/ppermute | solution.py:863
  288.4 19.2 %collective-permute-start.38 = (bf16[1024,384]{1,0:T(8,128)(2,1)}, bf16[1024,384]{1,0:T(8,128)(2,1)S(1)}, u32[]{:S(2)}, u32[]{:S(2)}) collective-permute-start(bf16[1024,384]{1,0:T(8,128)(2,1)} %get-tuple-element.299), channel_id=1, source_target_pairs={{0,1},{1,2},{2,3},{4,5},{5,6},{6,7},{8,9},{9,10},{10,11},{12,13},{... | collective-permute-start | bytes 2359304 | tf_op jit(solution)/shard_map/ppermute | solution.py:929
  293.7 17.9 %collective-permute-start.39 = (bf16[1024,384]{1,0:T(8,128)(2,1)}, bf16[1024,384]{1,0:T(8,128)(2,1)S(1)}, u32[]{:S(2)}, u32[]{:S(2)}) collective-permute-start(bf16[1024,384]{1,0:T(8,128)(2,1)} %get-tuple-element.300), channel_id=1, source_target_pairs={{3,2},{2,1},{1,0},{7,6},{6,5},{5,4},{11,10},{10,9},{9,8},{15,14},{... | collective-permute-start | bytes 2359304 | tf_op jit(solution)/shard_map/ppermute | solution.py:930
  298.4 14.4 %collective-permute-start.42 = (bf16[512,384]{1,0:T(8,128)(2,1)S(1)}, bf16[512,384]{1,0:T(8,128)(2,1)S(1)}, u32[]{:S(2)}, u32[]{:S(2)}) collective-permute-start(bf16[512,384]{1,0:T(8,128)(2,1)S(1)} %pad_maximum_fusion.refs_0_), channel_id=1, source_target_pairs={{0,12},{4,8},{8,4},{12,0},{1,13},{5,9},{9,5},{13,1},{2,14},{6,10},... | collective-permute-start | bytes 1179656 | tf_op jit(solution)/shard_map/ppermute | solution.py:863
  298.4 20.5 %collective-permute-start.41 = (bf16[512,384]{1,0:T(8,128)(2,1)S(1)}, bf16[512,384]{1,0:T(8,128)(2,1)S(1)}, u32[]{:S(2)}, u32[]{:S(2)}) collective-permute-start(bf16[512,384]{1,0:T(8,128)(2,1)S(1)} %pad_maximum_fusion.refs_0_), channel_id=1, source_target_pairs={{0,8},{4,12},{8,0},{12,4},{1,9},{5,13},{9,1},{13,5},{2,10},{6,14},... | collective-permute-start | bytes 1179656 | tf_op jit(solution)/shard_map/ppermute | solution.py:863
  299.3 19.6 %collective-permute-start.40 = (bf16[512,384]{1,0:T(8,128)(2,1)S(1)}, bf16[512,384]{1,0:T(8,128)(2,1)S(1)}, u32[]{:S(2)}, u32[]{:S(2)}) collective-permute-start(bf16[512,384]{1,0:T(8,128)(2,1)S(1)} %pad_maximum_fusion.refs_0_), channel_id=1, source_target_pairs={{0,4},{4,0},{8,12},{12,8},{1,5},{5,1},{9,13},{13,9},{2,6},{6,2},{1... | collective-permute-start | bytes 1179656 | tf_op jit(solution)/shard_map/ppermute | solution.py:863
  319.0 6.9 %collective-permute-start.43 = (bf16[3072,384]{1,0:T(8,128)(2,1)}, bf16[3072,384]{1,0:T(8,128)(2,1)S(1)}, u32[]{:S(2)}, u32[]{:S(2)}) collective-permute-start(bf16[3072,384]{1,0:T(8,128)(2,1)} %all-gather.2.cloned.1.call-done.here), channel_id=1, source_target_pairs={{0,16},{16,0},{1,17},{17,1},{2,18},{18,2},{3,19},{19,3},{4,20},{20... | collective-permute-start | bytes 7077896 | tf_op jit(solution)/shard_map/ppermute | solution.py:863
  320.1 10.1 %collective-permute-start.44 = (bf16[2048,384]{1,0:T(8,128)(2,1)}, bf16[2048,384]{1,0:T(8,128)(2,1)S(1)}, u32[]{:S(2)}, u32[]{:S(2)}) collective-permute-start(bf16[2048,384]{1,0:T(8,128)(2,1)} %shard_map.270.here), channel_id=1, source_target_pairs={{0,16},{16,0},{1,17},{17,1},{2,18},{18,2},{3,19},{19,3},{4,20},{20... | collective-permute-start | bytes 4718600 | tf_op jit(solution)/shard_map/ppermute | solution.py:863
  (45 other events, 312.4 us)
Sparse Core Ops, SparseCore 0:
  107.6 129.9 reduce-scatter.1
Sparse Core Ops, SparseCore 1:
  264.1 50.5 all-gather.1

commit v5 on v4

--- a/solution.py
+++ b/solution.py
@@ -1532,12 +1532,12 @@
     value_chunk = summed(value_stay, *after(sent, (first_got, second_got)))
     wide_chunk = summed(wide_stay, *after(value_chunk, (gate_got, out_got)))
     wide_here = lax.all_gather(wide_chunk, "ctx", tiled=True)
-    moving, narrow_got = lax.optimization_barrier(after(wide_chunk, (moving, narrow_got)))
+    output = (resid_part + after(wide_chunk, branch)).astype(bf16)
+    moving, narrow_got, output = lax.optimization_barrier(after(wide_chunk, (moving, narrow_got, output)))
     narrow_stay, narrow_away = pair_sums(narrow_keep, narrow_got)
     narrow_got = swapped(narrow_away, "ctx", 2)
     sent, moving = line_step(parts, 3, after(narrow_stay, moving), "tensor")
-    output = (resid_part + after(sent, branch)).astype(bf16)
-    narrow_total = over_dp(narrow_stay + after(output, narrow_got))
+    narrow_total = over_dp(narrow_stay + after(sent, narrow_got))
     chunk = jnp.concatenate([value_chunk, narrow_total[:LANES].astype(bf16)], axis=0)
     chunks = [swapped(chunk, "ctx", k) for k in range(1, ctx_size)]
     small_total = narrow_total[LANES:]
@@ -1554,13 +1554,14 @@
     at += gain_rows
     taps_grad = small_total[at : at + CONV * state2 // LANES].reshape(CONV, state2)
     smalls = (pre_gain_grad, kernel_grad, taps_grad, small[1], small[2], small[0], gain_grad)
-    moving, chunks, smalls = lax.optimization_barrier((moving, chunks, smalls))
+    moving, smalls = lax.optimization_barrier((moving, smalls))
+    input_grad = final(place, parts, moving, residual, cotangent, row(pre_gain), sums)
+    chunks = lax.optimization_barrier(after(input_grad, chunks))
     narrow_here = joined(chunk, *chunks)
     narrow_there = swapped(narrow_here, "dp", 1)
     wide_here = after(chunks, wide_here)
     wide_there = swapped(wide_here, "dp", 1)
-    input_grad = final(place, parts, after(narrow_here, moving), residual, cotangent, row(pre_gain), sums)
-    gate_weight_grad, out_weight_grad = wide_together(after(input_grad, plan), ctx_size, wide_here, wide_there)
+    gate_weight_grad, out_weight_grad = wide_together(after(narrow_here, plan), ctx_size, wide_here, wide_there)
     input_weight_grad, state_weight_grad, step_weight_grad = narrow_together(
         plan, ctx_size, narrow_here, after(gate_weight_grad, narrow_there), state_part, head_count
     )

time: 343 us -> 341 us (level)
    ppermute x22, waiting for transfers between devices: 29.4 us -> 24.5 us  [swapped(): lax.ppermute(value, axis, [(i, i ^ flip) for i in range(lax.axis_size(axi...]
where the time goes in v5:
time: 341 us; the launch traced here: 339 us
  Pallas kernels  157 us (46%)
  starting transfers between devices  81.1 us (24%)
  waiting for transfers between devices  62.3 us (18%)
  local copies, waits for them, and re-layouts  18.8 us (6%)
  between operations  16.3 us (5%)
    pallas_call x11, Pallas kernels, scalar_call(): pl.pallas_call(body, grid_spec=pltpu.PrefetchScalarGridSpec(num_scalar_pr...  70 us
    ppermute x6, starting transfers between devices, from_all(): lax.ppermute(value, axis, [(i, (i + by) % count) for i in range(count)])  26.5 us
    ppermute x22, waiting for transfers between devices, swapped(): lax.ppermute(value, axis, [(i, i ^ flip) for i in range(lax.axis_size(axi...  24.5 us
    ppermute x22, starting transfers between devices, swapped(): lax.ppermute(value, axis, [(i, i ^ flip) for i in range(lax.axis_size(axi...  19.7 us
    pallas_call x1, Pallas kernels, inner_back(): pl.pallas_call(body, grid=(first + tokens // BLOCK,), in_specs=[early(inn...  17.1 us
    ppermute x6, waiting for transfers between devices, from_all(): lax.ppermute(value, axis, [(i, (i + by) % count) for i in range(count)])  16.8 us
    ppermute x4, starting transfers between devices, from_before(): return lax.ppermute(value, axis, [(i, i + by) for i in range(count - by)])  14 us
    unnamed x124, local copies, waits for them, and re-layouts  13.1 us
  transfers between devices with their start and end apart: 47, of which 21 were waited for; matrix products, arithmetic and copies ran while one was open for 3% of the time, Pallas kernels for 43%

profile of v5, /device:TPU:0, one launch (start us, length us, event | category | flops | bytes accessed | tf_op | source)
XLA Modules:
  0.0 338.8 jit_solution(950374680376625256)
XLA Ops:
  9.3 1.9 copy-done
  11.2 1.7 copy-done.13
  14.8 6.2 %shard_map.245 = (bf16[1024,1536]{1,0:T(8,128)(2,1)}, bf16[1024,768]{1,0:T(8,128)(2,1)S(1)}, bf16[1024,256]{1,0:T(8,128)(2,1)S(1)}, f32[1024,128]{1,0:T(8,128)S(1)}) custom-call(bf16[1024,1536]{1,0:T(8,128)(2,1)S(1)} %bitcast.36, f32[1,1536]{1,0:T(1,128)S(1)} %reshape.72.gain_ref, bf16[1536,768]{1,0:T(8,128)(2,1)S(1)} %copy-done.13, ...), custom_call_target="tpu_custom_call" | custom-call | flops 5400000000 | bytes 18000000 | tf_op jit(solution)/shard_map/pallas_call | solution.py:151
  21.1 4.8 %collective-permute-start = (bf16[16,1536]{1,0:T(8,128)(2,1)S(1)}, bf16[16,1536]{1,0:T(8,128)(2,1)S(1)}, u32[]{:S(2)}, u32[]{:S(2)}) collective-permute-start(bf16[16,1536]{1,0:T(8,128)(2,1)S(1)} %slice_bitcast_fusion), channel_id=1, source_target_pairs={{0,4},{4,8},{8,12},{1,5},{5,9},{9,13},{2,6},{6,10},{10,14},{3,7},{... | collective-permute-start | bytes 147464 | tf_op jit(solution)/shard_map/ppermute | solution.py:845
  26.0 1.7 collective-permute-done.halo_ref
  27.8 10.6 %shard_map.246 = (f32[1024,768]{1,0:T(8,128)S(1)}, f32[1024,768]{1,0:T(8,128)}, f32[1024,256]{1,0:T(8,128)S(1)}, f32[1024,256]{1,0:T(8,128)S(1)}, f32[1024,128]{...) custom-call(bf16[1024,768]{1,0:T(8,128)(2,1)S(1)} %get-tuple-element, ...), custom_call_target="tpu_custom_call" | custom-call | flops 8999999488 | bytes 30000000 | tf_op jit(solution)/shard_map/pallas_call | solution.py:271
  38.5 5.4 %collective-permute-start.4 = (f32[136,768]{1,0:T(8,128)S(1)}, f32[136,768]{1,0:T(8,128)S(1)}, u32[]{:S(2)}, u32[]{:S(2)}) collective-permute-start(f32[136,768]{1,0:T(8,128)S(1)} %get-tuple-element.183.own_ref), channel_id=1, source_target_pairs={{0,12},{1,13},{2,14},{3,15},{16,28},{17,29},{18,30},{19,31}} | collective-permute-start | bytes 1253384 | tf_op jit(solution)/shard_map/ppermute | solution.py:845
  43.9 1.3 collective-permute-start.3
  45.2 2.5 collective-permute-start.2
  47.7 5.6 %shard_map.248 = (f32[1024,768]{1,0:T(8,128)S(1)}, f32[1024,768]{1,0:T(8,128)S(1)}) custom-call(bf16[1024,1536]{1,0:T(8,128)(2,1)S(1)} %copy-done.1, bf16[1536,768]{1,0:T(8,128)(2,1)S(1)} %copy-done.15, bf16[1024,1536]{1,0:T(8,128)(2,1)S(1)} %bitcast.40, bf16[768,1536]{1,0:T(8,128)(2,1)S(1)} %copy-done.12), custom_call_target="tpu_custom_call" | custom-call | flops 5400000000 | bytes 18000000 | tf_op jit(solution)/shard_map/pallas_call | solution.py:183
  53.3 5.4 %shard_map.247.intra_ref = f32[1024,768]{1,0:T(8,128)S(1)} custom-call(f32[1024,768]{1,0:T(8,128)S(1)} %get-tuple-element.177.conv_ref.refs_0_, f32[1024,128]{1,0:T(8,128)S(1)} %get-tuple-element.178.dt_ref.refs_1_.refs_5_, f32[1024,256]{1,0:T(8,128)S(1)} %get-tuple-element.179.rows_ref.refs_2_.refs_8_, ...), custom_call_target="tpu_custom_call" | custom-call | flops 5400000000 | bytes 18000000 | tf_op jit(solution)/shard_map/pallas_call | solution.py:351
  58.7 3.3 collective-permute-done.3.refs_1_
  62.1 5.7 %shard_map.249 = (f32[1024,768]{1,0:T(8,128)S(1)}, f32[8,1024]{1,0:T(8,128)S(1)}, f32[8,128,768]{2,1,0:T(8,128)}, f32[128,768]{1,0:T(8,128)S(1)}) custom-call(f32[1024,768]{1,0:T(8,128)S(1)} %shard_map.247.intra_ref, f32[1024,256]{1,0:T(8,128)S(1)} %get-tuple-element.179.rows_ref.refs_2_.refs_8_, f32[1024,128]{1,0:T(8,128)S(1)} %get-tuple-element.180.cum_ref.refs_3_.refs_6_, ...), custom_call_target="tpu_custom_call" | custom-call | flops 4499999744 | bytes 15000000 | tf_op jit(solution)/shard_map/pallas_call | solution.py:414
  67.7 3.6 %collective-permute-start.8 = (f32[8,1024]{1,0:T(8,128)S(1)}, f32[8,1024]{1,0:T(8,128)S(1)}, u32[]{:S(2)}, u32[]{:S(2)}) collective-permute-start(f32[8,1024]{1,0:T(8,128)S(1)} %get-tuple-element.192.refs_0_), channel_id=1, source_target_pairs={{0,3},{1,0},{2,1},{3,2},{4,7},{5,4},{6,5},{7,6},{8,11},{9,8},{10,9... | collective-permute-start | bytes 98312 | tf_op jit(solution)/shard_map/ppermute | solution.py:855
  72.9 3.2 collective-permute-done.7.refs_2_
  77.0 7.8 %shard_map.250 = (bf16[1024,768]{1,0:T(8,128)(2,1)}, bf16[1024,768]{1,0:T(8,128)(2,1)}, f32[1024,768]{1,0:T(8,128)}, f32[8,128,768]{2,1,0:T(8,128)}, f32[136,768]{1,0:T(8,128)S(1)}, /*index=5*/f32[8,768]{1,0:T(8,128)S(1)}) custom-call(f32[1024,768]{1,0:T(8,128)S(1)} %get-tuple-element.191.mixed_ref.refs_2_, ...), custom_call_target="tpu_custom_call" | custom-call | flops 6300000256 | bytes 21000000 | tf_op jit(solution)/shard_map/pallas_call | solution.py:501
  84.8 1.3 collective-permute-start.11
  86.1 1.3 collective-permute-start.10
  87.4 1.3 collective-permute-start.9
  88.7 17.1 %shard_map.251 = (f32[1024,1536]{1,0:T(8,128)}, f32[1024,768]{1,0:T(8,128)}, f32[1024,256]{1,0:T(8,128)}) custom-call(bf16[1024,768]{1,0:T(8,128)(2,1)} %get-tuple-element.219.normed_ref.refs_21_, bf16[768,1536]{1,0:T(8,128)(2,1)} %weight_ref.1, f32[1024,768]{1,0:T(8,128)S(1)} %get-tuple-element.177.conv_ref.refs_0_, f32[1024,128]{1,0:T(8,128)} %copy-done.6, ...), custom_call_target="tpu_custom_call" | custom-call | flops 900000000 | bytes 3000000 | tf_op jit(solution)/shard_map/pallas_call | solution.py:596
  108.1 12.6 %shard_map.252 = (f32[1024,256]{1,0:T(8,128)S(1)}, f32[8,128,768]{2,1,0:T(8,128)}, f32[8,512]{1,0:T(8,128)S(1)}) custom-call(f32[1024,256]{1,0:T(8,128)} %get-tuple-element.201.drows_ref, f32[1024,768]{1,0:T(8,128)} %get-tuple-element.211.refs_5_.dmix_ref.refs_1_, f32[1024,768]{1,0:T(8,128)} %copy-done.3, f32[1024,128]{1,0:T(8,128)} %copy-done.6, ...), custom_call_target="tpu_custom_call" | custom-call | tf_op jit(solution)/shard_map/pallas_call | solution.py:677
  120.7 1.3 collective-permute-start.12
  122.0 4.7 %collective-permute-done.12.ahead_ref.refs_7_ = f32[8,512]{1,0:T(8,128)S(1)} collective-permute-done((f32[8,512]{1,0:T(8,128)S(1)}, f32[8,512]{1,0:T(8,128)S(1)}, u32[]{:S(2)}, u32[]{:S(2)}) %collective-permute-start.12) | collective-permute-done | bytes 16416 | tf_op jit(solution)/shard_map/ppermute | solution.py:850
  126.7 2.0 shard_map.253
  130.6 2.9 collective-permute-start.17
  133.6 28.4 %shard_map.254 = (bf16[1024,768]{1,0:T(8,128)(2,1)S(1)}, bf16[1024,12]{1,0:T(8,128)(2,1)S(1)}, f32[16,768]{1,0:T(8,128)S(1)}, f32[8,768]{1,0:T(8,128)S(1)}, f32[...) custom-call(s32[3]{0:T(128)S(1)} %add_add_fusion.plan_ref, ...), custom_call_target="tpu_custom_call" | custom-call | tf_op jit(solution)/shard_map/pallas_call | solution.py:968
  162.6 1.4 collective-permute-start.18
  166.4 2.8 collective-permute-done.18.ahead_ref
  169.4 3.0 collective-permute-start.24
  172.8 7.7 %shard_map.257 = (f32[384,384]{1,0:T(8,128)S(1)}, f32[384,384]{1,0:T(8,128)}, f32[384,384]{1,0:T(8,128)S(1)}, f32[384,384]{1,0:T(8,128)}) custom-call(s32[3]{0:T(128)S(1)} %add_add_fusion.plan_ref, bf16[1024,1536]{1,0:T(8,128)(2,1)} %get-tuple-element.185.normed_ref.refs_17_.refs_0_.normed_a, bf16[1024,1536]{1,0:T(8,128)(2,1)} %copy-done.52, ...), custom_call_target="tpu_custom_call" | custom-call | tf_op jit(solution)/shard_map/pallas_call | solution.py:968
  182.1 3.0 collective-permute-start.26
  185.1 12.0 %shard_map.258 = (f32[4,1024,384]{2,1,0:T(8,128)}, f32[8,1024]{1,0:T(8,128)S(1)}, f32[8,1536]{1,0:T(8,128)S(1)}) custom-call(s32[1]{0:T(128)} %bitcast.2.plan_ref, bf16[1024,768]{1,0:T(8,128)(2,1)} %get-tuple-element.218.refs_19_.gate_ref, bf16[1024,768]{1,0:T(8,128)(2,1)S(1)} %shard_map.256.refs_2_.value_ref, ...), custom_call_target="tpu_custom_call" | custom-call | tf_op jit(solution)/shard_map/pallas_call | solution.py:968
  197.3 19.6 %collective-permute-start.23 = (f32[16,256]{1,0:T(8,128)S(1)}, f32[16,256]{1,0:T(8,128)S(1)}, u32[]{:S(2)}, u32[]{:S(2)}) collective-permute-start(f32[16,256]{1,0:T(8,128)S(1)} %shard_map.259.refs_0_), channel_id=1, source_target_pairs={{0,3},{1,0},{2,1},{3,2},{4,7},{5,4},{6,5},{7,6},{8,11},{9,8},{10,9... | collective-permute-start | bytes 49160 | tf_op jit(solution)/shard_map/ppermute | solution.py:855
  216.9 1.8 collective-permute-done.23.refs_3_
  219.7 6.3 %collective-permute-done.22.refs_2_ = f32[16,256]{1,0:T(8,128)S(1)} collective-permute-done((f32[16,256]{1,0:T(8,128)S(1)}, f32[16,256]{1,0:T(8,128)S(1)}, u32[]{:S(2)}, u32[]{:S(2)}) %collective-permute-start.22) | collective-permute-done | bytes 16416 | tf_op jit(solution)/shard_map/ppermute | solution.py:855
  227.3 1.4 shard_map.260
  228.7 4.0 %collective-permute-done.21.refs_1_ = f32[16,256]{1,0:T(8,128)S(1)} collective-permute-done((f32[16,256]{1,0:T(8,128)S(1)}, f32[16,256]{1,0:T(8,128)S(1)}, u32[]{:S(2)}, u32[]{:S(2)}) %collective-permute-start.21) | collective-permute-done | bytes 16416 | tf_op jit(solution)/shard_map/ppermute | solution.py:855
  232.7 1.3 collective-permute-start.29
  234.1 3.8 %shard_map.261 = (f32[768,384]{1,0:T(8,128)}, f32[384,384]{1,0:T(8,128)}, f32[384,384]{1,0:T(8,128)}) custom-call(f32[768,384]{1,0:T(8,128)} %copy-done.18, f32[768,384]{1,0:T(8,128)} %copy-done.19, f32[768,384]{1,0:T(8,128)} %collective-permute-done.24.got_a, f32[768,384]{1,0:T(8,128)} %collective-permute-done.25.got_b), custom_call_target="tpu_custom_call" | custom-call | tf_op jit(solution)/shard_map/pallas_call | solution.py:1288
  237.9 1.9 collective-permute-start.30
  240.7 2.6 shard_map.262
  246.8 5.0 %shard_map.264 = (f32[288,384]{1,0:T(8,128)S(1)}, f32[288,384]{1,0:T(8,128)S(1)}) custom-call(s32[3]{0:T(128)S(1)} %add_add_fusion.plan_ref, bf16[1024,1536]{1,0:T(8,128)(2,1)} %get-tuple-element.185.normed_ref.refs_17_.refs_0_.normed_a, bf16[1024,1536]{1,0:T(8,128)(2,1)} %copy-done.52, bf16[1024,128]{1,0:T(8,128)(2,1)S(1)} %get-tuple-element.231.narrow_ref.narrow_a, ...), custom_call_target="tpu_custom_call" | custom-call | tf_op jit(solution)/shard_map/pallas_call | solution.py:968
  254.4 1.9 collective-permute-done.31.got_b
  256.3 2.6 collective-permute-done.32.got_a
  259.5 2.6 shard_map.265
  264.0 1.5 collective-permute-start.34
  266.2 1.6 collective-permute-start.36
  267.8 2.8 fusion
  270.6 11.9 %collective-permute-done.36.got_ref = f32[288,384]{1,0:T(8,128)S(1)} collective-permute-done((f32[288,384]{1,0:T(8,128)}, f32[288,384]{1,0:T(8,128)S(1)}, u32[]{:S(2)}, u32[]{:S(2)}) %collective-permute-start.36) | collective-permute-done | bytes 442400 | tf_op jit(solution)/shard_map/ppermute | solution.py:863
  282.5 1.5 collective-permute-start.39
  284.1 3.4 shard_map.269
  287.4 5.4 %collective-permute-start.37 = (bf16[1024,384]{1,0:T(8,128)(2,1)}, bf16[1024,384]{1,0:T(8,128)(2,1)S(1)}, u32[]{:S(2)}, u32[]{:S(2)}) collective-permute-start(bf16[1024,384]{1,0:T(8,128)(2,1)} %get-tuple-element.306), channel_id=1, source_target_pairs={{0,1},{1,2},{2,3},{4,5},{5,6},{6,7},{8,9},{9,10},{10,11},{12,13},{... | collective-permute-start | bytes 2359304 | tf_op jit(solution)/shard_map/ppermute | solution.py:929
  292.9 1.3 collective-permute-start.38
  295.7 2.7 collective-permute-start.40
  299.6 1.3 slice_bitcast_fusion.2
  300.9 1.3 slice_bitcast_fusion.3
  302.1 1.3 slice_bitcast_fusion.1
  303.4 3.2 collective-permute-done.37.up_ref
  306.6 4.1 %collective-permute-done.38.down_ref = bf16[1024,384]{1,0:T(8,128)(2,1)S(1)} collective-permute-done((bf16[1024,384]{1,0:T(8,128)(2,1)}, bf16[1024,384]{1,0:T(8,128)(2,1)S(1)}, u32[]{:S(2)}, u32[]{:S(2)}) %collective-permute-start.38) | collective-permute-done | bytes 786464 | tf_op jit(solution)/shard_map/ppermute | solution.py:930
  310.7 5.0 %shard_map.270 = f32[1024,384]{1,0:T(8,128)} custom-call(s32[1]{0:T(128)} %bitcast.2.plan_ref, f32[4,1024,384]{2,1,0:T(8,128)} %get-tuple-element.241.part_ref.up_ref.down_ref, bf16[1024,384]{1,0:T(8,128)(2,1)S(1)} %collective-permute-done.37.up_ref, bf16[1024,384]{1,0:T(8,128)(2,1)S(1)} %collective-permute-done.38.down_ref, bf16[1024,1536]{1,0:T(8,128)(2,1)} %bitcast.34, ...), custom_call_target="tpu_custom_call" | custom-call | tf_op jit(solution)/shard_map/pallas_call | solution.py:968
  315.7 3.2 collective-permute-done.41.refs_2_
  320.7 3.0 collective-permute-done.43.there
  323.7 4.4 %shard_map.272 = (f32[1536,768]{1,0:T(8,128)}, f32[768,1536]{1,0:T(8,128)}) custom-call(s32[3]{0:T(128)S(1)} %add_add_fusion.plan_ref, bf16[3072,384]{1,0:T(8,128)(2,1)S(1)} %copy-done.11, bf16[3072,384]{1,0:T(8,128)(2,1)S(1)} %collective-permute-done.43.there), custom_call_target="tpu_custom_call" | custom-call | tf_op jit(solution)/shard_map/pallas_call | solution.py:968
  328.1 3.3 shard_map.273
  (204 shorter events, 32.4 us)
Async XLA Ops:
  8.0 259.7 %reduce-scatter.2.cloned.1.call-start = ((), (), s32[]{:S(2)}) async-start(), calls=%async_computation.1 | async-start | bytes 7864320 | tf_op jit(solution)/shard_map/reduce_scatter | solution.py:1481
  8.1 54.0 %collective-permute-start.1 = (bf16[1024,1536]{1,0:T(8,128)(2,1)}, bf16[1024,1536]{1,0:T(8,128)(2,1)S(1)}, u32[]{:S(2)}, u32[]{:S(2)}) collective-permute-start(bf16[1024,1536]{1,0:T(8,128)(2,1)} %bitcast.37), channel_id=1, source_target_pairs={{0,16},{16,0},{1,17},{17,1},{2,18},{18,2},{3,19},{19,3},{4,20},{20... | collective-permute-start | bytes 9437192 | tf_op jit(solution)/shard_map/ppermute | solution.py:863
  21.0 17.4 %copy-start.17 = (bf16[1024,768]{1,0:T(8,128)(2,1)}, bf16[1024,768]{1,0:T(8,128)(2,1)S(1)}, u32[]{:S(2)}) copy-start(bf16[1024,768]{1,0:T(8,128)(2,1)S(1)} %get-tuple-element.174.value_ref.refs_4_) | copy-start | bytes 4718596
  21.0 17.4 %copy-start.27 = (f32[1024,128]{1,0:T(8,128)}, f32[1024,128]{1,0:T(8,128)S(1)}, u32[]{:S(2)}) copy-start(f32[1024,128]{1,0:T(8,128)S(1)} %get-tuple-element.176.step_ref.refs_7_) | copy-start | bytes 1572868
  21.0 17.4 %copy-start.28 = (bf16[1024,256]{1,0:T(8,128)(2,1)}, bf16[1024,256]{1,0:T(8,128)(2,1)S(1)}, u32[]{:S(2)}) copy-start(bf16[1024,256]{1,0:T(8,128)(2,1)S(1)} %get-tuple-element.175.state_ref.refs_5_) | copy-start | bytes 1572868
  21.0 51.3 %collective-permute-start.5 = (bf16[1024,1536]{1,0:T(8,128)(2,1)}, bf16[1024,1536]{1,0:T(8,128)(2,1)S(1)}, u32[]{:S(2)}, u32[]{:S(2)}) collective-permute-start(bf16[1024,1536]{1,0:T(8,128)(2,1)} %get-tuple-element.185.normed_ref.refs_17_.refs_0_.normed_a), channel_id=1, source_target_pairs={{0,16},{16,0},{1,17},{17,1},{2,18},{18,2},{3,19},{19,3},{4,20},{20... | collective-permute-start | bytes 9437192 | tf_op jit(solution)/shard_map/ppermute | solution.py:863
  21.1 6.6 %collective-permute-start = (bf16[16,1536]{1,0:T(8,128)(2,1)S(1)}, bf16[16,1536]{1,0:T(8,128)(2,1)S(1)}, u32[]{:S(2)}, u32[]{:S(2)}) collective-permute-start(bf16[16,1536]{1,0:T(8,128)(2,1)S(1)} %slice_bitcast_fusion), channel_id=1, source_target_pairs={{0,4},{4,8},{8,12},{1,5},{5,9},{9,13},{2,6},{6,10},{10,14},{3,7},{... | collective-permute-start | bytes 147464 | tf_op jit(solution)/shard_map/ppermute | solution.py:845
  27.7 20.0 %copy-start.1 = (bf16[1024,1536]{1,0:T(8,128)(2,1)S(1)}, bf16[1024,1536]{1,0:T(8,128)(2,1)}, u32[]{:S(2)}) copy-start(bf16[1024,1536]{1,0:T(8,128)(2,1)} %get-tuple-element.185.normed_ref.refs_17_.refs_0_.normed_a) | copy-start | bytes 9437188
  27.7 20.0 %copy-start.2 = (bf16[1,1024,1536]{2,1,0:T(8,128)(2,1)S(1)}, bf16[1,1024,1536]{2,1,0:T(8,128)(2,1)}, u32[]{:S(2)}) copy-start(bf16[1,1024,1536]{2,1,0:T(8,128)(2,1)} %param.27) | copy-start | bytes 9437188
  27.7 20.0 %copy-start.12 = (bf16[768,1536]{1,0:T(8,128)(2,1)S(1)}, bf16[768,1536]{1,0:T(8,128)(2,1)}, u32[]{:S(2)}) copy-start(bf16[768,1536]{1,0:T(8,128)(2,1)} %weight_ref.1) | copy-start | bytes 7077892
  27.7 20.0 %copy-start.15 = (bf16[1536,768]{1,0:T(8,128)(2,1)S(1)}, bf16[1536,768]{1,0:T(8,128)(2,1)}, u32[]{:S(2)}) copy-start(bf16[1536,768]{1,0:T(8,128)(2,1)} %gate_w.3) | copy-start | bytes 7077892
  38.4 38.6 %copy-start.4 = (f32[1024,256]{1,0:T(8,128)}, f32[1024,256]{1,0:T(8,128)S(1)}, u32[]{:S(2)}) copy-start(f32[1024,256]{1,0:T(8,128)S(1)} %get-tuple-element.179.rows_ref.refs_2_.refs_8_) | copy-start | bytes 3145732
  38.5 38.6 %copy-start.7 = (f32[1024,128]{1,0:T(8,128)}, f32[1024,128]{1,0:T(8,128)S(1)}, u32[]{:S(2)}) copy-start(f32[1024,128]{1,0:T(8,128)S(1)} %get-tuple-element.180.cum_ref.refs_3_.refs_6_) | copy-start | bytes 1572868
  38.5 50.3 %copy-start.3 = (f32[1024,768]{1,0:T(8,128)}, f32[1024,768]{1,0:T(8,128)S(1)}, u32[]{:S(2)}) copy-start(f32[1024,768]{1,0:T(8,128)S(1)} %get-tuple-element.177.conv_ref.refs_0_) | copy-start | bytes 9437188
  38.5 20.2 %collective-permute-start.4 = (f32[136,768]{1,0:T(8,128)S(1)}, f32[136,768]{1,0:T(8,128)S(1)}, u32[]{:S(2)}, u32[]{:S(2)}) collective-permute-start(f32[136,768]{1,0:T(8,128)S(1)} %get-tuple-element.183.own_ref), channel_id=1, source_target_pairs={{0,12},{1,13},{2,14},{3,15},{16,28},{17,29},{18,30},{19,31}} | collective-permute-start | bytes 1253384 | tf_op jit(solution)/shard_map/ppermute | solution.py:845
  43.9 18.2 %collective-permute-start.3 = (f32[136,768]{1,0:T(8,128)S(1)}, f32[136,768]{1,0:T(8,128)S(1)}, u32[]{:S(2)}, u32[]{:S(2)}) collective-permute-start(f32[136,768]{1,0:T(8,128)S(1)} %get-tuple-element.183.own_ref), channel_id=1, source_target_pairs={{0,8},{4,12},{1,9},{5,13},{2,10},{6,14},{3,11},{7,15},{16,24},{20,... | collective-permute-start | bytes 1253384 | tf_op jit(solution)/shard_map/ppermute | solution.py:845
  45.2 16.9 %collective-permute-start.2 = (f32[136,768]{1,0:T(8,128)S(1)}, f32[136,768]{1,0:T(8,128)S(1)}, u32[]{:S(2)}, u32[]{:S(2)}) collective-permute-start(f32[136,768]{1,0:T(8,128)S(1)} %get-tuple-element.183.own_ref), channel_id=1, source_target_pairs={{0,4},{4,8},{8,12},{1,5},{5,9},{9,13},{2,6},{6,10},{10,14},{3,7},{... | collective-permute-start | bytes 1253384 | tf_op jit(solution)/shard_map/ppermute | solution.py:845
  67.7 17.1 %copy-start.32 = (f32[128,768]{1,0:T(8,128)}, f32[128,768]{1,0:T(8,128)S(1)}, u32[]{:S(2)}) copy-start(f32[128,768]{1,0:T(8,128)S(1)} %get-tuple-element.213.refs_10_) | copy-start | bytes 1179652
  67.7 5.2 %collective-permute-start.8 = (f32[8,1024]{1,0:T(8,128)S(1)}, f32[8,1024]{1,0:T(8,128)S(1)}, u32[]{:S(2)}, u32[]{:S(2)}) collective-permute-start(f32[8,1024]{1,0:T(8,128)S(1)} %get-tuple-element.192.refs_0_), channel_id=1, source_target_pairs={{0,3},{1,0},{2,1},{3,2},{4,7},{5,4},{6,5},{7,6},{8,11},{9,8},{10,9... | collective-permute-start | bytes 98312 | tf_op jit(solution)/shard_map/ppermute | solution.py:855
  71.3 4.8 %collective-permute-start.7 = (f32[8,1024]{1,0:T(8,128)S(1)}, f32[8,1024]{1,0:T(8,128)S(1)}, u32[]{:S(2)}, u32[]{:S(2)}) collective-permute-start(f32[8,1024]{1,0:T(8,128)S(1)} %get-tuple-element.192.refs_0_), channel_id=1, source_target_pairs={{0,2},{1,3},{2,0},{3,1},{4,6},{5,7},{6,4},{7,5},{8,10},{9,11},{10,... | collective-permute-start | bytes 98312 | tf_op jit(solution)/shard_map/ppermute | solution.py:855
  71.3 5.7 %collective-permute-start.6 = (f32[8,1024]{1,0:T(8,128)S(1)}, f32[8,1024]{1,0:T(8,128)S(1)}, u32[]{:S(2)}, u32[]{:S(2)}) collective-permute-start(f32[8,1024]{1,0:T(8,128)S(1)} %get-tuple-element.192.refs_0_), channel_id=1, source_target_pairs={{0,1},{1,2},{2,3},{3,0},{4,5},{5,6},{6,7},{7,4},{8,9},{9,10},{10,1... | collective-permute-start | bytes 98312 | tf_op jit(solution)/shard_map/ppermute | solution.py:855
  84.8 21.0 %copy-start.40 = (f32[8,768]{1,0:T(8,128)}, f32[8,768]{1,0:T(8,128)S(1)}, u32[]{:S(2)}) copy-start(f32[8,768]{1,0:T(8,128)S(1)} %get-tuple-element.267.refs_5_) | copy-start | bytes 73732
  84.8 21.0 %collective-permute-start.11 = (f32[136,768]{1,0:T(8,128)S(1)}, f32[136,768]{1,0:T(8,128)S(1)}, u32[]{:S(2)}, u32[]{:S(2)}) collective-permute-start(f32[136,768]{1,0:T(8,128)S(1)} %get-tuple-element.197), channel_id=1, source_target_pairs={{12,0},{13,1},{14,2},{15,3},{28,16},{29,17},{30,18},{31,19}} | collective-permute-start | bytes 1253384 | tf_op jit(solution)/shard_map/ppermute | solution.py:850
  86.1 19.7 %collective-permute-start.10 = (f32[136,768]{1,0:T(8,128)S(1)}, f32[136,768]{1,0:T(8,128)S(1)}, u32[]{:S(2)}, u32[]{:S(2)}) collective-permute-start(f32[136,768]{1,0:T(8,128)S(1)} %get-tuple-element.197), channel_id=1, source_target_pairs={{8,0},{12,4},{9,1},{13,5},{10,2},{14,6},{11,3},{15,7},{24,16},{28,... | collective-permute-start | bytes 1253384 | tf_op jit(solution)/shard_map/ppermute | solution.py:850
  87.4 18.4 %collective-permute-start.9 = (f32[136,768]{1,0:T(8,128)S(1)}, f32[136,768]{1,0:T(8,128)S(1)}, u32[]{:S(2)}, u32[]{:S(2)}) collective-permute-start(f32[136,768]{1,0:T(8,128)S(1)} %get-tuple-element.197), channel_id=1, source_target_pairs={{4,0},{8,4},{12,8},{5,1},{9,5},{13,9},{6,2},{10,6},{14,10},{7,3},{... | collective-permute-start | bytes 1253384 | tf_op jit(solution)/shard_map/ppermute | solution.py:850
  107.4 211.4 %all-gather.2.cloned.1.call-start = ((), (), s32[]{:S(2)}) async-start(), calls=%async_computation.2 | async-start | bytes 2949120 | tf_op jit(solution)/shard_map/all_gather | solution.py:1534
  107.5 26.1 %collective-permute-start.13 = (bf16[1024,768]{1,0:T(8,128)(2,1)}, bf16[1024,768]{1,0:T(8,128)(2,1)}, u32[]{:S(2)}, u32[]{:S(2)}) collective-permute-start(bf16[1024,768]{1,0:T(8,128)(2,1)} %get-tuple-element.218.refs_19_.gate_ref), channel_id=1, source_target_pairs={{0,16},{16,0},{1,17},{17,1},{2,18},{18,2},{3,19},{19,3},{4,20},{20... | collective-permute-start | bytes 4718600 | tf_op jit(solution)/shard_map/ppermute | solution.py:863
  107.6 26.0 %collective-permute-start.14 = (bf16[1024,768]{1,0:T(8,128)(2,1)}, bf16[1024,768]{1,0:T(8,128)(2,1)}, u32[]{:S(2)}, u32[]{:S(2)}) collective-permute-start(bf16[1024,768]{1,0:T(8,128)(2,1)} %get-tuple-element.219.normed_ref.refs_21_), channel_id=1, source_target_pairs={{0,16},{16,0},{1,17},{17,1},{2,18},{18,2},{3,19},{19,3},{4,20},{20... | collective-permute-start | bytes 4718600 | tf_op jit(solution)/shard_map/ppermute | solution.py:863
  120.7 6.0 %collective-permute-start.12 = (f32[8,512]{1,0:T(8,128)S(1)}, f32[8,512]{1,0:T(8,128)S(1)}, u32[]{:S(2)}, u32[]{:S(2)}) collective-permute-start(f32[8,512]{1,0:T(8,128)S(1)} %get-tuple-element.209), channel_id=1, source_target_pairs={{4,0},{8,4},{12,8},{5,1},{9,5},{13,9},{6,2},{10,6},{14,10},{7,3},{... | collective-permute-start | bytes 49160 | tf_op jit(solution)/shard_map/ppermute | solution.py:850
  129.4 34.6 %collective-permute-start.15 = (f32[520,128]{1,0:T(8,128)}, f32[520,128]{1,0:T(8,128)S(1)}, u32[]{:S(2)}, u32[]{:S(2)}) collective-permute-start(f32[520,128]{1,0:T(8,128)} %get-tuple-element.223), channel_id=1, source_target_pairs={{0,1},{1,2},{2,3},{3,0},{4,5},{5,6},{6,7},{7,4},{8,9},{9,10},{10,1... | collective-permute-start | bytes 798728 | tf_op jit(solution)/shard_map/ppermute | solution.py:1488
  129.4 35.7 %collective-permute-start.16 = (f32[520,128]{1,0:T(8,128)}, f32[520,128]{1,0:T(8,128)S(1)}, u32[]{:S(2)}, u32[]{:S(2)}) collective-permute-start(f32[520,128]{1,0:T(8,128)} %get-tuple-element.224), channel_id=1, source_target_pairs={{0,2},{1,3},{2,0},{3,1},{4,6},{5,7},{6,4},{7,5},{8,10},{9,11},{10,... | collective-permute-start | bytes 798728 | tf_op jit(solution)/shard_map/ppermute | solution.py:1488
  130.6 34.5 %collective-permute-start.17 = (f32[520,128]{1,0:T(8,128)}, f32[520,128]{1,0:T(8,128)S(1)}, u32[]{:S(2)}, u32[]{:S(2)}) collective-permute-start(f32[520,128]{1,0:T(8,128)} %get-tuple-element.225), channel_id=1, source_target_pairs={{0,3},{1,0},{2,1},{3,2},{4,7},{5,4},{6,5},{7,6},{8,11},{9,8},{10,9... | collective-permute-start | bytes 798728 | tf_op jit(solution)/shard_map/ppermute | solution.py:1488
  133.6 31.6 %copy-start.9 = (f32[1024,256]{1,0:T(8,128)S(1)}, f32[1024,256]{1,0:T(8,128)}, u32[]{:S(2)}) copy-start(f32[1024,256]{1,0:T(8,128)} %copy-done.8) | copy-start | bytes 3145732
  133.6 31.6 %copy-start.29 = (bf16[1024,256]{1,0:T(8,128)(2,1)S(1)}, bf16[1024,256]{1,0:T(8,128)(2,1)}, u32[]{:S(2)}) copy-start(bf16[1024,256]{1,0:T(8,128)(2,1)} %copy-done.28) | copy-start | bytes 1572868
  133.6 31.6 %copy-start.34 = (f32[520,128]{1,0:T(8,128)S(1)}, f32[520,128]{1,0:T(8,128)}, u32[]{:S(2)}) copy-start(f32[520,128]{1,0:T(8,128)} %copy-done.33) | copy-start | bytes 798724
  162.6 6.7 %collective-permute-start.18 = (f32[8,768]{1,0:T(8,128)S(1)}, f32[8,768]{1,0:T(8,128)S(1)}, u32[]{:S(2)}, u32[]{:S(2)}) collective-permute-start(f32[8,768]{1,0:T(8,128)S(1)} %get-tuple-element.222), channel_id=1, source_target_pairs={{4,0},{8,4},{12,8},{5,1},{9,5},{13,9},{6,2},{10,6},{14,10},{7,3},{... | collective-permute-start | bytes 73736 | tf_op jit(solution)/shard_map/ppermute | solution.py:850
  169.3 3.5 %collective-permute-start.19 = (bf16[1024,768]{1,0:T(8,128)(2,1)S(1)}, bf16[1024,768]{1,0:T(8,128)(2,1)S(1)}, u32[]{:S(2)}, u32[]{:S(2)}) collective-permute-start(bf16[1024,768]{1,0:T(8,128)(2,1)S(1)} %shard_map.256.refs_2_.value_ref), channel_id=1, source_target_pairs={{0,16},{16,0},{1,17},{17,1},{2,18},{18,2},{3,19},{19,3},{4,20},{20... | collective-permute-start | bytes 4718600 | tf_op jit(solution)/shard_map/ppermute | solution.py:863
  169.4 64.7 %collective-permute-start.24 = (f32[768,384]{1,0:T(8,128)}, f32[768,384]{1,0:T(8,128)}, u32[]{:S(2)}, u32[]{:S(2)}) collective-permute-start(f32[768,384]{1,0:T(8,128)} %get-tuple-element.247), channel_id=1, source_target_pairs={{0,4},{4,0},{8,12},{12,8},{1,5},{5,1},{9,13},{13,9},{2,6},{6,2},{1... | collective-permute-start | bytes 3538952 | tf_op jit(solution)/shard_map/ppermute | solution.py:863
  172.4 61.7 %collective-permute-start.25 = (f32[768,384]{1,0:T(8,128)}, f32[768,384]{1,0:T(8,128)}, u32[]{:S(2)}, u32[]{:S(2)}) collective-permute-start(f32[768,384]{1,0:T(8,128)} %get-tuple-element.248), channel_id=1, source_target_pairs={{0,8},{4,12},{8,0},{12,4},{1,9},{5,13},{9,1},{13,5},{2,10},{6,14},... | collective-permute-start | bytes 3538952 | tf_op jit(solution)/shard_map/ppermute | solution.py:863
  172.4 12.7 %collective-permute-start.20 = (bf16[1024,128]{1,0:T(8,128)(2,1)S(1)}, bf16[1024,128]{1,0:T(8,128)(2,1)S(1)}, u32[]{:S(2)}, u32[]{:S(2)}) collective-permute-start(bf16[1024,128]{1,0:T(8,128)(2,1)S(1)} %get-tuple-element.231.narrow_ref.narrow_a), channel_id=1, source_target_pairs={{0,16},{16,0},{1,17},{17,1},{2,18},{18,2},{3,19},{19,3},{4,20},{20... | collective-permute-start | bytes 786440 | tf_op jit(solution)/shard_map/ppermute | solution.py:863
  182.1 58.6 %collective-permute-start.26 = (f32[384,384]{1,0:T(8,128)}, f32[384,384]{1,0:T(8,128)}, u32[]{:S(2)}, u32[]{:S(2)}) collective-permute-start(f32[384,384]{1,0:T(8,128)} %get-tuple-element.253), channel_id=1, source_target_pairs={{0,4},{4,0},{8,12},{12,8},{1,5},{5,1},{9,13},{13,9},{2,6},{6,2},{1... | collective-permute-start | bytes 1769480 | tf_op jit(solution)/shard_map/ppermute | solution.py:863
  185.1 55.7 %collective-permute-start.27 = (f32[384,384]{1,0:T(8,128)}, f32[384,384]{1,0:T(8,128)}, u32[]{:S(2)}, u32[]{:S(2)}) collective-permute-start(f32[384,384]{1,0:T(8,128)} %get-tuple-element.254), channel_id=1, source_target_pairs={{0,8},{4,12},{8,0},{12,4},{1,9},{5,13},{9,1},{13,5},{2,10},{6,14},... | collective-permute-start | bytes 1769480 | tf_op jit(solution)/shard_map/ppermute | solution.py:863
  197.3 31.4 %copy-start.36 = (f32[16,256]{1,0:T(8,128)}, f32[16,256]{1,0:T(8,128)S(1)}, u32[]{:S(2)}) copy-start(f32[16,256]{1,0:T(8,128)S(1)} %shard_map.259.refs_0_) | copy-start | bytes 49156
  197.3 21.4 %collective-permute-start.23 = (f32[16,256]{1,0:T(8,128)S(1)}, f32[16,256]{1,0:T(8,128)S(1)}, u32[]{:S(2)}, u32[]{:S(2)}) collective-permute-start(f32[16,256]{1,0:T(8,128)S(1)} %shard_map.259.refs_0_), channel_id=1, source_target_pairs={{0,3},{1,0},{2,1},{3,2},{4,7},{5,4},{6,5},{7,6},{8,11},{9,8},{10,9... | collective-permute-start | bytes 49160 | tf_op jit(solution)/shard_map/ppermute | solution.py:855
  218.7 7.4 %collective-permute-start.22 = (f32[16,256]{1,0:T(8,128)S(1)}, f32[16,256]{1,0:T(8,128)S(1)}, u32[]{:S(2)}, u32[]{:S(2)}) collective-permute-start(f32[16,256]{1,0:T(8,128)S(1)} %shard_map.259.refs_0_), channel_id=1, source_target_pairs={{0,2},{1,3},{2,0},{3,1},{4,6},{5,7},{6,4},{7,5},{8,10},{9,11},{10,... | collective-permute-start | bytes 49160 | tf_op jit(solution)/shard_map/ppermute | solution.py:855
  226.0 6.7 %collective-permute-start.21 = (f32[16,256]{1,0:T(8,128)S(1)}, f32[16,256]{1,0:T(8,128)S(1)}, u32[]{:S(2)}, u32[]{:S(2)}) collective-permute-start(f32[16,256]{1,0:T(8,128)S(1)} %shard_map.259.refs_0_), channel_id=1, source_target_pairs={{0,1},{1,2},{2,3},{3,0},{4,5},{5,6},{6,7},{7,4},{8,9},{9,10},{10,1... | collective-permute-start | bytes 49160 | tf_op jit(solution)/shard_map/ppermute | solution.py:855
  232.7 23.6 %collective-permute-start.29 = (bf16[1024,384]{1,0:T(8,128)(2,1)S(1)}, bf16[1024,384]{1,0:T(8,128)(2,1)S(1)}, u32[]{:S(2)}, u32[]{:S(2)}) collective-permute-start(bf16[1024,384]{1,0:T(8,128)(2,1)S(1)} %shard_map.260), channel_id=1, source_target_pairs={{0,1},{3,2},{4,5},{7,6},{8,9},{11,10},{12,13},{15,14},{16,17},{19,... | collective-permute-start | bytes 2359304 | tf_op jit(solution)/shard_map/ppermute | solution.py:1517
  237.9 16.5 %collective-permute-start.30 = (f32[384,384]{1,0:T(8,128)}, f32[384,384]{1,0:T(8,128)S(1)}, u32[]{:S(2)}, u32[]{:S(2)}) collective-permute-start(f32[384,384]{1,0:T(8,128)} %get-tuple-element.272), channel_id=1, source_target_pairs={{0,8},{4,12},{8,0},{12,4},{1,9},{5,13},{9,1},{13,5},{2,10},{6,14},... | collective-permute-start | bytes 1769480 | tf_op jit(solution)/shard_map/ppermute | solution.py:863
  239.8 16.5 %collective-permute-start.31 = (f32[384,384]{1,0:T(8,128)}, f32[384,384]{1,0:T(8,128)S(1)}, u32[]{:S(2)}, u32[]{:S(2)}) collective-permute-start(f32[384,384]{1,0:T(8,128)} %get-tuple-element.273), channel_id=1, source_target_pairs={{0,4},{4,0},{8,12},{12,8},{1,5},{5,1},{9,13},{13,9},{2,6},{6,2},{1... | collective-permute-start | bytes 1769480 | tf_op jit(solution)/shard_map/ppermute | solution.py:863
  244.2 1.3 collective-permute-start.28
  244.3 14.5 %collective-permute-start.32 = (f32[192,384]{1,0:T(8,128)}, f32[192,384]{1,0:T(8,128)S(1)}, u32[]{:S(2)}, u32[]{:S(2)}) collective-permute-start(f32[192,384]{1,0:T(8,128)} %get-tuple-element.274), channel_id=1, source_target_pairs={{0,8},{4,12},{8,0},{12,4},{1,9},{5,13},{9,1},{13,5},{2,10},{6,14},... | collective-permute-start | bytes 884744 | tf_op jit(solution)/shard_map/ppermute | solution.py:863
  245.5 14.0 %collective-permute-start.33 = (f32[192,384]{1,0:T(8,128)}, f32[192,384]{1,0:T(8,128)S(1)}, u32[]{:S(2)}, u32[]{:S(2)}) collective-permute-start(f32[192,384]{1,0:T(8,128)} %get-tuple-element.275), channel_id=1, source_target_pairs={{0,4},{4,0},{8,12},{12,8},{1,5},{5,1},{9,13},{13,9},{2,6},{6,2},{1... | collective-permute-start | bytes 884744 | tf_op jit(solution)/shard_map/ppermute | solution.py:863
  264.0 18.5 %copy-start.31 = (f32[288,384]{1,0:T(8,128)S(1)}, f32[288,384]{1,0:T(8,128)}, u32[]{:S(2)}) copy-start(f32[288,384]{1,0:T(8,128)} %copy-done.30) | copy-start | bytes 1327108
  264.0 18.5 %collective-permute-start.34 = (bf16[1024,384]{1,0:T(8,128)(2,1)}, bf16[1024,384]{1,0:T(8,128)(2,1)S(1)}, u32[]{:S(2)}, u32[]{:S(2)}) collective-permute-start(bf16[1024,384]{1,0:T(8,128)(2,1)} %copy-done.50), channel_id=1, source_target_pairs={{0,1},{1,2},{4,5},{5,6},{8,9},{9,10},{12,13},{13,14},{16,17},{17,1... | collective-permute-start | bytes 2359304 | tf_op jit(solution)/shard_map/ppermute | solution.py:929
  265.5 17.0 %collective-permute-start.35 = (bf16[1024,384]{1,0:T(8,128)(2,1)}, bf16[1024,384]{1,0:T(8,128)(2,1)S(1)}, u32[]{:S(2)}, u32[]{:S(2)}) collective-permute-start(bf16[1024,384]{1,0:T(8,128)(2,1)} %copy-done.49), channel_id=1, source_target_pairs={{3,2},{2,1},{7,6},{6,5},{11,10},{10,9},{15,14},{14,13},{19,18},{18... | collective-permute-start | bytes 2359304 | tf_op jit(solution)/shard_map/ppermute | solution.py:930
  266.2 16.3 %collective-permute-start.36 = (f32[288,384]{1,0:T(8,128)}, f32[288,384]{1,0:T(8,128)S(1)}, u32[]{:S(2)}, u32[]{:S(2)}) collective-permute-start(f32[288,384]{1,0:T(8,128)} %copy-done.51), channel_id=1, source_target_pairs={{0,4},{4,0},{8,12},{12,8},{1,5},{5,1},{9,13},{13,9},{2,6},{6,2},{1... | collective-permute-start | bytes 1327112 | tf_op jit(solution)/shard_map/ppermute | solution.py:863
  282.5 11.6 %collective-permute-start.39 = (f32[144,384]{1,0:T(8,128)S(1)}, f32[144,384]{1,0:T(8,128)S(1)}, u32[]{:S(2)}, u32[]{:S(2)}) collective-permute-start(f32[144,384]{1,0:T(8,128)S(1)} %get-tuple-element.308), channel_id=1, source_target_pairs={{0,8},{4,12},{8,0},{12,4},{1,9},{5,13},{9,1},{13,5},{2,10},{6,14},... | collective-permute-start | bytes 663560 | tf_op jit(solution)/shard_map/ppermute | solution.py:863
  287.4 19.2 %collective-permute-start.37 = (bf16[1024,384]{1,0:T(8,128)(2,1)}, bf16[1024,384]{1,0:T(8,128)(2,1)S(1)}, u32[]{:S(2)}, u32[]{:S(2)}) collective-permute-start(bf16[1024,384]{1,0:T(8,128)(2,1)} %get-tuple-element.306), channel_id=1, source_target_pairs={{0,1},{1,2},{2,3},{4,5},{5,6},{6,7},{8,9},{9,10},{10,11},{12,13},{... | collective-permute-start | bytes 2359304 | tf_op jit(solution)/shard_map/ppermute | solution.py:929
  292.9 17.8 %collective-permute-start.38 = (bf16[1024,384]{1,0:T(8,128)(2,1)}, bf16[1024,384]{1,0:T(8,128)(2,1)S(1)}, u32[]{:S(2)}, u32[]{:S(2)}) collective-permute-start(bf16[1024,384]{1,0:T(8,128)(2,1)} %get-tuple-element.307), channel_id=1, source_target_pairs={{3,2},{2,1},{1,0},{7,6},{6,5},{5,4},{11,10},{10,9},{9,8},{15,14},{... | collective-permute-start | bytes 2359304 | tf_op jit(solution)/shard_map/ppermute | solution.py:930
  294.9 20.8 %collective-permute-start.42 = (bf16[512,384]{1,0:T(8,128)(2,1)S(1)}, bf16[512,384]{1,0:T(8,128)(2,1)S(1)}, u32[]{:S(2)}, u32[]{:S(2)}) collective-permute-start(bf16[512,384]{1,0:T(8,128)(2,1)S(1)} %pad_maximum_fusion.refs_0_), channel_id=1, source_target_pairs={{0,12},{4,8},{8,4},{12,0},{1,13},{5,9},{9,5},{13,1},{2,14},{6,10},... | collective-permute-start | bytes 1179656 | tf_op jit(solution)/shard_map/ppermute | solution.py:863
  294.9 23.9 %collective-permute-start.41 = (bf16[512,384]{1,0:T(8,128)(2,1)S(1)}, bf16[512,384]{1,0:T(8,128)(2,1)S(1)}, u32[]{:S(2)}, u32[]{:S(2)}) collective-permute-start(bf16[512,384]{1,0:T(8,128)(2,1)S(1)} %pad_maximum_fusion.refs_0_), channel_id=1, source_target_pairs={{0,8},{4,12},{8,0},{12,4},{1,9},{5,13},{9,1},{13,5},{2,10},{6,14},... | collective-permute-start | bytes 1179656 | tf_op jit(solution)/shard_map/ppermute | solution.py:863
  295.7 23.1 %collective-permute-start.40 = (bf16[512,384]{1,0:T(8,128)(2,1)S(1)}, bf16[512,384]{1,0:T(8,128)(2,1)S(1)}, u32[]{:S(2)}, u32[]{:S(2)}) collective-permute-start(bf16[512,384]{1,0:T(8,128)(2,1)S(1)} %pad_maximum_fusion.refs_0_), channel_id=1, source_target_pairs={{0,4},{4,0},{8,12},{12,8},{1,5},{5,1},{9,13},{13,9},{2,6},{6,2},{1... | collective-permute-start | bytes 1179656 | tf_op jit(solution)/shard_map/ppermute | solution.py:863
  318.8 4.8 %collective-permute-start.43 = (bf16[3072,384]{1,0:T(8,128)(2,1)}, bf16[3072,384]{1,0:T(8,128)(2,1)S(1)}, u32[]{:S(2)}, u32[]{:S(2)}) collective-permute-start(bf16[3072,384]{1,0:T(8,128)(2,1)} %all-gather.2.cloned.1.call-done.here), channel_id=1, source_target_pairs={{0,16},{16,0},{1,17},{17,1},{2,18},{18,2},{3,19},{19,3},{4,20},{20... | collective-permute-start | bytes 7077896 | tf_op jit(solution)/shard_map/ppermute | solution.py:863
  320.1 8.0 %collective-permute-start.44 = (bf16[2048,384]{1,0:T(8,128)(2,1)}, bf16[2048,384]{1,0:T(8,128)(2,1)S(1)}, u32[]{:S(2)}, u32[]{:S(2)}) collective-permute-start(bf16[2048,384]{1,0:T(8,128)(2,1)} %shard_map.271.here), channel_id=1, source_target_pairs={{0,16},{16,0},{1,17},{17,1},{2,18},{18,2},{3,19},{19,3},{4,20},{20... | collective-permute-start | bytes 4718600 | tf_op jit(solution)/shard_map/ppermute | solution.py:863
  (45 other events, 325.4 us)
Sparse Core Ops, SparseCore 0:
  107.6 129.9 reduce-scatter.1
Sparse Core Ops, SparseCore 1:
  264.1 53.9 all-gather.1
